TPU v7x, 32 devices: a whole 2x2x4 slice. The times are simulated.
32 devices in a mesh: dp: 8 (over z, x), head: 4 (over y, core).
Axes of the slice: x: 2, y: 2, z: 4, core: 2. Of those that a mesh axis runs over, the one named last changes fastest.
Arguments:
- layer_input: bfloat16 [4096, 768], P(('dp', 'head')), may hold values from -6 to 6
- segment_ids: int32 [4096], P('dp'), may hold values from 0 to 132, as said below
- upstream: bfloat16 [4096, 768], P(('dp', 'head')), may hold values from -6 to 6
- query_weight: float32 [768, 768], P(('dp', 'head')), may hold values from -0.21875 to 0.21875
- key_weight: float32 [768, 768], P(('dp', 'head')), may hold values from -0.21875 to 0.21875
- value_weight: float32 [768, 768], P(('dp', 'head')), may hold values from -0.21875 to 0.21875
- query_bias: float32 [768], P(('dp', 'head')), may hold values from -3 to 3
- value_bias: float32 [768], P(('dp', 'head')), may hold values from -0.6 to 0.6
- output_weight: float32 [768, 768], P(('dp', 'head')), may hold values from -1.75 to 1.75
- output_bias: float32 [768], P(('dp', 'head')), may hold values from -3 to 3
- attn_gain: float32 [768], P(('dp', 'head')), may hold values from 0.5 to 1.5
- attn_shift: float32 [768], P(('dp', 'head')), may hold values from -3 to 3
- up_weight: float32 [768, 3072], P(('dp', 'head')), may hold values from -0.21875 to 0.21875
- up_bias: float32 [3072], P(('dp', 'head')), may hold values from -3 to 3
- down_weight: float32 [3072, 768], P(('dp', 'head')), may hold values from -0.109375 to 0.109375
- down_bias: float32 [768], P(('dp', 'head')), may hold values from -3 to 3
- final_gain: float32 [768], P(('dp', 'head')), may hold values from 0.5 to 1.5
- final_shift: float32 [768], P(('dp', 'head')), may hold values from -3 to 3
Outputs:
- layer_output: bfloat16 [4096, 768], P(('dp', 'head'))
- input_grad: bfloat16 [4096, 768], P(('dp', 'head'))
- query_weight_grad: float32 [768, 768], P(('dp', 'head'))
- key_weight_grad: float32 [768, 768], P(('dp', 'head'))
- value_weight_grad: float32 [768, 768], P(('dp', 'head'))
- query_bias_grad: float32 [768], P(('dp', 'head'))
- value_bias_grad: float32 [768], P(('dp', 'head'))
- output_weight_grad: float32 [768, 768], P(('dp', 'head'))
- output_bias_grad: float32 [768], P(('dp', 'head'))
- attn_gain_grad: float32 [768], P(('dp', 'head'))
- attn_shift_grad: float32 [768], P(('dp', 'head'))
- up_weight_grad: float32 [768, 3072], P(('dp', 'head'))
- up_bias_grad: float32 [3072], P(('dp', 'head'))
- down_weight_grad: float32 [3072, 768], P(('dp', 'head'))
- down_bias_grad: float32 [768], P(('dp', 'head'))
- final_gain_grad: float32 [768], P(('dp', 'head'))
- final_shift_grad: float32 [768], P(('dp', 'head'))
Inputs may be any that keep to these rules, and one draw needn't show every extreme that they name: `segment_ids`: along each packed row of 512 tokens the nonzero document numbers never fall, the row's last document is numbered 128 + 4, and 0 marks padding at the row's end, one token or more in every row; only tokens with equal numbers in one row see each other.
All inputs are finite; a program needn't handle non-finite values.
Results may differ from a plain program's by a relative error of at most 0.015.
The roundings to bfloat16 on the way count: a program that leaves them out, or rounds other values in their place, can miss the bound.
Values may be sent and summed in bfloat16 or wider, within the bound.
No kernel may reach another device: no remote copies, remote signals or barrier semaphores. Data moves between devices by JAX's collectives and lax.ppermute only.
A program may use at most 128 MiB of HBM per device.

v0:
```python
import math

import jax
import jax.numpy as jnp
from jax import lax
from jax.sharding import PartitionSpec as P

H = 12
HD = 64


EPSILON = 1e-12
NEG_FILL = -1000000000.0
BLOCK_LIMIT = 512


def layer_norm(values, gain, shift):
    center = values - jnp.mean(values, axis=-1, keepdims=True)
    spread = jnp.mean(center * center, axis=-1, keepdims=True)
    return center * lax.rsqrt(spread + EPSILON) * gain + shift


def gelu_exact(values):
    return jax.nn.gelu(values, approximate=False)


def pack_projection(query_full, key_full, value_full):
    model_width = query_full.shape[0]
    stacked = jnp.stack(
        [
            query_full.reshape(model_width, H, HD),
            key_full.reshape(model_width, H, HD),
            value_full.reshape(model_width, H, HD),
        ],
        axis=2,
    )
    return stacked.reshape(model_width, 3 * model_width)


def attend_forward(packed, seg_row):
    row_count = packed.shape[0]
    head_size = packed.shape[2] // 3
    block_rows = min(BLOCK_LIMIT, row_count)
    block_count = row_count // block_rows
    scale = 1.0 / math.sqrt(head_size)
    seg_blocks = seg_row.reshape(block_count, block_rows)

    def one_head(head_rows):
        queries = head_rows[:, :head_size]
        key_rows = head_rows[:, head_size : 2 * head_size]
        value_rows = head_rows[:, 2 * head_size :]

        def one_block(block_args):
            query_block, seg_block = block_args
            scores = jnp.dot(query_block, key_rows.T, preferred_element_type=jnp.float32) * scale
            same_doc = seg_block[:, None] == seg_row[None, :]
            scores = jnp.where(same_doc, scores, NEG_FILL)
            row_top = jnp.max(scores, axis=1, keepdims=True)
            raised = jnp.exp(scores - row_top)
            totals = jnp.sum(raised, axis=1, keepdims=True)
            attn_probs = (raised / totals).astype(jnp.bfloat16)
            context = jnp.dot(attn_probs, value_rows, preferred_element_type=jnp.float32)
            return (context.astype(jnp.bfloat16), (row_top + jnp.log(totals))[:, 0])

        contexts, log_sums = lax.map(
            one_block, (queries.reshape(block_count, block_rows, head_size), seg_blocks)
        )
        return (contexts.reshape(row_count, head_size), log_sums.reshape(row_count))

    contexts, log_sums = lax.map(one_head, packed.transpose(1, 0, 2))
    return (contexts.transpose(1, 0, 2), log_sums.transpose(1, 0), packed)


def attend_backward(packed, log_sums, d_context, seg_row):
    row_count = packed.shape[0]
    head_size = packed.shape[2] // 3
    block_rows = min(BLOCK_LIMIT, row_count)
    block_count = row_count // block_rows
    scale = 1.0 / math.sqrt(head_size)
    seg_blocks = seg_row.reshape(block_count, block_rows)

    def one_head(head_args):
        head_rows, head_sums, head_grads = head_args
        queries = head_rows[:, :head_size]
        key_rows = head_rows[:, head_size : 2 * head_size]
        value_rows = head_rows[:, 2 * head_size :]

        def one_block(carry, block_args):
            key_acc, value_acc = carry
            query_block, seg_block, sum_block, grad_block = block_args
            scores = jnp.dot(query_block, key_rows.T, preferred_element_type=jnp.float32) * scale
            same_doc = seg_block[:, None] == seg_row[None, :]
            scores = jnp.where(same_doc, scores, NEG_FILL)
            attn_probs = jnp.exp(scores - sum_block[:, None])
            low_probs = attn_probs.astype(jnp.bfloat16)
            d_probs = jnp.dot(grad_block, value_rows.T, preferred_element_type=jnp.float32)
            inner_sum = jnp.sum(d_probs * attn_probs, axis=1, keepdims=True)
            d_scores = (attn_probs * (d_probs - inner_sum)).astype(jnp.bfloat16)
            d_query = jnp.dot(d_scores, key_rows, preferred_element_type=jnp.float32) * scale
            key_acc = (
                key_acc
                + jnp.dot(d_scores.T, query_block, preferred_element_type=jnp.float32) * scale
            )
            value_acc = value_acc + jnp.dot(
                low_probs.T, grad_block, preferred_element_type=jnp.float32
            )
            return ((key_acc, value_acc), d_query)

        zero_rows = jnp.zeros((row_count, head_size), jnp.float32)
        (key_acc, value_acc), d_queries = lax.scan(
            one_block,
            (zero_rows, zero_rows),
            (
                queries.reshape(block_count, block_rows, head_size),
                seg_blocks,
                head_sums.reshape(block_count, block_rows),
                head_grads.reshape(block_count, block_rows, head_size),
            ),
        )
        return jnp.concatenate(
            [d_queries.reshape(row_count, head_size), key_acc, value_acc], axis=1
        ).astype(jnp.bfloat16)

    result = lax.map(
        one_head,
        (packed.transpose(1, 0, 2), log_sums.transpose(1, 0), d_context.transpose(1, 0, 2)),
    )
    return result.transpose(1, 0, 2)


def body(
    layer_input,
    segment_ids,
    upstream,
    query_weight,
    key_weight,
    value_weight,
    query_bias,
    value_bias,
    output_weight,
    output_bias,
    attn_gain,
    attn_shift,
    up_weight,
    up_bias,
    down_weight,
    down_bias,
    final_gain,
    final_shift,
):
    (
        query_full,
        key_full,
        value_full,
        output_full,
        up_full,
        down_full,
        query_bias_full,
        value_bias_full,
        output_bias_full,
        attn_gain_full,
        attn_shift_full,
        up_bias_full,
        down_bias_full,
        final_gain_full,
        final_shift_full,
    ) = (
        lax.all_gather(query_weight.astype(jnp.bfloat16), ("dp", "head"), axis=0, tiled=True),
        lax.all_gather(key_weight.astype(jnp.bfloat16), ("dp", "head"), axis=0, tiled=True),
        lax.all_gather(value_weight.astype(jnp.bfloat16), ("dp", "head"), axis=0, tiled=True),
        lax.all_gather(output_weight.astype(jnp.bfloat16), ("dp", "head"), axis=0, tiled=True),
        lax.all_gather(up_weight.astype(jnp.bfloat16), ("dp", "head"), axis=0, tiled=True),
        lax.all_gather(down_weight.astype(jnp.bfloat16), ("dp", "head"), axis=0, tiled=True),
        lax.all_gather(query_bias.astype(jnp.bfloat16), ("dp", "head"), axis=0, tiled=True),
        lax.all_gather(value_bias.astype(jnp.bfloat16), ("dp", "head"), axis=0, tiled=True),
        lax.all_gather(output_bias.astype(jnp.bfloat16), ("dp", "head"), axis=0, tiled=True),
        lax.all_gather(attn_gain.astype(jnp.bfloat16), ("dp", "head"), axis=0, tiled=True),
        lax.all_gather(attn_shift.astype(jnp.bfloat16), ("dp", "head"), axis=0, tiled=True),
        lax.all_gather(up_bias.astype(jnp.bfloat16), ("dp", "head"), axis=0, tiled=True),
        lax.all_gather(down_bias.astype(jnp.bfloat16), ("dp", "head"), axis=0, tiled=True),
        lax.all_gather(final_gain.astype(jnp.bfloat16), ("dp", "head"), axis=0, tiled=True),
        lax.all_gather(final_shift.astype(jnp.bfloat16), ("dp", "head"), axis=0, tiled=True),
    )
    tok_count = layer_input.shape[0]
    model_width = query_full.shape[0]
    group_count = lax.axis_size("head")
    packed_weight = pack_projection(query_full, key_full, value_full)
    packed_bias = jnp.stack(
        [
            query_bias_full.astype(jnp.float32).reshape(H, HD),
            jnp.zeros((H, HD), jnp.float32),
            value_bias_full.astype(jnp.float32).reshape(H, HD),
        ],
        axis=1,
    ).reshape(3 * model_width)
    qkv = jnp.dot(layer_input, packed_weight, preferred_element_type=jnp.float32) + packed_bias
    qkv = qkv.astype(jnp.bfloat16).reshape(tok_count, group_count, H // group_count, 3 * HD)
    context_heads, log_sums, kept = attend_forward(
        lax.all_to_all(qkv, "head", split_axis=1, concat_axis=0, tiled=True)[:, 0], segment_ids
    )
    context = lax.all_to_all(
        context_heads, "head", split_axis=0, concat_axis=1, tiled=True
    ).reshape(tok_count, model_width)
    first_sum = (
        layer_input.astype(jnp.float32)
        + jnp.dot(context, output_full, preferred_element_type=jnp.float32)
        + output_bias_full.astype(jnp.float32)
    )
    normed, first_back = jax.vjp(
        layer_norm,
        first_sum,
        attn_gain_full.astype(jnp.float32),
        attn_shift_full.astype(jnp.float32),
    )
    normed_low = normed.astype(jnp.bfloat16)
    hidden_pre = jnp.dot(
        normed_low, up_full, preferred_element_type=jnp.float32
    ) + up_bias_full.astype(jnp.float32)
    activated, gelu_back = jax.vjp(gelu_exact, hidden_pre)
    activated_low = activated.astype(jnp.bfloat16)
    second_sum = (
        normed
        + jnp.dot(activated_low, down_full, preferred_element_type=jnp.float32)
        + down_bias_full.astype(jnp.float32)
    )
    result, final_back = jax.vjp(
        layer_norm,
        second_sum,
        final_gain_full.astype(jnp.float32),
        final_shift_full.astype(jnp.float32),
    )
    layer_output = result.astype(jnp.bfloat16)
    query_back, key_back, value_back, output_back, up_back, down_back = (
        lax.all_gather(query_weight.astype(jnp.bfloat16), ("dp", "head"), axis=0, tiled=True),
        lax.all_gather(key_weight.astype(jnp.bfloat16), ("dp", "head"), axis=0, tiled=True),
        lax.all_gather(value_weight.astype(jnp.bfloat16), ("dp", "head"), axis=0, tiled=True),
        lax.all_gather(output_weight.astype(jnp.bfloat16), ("dp", "head"), axis=0, tiled=True),
        lax.all_gather(up_weight.astype(jnp.bfloat16), ("dp", "head"), axis=0, tiled=True),
        lax.all_gather(down_weight.astype(jnp.bfloat16), ("dp", "head"), axis=0, tiled=True),
    )
    packed_back = pack_projection(query_back, key_back, value_back)
    d_second, final_gain_grad, final_shift_grad = final_back(upstream.astype(jnp.float32))
    d_second_low = d_second.astype(jnp.bfloat16)
    down_weight_grad = jnp.dot(activated_low.T, d_second_low, preferred_element_type=jnp.float32)
    down_bias_grad = jnp.sum(d_second, axis=0)
    (d_hidden,) = gelu_back(jnp.dot(d_second_low, down_back.T, preferred_element_type=jnp.float32))
    d_hidden_low = d_hidden.astype(jnp.bfloat16)
    up_weight_grad = jnp.dot(normed_low.T, d_hidden_low, preferred_element_type=jnp.float32)
    up_bias_grad = jnp.sum(d_hidden, axis=0)
    d_normed = d_second + jnp.dot(d_hidden_low, up_back.T, preferred_element_type=jnp.float32)
    d_first, attn_gain_grad, attn_shift_grad = first_back(d_normed)
    d_first_low = d_first.astype(jnp.bfloat16)
    output_weight_grad = jnp.dot(context.T, d_first_low, preferred_element_type=jnp.float32)
    output_bias_grad = jnp.sum(d_first, axis=0)
    d_context = jnp.dot(d_first_low, output_back.T, preferred_element_type=jnp.float32)
    d_context = d_context.astype(jnp.bfloat16).reshape(tok_count, H, HD)
    d_context_heads = lax.all_to_all(d_context, "head", split_axis=1, concat_axis=0, tiled=True)
    d_packed = attend_backward(kept, log_sums, d_context_heads, segment_ids)
    d_qkv = lax.all_to_all(d_packed, "head", split_axis=0, concat_axis=1, tiled=True).reshape(
        tok_count, 3 * model_width
    )
    grad_packed = jnp.dot(layer_input.T, d_qkv, preferred_element_type=jnp.float32).reshape(
        model_width, H, 3, HD
    )
    query_weight_grad = grad_packed[:, :, 0, :].reshape(model_width, model_width)
    key_weight_grad = grad_packed[:, :, 1, :].reshape(model_width, model_width)
    value_weight_grad = grad_packed[:, :, 2, :].reshape(model_width, model_width)
    bias_packed = jnp.sum(d_qkv.astype(jnp.float32), axis=0).reshape(H, 3, HD)
    query_bias_grad = bias_packed[:, 0, :].reshape(model_width)
    value_bias_grad = bias_packed[:, 2, :].reshape(model_width)
    input_grad = (
        d_first + jnp.dot(d_qkv, packed_back.T, preferred_element_type=jnp.float32)
    ).astype(jnp.bfloat16)
    (
        query_weight_part,
        key_weight_part,
        value_weight_part,
        query_bias_part,
        value_bias_part,
        output_weight_part,
        output_bias_part,
        attn_gain_part,
        attn_shift_part,
        up_weight_part,
        up_bias_part,
        down_weight_part,
        down_bias_part,
        final_gain_part,
        final_shift_part,
    ) = (
        lax.psum_scatter(query_weight_grad, ("dp", "head"), scatter_dimension=0, tiled=True),
        lax.psum_scatter(key_weight_grad, ("dp", "head"), scatter_dimension=0, tiled=True),
        lax.psum_scatter(value_weight_grad, ("dp", "head"), scatter_dimension=0, tiled=True),
        lax.psum_scatter(query_bias_grad, ("dp", "head"), scatter_dimension=0, tiled=True),
        lax.psum_scatter(value_bias_grad, ("dp", "head"), scatter_dimension=0, tiled=True),
        lax.psum_scatter(output_weight_grad, ("dp", "head"), scatter_dimension=0, tiled=True),
        lax.psum_scatter(output_bias_grad, ("dp", "head"), scatter_dimension=0, tiled=True),
        lax.psum_scatter(attn_gain_grad, ("dp", "head"), scatter_dimension=0, tiled=True),
        lax.psum_scatter(attn_shift_grad, ("dp", "head"), scatter_dimension=0, tiled=True),
        lax.psum_scatter(up_weight_grad, ("dp", "head"), scatter_dimension=0, tiled=True),
        lax.psum_scatter(up_bias_grad, ("dp", "head"), scatter_dimension=0, tiled=True),
        lax.psum_scatter(down_weight_grad, ("dp", "head"), scatter_dimension=0, tiled=True),
        lax.psum_scatter(down_bias_grad, ("dp", "head"), scatter_dimension=0, tiled=True),
        lax.psum_scatter(final_gain_grad, ("dp", "head"), scatter_dimension=0, tiled=True),
        lax.psum_scatter(final_shift_grad, ("dp", "head"), scatter_dimension=0, tiled=True),
    )
    return (
        layer_output,
        input_grad,
        query_weight_part,
        key_weight_part,
        value_weight_part,
        query_bias_part,
        value_bias_part,
        output_weight_part,
        output_bias_part,
        attn_gain_part,
        attn_shift_part,
        up_weight_part,
        up_bias_part,
        down_weight_part,
        down_bias_part,
        final_gain_part,
        final_shift_part,
    )


def solution(mesh):
    placed = (
        P(("dp", "head"), None),
        P("dp"),
        P(("dp", "head"), None),
        P(("dp", "head"), None),
        P(("dp", "head"), None),
        P(("dp", "head"), None),
        P(("dp", "head")),
        P(("dp", "head")),
        P(("dp", "head"), None),
        P(("dp", "head")),
        P(("dp", "head")),
        P(("dp", "head")),
        P(("dp", "head"), None),
        P(("dp", "head")),
        P(("dp", "head"), None),
        P(("dp", "head")),
        P(("dp", "head")),
        P(("dp", "head")),
    )
    return jax.shard_map(
        body,
        mesh=mesh,
        in_specs=placed,
        out_specs=(
            P(("dp", "head"), None),
            P(("dp", "head"), None),
            P(("dp", "head"), None),
            P(("dp", "head"), None),
            P(("dp", "head"), None),
            P(("dp", "head")),
            P(("dp", "head")),
            P(("dp", "head"), None),
            P(("dp", "head")),
            P(("dp", "head")),
            P(("dp", "head")),
            P(("dp", "head"), None),
            P(("dp", "head")),
            P(("dp", "head"), None),
            P(("dp", "head")),
            P(("dp", "head")),
            P(("dp", "head")),
        ),
        check_vma=False,
    )
```

profile of v0, /device:TPU:0, one launch (start us, length us, event | category | flops | bytes accessed | tf_op | source)
XLA Modules:
  0.0 1095.6 jit_solution(7034287809141628485)
XLA Ops:
  7.3 1.5 convert_element_type.141
  8.9 1.5 convert_element_type.140
  13.7 1.6 convert_element_type.154
  15.4 1.6 convert_element_type.158
  19.1 42.9 %all-reduce.19 = (bf16[768]{0:T(1024)(128)(2,1)S(1)}, bf16[768]{0:T(1024)(128)(2,1)S(1)}, bf16[3072]{0:T(1024)(128)(2,1)}, bf16[768]{0:T(1024)(128)(2,1)}, bf16[...) all-reduce(bf16[768]{0:T(1024)(128)(2,1)S(1)} %dynamic-update-slice, ...), channel_id=1, replica_groups=mesh['dp'=8,'head'=4] {'dp','head'}, use_global_device_ids=true, to_apply=%add | all-reduce | flops 9216 | bytes 36864
  62.4 6.1 all-gather.11.cloned.1.call-done
  68.5 1.6 copy.70
  70.1 55.1 %all-gather.9.cloned.1.call-done = bf16[768,768]{1,0:T(8,128)(2,1)} async-done(((bf16[24,768]{1,0:T(8,128)(2,1)}), bf16[768,768]{1,0:T(8,128)(2,1)}) %all-gather.9.cloned.1.call-update) | async-done | bytes 1179664 | tf_op jit(solution)/shard_map/all_gather | solution.py:169
  125.2 1.6 copy.69
  126.8 55.0 %all-gather.7.cloned.1.call-done = bf16[768,768]{1,0:T(8,128)(2,1)} async-done(((bf16[24,768]{1,0:T(8,128)(2,1)}), bf16[768,768]{1,0:T(8,128)(2,1)}) %all-gather.7.cloned.1.call-update) | async-done | bytes 1179664 | tf_op jit(solution)/shard_map/all_gather | solution.py:168
  181.8 1.6 copy.68
  184.7 1.9 fusion.28
  186.6 3.6 all-to-all-start
  190.3 9.8 all-to-all-done
  200.3 3.0 while.18
  204.7 3.5 all-to-all-start.1
  208.4 5.2 all-to-all-done.1
  214.2 24.1 %all-gather.13.cloned.1.call-done = bf16[768,768]{1,0:T(8,128)(2,1)} async-done(((bf16[24,768]{1,0:T(8,128)(2,1)}), bf16[768,768]{1,0:T(8,128)(2,1)}) %all-gather.13.cloned.1.call-update) | async-done | bytes 1179664 | tf_op jit(solution)/shard_map/all_gather | solution.py:171
  238.2 1.7 fusion.58
  240.2 63.9 %all-gather.15.cloned.1.call-done = bf16[768,3072]{1,0:T(8,128)(2,1)} async-done(((bf16[24,3072]{1,0:T(8,128)(2,1)}), bf16[768,3072]{1,0:T(8,128)(2,1)}) %all-gather.15.cloned.1.call-update) | async-done | bytes 4718608 | tf_op jit(solution)/shard_map/all_gather | solution.py:172
  304.1 8.4 multiply_convert_fusion.1
  312.5 57.4 %all-gather.17.cloned.1.call-done = bf16[3072,768]{1,0:T(8,128)(2,1)} async-done(((bf16[96,768]{1,0:T(8,128)(2,1)}), bf16[3072,768]{1,0:T(8,128)(2,1)}) %all-gather.17.cloned.1.call-update) | async-done | bytes 4718608 | tf_op jit(solution)/shard_map/all_gather | solution.py:173
  369.9 3.4 fusion.59
  375.2 2.5 fusion.60
  377.7 2.4 multiply_reduce_fusion.1
  382.9 3.4 all-to-all-start.2
  386.3 1.9 fusion.50
  388.3 3.2 all-to-all-done.2
  391.6 5.9 while.19
  398.3 1.6 copy.79
  399.9 16.9 %all_to_all.63 = bf16[512,3,192]{2,1,0:T(4,128)(2,1)S(1)} all-to-all(bf16[512,3,192]{2,1,0:T(4,128)(2,1)S(1)} %bitcast.147), channel_id=1, replica_groups=mesh['dp'=8,'head'=4] {'head'}, dimensions={0} | all-to-all | bytes 1179648 | tf_op jit(solution)/shard_map/all_to_all | solution.py:259
  418.5 2.7 fusion.57
  421.2 3.1 copy.93
  424.4 3.1 copy.95
  427.6 2.0 copy.97
  430.7 5.2 fusion.42
  437.1 5.1 fusion.48
  442.8 1.8 add_reduce_fusion
  444.7 1.7 add_reduce_fusion.1
  446.3 2.5 copy.91
  448.8 2.5 convert_reduce_fusion
  454.7 41.7 %all-reduce.18 = (f32[768]{0:T(1024)}, f32[768]{0:T(1024)}, f32[768]{0:T(1024)}, f32[768]{0:T(1024)}, f32[768]{0:T(1024)}, /*index=5*/f32[3072]{0:T(1024)}, f32[...) all-reduce(f32[768]{0:T(1024)} %reshape_squeeze.18, ...), channel_id=5, replica_groups=mesh['dp'=8,'head'=4] {'dp','head'}, use_global_device_ids=true, to_apply=%region_19.20.clone | all-reduce | flops 9216 | bytes 73728
  505.8 2.6 fusion.37
  508.4 88.7 %reduce-scatter.19.cloned.1.call-done = f32[24,768]{1,0:T(8,128)} async-done(((f32[768,768]{1,0:T(8,128)}), f32[24,768]{1,0:T(8,128)}) %reduce-scatter.19.cloned.1.call-update) | async-done | bytes 73744
  597.1 103.9 %reduce-scatter.21.cloned.1.call-done = f32[24,768]{1,0:T(8,128)} async-done(((f32[768,768]{1,0:T(8,128)}), f32[24,768]{1,0:T(8,128)}) %reduce-scatter.21.cloned.1.call-update) | async-done | bytes 73744
  700.9 104.7 %reduce-scatter.23.cloned.1.call-done = f32[24,768]{1,0:T(8,128)} async-done(((f32[768,768]{1,0:T(8,128)}), f32[24,768]{1,0:T(8,128)}) %reduce-scatter.23.cloned.1.call-update) | async-done | bytes 73744
  805.6 141.2 %reduce-scatter.15.cloned.1.call-done = f32[24,3072]{1,0:T(8,128)} async-done(((f32[768,3072]{1,0:T(8,128)}), f32[24,3072]{1,0:T(8,128)}) %reduce-scatter.15.cloned.1.call-update) | async-done | bytes 294928 | tf_op jit(solution)/shard_map/reduce_scatter | solution.py:300
  946.8 142.0 %reduce-scatter.17.cloned.1.call-done = f32[96,768]{1,0:T(8,128)} async-done(((f32[3072,768]{1,0:T(8,128)}), f32[96,768]{1,0:T(8,128)}) %reduce-scatter.17.cloned.1.call-update) | async-done | bytes 294928 | tf_op jit(solution)/shard_map/reduce_scatter | solution.py:302
  (237 shorter events, 41.2 us)
Async XLA Ops:
  7.2 9.9 copy-start.26
  7.2 9.9 copy-start.27
  7.2 9.9 copy-start.28
  7.2 9.9 copy-start.29
  7.2 9.9 copy-start.30
  7.2 9.9 copy-start.31
  7.3 9.9 copy-start.32
  7.3 9.9 copy-start.33
  7.3 10.0 copy-start.34
  7.3 61.2 %all-gather.11.cloned.1.call-start = ((), (), s32[]{:S(2)}) async-start(), calls=%async_computation.12 | async-start | bytes 1216512 | tf_op jit(solution)/shard_map/all_gather | solution.py:170
  8.9 116.3 %all-gather.9.cloned.1.call-start = ((), (), s32[]{:S(2)}) async-start(), calls=%async_computation.11 | async-start | bytes 1216512 | tf_op jit(solution)/shard_map/all_gather | solution.py:169
  10.4 171.3 %all-gather.7.cloned.1.call-start = ((), (), s32[]{:S(2)}) async-start(), calls=%async_computation.10 | async-start | bytes 1216512 | tf_op jit(solution)/shard_map/all_gather | solution.py:168
  12.0 226.2 %all-gather.13.cloned.1.call-start = ((), (), s32[]{:S(2)}) async-start(), calls=%async_computation.13 | async-start | bytes 1216512 | tf_op jit(solution)/shard_map/all_gather | solution.py:171
  13.6 290.5 %all-gather.15.cloned.1.call-start = ((), (), s32[]{:S(2)}) async-start(), calls=%async_computation.14 | async-start | bytes 4866048 | tf_op jit(solution)/shard_map/all_gather | solution.py:172
  15.3 354.5 %all-gather.17.cloned.1.call-start = ((), (), s32[]{:S(2)}) async-start(), calls=%async_computation.15 | async-start | bytes 4866048 | tf_op jit(solution)/shard_map/all_gather | solution.py:173
  184.2 2.5 copy-start
  186.6 13.7 %copy-start.25 = (s32[512]{0:T(512)S(1)}, s32[512]{0:T(512)}, u32[]{:S(2)}) copy-start(s32[512]{0:T(512)} %param.23) | copy-start | bytes 6148
  186.6 13.4 %all-to-all-start = ((bf16[128,4,3,192]{0,3,2,1:T(8,128)(2,1)}), bf16[128,4,3,192]{0,3,2,1:T(8,128)(2,1)S(1)}, u32[]{:S(2)}, u32[]{:S(2)}) async-start(bf16[128,4,3,192]{0,3,2,1:T(8,128)(2,1)} %bitcast.17), calls=%async_computation | async-start | bytes 1179648 | tf_op jit(solution)/shard_map/all_to_all | solution.py:199
  203.3 5.0 copy-start.24
  203.3 5.0 copy-start.17
  203.3 5.0 copy-start.23
  203.3 5.0 copy-start.22
  203.3 5.0 copy-start.21
  203.3 5.0 copy-start.20
  204.7 8.9 all-to-all-start.1
  312.5 60.8 %copy-start.8 = (bf16[128,3072]{1,0:T(8,128)(2,1)}, bf16[128,3072]{1,0:T(8,128)(2,1)S(1)}, u32[]{:S(2)}) copy-start(bf16[128,3072]{1,0:T(8,128)(2,1)S(1)} %get-tuple-element.268) | copy-start | bytes 2359300
  369.9 5.3 slice-start
  369.9 3.6 copy-start.12
  369.9 5.3 slice-start.1
  369.9 5.3 copy-start.36
  373.3 1.9 copy-start.35
  374.3 3.4 slice-start.2
  375.2 2.5 copy-start.5
  375.2 2.5 copy-start.18
  375.2 2.5 slice-start.3
  377.7 2.4 copy-start.10
  380.1 1.4 copy-start.7
  380.3 7.9 copy-start.2
  380.4 7.9 copy-start.15
  382.9 8.7 all-to-all-start.2
  386.2 122.1 %reduce-scatter.13.cloned.1.call-start = ((), (), s32[]{:S(2)}) async-start(), calls=%async_computation.16 | async-start | bytes 2433024 | tf_op jit(solution)/shard_map/reduce_scatter | solution.py:296
  388.2 208.8 %reduce-scatter.19.cloned.1.call-start = ((), (), s32[]{:S(2)}) async-start(), calls=%async_computation.19 | async-start | bytes 2433024
  416.8 1.7 copy-start.3
  424.4 276.6 %reduce-scatter.21.cloned.1.call-start = ((), (), s32[]{:S(2)}) async-start(), calls=%async_computation.20 | async-start | bytes 2433024
  427.6 378.1 %reduce-scatter.23.cloned.1.call-start = ((), (), s32[]{:S(2)}) async-start(), calls=%async_computation.21 | async-start | bytes 2433024
  429.6 517.2 %reduce-scatter.15.cloned.1.call-start = ((), (), s32[]{:S(2)}) async-start(), calls=%async_computation.17 | async-start | bytes 9732096 | tf_op jit(solution)/shard_map/reduce_scatter | solution.py:300
  435.9 652.9 %reduce-scatter.17.cloned.1.call-start = ((), (), s32[]{:S(2)}) async-start(), calls=%async_computation.18 | async-start | bytes 9732096 | tf_op jit(solution)/shard_map/reduce_scatter | solution.py:302
  442.8 63.0 %copy-start.1 = (bf16[768,12,3,64]{0,3,2,1:T(8,128)(2,1)S(1)}, bf16[768,12,3,64]{0,3,2,1:T(8,128)(2,1)}, u32[]{:S(2)}) copy-start(bf16[768,12,3,64]{0,3,2,1:T(8,128)(2,1)} %copy-done) | copy-start | bytes 10616836
  (8 other events, 8.1 us)
Sparse Core Ops, SparseCore 0:
  11.6 56.8 all-gather.10
  72.0 53.1 all-gather.8
  128.7 53.0 all-gather.6
  185.1 53.0 all-gather.12
  241.6 62.5 all-gather.14
  307.4 62.3 all-gather.16
  392.9 99.2 reduce-scatter.12
  499.0 98.0 reduce-scatter.18
  602.9 97.9 reduce-scatter.20
  707.5 98.0 reduce-scatter.22
  812.1 134.6 reduce-scatter.14
  954.2 134.5 reduce-scatter.16
where the time goes:
time: 1100 us
  waiting for transfers between devices  860 us (78%)
  blocking collectives  102 us (9%)
  local copies, waits for them, and re-layouts  44.3 us (4%)
  matrix products  43.3 us (4%)
  other arithmetic  19.7 us (2%)
  between operations  15 us (1%)
  starting transfers between devices  11 us (1%)
    unnamed x15, waiting for transfers between devices  297 us
    reduce_scatter x1, waiting for transfers between devices, body(): lax.psum_scatter(down_weight_grad, ('dp', 'head'), scatter_dimension=0, t...  142 us
    reduce_scatter x1, waiting for transfers between devices, body(): lax.psum_scatter(up_weight_grad, ('dp', 'head'), scatter_dimension=0, til...  141 us
    unnamed x2, blocking collectives  84.6 us
    all_gather x1, waiting for transfers between devices, body(): lax.all_gather(up_weight.astype(jnp.bfloat16), ('dp', 'head'), axis=0, ti...  63.9 us
    all_gather x1, waiting for transfers between devices, body(): lax.all_gather(down_weight.astype(jnp.bfloat16), ('dp', 'head'), axis=0,...  57.4 us
    all_gather x1, waiting for transfers between devices, body(): lax.all_gather(key_weight.astype(jnp.bfloat16), ('dp', 'head'), axis=0, t...  55.1 us
    all_gather x1, waiting for transfers between devices, body(): lax.all_gather(query_weight.astype(jnp.bfloat16), ('dp', 'head'), axis=0,...  55 us
  transfers between devices with their start and end apart: 15, of which 14 were waited for; matrix products, arithmetic and copies ran while one was open for 8% of the time, Pallas kernels for 0%

commit v1 on v0

v1 whole, which is shorter than its diff:
```python
import math

import jax
import jax.numpy as jnp
from jax import lax
from jax.sharding import PartitionSpec as P

H = 12
HD = 64
EPSILON = 1e-12
NEG_FILL = -1000000000.0
BF = jnp.bfloat16
F32 = jnp.float32
ALL = ("dp", "head")
CORE = [(i, i ^ 1) for i in range(4)]
CHIP = [(i, i ^ 2) for i in range(4)]
XSWAP = [(i, i ^ 1) for i in range(8)]


def zshift(k):
    return [(i, (i + 2 * k) % 8) for i in range(8)]


def dot(left, right):
    return jnp.dot(left, right, preferred_element_type=F32)


def gather_dp(piece):
    count = lax.axis_size("dp")
    if count != 8:
        return lax.all_gather(piece, "dp", axis=0, tiled=True)
    place = lax.axis_index("dp")
    found = [piece] + [lax.ppermute(piece, "dp", zshift(k)) for k in (1, 2, 3)]
    found = jnp.stack(found + [lax.ppermute(part, "dp", XSWAP) for part in found])
    wanted = jnp.arange(8)
    order = (place // 2 - wanted // 2) % 4 + 4 * ((place ^ wanted) & 1)
    return jnp.take(found, order, axis=0).reshape(8 * piece.shape[0], piece.shape[1])


def scatter_dp(whole):
    count = lax.axis_size("dp")
    rows = whole.shape[0] // count
    if count != 8:
        return lax.psum_scatter(whole, "dp", scatter_dimension=0, tiled=True)
    place = lax.axis_index("dp")
    chunks = whole.reshape(4, 2, rows, whole.shape[1])
    mine = lax.dynamic_index_in_dim(chunks, place % 2, 1, keepdims=False)
    theirs = lax.dynamic_index_in_dim(chunks, 1 - place % 2, 1, keepdims=False).astype(BF)
    mine = mine + lax.ppermute(theirs, "dp", XSWAP).astype(F32)
    total = lax.dynamic_index_in_dim(mine, place // 2, 0, keepdims=False)
    for k in (1, 2, 3):
        part = lax.dynamic_index_in_dim(mine, (place // 2 + k) % 4, 0, keepdims=False)
        total = total + lax.ppermute(part.astype(BF), "dp", zshift(k)).astype(F32)
    return total


def blocks(values, order):
    tokens = values.shape[0] // 4
    parts = values.reshape(4, tokens, values.shape[1])
    return jnp.concatenate([parts[i] for i in order], axis=0)


def norm_stats(values):
    center = values - jnp.mean(values, axis=-1, keepdims=True)
    spread = jnp.mean(center * center, axis=-1, keepdims=True)
    rate = lax.rsqrt(spread + EPSILON)
    return center * rate, rate


def norm_back(unit, rate, dyg):
    return rate * (
        dyg
        - jnp.mean(dyg, axis=-1, keepdims=True)
        - unit * jnp.mean(dyg * unit, axis=-1, keepdims=True)
    )


def body(
    layer_input,
    segment_ids,
    upstream,
    query_weight,
    key_weight,
    value_weight,
    query_bias,
    value_bias,
    output_weight,
    output_bias,
    attn_gain,
    attn_shift,
    up_weight,
    up_bias,
    down_weight,
    down_bias,
    final_gain,
    final_shift,
):
    tok, width = layer_input.shape
    dp_count = lax.axis_size("dp")
    heads = lax.axis_size("head")
    here = lax.axis_index("head")
    core = here % 2
    rows = query_weight.shape[0]
    group_rows = heads * rows
    share = width // heads
    hidden_piece = down_weight.shape[0]
    scale = 1.0 / math.sqrt(HD)
    my_heads = H // heads

    x_chip = lax.ppermute(layer_input, "head", CHIP)
    x_pair = jnp.concatenate([layer_input, x_chip], axis=0)
    xs = jnp.concatenate([x_pair, lax.ppermute(x_pair, "head", CORE)], axis=0)
    up_pair = jnp.concatenate([upstream, lax.ppermute(upstream, "head", CHIP)], axis=0)
    order = jnp.stack([here, here ^ 2, here ^ 1, here ^ 3])
    seg = jnp.take(segment_ids.reshape(heads, tok), order, axis=0).reshape(heads * tok)

    def by_head(weight):
        return weight.reshape(rows, heads, share).transpose(1, 0, 2)

    bias_cols = jnp.stack(
        [
            query_bias,
            value_bias,
            output_bias,
            attn_gain,
            attn_shift,
            down_bias,
            final_gain,
            final_shift,
        ],
        axis=1,
    )
    bias_cols = jnp.pad(bias_cols, ((0, 0), (0, 120)))
    first_send = jnp.concatenate(
        [
            by_head(query_weight),
            by_head(key_weight),
            by_head(value_weight),
            jnp.broadcast_to(bias_cols[None], (heads, rows, 128)),
        ],
        axis=2,
    ).astype(BF)
    first_send = first_send.reshape(group_rows, 3 * share + 128)
    first_piece = lax.all_to_all(first_send, "head", 0, 0, tiled=True)
    halves = output_weight.reshape(rows, 2, width // 2).transpose(1, 0, 2)
    up_cols = up_weight.reshape(rows, dp_count, heads, hidden_piece).transpose(2, 0, 1, 3)
    second_send = jnp.concatenate(
        [up_cols.reshape(heads, rows, width), jnp.concatenate([halves, halves], axis=0)], axis=2
    ).astype(BF)
    second_piece = lax.all_to_all(
        second_send.reshape(group_rows, width + width // 2), "head", 0, 0, tiled=True
    )
    third_piece = jnp.concatenate(
        [down_weight, jnp.pad(up_bias[:, None], ((0, 0), (0, 127)))], axis=1
    ).astype(BF)

    first_full = gather_dp(first_piece)
    second_full = gather_dp(second_piece)
    third_full = gather_dp(third_piece)
    qkv_weight = first_full[:, : 3 * share]
    bias_rows = first_full[:, 3 * share : 3 * share + 8].T.astype(F32)
    q_bias, v_bias, o_bias, a_gain, a_shift, d_bias, f_gain, f_shift = [bias_rows[i] for i in range(8)]
    q_bias = lax.dynamic_slice_in_dim(q_bias, here * share, share)
    v_bias = lax.dynamic_slice_in_dim(v_bias, here * share, share)
    up_full = second_full[:, :width]
    half = second_full[:, width:]
    other = lax.ppermute(half, "head", CORE)
    output_full = jnp.concatenate(
        [jnp.where(core == 0, half, other), jnp.where(core == 0, other, half)], axis=1
    )
    down_full = third_full[:, :width]
    u_bias = third_full[:, width].astype(F32)

    qkv_bias = jnp.concatenate([q_bias, jnp.zeros_like(q_bias), v_bias])
    qkv = (dot(xs, qkv_weight) + qkv_bias).astype(BF)
    same = seg[:, None] == seg[None, :]
    contexts, sums = [], []
    for j in range(my_heads):
        q = qkv[:, j * HD : (j + 1) * HD]
        k = qkv[:, share + j * HD : share + (j + 1) * HD]
        v = qkv[:, 2 * share + j * HD : 2 * share + (j + 1) * HD]
        scores = jnp.where(same, dot(q, k.T) * scale, NEG_FILL)
        top = jnp.max(scores, axis=1, keepdims=True)
        raised = jnp.exp(scores - top)
        totals = jnp.sum(raised, axis=1, keepdims=True)
        contexts.append(dot((raised / totals).astype(BF), v).astype(BF))
        sums.append(top + jnp.log(totals))
    ctx = jnp.concatenate(contexts, axis=1)

    ctx_chip = lax.ppermute(ctx, "head", CHIP)
    ctx_core = lax.ppermute(jnp.stack([ctx, ctx_chip]), "head", CORE)
    ctx_of = [
        (here, ctx),
        (here ^ 2, blocks(ctx_chip, (1, 0, 3, 2))),
        (here ^ 1, blocks(ctx_core[0], (2, 3, 0, 1))),
        (here ^ 3, blocks(ctx_core[1], (3, 2, 1, 0))),
    ]
    first_sum = xs.astype(F32) + o_bias
    for rank, part in ctx_of:
        first_sum = first_sum + dot(
            part, lax.dynamic_slice_in_dim(output_full, rank * share, share, 0)
        )
    unit1, rate1 = norm_stats(first_sum)
    normed = unit1 * a_gain + a_shift
    normed_low = normed.astype(BF)
    mine = 2 * tok
    unit1, rate1, normed = unit1[:mine], rate1[:mine], normed[:mine]
    pre = dot(normed_low, up_full) + u_bias
    phi = 0.5 * (1.0 + lax.erf(pre * math.sqrt(0.5)))
    act = (pre * phi).astype(BF)
    slope = phi + pre * jnp.exp(-0.5 * pre * pre) * (1.0 / math.sqrt(2 * math.pi))
    part = dot(act, down_full)

    def pair_sum(part):
        total = part[:mine] + lax.ppermute(part[mine:].astype(BF), "head", CORE).astype(F32)
        far = lax.ppermute(total.astype(BF), "head", CHIP).astype(F32)
        return total + jnp.concatenate([far[tok:], far[:tok]], axis=0)

    second = normed + pair_sum(part) + d_bias
    unit2, rate2 = norm_stats(second)
    layer_output = (unit2[:tok] * f_gain + f_shift).astype(BF)
    dy = up_pair.astype(F32)
    d_second = norm_back(unit2, rate2, dy * f_gain)
    f_gain_grad = jnp.sum(dy[:tok] * unit2[:tok], axis=0)
    f_shift_grad = jnp.sum(dy[:tok], axis=0)
    d_bias_grad = jnp.sum(d_second[:tok], axis=0)
    ds_low = d_second.astype(BF)
    ds_low = jnp.concatenate([ds_low, lax.ppermute(ds_low, "head", CORE)], axis=0)
    d_hidden = dot(ds_low, down_full.T) * slope
    u_bias_grad = jnp.sum(d_hidden, axis=0)
    dh_low = d_hidden.astype(BF)
    d_normed = d_second + pair_sum(dot(dh_low, up_full.T))
    down_grad = dot(act.T, ds_low)
    up_grad = dot(normed_low.T, dh_low)
    d_first = norm_back(unit1, rate1, d_normed * a_gain)
    a_gain_grad = jnp.sum(d_normed[:tok] * unit1[:tok], axis=0)
    a_shift_grad = jnp.sum(d_normed[:tok], axis=0)
    o_bias_grad = jnp.sum(d_first[:tok], axis=0)
    df_low = d_first.astype(BF)
    df_low = jnp.concatenate([df_low, lax.ppermute(df_low, "head", CORE)], axis=0)
    my_output = lax.dynamic_slice_in_dim(output_full, here * share, share, 0)
    d_ctx = dot(df_low, my_output.T).astype(BF)
    df_cols = lax.dynamic_slice_in_dim(df_low, here * share, share, 1)
    output_grad = jnp.zeros((width, share), F32)
    for rank, part in ctx_of:
        output_grad = lax.dynamic_update_slice_in_dim(
            output_grad, dot(part.T, df_cols), rank * share, 0
        )

    d_parts = [[], [], []]
    for j in range(my_heads):
        q = qkv[:, j * HD : (j + 1) * HD]
        k = qkv[:, share + j * HD : share + (j + 1) * HD]
        v = qkv[:, 2 * share + j * HD : 2 * share + (j + 1) * HD]
        grad = d_ctx[:, j * HD : (j + 1) * HD]
        scores = jnp.where(same, dot(q, k.T) * scale, NEG_FILL)
        probs = jnp.exp(scores - sums[j])
        low_probs = probs.astype(BF)
        d_probs = dot(grad, v.T)
        inner = jnp.sum(d_probs * probs, axis=1, keepdims=True)
        d_scores = (probs * (d_probs - inner)).astype(BF)
        d_parts[0].append((dot(d_scores, k) * scale).astype(BF))
        d_parts[1].append((dot(d_scores.T, q) * scale).astype(BF))
        d_parts[2].append(dot(low_probs.T, grad).astype(BF))
    d_qkv = jnp.concatenate(d_parts[0] + d_parts[1] + d_parts[2], axis=1)
    qkv_grad = dot(xs.T, d_qkv)
    qkv_bias_grad = jnp.sum(d_qkv.astype(F32), axis=0)
    part = dot(d_qkv, qkv_weight.T)
    total = part[:mine] + lax.ppermute(part[mine:].astype(BF), "head", CORE).astype(F32)
    far = lax.ppermute(total[tok:].astype(BF), "head", CHIP).astype(F32)
    input_grad = (d_first[:tok] + total[:tok] + far).astype(BF)

    wide = jnp.zeros((width,), F32)
    q_wide = lax.dynamic_update_slice_in_dim(wide, qkv_bias_grad[:share], here * share, 0)
    v_wide = lax.dynamic_update_slice_in_dim(wide, qkv_bias_grad[2 * share :], here * share, 0)
    bias_grads = jnp.stack(
        [
            q_wide,
            v_wide,
            o_bias_grad,
            a_gain_grad,
            a_shift_grad,
            d_bias_grad,
            f_gain_grad,
            f_shift_grad,
        ],
        axis=1,
    )
    bias_grads = jnp.pad(bias_grads, ((0, 0), (0, 120)))
    last = jnp.concatenate([qkv_grad, bias_grads], axis=1).astype(BF)
    last = lax.all_to_all(last, ALL, 0, 0, tiled=True).astype(F32)
    last = jnp.sum(last.reshape(dp_count, heads, rows, 3 * share + 128), axis=0)

    def by_row(grad):
        return grad.transpose(1, 0, 2).reshape(rows, -1)

    query_grad = by_row(last[:, :, :share])
    key_grad = by_row(last[:, :, share : 2 * share])
    value_grad = by_row(last[:, :, 2 * share : 3 * share])
    bias_out = jnp.sum(last[:, :, 3 * share : 3 * share + 8], axis=0).T

    down_part = scatter_dp(
        jnp.concatenate([down_grad, jnp.pad(u_bias_grad[:, None], ((0, 0), (0, 127)))], axis=1)
    )
    up_part = scatter_dp(jnp.concatenate([up_grad, output_grad], axis=1)).astype(BF)
    up_part = lax.all_to_all(up_part, "head", 0, 0, tiled=True).astype(F32)
    up_part = up_part.reshape(heads, rows, width + share)
    up_out = up_part[:, :, :width].reshape(heads, rows, dp_count, hidden_piece)
    up_out = up_out.transpose(1, 2, 0, 3).reshape(rows, -1)
    output_out = by_row(up_part[:, :, width:])

    return (
        layer_output,
        input_grad,
        query_grad,
        key_grad,
        value_grad,
        bias_out[0],
        bias_out[1],
        output_out,
        bias_out[2],
        bias_out[3],
        bias_out[4],
        up_out,
        down_part[:, width],
        down_part[:, :width],
        bias_out[5],
        bias_out[6],
        bias_out[7],
    )


def solution(mesh):
    matrix = P(ALL, None)
    vector = P(ALL)
    placed = (
        matrix, P("dp"), matrix, matrix, matrix, matrix, vector, vector, matrix,
        vector, vector, vector, matrix, vector, matrix, vector, vector, vector,
    )
    given = (
        matrix, matrix, matrix, matrix, matrix, vector, vector, matrix, vector,
        vector, vector, matrix, vector, matrix, vector, vector, vector,
    )
    return jax.shard_map(body, mesh=mesh, in_specs=placed, out_specs=given, check_vma=False)
```

time: 1100 us -> 324 us (0.29)
  waiting for transfers between devices: 860 us -> 135 us
  blocking collectives: 102 us -> 0 us
  starting transfers between devices: 11 us -> 61.9 us
  local copies, waits for them, and re-layouts: 44.3 us -> 65.2 us
  matrix products: 43.3 us -> 24 us
  other arithmetic: 19.7 us -> 32.9 us
  between operations: 15 us -> 2.51 us
    unnamed x15 -> x0, waiting for transfers between devices: 297 us -> none
    reduce_scatter x3 -> x0, waiting for transfers between devices: 283 us -> none  [the longest x1 142 us: body(): lax.psum_scatter(down_weight_grad, ('dp', 'head'), scatter_dimension=0, t...]
    all_gather x6 -> x0, waiting for transfers between devices: 262 us -> none  [the longest x1 63.9 us: body(): lax.all_gather(up_weight.astype(jnp.bfloat16), ('dp', 'head'), axis=0, ti...]
    ppermute x0 -> x43, waiting for transfers between devices: none -> 127 us  [the longest x2 34.5 us: scatter_dp(): mine = mine + lax.ppermute(theirs, 'dp', XSWAP).astype(F32)]
    unnamed x2 -> x0, blocking collectives: 84.6 us -> none
    ppermute x0 -> x43, starting transfers between devices: none -> 47.8 us  [the longest x6 13.1 us: scatter_dp(): total = total + lax.ppermute(part.astype(BF), 'dp', zshift(k)).astype(F32)]
    dot_general x33 -> x36, matrix products: 43.3 us -> 24 us  [dot(): return jnp.dot(left, right, preferred_element_type=F32)]
    all_to_all x1 -> x0, blocking collectives: 16.9 us -> none  [body(): lax.all_to_all(d_packed, 'head', split_axis=0, concat_axis=1, tiled=True)]
  transfers between devices with their start and end apart: 15 -> 47, of which waited for: 14 -> 23; matrix products, arithmetic and copies ran while one was open for 8% -> 25% of each run, Pallas kernels for 0% -> 0%
where the time goes in v1:
time: 324 us; the launch traced here: 322 us
  waiting for transfers between devices  135 us (42%)
  local copies, waits for them, and re-layouts  65.2 us (20%)
  starting transfers between devices  61.9 us (19%)
  other arithmetic  32.9 us (10%)
  matrix products  24 us (7%)
    ppermute x2, waiting for transfers between devices, scatter_dp(): mine = mine + lax.ppermute(theirs, 'dp', XSWAP).astype(F32)  34.5 us
    ppermute x12, waiting for transfers between devices, gather_dp(): lax.ppermute(part, 'dp', XSWAP)  30.7 us
    ppermute x6, waiting for transfers between devices, scatter_dp(): total = total + lax.ppermute(part.astype(BF), 'dp', zshift(k)).astype(F32)  29.7 us
    unnamed x233, local copies, waits for them, and re-layouts  24.1 us
    dot_general x36, matrix products, dot(): return jnp.dot(left, right, preferred_element_type=F32)  24 us
    ppermute x1, waiting for transfers between devices, body(): lax.ppermute(upstream, 'head', CHIP)  13.5 us
    ppermute x6, starting transfers between devices, scatter_dp(): total = total + lax.ppermute(part.astype(BF), 'dp', zshift(k)).astype(F32)  13.1 us
    ppermute x9, starting transfers between devices, gather_dp(): found = [piece] + [lax.ppermute(piece, 'dp', zshift(k)) for k in (1, 2, 3)]  13 us
  transfers between devices with their start and end apart: 47, of which 23 were waited for; matrix products, arithmetic and copies ran while one was open for 25% of the time, Pallas kernels for 0%

profile of v1, /device:TPU:0, one launch (start us, length us, event | category | flops | bytes accessed | tf_op | source)
XLA Modules:
  0.0 322.0 jit_solution(16953051795563013833)
XLA Ops:
  3.2 3.0 collective-permute-start.19
  6.3 2.6 collective-permute-start.20
  16.5 3.3 %all-to-all-start = ((bf16[4,24,704]{2,1,0:T(8,128)(2,1)}), bf16[4,24,704]{2,1,0:T(8,128)(2,1)S(1)}, u32[]{:S(2)}, u32[]{:S(2)}) async-start(bf16[4,24,704]{2,1,0:T(8,128)(2,1)} %copy.127), calls=%async_computation | async-start | bytes 294912 | tf_op jit(solution)/shard_map/all_to_all | solution.py:144
  19.8 2.0 collective-permute-start
  25.0 4.0 %all-to-all-start.1 = ((bf16[4,24,1152]{2,1,0:T(8,128)(2,1)}), bf16[4,24,1152]{2,1,0:T(8,128)(2,1)}, u32[]{:S(2)}, u32[]{:S(2)}) async-start(bf16[4,24,1152]{2,1,0:T(8,128)(2,1)} %maximum_maximum_fusion), calls=%async_computation.1 | async-start | bytes 442368 | tf_op jit(solution)/shard_map/all_to_all | solution.py:150
  30.2 4.5 %all-to-all-done.1 = bf16[4,24,1152]{2,1,0:T(8,128)(2,1)} async-done(((bf16[4,24,1152]{2,1,0:T(8,128)(2,1)}), bf16[4,24,1152]{2,1,0:T(8,128)(2,1)}, u32[]{:S(2)}, u32[]{:S(2)}) %all-to-all-start.1) | async-done | bytes 221216 | tf_op jit(solution)/shard_map/all_to_all | solution.py:150
  34.7 1.6 bitcast_dynamic-update-slice_fusion.7
  39.4 2.9 collective-permute-start.4
  46.3 1.7 pad_maximum_fusion.7
  50.4 8.0 %collective-permute-done.3 = bf16[96,704]{1,0:T(8,128)(2,1)S(1)} collective-permute-done((bf16[96,704]{1,0:T(8,128)(2,1)}, bf16[96,704]{1,0:T(8,128)(2,1)S(1)}, u32[]{:S(2)}, u32[]{:S(2)}) %collective-permute-start.3) | collective-permute-done | bytes 135200 | tf_op jit(solution)/shard_map/ppermute | solution.py:33
  60.7 7.3 %collective-permute-done.23 = bf16[96,896]{1,0:T(8,128)(2,1)S(1)} collective-permute-done((bf16[96,896]{1,0:T(8,128)(2,1)}, bf16[96,896]{1,0:T(8,128)(2,1)S(1)}, u32[]{:S(2)}, u32[]{:S(2)}) %collective-permute-start.23) | collective-permute-done | bytes 172064 | tf_op jit(solution)/shard_map/ppermute | solution.py:34
  68.5 5.9 %collective-permute-done.24 = bf16[96,896]{1,0:T(8,128)(2,1)S(1)} collective-permute-done((bf16[96,896]{1,0:T(8,128)(2,1)}, bf16[96,896]{1,0:T(8,128)(2,1)S(1)}, u32[]{:S(2)}, u32[]{:S(2)}) %collective-permute-start.24) | collective-permute-done | bytes 172064 | tf_op jit(solution)/shard_map/ppermute | solution.py:34
  75.1 6.2 %collective-permute-done.25 = bf16[96,896]{1,0:T(8,128)(2,1)S(1)} collective-permute-done((bf16[96,896]{1,0:T(8,128)(2,1)}, bf16[96,896]{1,0:T(8,128)(2,1)S(1)}, u32[]{:S(2)}, u32[]{:S(2)}) %collective-permute-start.25) | collective-permute-done | bytes 172064 | tf_op jit(solution)/shard_map/ppermute | solution.py:34
  84.3 2.5 collective-permute-done.6
  88.2 3.9 %collective-permute-done.7 = bf16[96,704]{1,0:T(8,128)(2,1)S(1)} collective-permute-done((bf16[96,704]{1,0:T(8,128)(2,1)}, bf16[96,704]{1,0:T(8,128)(2,1)S(1)}, u32[]{:S(2)}, u32[]{:S(2)}) %collective-permute-start.7) | collective-permute-done | bytes 135200 | tf_op jit(solution)/shard_map/ppermute | solution.py:34
  92.7 4.6 %collective-permute-done.8 = bf16[96,704]{1,0:T(8,128)(2,1)S(1)} collective-permute-done((bf16[96,704]{1,0:T(8,128)(2,1)S(1)}, bf16[96,704]{1,0:T(8,128)(2,1)S(1)}, u32[]{:S(2)}, u32[]{:S(2)}) %collective-permute-start.8) | collective-permute-done | bytes 135200 | tf_op jit(solution)/shard_map/ppermute | solution.py:34
  100.4 1.7 bitcast_dynamic-update-slice_fusion.6
  103.6 1.7 bitcast_dynamic-update-slice_fusion.5
  105.8 1.7 bitcast_dynamic-update-slice_fusion.4
  118.1 3.5 %gather_fusion.2 = bf16[8,96,1152]{2,1,0:T(8,128)(2,1)} fusion(bf16[8,96,1152]{2,1,0:T(8,128)(2,1)} %bitcast_dynamic-update-slice_fusion, s32[1024]{0:T(1024)} %copy-done.102), kind=kCustom, calls=%fused_computation.2 | custom fusion | bytes 3538976 | tf_op jit(solution)/shard_map/jit(_take)/gather | solution.py:37
  121.6 1.7 bitcast_select_fusion
  131.6 2.1 multiply_convert_fusion
  134.7 1.7 collective-permute-done.26
  139.4 13.5 %collective-permute-done.28 = bf16[128,768]{1,0:T(8,128)(2,1)S(1)} collective-permute-done((bf16[128,768]{1,0:T(8,128)(2,1)S(1)}, bf16[128,768]{1,0:T(8,128)(2,1)S(1)}, u32[]{:S(2)}, u32[]{:S(2)}) %collective-permute-start.28) | collective-permute-done | bytes 196640 | tf_op jit(solution)/shard_map/ppermute | solution.py:113
  162.3 1.7 collective-permute-start.31
  165.2 2.5 fusion.55
  167.7 5.8 %collective-permute-done.31 = bf16[256,768]{1,0:T(8,128)(2,1)S(1)} collective-permute-done((bf16[256,768]{1,0:T(8,128)(2,1)S(1)}, bf16[256,768]{1,0:T(8,128)(2,1)S(1)}, u32[]{:S(2)}, u32[]{:S(2)}) %collective-permute-start.31) | collective-permute-done | bytes 393248 | tf_op jit(solution)/shard_map/ppermute | solution.py:216
  175.4 2.2 fusion.46
  192.8 1.8 dynamic_update_slice.24
  195.8 1.9 pad_maximum_fusion
  197.6 2.3 copy.140
  199.9 2.6 fusion.33
  205.5 2.4 copy.134
  210.9 1.8 collective-permute-start.34
  212.7 10.1 %collective-permute-done.35 = bf16[4,96,960]{2,1,0:T(8,128)(2,1)} collective-permute-done((bf16[4,96,960]{2,1,0:T(8,128)(2,1)}, bf16[4,96,960]{2,1,0:T(8,128)(2,1)}, u32[]{:S(2)}, u32[]{:S(2)}) %collective-permute-start.35) | collective-permute-done | bytes 737312 | tf_op jit(solution)/shard_map/ppermute | solution.py:49
  225.7 8.4 %collective-permute-start.37 = (bf16[96,960]{1,0:T(8,128)(2,1)S(1)}, bf16[96,960]{1,0:T(8,128)(2,1)S(1)}, u32[]{:S(2)}, u32[]{:S(2)}) collective-permute-start(bf16[96,960]{1,0:T(8,128)(2,1)S(1)} %get-tuple-element.53), channel_id=1, source_target_pairs={{0,16},{4,20},{8,24},{12,28},{16,0},{20,4},{24,8},{28,12},{1,17},{... | collective-permute-start | bytes 552968 | tf_op jit(solution)/shard_map/ppermute | solution.py:53
  235.2 2.2 collective-permute-done.38
  237.4 13.8 %collective-permute-done.37 = bf16[96,960]{1,0:T(8,128)(2,1)S(1)} collective-permute-done((bf16[96,960]{1,0:T(8,128)(2,1)S(1)}, bf16[96,960]{1,0:T(8,128)(2,1)S(1)}, u32[]{:S(2)}, u32[]{:S(2)}) %collective-permute-start.37) | collective-permute-done | bytes 184352 | tf_op jit(solution)/shard_map/ppermute | solution.py:53
  251.2 1.8 fusion.54
  253.0 3.4 %all-to-all-start.3 = ((bf16[4,24,960]{2,1,0:T(8,128)(2,1)}), bf16[4,24,960]{2,1,0:T(8,128)(2,1)S(1)}, u32[]{:S(2)}, u32[]{:S(2)}) async-start(bf16[4,24,960]{2,1,0:T(8,128)(2,1)} %bitcast.85), calls=%async_computation.3 | async-start | bytes 393216 | tf_op jit(solution)/shard_map/all_to_all | solution.py:306
  257.7 3.9 %all-to-all-done.3 = bf16[4,24,960]{2,1,0:T(8,128)(2,1)S(1)} async-done(((bf16[4,24,960]{2,1,0:T(8,128)(2,1)}), bf16[4,24,960]{2,1,0:T(8,128)(2,1)S(1)}, u32[]{:S(2)}, u32[]{:S(2)}) %all-to-all-start.3) | async-done | bytes 184352 | tf_op jit(solution)/shard_map/all_to_all | solution.py:306
  261.6 3.4 %all-to-all-start.2 = ((bf16[32,24,704]{2,1,0:T(8,128)(2,1)}), bf16[32,24,704]{2,1,0:T(8,128)(2,1)}, u32[]{:S(2)}, u32[]{:S(2)}) async-start(bf16[32,24,704]{2,1,0:T(8,128)(2,1)} %pad_maximum_fusion.1), calls=%async_computation.2 | async-start | bytes 2359296 | tf_op jit(solution)/shard_map/all_to_all | solution.py:291
  265.1 1.7 select_maximum_fusion
  266.7 2.2 copy.143
  270.7 24.5 %collective-permute-done.39 = bf16[4,96,896]{2,1,0:T(8,128)(2,1)S(1)} collective-permute-done((bf16[4,96,896]{2,1,0:T(8,128)(2,1)S(1)}, bf16[4,96,896]{2,1,0:T(8,128)(2,1)S(1)}, u32[]{:S(2)}, u32[]{:S(2)}) %collective-permute-start.39) | collective-permute-done | bytes 688160 | tf_op jit(solution)/shard_map/ppermute | solution.py:49
  295.4 3.3 %collective-permute-start.42 = (bf16[96,896]{1,0:T(8,128)(2,1)S(1)}, bf16[96,896]{1,0:T(8,128)(2,1)S(1)}, u32[]{:S(2)}, u32[]{:S(2)}) collective-permute-start(bf16[96,896]{1,0:T(8,128)(2,1)S(1)} %get-tuple-element.55), channel_id=1, source_target_pairs={{0,24},{4,28},{8,0},{12,4},{16,8},{20,12},{24,16},{28,20},{1,25},{... | collective-permute-start | bytes 516104 | tf_op jit(solution)/shard_map/ppermute | solution.py:53
  299.7 3.8 %collective-permute-done.42 = bf16[96,896]{1,0:T(8,128)(2,1)S(1)} collective-permute-done((bf16[96,896]{1,0:T(8,128)(2,1)S(1)}, bf16[96,896]{1,0:T(8,128)(2,1)S(1)}, u32[]{:S(2)}, u32[]{:S(2)}) %collective-permute-start.42) | collective-permute-done | bytes 172064 | tf_op jit(solution)/shard_map/ppermute | solution.py:53
  303.5 9.9 %collective-permute-done.41 = bf16[96,896]{1,0:T(8,128)(2,1)S(1)} collective-permute-done((bf16[96,896]{1,0:T(8,128)(2,1)S(1)}, bf16[96,896]{1,0:T(8,128)(2,1)S(1)}, u32[]{:S(2)}, u32[]{:S(2)}) %collective-permute-start.41) | collective-permute-done | bytes 172064 | tf_op jit(solution)/shard_map/ppermute | solution.py:53
  (472 shorter events, 110.6 us)
Async XLA Ops:
  3.2 33.1 %collective-permute-start.19 = (bf16[96,896]{1,0:T(8,128)(2,1)}, bf16[96,896]{1,0:T(8,128)(2,1)}, u32[]{:S(2)}, u32[]{:S(2)}) collective-permute-start(bf16[96,896]{1,0:T(8,128)(2,1)} %pad_maximum_fusion.14), channel_id=1, source_target_pairs={{0,8},{4,12},{8,16},{12,20},{16,24},{20,28},{24,0},{28,4},{1,9},{5... | collective-permute-start | bytes 516104 | tf_op jit(solution)/shard_map/ppermute | solution.py:33
  6.3 31.7 %collective-permute-start.20 = (bf16[96,896]{1,0:T(8,128)(2,1)}, bf16[96,896]{1,0:T(8,128)(2,1)}, u32[]{:S(2)}, u32[]{:S(2)}) collective-permute-start(bf16[96,896]{1,0:T(8,128)(2,1)} %pad_maximum_fusion.14), channel_id=1, source_target_pairs={{0,16},{4,20},{8,24},{12,28},{16,0},{20,4},{24,8},{28,12},{1,17},{... | collective-permute-start | bytes 516104 | tf_op jit(solution)/shard_map/ppermute | solution.py:33
  8.9 30.5 %collective-permute-start.21 = (bf16[96,896]{1,0:T(8,128)(2,1)}, bf16[96,896]{1,0:T(8,128)(2,1)}, u32[]{:S(2)}, u32[]{:S(2)}) collective-permute-start(bf16[96,896]{1,0:T(8,128)(2,1)} %pad_maximum_fusion.14), channel_id=1, source_target_pairs={{0,24},{4,28},{8,0},{12,4},{16,8},{20,12},{24,16},{28,20},{1,25},{... | collective-permute-start | bytes 516104 | tf_op jit(solution)/shard_map/ppermute | solution.py:33
  10.2 33.0 %collective-permute-start.22 = (bf16[96,896]{1,0:T(8,128)(2,1)}, bf16[96,896]{1,0:T(8,128)(2,1)}, u32[]{:S(2)}, u32[]{:S(2)}) collective-permute-start(bf16[96,896]{1,0:T(8,128)(2,1)} %pad_maximum_fusion.14), channel_id=1, source_target_pairs={{0,4},{4,0},{8,12},{12,8},{16,20},{20,16},{24,28},{28,24},{1,5},{5... | collective-permute-start | bytes 516104 | tf_op jit(solution)/shard_map/ppermute | solution.py:34
  16.5 8.6 %all-to-all-start = ((bf16[4,24,704]{2,1,0:T(8,128)(2,1)}), bf16[4,24,704]{2,1,0:T(8,128)(2,1)S(1)}, u32[]{:S(2)}, u32[]{:S(2)}) async-start(bf16[4,24,704]{2,1,0:T(8,128)(2,1)} %copy.127), calls=%async_computation | async-start | bytes 294912 | tf_op jit(solution)/shard_map/all_to_all | solution.py:144
  19.8 24.9 %collective-permute-start = (bf16[128,768]{1,0:T(8,128)(2,1)S(1)}, bf16[128,768]{1,0:T(8,128)(2,1)}, u32[]{:S(2)}, u32[]{:S(2)}) collective-permute-start(bf16[128,768]{1,0:T(8,128)(2,1)S(1)} %copy-done.34), channel_id=1, source_target_pairs={{0,2},{1,3},{2,0},{3,1},{4,6},{5,7},{6,4},{7,5},{8,10},{9,11},{10,... | collective-permute-start | bytes 589832 | tf_op jit(solution)/shard_map/ppermute | solution.py:110
  24.6 72.7 %copy-start.102 = (s32[1024]{0:T(1024)}, s32[1024]{0:T(1024)S(1)}, u32[]{:S(2)}) copy-start(s32[1024]{0:T(1024)S(1)} %pad_clamp_fusion.1) | copy-start | bytes 12292
  25.0 9.7 %all-to-all-start.1 = ((bf16[4,24,1152]{2,1,0:T(8,128)(2,1)}), bf16[4,24,1152]{2,1,0:T(8,128)(2,1)}, u32[]{:S(2)}, u32[]{:S(2)}) async-start(bf16[4,24,1152]{2,1,0:T(8,128)(2,1)} %maximum_maximum_fusion), calls=%async_computation.1 | async-start | bytes 442368 | tf_op jit(solution)/shard_map/all_to_all | solution.py:150
  36.4 11.6 %collective-permute-start.2 = (bf16[96,704]{1,0:T(8,128)(2,1)}, bf16[96,704]{1,0:T(8,128)(2,1)}, u32[]{:S(2)}, u32[]{:S(2)}) collective-permute-start(bf16[96,704]{1,0:T(8,128)(2,1)} %bitcast.205), channel_id=1, source_target_pairs={{0,8},{4,12},{8,16},{12,20},{16,24},{20,28},{24,0},{28,4},{1,9},{5... | collective-permute-start | bytes 405512 | tf_op jit(solution)/shard_map/ppermute | solution.py:33
  38.0 20.4 %collective-permute-start.3 = (bf16[96,704]{1,0:T(8,128)(2,1)}, bf16[96,704]{1,0:T(8,128)(2,1)S(1)}, u32[]{:S(2)}, u32[]{:S(2)}) collective-permute-start(bf16[96,704]{1,0:T(8,128)(2,1)} %bitcast.206), channel_id=1, source_target_pairs={{0,16},{4,20},{8,24},{12,28},{16,0},{20,4},{24,8},{28,12},{1,17},{... | collective-permute-start | bytes 405512 | tf_op jit(solution)/shard_map/ppermute | solution.py:33
  39.4 19.1 %collective-permute-start.4 = (bf16[96,704]{1,0:T(8,128)(2,1)}, bf16[96,704]{1,0:T(8,128)(2,1)S(1)}, u32[]{:S(2)}, u32[]{:S(2)}) collective-permute-start(bf16[96,704]{1,0:T(8,128)(2,1)} %bitcast.207), channel_id=1, source_target_pairs={{0,24},{4,28},{8,0},{12,4},{16,8},{20,12},{24,16},{28,20},{1,25},{... | collective-permute-start | bytes 405512 | tf_op jit(solution)/shard_map/ppermute | solution.py:33
  43.2 16.0 %collective-permute-start.5 = (bf16[96,704]{1,0:T(8,128)(2,1)}, bf16[96,704]{1,0:T(8,128)(2,1)S(1)}, u32[]{:S(2)}, u32[]{:S(2)}) collective-permute-start(bf16[96,704]{1,0:T(8,128)(2,1)} %bitcast.208), channel_id=1, source_target_pairs={{0,4},{4,0},{8,12},{12,8},{16,20},{20,16},{24,28},{28,24},{1,5},{5... | collective-permute-start | bytes 405512 | tf_op jit(solution)/shard_map/ppermute | solution.py:34
  44.7 55.1 %collective-permute-start.9 = (bf16[96,1152]{1,0:T(8,128)(2,1)}, bf16[96,1152]{1,0:T(8,128)(2,1)}, u32[]{:S(2)}, u32[]{:S(2)}) collective-permute-start(bf16[96,1152]{1,0:T(8,128)(2,1)} %bitcast.39), channel_id=1, source_target_pairs={{0,8},{4,12},{8,16},{12,20},{16,24},{20,28},{24,0},{28,4},{1,9},{5... | collective-permute-start | bytes 663560 | tf_op jit(solution)/shard_map/ppermute | solution.py:33
  48.0 54.1 %collective-permute-start.10 = (bf16[96,1152]{1,0:T(8,128)(2,1)}, bf16[96,1152]{1,0:T(8,128)(2,1)}, u32[]{:S(2)}, u32[]{:S(2)}) collective-permute-start(bf16[96,1152]{1,0:T(8,128)(2,1)} %bitcast.39), channel_id=1, source_target_pairs={{0,16},{4,20},{8,24},{12,28},{16,0},{20,4},{24,8},{28,12},{1,17},{... | collective-permute-start | bytes 663560 | tf_op jit(solution)/shard_map/ppermute | solution.py:33
  58.4 46.8 %collective-permute-start.11 = (bf16[96,1152]{1,0:T(8,128)(2,1)}, bf16[96,1152]{1,0:T(8,128)(2,1)}, u32[]{:S(2)}, u32[]{:S(2)}) collective-permute-start(bf16[96,1152]{1,0:T(8,128)(2,1)} %bitcast.39), channel_id=1, source_target_pairs={{0,24},{4,28},{8,0},{12,4},{16,8},{20,12},{24,16},{28,20},{1,25},{... | collective-permute-start | bytes 663560 | tf_op jit(solution)/shard_map/ppermute | solution.py:33
  58.5 49.0 %collective-permute-start.12 = (bf16[96,1152]{1,0:T(8,128)(2,1)}, bf16[96,1152]{1,0:T(8,128)(2,1)}, u32[]{:S(2)}, u32[]{:S(2)}) collective-permute-start(bf16[96,1152]{1,0:T(8,128)(2,1)} %bitcast.39), channel_id=1, source_target_pairs={{0,4},{4,0},{8,12},{12,8},{16,20},{20,16},{24,28},{28,24},{1,5},{5... | collective-permute-start | bytes 663560 | tf_op jit(solution)/shard_map/ppermute | solution.py:34
  59.2 8.7 %collective-permute-start.23 = (bf16[96,896]{1,0:T(8,128)(2,1)}, bf16[96,896]{1,0:T(8,128)(2,1)S(1)}, u32[]{:S(2)}, u32[]{:S(2)}) collective-permute-start(bf16[96,896]{1,0:T(8,128)(2,1)} %collective-permute-done.19), channel_id=1, source_target_pairs={{0,4},{4,0},{8,12},{12,8},{16,20},{20,16},{24,28},{28,24},{1,5},{5... | collective-permute-start | bytes 516104 | tf_op jit(solution)/shard_map/ppermute | solution.py:34
  67.9 6.5 %collective-permute-start.24 = (bf16[96,896]{1,0:T(8,128)(2,1)}, bf16[96,896]{1,0:T(8,128)(2,1)S(1)}, u32[]{:S(2)}, u32[]{:S(2)}) collective-permute-start(bf16[96,896]{1,0:T(8,128)(2,1)} %collective-permute-done.20), channel_id=1, source_target_pairs={{0,4},{4,0},{8,12},{12,8},{16,20},{20,16},{24,28},{28,24},{1,5},{5... | collective-permute-start | bytes 516104 | tf_op jit(solution)/shard_map/ppermute | solution.py:34
  74.4 6.9 %collective-permute-start.25 = (bf16[96,896]{1,0:T(8,128)(2,1)}, bf16[96,896]{1,0:T(8,128)(2,1)S(1)}, u32[]{:S(2)}, u32[]{:S(2)}) collective-permute-start(bf16[96,896]{1,0:T(8,128)(2,1)} %collective-permute-done.21), channel_id=1, source_target_pairs={{0,4},{4,0},{8,12},{12,8},{16,20},{20,16},{24,28},{28,24},{1,5},{5... | collective-permute-start | bytes 516104 | tf_op jit(solution)/shard_map/ppermute | solution.py:34
  81.3 5.5 %collective-permute-start.6 = (bf16[96,704]{1,0:T(8,128)(2,1)}, bf16[96,704]{1,0:T(8,128)(2,1)}, u32[]{:S(2)}, u32[]{:S(2)}) collective-permute-start(bf16[96,704]{1,0:T(8,128)(2,1)} %collective-permute-done.2), channel_id=1, source_target_pairs={{0,4},{4,0},{8,12},{12,8},{16,20},{20,16},{24,28},{28,24},{1,5},{5... | collective-permute-start | bytes 405512 | tf_op jit(solution)/shard_map/ppermute | solution.py:34
  86.8 5.4 %collective-permute-start.7 = (bf16[96,704]{1,0:T(8,128)(2,1)}, bf16[96,704]{1,0:T(8,128)(2,1)S(1)}, u32[]{:S(2)}, u32[]{:S(2)}) collective-permute-start(bf16[96,704]{1,0:T(8,128)(2,1)} %copy-done.80), channel_id=1, source_target_pairs={{0,4},{4,0},{8,12},{12,8},{16,20},{20,16},{24,28},{28,24},{1,5},{5... | collective-permute-start | bytes 405512 | tf_op jit(solution)/shard_map/ppermute | solution.py:34
  92.1 5.1 %collective-permute-start.8 = (bf16[96,704]{1,0:T(8,128)(2,1)S(1)}, bf16[96,704]{1,0:T(8,128)(2,1)S(1)}, u32[]{:S(2)}, u32[]{:S(2)}) collective-permute-start(bf16[96,704]{1,0:T(8,128)(2,1)S(1)} %copy-done.79), channel_id=1, source_target_pairs={{0,4},{4,0},{8,12},{12,8},{16,20},{20,16},{24,28},{28,24},{1,5},{5... | collective-permute-start | bytes 405512 | tf_op jit(solution)/shard_map/ppermute | solution.py:34
  97.3 11.9 %collective-permute-start.1 = (bf16[256,768]{1,0:T(8,128)(2,1)}, bf16[256,768]{1,0:T(8,128)(2,1)}, u32[]{:S(2)}, u32[]{:S(2)}) collective-permute-start(bf16[256,768]{1,0:T(8,128)(2,1)} %pad_maximum_fusion.7), channel_id=1, source_target_pairs={{0,1},{1,0},{2,3},{3,2},{4,5},{5,4},{6,7},{7,6},{8,9},{9,8},{10,11... | collective-permute-start | bytes 1179656 | tf_op jit(solution)/shard_map/ppermute | solution.py:112
  99.8 15.7 %collective-permute-start.13 = (bf16[96,1152]{1,0:T(8,128)(2,1)}, bf16[96,1152]{1,0:T(8,128)(2,1)S(1)}, u32[]{:S(2)}, u32[]{:S(2)}) collective-permute-start(bf16[96,1152]{1,0:T(8,128)(2,1)} %collective-permute-done.9), channel_id=1, source_target_pairs={{0,4},{4,0},{8,12},{12,8},{16,20},{20,16},{24,28},{28,24},{1,5},{5... | collective-permute-start | bytes 663560 | tf_op jit(solution)/shard_map/ppermute | solution.py:34
  102.1 14.2 %collective-permute-start.14 = (bf16[96,1152]{1,0:T(8,128)(2,1)}, bf16[96,1152]{1,0:T(8,128)(2,1)S(1)}, u32[]{:S(2)}, u32[]{:S(2)}) collective-permute-start(bf16[96,1152]{1,0:T(8,128)(2,1)} %collective-permute-done.10), channel_id=1, source_target_pairs={{0,4},{4,0},{8,12},{12,8},{16,20},{20,16},{24,28},{28,24},{1,5},{5... | collective-permute-start | bytes 663560 | tf_op jit(solution)/shard_map/ppermute | solution.py:34
  105.2 12.1 %collective-permute-start.15 = (bf16[96,1152]{1,0:T(8,128)(2,1)}, bf16[96,1152]{1,0:T(8,128)(2,1)S(1)}, u32[]{:S(2)}, u32[]{:S(2)}) collective-permute-start(bf16[96,1152]{1,0:T(8,128)(2,1)} %collective-permute-done.11), channel_id=1, source_target_pairs={{0,4},{4,0},{8,12},{12,8},{16,20},{20,16},{24,28},{28,24},{1,5},{5... | collective-permute-start | bytes 663560 | tf_op jit(solution)/shard_map/ppermute | solution.py:34
  115.5 8.0 %collective-permute-start.17 = (bf16[512,192]{0,1:T(8,128)(2,1)}, bf16[512,192]{0,1:T(8,128)(2,1)S(1)}, u32[]{:S(2)}, u32[]{:S(2)}) collective-permute-start(bf16[512,192]{0,1:T(8,128)(2,1)} %get-tuple-element.80), channel_id=1, source_target_pairs={{0,2},{1,3},{2,0},{3,1},{4,6},{5,7},{6,4},{7,5},{8,10},{9,11},{10,... | collective-permute-start | bytes 589832 | tf_op jit(solution)/shard_map/ppermute | solution.py:190
  123.5 2.8 collective-permute-start.16
  123.6 2.5 collective-permute-start.18
  134.6 1.8 collective-permute-start.26
  137.3 15.6 %collective-permute-start.27 = (bf16[256,768]{1,0:T(8,128)(2,1)}, bf16[256,768]{1,0:T(8,128)(2,1)}, u32[]{:S(2)}, u32[]{:S(2)}) collective-permute-start(bf16[256,768]{1,0:T(8,128)(2,1)} %fusion.47), channel_id=1, source_target_pairs={{0,2},{1,3},{2,0},{3,1},{4,6},{5,7},{6,4},{7,5},{8,10},{9,11},{10,... | collective-permute-start | bytes 1179656 | tf_op jit(solution)/shard_map/ppermute | solution.py:216
  139.0 14.0 %collective-permute-start.28 = (bf16[128,768]{1,0:T(8,128)(2,1)S(1)}, bf16[128,768]{1,0:T(8,128)(2,1)S(1)}, u32[]{:S(2)}, u32[]{:S(2)}) collective-permute-start(bf16[128,768]{1,0:T(8,128)(2,1)S(1)} %copy-done.18), channel_id=1, source_target_pairs={{0,2},{1,3},{2,0},{3,1},{4,6},{5,7},{6,4},{7,5},{8,10},{9,11},{10,... | collective-permute-start | bytes 589832 | tf_op jit(solution)/shard_map/ppermute | solution.py:113
  156.3 1.8 collective-permute-start.29
  160.4 1.8 collective-permute-start.30
  162.3 11.2 %collective-permute-start.31 = (bf16[256,768]{1,0:T(8,128)(2,1)S(1)}, bf16[256,768]{1,0:T(8,128)(2,1)S(1)}, u32[]{:S(2)}, u32[]{:S(2)}) collective-permute-start(bf16[256,768]{1,0:T(8,128)(2,1)S(1)} %fusion.48), channel_id=1, source_target_pairs={{0,2},{1,3},{2,0},{3,1},{4,6},{5,7},{6,4},{7,5},{8,10},{9,11},{10,... | collective-permute-start | bytes 1179656 | tf_op jit(solution)/shard_map/ppermute | solution.py:216
  175.4 3.0 collective-permute-start.32
  189.4 20.1 %collective-permute-start.33 = (bf16[256,768]{1,0:T(8,128)(2,1)}, bf16[256,768]{1,0:T(8,128)(2,1)}, u32[]{:S(2)}, u32[]{:S(2)}) collective-permute-start(bf16[256,768]{1,0:T(8,128)(2,1)} %slice.562), channel_id=1, source_target_pairs={{0,1},{1,0},{2,3},{3,2},{4,5},{5,4},{6,7},{7,6},{8,9},{9,8},{10,11... | collective-permute-start | bytes 1179656 | tf_op jit(solution)/shard_map/ppermute | solution.py:269
  202.5 20.2 %collective-permute-start.35 = (bf16[4,96,960]{2,1,0:T(8,128)(2,1)}, bf16[4,96,960]{2,1,0:T(8,128)(2,1)}, u32[]{:S(2)}, u32[]{:S(2)}) collective-permute-start(bf16[4,96,960]{2,1,0:T(8,128)(2,1)} %fusion.33), channel_id=1, source_target_pairs={{0,4},{4,0},{8,12},{12,8},{16,20},{20,16},{24,28},{28,24},{1,5},{5... | collective-permute-start | bytes 2211848 | tf_op jit(solution)/shard_map/ppermute | solution.py:49
  210.9 23.3 %collective-permute-start.34 = (bf16[128,768]{1,0:T(8,128)(2,1)S(1)}, bf16[128,768]{1,0:T(8,128)(2,1)S(1)}, u32[]{:S(2)}, u32[]{:S(2)}) collective-permute-start(bf16[128,768]{1,0:T(8,128)(2,1)S(1)} %slice.565), channel_id=1, source_target_pairs={{0,2},{1,3},{2,0},{3,1},{4,6},{5,7},{6,4},{7,5},{8,10},{9,11},{10,... | collective-permute-start | bytes 589832 | tf_op jit(solution)/shard_map/ppermute | solution.py:270
  225.4 12.0 %collective-permute-start.38 = (bf16[96,960]{1,0:T(8,128)(2,1)S(1)}, bf16[96,960]{1,0:T(8,128)(2,1)S(1)}, u32[]{:S(2)}, u32[]{:S(2)}) collective-permute-start(bf16[96,960]{1,0:T(8,128)(2,1)S(1)} %get-tuple-element.52), channel_id=1, source_target_pairs={{0,24},{4,28},{8,0},{12,4},{16,8},{20,12},{24,16},{28,20},{1,25},{... | collective-permute-start | bytes 552968 | tf_op jit(solution)/shard_map/ppermute | solution.py:53
  225.7 25.5 %collective-permute-start.37 = (bf16[96,960]{1,0:T(8,128)(2,1)S(1)}, bf16[96,960]{1,0:T(8,128)(2,1)S(1)}, u32[]{:S(2)}, u32[]{:S(2)}) collective-permute-start(bf16[96,960]{1,0:T(8,128)(2,1)S(1)} %get-tuple-element.53), channel_id=1, source_target_pairs={{0,16},{4,20},{8,24},{12,28},{16,0},{20,4},{24,8},{28,12},{1,17},{... | collective-permute-start | bytes 552968 | tf_op jit(solution)/shard_map/ppermute | solution.py:53
  234.1 17.1 %collective-permute-start.36 = (bf16[96,960]{1,0:T(8,128)(2,1)S(1)}, bf16[96,960]{1,0:T(8,128)(2,1)S(1)}, u32[]{:S(2)}, u32[]{:S(2)}) collective-permute-start(bf16[96,960]{1,0:T(8,128)(2,1)S(1)} %get-tuple-element.51), channel_id=1, source_target_pairs={{0,8},{4,12},{8,16},{12,20},{16,24},{20,28},{24,0},{28,4},{1,9},{5... | collective-permute-start | bytes 552968 | tf_op jit(solution)/shard_map/ppermute | solution.py:53
  253.0 8.7 %all-to-all-start.3 = ((bf16[4,24,960]{2,1,0:T(8,128)(2,1)}), bf16[4,24,960]{2,1,0:T(8,128)(2,1)S(1)}, u32[]{:S(2)}, u32[]{:S(2)}) async-start(bf16[4,24,960]{2,1,0:T(8,128)(2,1)} %bitcast.85), calls=%async_computation.3 | async-start | bytes 393216 | tf_op jit(solution)/shard_map/all_to_all | solution.py:306
  261.6 55.6 %all-to-all-start.2 = ((bf16[32,24,704]{2,1,0:T(8,128)(2,1)}), bf16[32,24,704]{2,1,0:T(8,128)(2,1)}, u32[]{:S(2)}, u32[]{:S(2)}) async-start(bf16[32,24,704]{2,1,0:T(8,128)(2,1)} %pad_maximum_fusion.1), calls=%async_computation.2 | async-start | bytes 2359296 | tf_op jit(solution)/shard_map/all_to_all | solution.py:291
  269.1 26.1 %collective-permute-start.39 = (bf16[4,96,896]{2,1,0:T(8,128)(2,1)S(1)}, bf16[4,96,896]{2,1,0:T(8,128)(2,1)S(1)}, u32[]{:S(2)}, u32[]{:S(2)}) collective-permute-start(bf16[4,96,896]{2,1,0:T(8,128)(2,1)S(1)} %fusion.39), channel_id=1, source_target_pairs={{0,4},{4,0},{8,12},{12,8},{16,20},{20,16},{24,28},{28,24},{1,5},{5... | collective-permute-start | bytes 2064392 | tf_op jit(solution)/shard_map/ppermute | solution.py:49
  295.4 8.1 %collective-permute-start.42 = (bf16[96,896]{1,0:T(8,128)(2,1)S(1)}, bf16[96,896]{1,0:T(8,128)(2,1)S(1)}, u32[]{:S(2)}, u32[]{:S(2)}) collective-permute-start(bf16[96,896]{1,0:T(8,128)(2,1)S(1)} %get-tuple-element.55), channel_id=1, source_target_pairs={{0,24},{4,28},{8,0},{12,4},{16,8},{20,12},{24,16},{28,20},{1,25},{... | collective-permute-start | bytes 516104 | tf_op jit(solution)/shard_map/ppermute | solution.py:53
  298.7 14.7 %collective-permute-start.41 = (bf16[96,896]{1,0:T(8,128)(2,1)S(1)}, bf16[96,896]{1,0:T(8,128)(2,1)S(1)}, u32[]{:S(2)}, u32[]{:S(2)}) collective-permute-start(bf16[96,896]{1,0:T(8,128)(2,1)S(1)} %get-tuple-element.56), channel_id=1, source_target_pairs={{0,16},{4,20},{8,24},{12,28},{16,0},{20,4},{24,8},{28,12},{1,17},{... | collective-permute-start | bytes 516104 | tf_op jit(solution)/shard_map/ppermute | solution.py:53
  298.7 14.7 %collective-permute-start.40 = (bf16[96,896]{1,0:T(8,128)(2,1)S(1)}, bf16[96,896]{1,0:T(8,128)(2,1)S(1)}, u32[]{:S(2)}, u32[]{:S(2)}) collective-permute-start(bf16[96,896]{1,0:T(8,128)(2,1)S(1)} %get-tuple-element.54), channel_id=1, source_target_pairs={{0,8},{4,12},{8,16},{12,20},{16,24},{20,28},{24,0},{28,4},{1,9},{5... | collective-permute-start | bytes 516104 | tf_op jit(solution)/shard_map/ppermute | solution.py:53
  (105 other events, 572.0 us)

commit v2 on v1

v2 whole, which is shorter than its diff:
```python
import functools
import math

import jax
import jax.numpy as jnp
from jax import lax
from jax.experimental import pallas as pl
from jax.experimental.pallas import tpu as pltpu
from jax.sharding import PartitionSpec as P

H = 12
HD = 64
EPSILON = 1e-12
NEG_FILL = -1000000000.0
BF = jnp.bfloat16
F32 = jnp.float32
ALL = ("dp", "head")
CORE = [(i, i ^ 1) for i in range(4)]
CHIP = [(i, i ^ 2) for i in range(4)]
XSWAP = [(i, i ^ 1) for i in range(8)]
GROUPS = [[(2 * z + x) * 4 + h for z in range(4) for h in range(4)] for x in range(2)]


def zshift(k):
    return [(i, (i + 2 * k) % 8) for i in range(8)]


def shape(dims, kind):
    return jax.ShapeDtypeStruct(dims, kind)


def call(kernel, outs, *args, after=(), micros=2, limit=8):
    spec = pl.BlockSpec(memory_space=pltpu.VMEM)
    count, extra = len(args), len(after)

    def run(*refs):
        kernel(*refs[:count], *refs[count + extra :])

    return pl.pallas_call(
        run,
        out_shape=outs,
        in_specs=[spec] * count + [pl.BlockSpec(memory_space=pl.ANY)] * extra,
        out_specs=jax.tree.map(lambda _: spec, outs),
        compiler_params=pltpu.CompilerParams(vmem_limit_bytes=limit << 20),
        cost_estimate=pl.CostEstimate(
            flops=int(micros * 2e7), bytes_accessed=int(micros * 1e5), transcendentals=0
        ),
    )(*args, *after)


def later(value, *after):
    anywhere = pl.BlockSpec(memory_space=pl.ANY)
    return pl.pallas_call(
        lambda *refs: None,
        out_shape=shape(value.shape, value.dtype),
        in_specs=[anywhere] * (1 + len(after)),
        out_specs=anywhere,
        input_output_aliases={0: 0},
        compiler_params=pltpu.CompilerParams(vmem_limit_bytes=1 << 20),
        cost_estimate=pl.CostEstimate(flops=0, bytes_accessed=0, transcendentals=0),
    )(value, *after)


def dot(left, right, dims=((1,), (0,))):
    return lax.dot_general(left, right, (dims, ((), ())), preferred_element_type=F32)


NT = ((1,), (1,))
TN = ((0,), (0,))


def norm_stats(values):
    center = values - jnp.mean(values, axis=-1, keepdims=True)
    spread = jnp.mean(center * center, axis=-1, keepdims=True)
    rate = lax.rsqrt(spread + EPSILON)
    return center * rate, rate


def norm_back(unit, rate, dyg):
    return rate * (
        dyg
        - jnp.mean(dyg, axis=-1, keepdims=True)
        - unit * jnp.mean(dyg * unit, axis=-1, keepdims=True)
    )


def transpose_wide(values):
    rows, lanes = values.shape
    full = jnp.concatenate([values, jnp.zeros((128 - rows, lanes), F32)], axis=0)
    tiles = [full[:, i : i + 128].T for i in range(0, lanes, 128)]
    return jnp.concatenate(tiles, axis=0)


SPARE = 64


def pack_kernel(query, key, value, output, up, down, *refs):
    biases, outs, scratch = refs[:9], refs[9:14], refs[14:]
    second, third = outs[:4], outs[4]
    matrices, vectors, square, sems = scratch[:6], scratch[6:15], scratch[15], scratch[16]
    pairs = list(zip((query, key, value, output, up, down) + biases, matrices + vectors))
    copies = [pltpu.make_async_copy(a, b, sems.at[i]) for i, (a, b) in enumerate(pairs)]
    for copy in copies:
        copy.start()
    rows, width = query.shape
    share = width // 4
    piece = down.shape[0]
    here = lax.axis_index("head")
    square[...] = jnp.zeros_like(square)
    for copy in copies:
        copy.wait()
    query, key, value, output, up, down = matrices
    for i in range(8):
        square[i : i + 1, 0:rows] = vectors[i][...].reshape(1, rows)
    long = vectors[8][...].reshape(1, piece)
    for j in range(4):
        square[8 + j : 9 + j, 0:rows] = long[:, j * rows : (j + 1) * rows]
    columns = square[...].T[:rows, :SPARE]
    slabs = []
    for h in range(4):
        half = (h % 2) * (width // 2)
        slabs.append(
            jnp.concatenate(
                [w[:, h * share : (h + 1) * share] for w in (query, key, value)]
                + [columns]
                + [up[:, piece * (4 * j + h) : piece * (4 * j + h + 1)] for j in range(width // piece)]
                + [output[:, half : half + width // 2]],
                axis=1,
            )
        )
        third[h] = down[h * rows : (h + 1) * rows, :].astype(BF)
    for flip in range(4):
        chosen = slabs[flip]
        for h in range(1, 4):
            chosen = jnp.where(here == h, slabs[h ^ flip], chosen)
        second[flip][...] = chosen.astype(BF)


def pack(matrices, biases):
    rows, width = matrices[0].shape
    piece = matrices[5].shape[0]
    share = width // 4
    hbm = pl.BlockSpec(memory_space=pltpu.HBM)
    vmem = pl.BlockSpec(memory_space=pltpu.VMEM)
    return pl.pallas_call(
        pack_kernel,
        out_shape=(shape((rows, 3 * share + SPARE + width + width // 2), BF),) * 4
        + (shape((4, rows, width), BF),),
        in_specs=[hbm] * 15,
        out_specs=(vmem,) * 5,
        scratch_shapes=[pltpu.VMEM(v.shape, F32) for v in matrices + biases]
        + [pltpu.VMEM((128, 128), F32), pltpu.SemaphoreType.DMA((15,))],
        compiler_params=pltpu.CompilerParams(vmem_limit_bytes=56 << 20),
    )(*matrices, *biases)


def gather_any(matrices, biases):
    query, key, value, output, up, down = matrices
    rows, width = query.shape
    piece = down.shape[0]
    share = width // 4

    def by_head(weight):
        return weight.reshape(rows, 4, share).transpose(1, 0, 2)

    columns = jnp.concatenate([jnp.stack(biases[:8]), biases[8].reshape(4, rows)], axis=0).T
    columns = jnp.pad(columns, ((0, 0), (0, SPARE - 12)))
    columns = jnp.broadcast_to(columns[None], (4, rows, SPARE))
    halves = output.reshape(rows, 2, width // 2).transpose(1, 0, 2)
    ups = up.reshape(rows, width // piece, 4, piece).transpose(2, 0, 1, 3).reshape(4, rows, width)
    every = jnp.concatenate(
        [by_head(query), by_head(key), by_head(value), columns, ups]
        + [jnp.concatenate([halves, halves], axis=0)],
        axis=2,
    ).astype(BF)
    every = lax.all_to_all(every, "head", 0, 0, tiled=True).reshape(4 * rows, -1)
    every = jnp.concatenate([every, down.astype(BF)], axis=1)
    every = lax.all_gather(every, "dp", axis=0, tiled=True)
    cuts = [3 * share, 3 * share + SPARE, 3 * share + SPARE + width]
    cuts.append(cuts[-1] + width // 2)
    return jnp.split(every, cuts, axis=1)


def merge_kernel(own, core, chip, far, third, first_out, second_out):
    here = lax.axis_index("head")
    cut = first_out.shape[2]
    rest = own.shape[1] - cut
    for flip, piece in ((0, own), (1, core), (2, chip), (3, far)):
        first_out[here ^ flip] = piece[:, :cut]
        second_out[here ^ flip, :, :rest] = piece[:, cut:]
    second_out[:, :, rest:] = third[...]


def join_kernel(splits, *refs):
    outs = refs[-len(splits) :]
    pieces = refs[: -len(splits)]
    rows = pieces[0].shape[0]
    place = lax.axis_index("dp")
    for i, piece in enumerate(pieces):
        owner = lax.rem(place + 8 - 2 * (i % 4), 8) ^ (i // 4)
        at = pl.ds(pl.multiple_of(owner * rows, 16), rows)
        column = 0
        for out in outs:
            out[at, :] = piece[:, column : column + out.shape[1]]
            column += out.shape[1]


def attend_kernel(rows, seg, x0, x1, x2, x3, weight, columns, qkv_out, probs_out, ctx_out, bias_out):
    share = ctx_out.shape[1]
    width = x0.shape[1]
    tok = seg.shape[1]
    here = lax.axis_index("head")
    across = columns[...].astype(F32)
    across = jnp.concatenate([across, jnp.zeros((width, 128 - SPARE), F32)], axis=1)
    across = jnp.concatenate(
        [across[i : i + 128].T[:16] for i in range(0, width, 128)], axis=1
    )
    mine = pltpu.roll(across[:8], lax.rem(width - here * share, width), 1)
    lane = lax.broadcasted_iota(jnp.int32, (8, width), 1)
    up_bias = jnp.zeros((8, width), F32)
    for j in range(4):
        moved = pltpu.roll(across[8:], lax.rem(width + rows * (j - here), width), 1)
        up_bias = jnp.where(lax.rem(lane, 4 * rows) // rows == j, moved[j : j + 1], up_bias)
    bias_out[...] = jnp.concatenate([mine[:2], across[2:8], up_bias], axis=0)
    q_bias = mine[0:1, :share]
    v_bias = mine[1:2, :share]
    bias = jnp.concatenate([q_bias, jnp.zeros((1, share), F32), v_bias], axis=1)
    scale = 1.0 / math.sqrt(HD)
    factor = jnp.concatenate(
        [jnp.full((1, share), scale, F32), jnp.ones((1, 2 * share), F32)], axis=1
    )
    xs = jnp.concatenate([x0[...], x1[...], x2[...], x3[...]], axis=0)
    qkv = (dot(xs, weight[...]) + bias).astype(BF)
    qkv = (qkv.astype(F32) * factor).astype(BF)
    qkv_out[...] = qkv
    ids = [seg[pl.ds(here ^ flip, 1), :].astype(F32) for flip in (0, 2, 1, 3)]
    contexts = []
    for b in range(4):
        column = jnp.broadcast_to(ids[b], (tok, tok)).T
        same = jnp.concatenate([column == ids[t] for t in range(4)], axis=1)
        parts = []
        for j in range(share // HD):
            q = qkv[b * tok : (b + 1) * tok, j * HD : (j + 1) * HD]
            k = qkv[:, share + j * HD : share + (j + 1) * HD]
            v = qkv[:, 2 * share + j * HD : 2 * share + (j + 1) * HD]
            scores = jnp.where(same, dot(q, k, NT), NEG_FILL)
            raised = jnp.exp(scores - jnp.max(scores, axis=1, keepdims=True))
            probs = raised * (1.0 / jnp.sum(raised, axis=1, keepdims=True))
            probs_out[j, b * tok : (b + 1) * tok, :] = probs
            parts.append(dot(probs.astype(BF), v))
        contexts.append(jnp.concatenate(parts, axis=1).astype(BF))
    ctx_out[...] = jnp.concatenate(contexts, axis=0)


def ffn_kernel(half, x0, x1, ctx, ctx_chip, ctx_core, ctx_far, near, other, up, down, bias, *outs):
    if half == 0:
        nl_out, act_out, slope_out, part_out, unit_out, rate_out, normed_out = outs
    else:
        nl_out, act_out, slope_out, part_out = outs
    mine = nl_out.shape[0]
    tok = mine // 2
    share = ctx.shape[1]
    here = lax.axis_index("head")
    o_bias, a_gain, a_shift, u_bias = [bias[i : i + 1, :] for i in (2, 3, 4, 8)]
    total = jnp.concatenate([x0[...], x1[...]], axis=0).astype(F32) + o_bias
    sums = [jnp.zeros((mine, near.shape[1]), F32)] * 2

    def pick(ref, order):
        order = order[2 * half : 2 * half + 2]
        return jnp.concatenate([ref[i * tok : (i + 1) * tok, :] for i in order], axis=0)

    for flip, ref, order in (
        (0, ctx, (0, 1, 2, 3)),
        (2, ctx_chip, (1, 0, 3, 2)),
        (1, ctx_core, (2, 3, 0, 1)),
        (3, ctx_far, (3, 2, 1, 0)),
    ):
        at = pl.multiple_of((here ^ flip) * share, 64)
        part = pick(ref, order)
        sums = [t + dot(part, w[pl.ds(at, share), :]) for t, w in zip(sums, (near, other))]
    total = total + jnp.concatenate(in_order(*sums), axis=1)
    unit, rate = norm_stats(total)
    normed = unit * a_gain + a_shift
    low = normed.astype(BF)
    nl_out[...] = low
    if half == 0:
        unit_out[...] = unit
        rate_out[...] = jnp.broadcast_to(rate, rate_out.shape)
        normed_out[...] = normed
    pre = dot(low, up[...]) + u_bias
    phi = 0.5 * (1.0 + lax.erf(pre * math.sqrt(0.5)))
    act = (pre * phi).astype(BF)
    act_out[...] = act
    slope_out[...] = phi + pre * jnp.exp(-0.5 * pre * pre) * (1.0 / math.sqrt(2 * math.pi))
    part_out[...] = dot(act, down[...]).astype(part_out.dtype)


def in_order(near, other):
    first = lax.axis_index("head") % 2 == 0
    return [jnp.where(first, near, other), jnp.where(first, other, near)]


def add_kernel(part, got, kept, sent):
    total = part[...] + got[...].astype(F32)
    kept[...] = total
    sent[...] = total.astype(BF)


def swap_blocks(values):
    tok = values.shape[0] // 2
    return jnp.concatenate([values[tok:], values[:tok]], axis=0)


def final_kernel(part, far, normed, up0, up1, bias, layer_out, d_second_out, low_out, grads):
    tok = layer_out.shape[0]
    d_bias, f_gain, f_shift = [bias[i : i + 1, :] for i in (5, 6, 7)]
    second = normed[...] + part[...] + swap_blocks(far[...].astype(F32)) + d_bias
    unit, rate = norm_stats(second)
    layer_out[...] = (unit[:tok] * f_gain + f_shift).astype(BF)
    dy = jnp.concatenate([up0[...], up1[...]], axis=0).astype(F32)
    d_second = norm_back(unit, rate, dy * f_gain)
    d_second_out[...] = d_second
    low_out[...] = d_second.astype(BF)
    sums = [d_second[:tok], dy[:tok] * unit[:tok], dy[:tok]]
    sums = [jnp.sum(s, axis=0, keepdims=True) for s in sums]
    grads[...] = jnp.concatenate(sums + [jnp.zeros_like(grads[3:, :])], axis=0)


def ffn_back_kernel(low, slope, up, down, dh_out, part_out, sum_out):
    d_hidden = dot(low[...], down[...], NT) * slope[...]
    total = jnp.sum(d_hidden, axis=0, keepdims=True)
    sum_out[...] = jnp.broadcast_to(total, sum_out.shape)
    dh = d_hidden.astype(BF)
    dh_out[...] = dh
    part_out[...] = dot(dh, up[...], NT).astype(part_out.dtype)


def split_rows(kept, sent, values):
    if sent is None:
        kept[...] = values
        return
    rows = kept.shape[1]
    mine = lax.axis_index("dp") & 1
    pieces = values.reshape(4, 2, rows, values.shape[1])
    for z in range(4):
        even, odd = pieces[z, 0], pieces[z, 1]
        kept[z] = jnp.where(mine == 0, even, odd)
        sent[z] = jnp.where(mine == 0, odd, even).astype(BF)


def weight_grad_kernel(left0, left1, right0, right1, kept, *sent):
    grad = dot(left0[...], right0[...], TN) + dot(left1[...], right1[...], TN)
    split_rows(kept, sent[0] if sent else None, grad)


def first_back_kernel(part, far, d_second, unit, rate, bias, d_first_out, low_out, grads):
    tok = unit.shape[0] // 2
    a_gain = bias[3:4, :]
    d_normed = d_second[...] + part[...] + swap_blocks(far[...].astype(F32))
    u = unit[...]
    d_first = norm_back(u, rate[:, 0:1], d_normed * a_gain)
    d_first_out[...] = d_first[:tok]
    low_out[...] = d_first.astype(BF)
    sums = [d_first[:tok], d_normed[:tok] * u[:tok], d_normed[:tok]]
    sums = [jnp.sum(s, axis=0, keepdims=True) for s in sums]
    grads[...] = jnp.concatenate(sums + [jnp.zeros_like(grads[3:, :])], axis=0)


def attend_back_kernel(low0, low1, near, other, qkv, probs, d_qkv_out):
    share = qkv.shape[1] // 3
    here = lax.axis_index("head")
    at = pl.multiple_of(here * share, 64)
    halves = [near[pl.ds(at, share), :].astype(F32), other[pl.ds(at, share), :].astype(F32)]
    mine = jnp.concatenate(in_order(*halves), axis=1).astype(BF)
    d_ctx = jnp.concatenate([dot(low0[...], mine, NT), dot(low1[...], mine, NT)], axis=0).astype(BF)
    scale = 1.0 / math.sqrt(HD)
    parts = [[], [], []]
    for j in range(share // HD):
        q = qkv[:, j * HD : (j + 1) * HD]
        k = qkv[:, share + j * HD : share + (j + 1) * HD]
        v = qkv[:, 2 * share + j * HD : 2 * share + (j + 1) * HD]
        grad = d_ctx[:, j * HD : (j + 1) * HD]
        p = probs[j]
        d_probs = dot(grad, v, NT)
        inner = jnp.sum(d_probs * p, axis=1, keepdims=True)
        d_scores = (p * (d_probs - inner)).astype(BF)
        parts[0].append(dot(d_scores, k) * scale)
        parts[1].append(dot(d_scores, q, TN))
        parts[2].append(dot(p.astype(BF), grad, TN))
    d_qkv_out[...] = jnp.concatenate(parts[0] + parts[1] + parts[2], axis=1).astype(BF)


def output_grad_kernel(ctx, ctx_chip, ctx_core, ctx_far, low0, low1, *outs):
    out, kept, *sent = outs[-1:] + outs[:-1]
    share = ctx.shape[1]
    width = low0.shape[1]
    tok = ctx.shape[0] // 4
    here = lax.axis_index("head")
    low = jnp.concatenate([low0[...], low1[...]], axis=0).astype(F32)
    low = pltpu.roll(low, lax.rem(width - here * share, width), 1)[:, :share].astype(BF)

    def pick(ref, order):
        return jnp.concatenate([ref[i * tok : (i + 1) * tok, :] for i in order], axis=0)

    for flip, ref, order in (
        (0, ctx, (0, 1, 2, 3)),
        (2, ctx_chip, (1, 0, 3, 2)),
        (1, ctx_core, (2, 3, 0, 1)),
        (3, ctx_far, (3, 2, 1, 0)),
    ):
        at = pl.multiple_of((here ^ flip) * share, 64)
        out[pl.ds(at, share), :] = dot(pick(ref, order), low, TN)
    split_rows(kept, sent[0] if sent else None, out[...])


def last_grad_kernel(rows, x0, x1, x2, x3, d_qkv, grads2, grads1, sum0, sum1, kept, *sent):
    width = x0.shape[1]
    share = width // 4
    here = lax.axis_index("head")
    d = d_qkv[...]
    xs = jnp.concatenate([x0[...], x1[...], x2[...], x3[...]], axis=0)
    weights = dot(xs, d, TN)
    sums = jnp.sum(d.astype(F32), axis=0, keepdims=True)
    zero = jnp.zeros((1, width - share), F32)
    two = jnp.concatenate(
        [
            jnp.concatenate([sums[:, :share], zero], axis=1),
            jnp.concatenate([sums[:, 2 * share :], zero], axis=1),
            jnp.zeros((6, width), F32),
        ],
        axis=0,
    )
    two = pltpu.roll(two, here * share, 1)
    hidden = sum0[...] + sum1[...]
    lane = lax.broadcasted_iota(jnp.int32, (1, width), 1)
    owner = lax.rem(lane, 4 * rows) // rows == here
    ups = [
        jnp.where(owner, pltpu.roll(hidden, lax.rem(width + rows * (here - j), width), 1)[0:1], 0.0)
        for j in range(4)
    ]
    g1, g2 = grads1[...], grads2[...]
    every = jnp.concatenate([two[:2], g1[0:3], g2[0:3]] + ups, axis=0)
    every = jnp.concatenate([every, jnp.zeros((4, width), F32)], axis=0)
    columns = transpose_wide(every)[:, :SPARE]
    split_rows(kept, sent[0] if sent else None, jnp.concatenate([weights, columns], axis=1))


def finish_up_kernel(rows, got, up_out, output_out):
    depth, _, _, columns = got.shape
    width = output_out.shape[1]
    share = width // 4
    piece = 4 * rows
    sums = []
    for h in range(4):
        total = got[0, h].astype(F32)
        for z in range(1, depth):
            total = total + got[z, h].astype(F32)
        sums.append(total)
    output_out[...] = jnp.concatenate([t[:, width : width + share] for t in sums], axis=1)
    up_out[...] = jnp.concatenate(
        [sums[h][:, j * piece : (j + 1) * piece] for j in range(width // piece) for h in range(4)],
        axis=1,
    )


def finish_last_kernel(got, query_out, key_out, value_out, *bias_outs):
    depth, _, rows, columns = got.shape
    share = query_out.shape[1] // 4
    sums = []
    for h in range(4):
        total = got[0, h].astype(F32)
        for z in range(1, depth):
            total = total + got[z, h].astype(F32)
        sums.append(total)
    for i, out in enumerate((query_out, key_out, value_out)):
        out[...] = jnp.concatenate([t[:, i * share : (i + 1) * share] for t in sums], axis=1)
    every = sums[0] + sums[1] + sums[2] + sums[3]
    every = jnp.concatenate([every[:, 3 * share :], jnp.zeros((rows, 128 - SPARE), F32)], axis=1)
    every = jnp.concatenate([every, jnp.zeros((128 - rows, 128), F32)], axis=0).T
    for i in range(8):
        bias_outs[i][...] = every[i : i + 1, :rows].reshape(rows)
    long = jnp.concatenate([every[8 + j : 9 + j, :rows] for j in range(4)], axis=1)
    bias_outs[8][...] = long.reshape(4 * rows)


def sum_up_kernel(kept0, got0, kept1, got1, out):
    cut = kept0.shape[2]
    out[:, :, :cut] = (kept0[...] + got0[...].astype(F32)).astype(BF)
    out[:, :, cut:] = (kept1[...] + got1[...].astype(F32)).astype(BF)


def sum_one_kernel(kept, got, out):
    out[...] = (kept[...] + got[...].astype(F32)).astype(BF)


def to_owners(summed, rows):
    columns = summed.shape[2]
    got = lax.all_to_all(
        summed.reshape(16 * rows, columns), ALL, 0, 0, tiled=True, axis_index_groups=GROUPS
    )
    return got.reshape(4, 4, rows, columns)


def to_owners_any(whole, rows):
    part = lax.psum_scatter(whole, "dp", scatter_dimension=0, tiled=True).astype(BF)
    return lax.all_to_all(part, "head", 0, 0, tiled=True).reshape(1, 4, rows, -1)


def rows_kernel(kept, got, mine, *sent):
    z = lax.axis_index("dp") // 2
    mine[...] = kept[z] + got[z].astype(F32)
    for k in (1, 2, 3):
        at = lax.rem(z + k, 4)
        sent[k - 1][...] = (kept[at] + got[at].astype(F32)).astype(BF)


def sum_kernel(mine, a, b, c, out):
    total = mine[...] + a[...].astype(F32) + b[...].astype(F32) + c[...].astype(F32)
    out[...] = total.astype(out.dtype)


def body(
    layer_input,
    segment_ids,
    upstream,
    query_weight,
    key_weight,
    value_weight,
    query_bias,
    value_bias,
    output_weight,
    output_bias,
    attn_gain,
    attn_shift,
    up_weight,
    up_bias,
    down_weight,
    down_bias,
    final_gain,
    final_shift,
):
    tok, width = layer_input.shape
    cube = lax.axis_size("dp") == 8
    rows = query_weight.shape[0]
    share = width // 4
    mine = 2 * tok

    x1 = lax.ppermute(layer_input, "head", CHIP)
    x2 = lax.ppermute(layer_input, "head", CORE)
    x3 = lax.ppermute(x1, "head", CORE)
    x = (layer_input, x1, x2, x3)

    up1 = lax.ppermute(upstream, "head", CHIP)
    matrices = (query_weight, key_weight, value_weight, output_weight, up_weight, down_weight)
    biases = (
        query_bias,
        value_bias,
        output_bias,
        attn_gain,
        attn_shift,
        down_bias,
        final_gain,
        final_shift,
        up_bias,
    )
    if cube:
        *pieces, third = pack(matrices, biases)
        for flip in (3, 2, 1):
            pieces[flip] = lax.ppermute(pieces[flip], "head", [(i, i ^ flip) for i in range(4)])
        narrow, wide = call(
            merge_kernel,
            (
                shape((4, rows, 3 * share + SPARE), BF),
                shape((4, rows, 2 * width + width // 2), BF),
            ),
            *pieces,
            third,
            micros=1,
        )
        wide = wide.reshape(4 * rows, -1)
        parts = [narrow.reshape(4 * rows, -1)]
        parts += [lax.ppermute(parts[0], "dp", zshift(k)) for k in (1, 2, 3)]
        parts += [lax.ppermute(part, "dp", XSWAP) for part in parts]
        found = [wide, later(lax.ppermute(wide, "dp", zshift(1)), *parts[1:4])]
        qkv_weight, columns = call(
            functools.partial(join_kernel, (3 * share, SPARE)),
            (shape((width, 3 * share), BF), shape((width, SPARE), BF)),
            *parts,
            after=(found[1],),
            micros=1,
        )
    else:
        qkv_weight, columns, up_full, near, down_full = gather_any(matrices, biases)
    qkv, probs, ctx, bias = call(
        functools.partial(attend_kernel, rows),
        (
            shape((4 * tok, 3 * share), BF),
            shape((share // HD, 4 * tok, 4 * tok), F32),
            shape((4 * tok, share), BF),
            shape((16, width), F32),
        ),
        segment_ids.reshape(4, tok),
        *x,
        qkv_weight,
        columns,
        after=(up1,),
        micros=5,
    )
    ctx_chip = lax.ppermute(ctx, "head", CHIP)
    ctx_core = lax.ppermute(ctx, "head", CORE)
    ctx_far = lax.ppermute(ctx_chip, "head", CORE)
    contexts = (ctx, ctx_chip, ctx_core, ctx_far)
    if cube:
        found.append(later(lax.ppermute(found[1], "dp", zshift(1)), ctx))
        found.append(later(lax.ppermute(found[2], "dp", zshift(1)), ctx_far))
        parts = found + [lax.ppermute(part, "dp", XSWAP) for part in found]
        splits = (width, width // 2, width)
        up_full, near, down_full = call(
            functools.partial(join_kernel, splits),
            tuple(shape((width, s), BF) for s in splits),
            *parts,
            micros=1,
        )
    other = lax.ppermute(near, "head", CORE)

    def ffn(half):
        outs = (
            shape((mine, width), BF),
            shape((mine, width), BF),
            shape((mine, width), F32),
            shape((mine, width), F32 if half == 0 else BF),
        )
        if half == 0:
            outs += (shape((mine, width), F32), shape((mine, 128), F32), shape((mine, width), F32))
        return call(
            functools.partial(ffn_kernel, half),
            outs,
            *x[2 * half : 2 * half + 2],
            *contexts,
            near,
            other,
            up_full,
            down_full,
            bias,
            micros=3,
        )

    def pair_sum(part, sent):
        got = lax.ppermute(sent, "head", CORE)
        kept, low = call(
            add_kernel, (shape((mine, width), F32), shape((mine, width), BF)), part, got, micros=1
        )
        return kept, lax.ppermute(low, "head", CHIP)

    nl1, act1, slope1, sent = ffn(1)
    nl0, act0, slope0, part, unit1, rate1, normed = ffn(0)
    part, far = pair_sum(part, sent)
    layer_output, d_second, ds0, grads2 = call(
        final_kernel,
        (
            shape((tok, width), BF),
            shape((mine, width), F32),
            shape((mine, width), BF),
            shape((8, width), F32),
        ),
        part,
        far,
        normed,
        upstream,
        up1,
        bias,
    )
    ds1 = lax.ppermute(ds0, "head", CORE)

    def grad_outs(columns):
        if cube:
            dims = (4, width // 8, columns)
            return (shape(dims, F32), shape(dims, BF))
        return (shape((width, columns), F32),)

    def ffn_back(low, slope, kind, after):
        return call(
            ffn_back_kernel,
            (shape((mine, width), BF), shape((mine, width), kind), shape((8, width), F32)),
            low,
            slope,
            up_full,
            down_full,
            after=after,
            micros=1,
        )

    down_terms = call(
        weight_grad_kernel, grad_outs(width), act0, act1, ds0, ds1, micros=1
    )
    dh1, sent, hidden1 = ffn_back(ds1, slope1, BF, (down_terms[-1],))
    dh0, part, hidden0 = ffn_back(ds0, slope0, F32, (down_terms[-1],))
    part, far = pair_sum(part, sent)
    up_terms = call(
        weight_grad_kernel, grad_outs(width), nl0, nl1, dh0, dh1, after=(part,), micros=1
    )
    order = (up_terms[-1],)
    if cube:
        got_down = lax.ppermute(down_terms[1], "dp", XSWAP)
        order += (got_down,)
    d_first, df0, grads1 = call(
        first_back_kernel,
        (shape((tok, width), F32), shape((mine, width), BF), shape((8, width), F32)),
        part,
        far,
        d_second,
        unit1,
        rate1,
        bias,
        after=order,
        micros=1,
    )
    df1 = lax.ppermute(df0, "head", CORE)
    order = ()
    if cube:
        down_kept, *down_sent = call(
            rows_kernel,
            (shape((4 * rows, width), F32),) + (shape((4 * rows, width), BF),) * 3,
            down_terms[0],
            got_down,
            after=(df0,),
            micros=1,
        )
        down_got = [lax.ppermute(o, "dp", zshift(k)) for k, o in zip((1, 2, 3), down_sent)]
        order = (down_sent[0],)
    output_terms = call(
        output_grad_kernel,
        grad_outs(share) + (shape((width, share), F32),),
        *contexts,
        df0,
        df1,
        after=order,
        micros=1,
    )[:-1]
    d_qkv = call(
        attend_back_kernel,
        shape((4 * tok, 3 * share), BF),
        df0,
        df1,
        near,
        other,
        qkv,
        probs,
        after=(output_terms[-1],),
        micros=4,
    )
    order = ()
    if cube:
        got_up = lax.ppermute(up_terms[1], "dp", XSWAP)
        got_output = lax.ppermute(output_terms[1], "dp", XSWAP)
        down_grad = call(
            sum_kernel,
            shape((4 * rows, width), F32),
            down_kept,
            *down_got,
            after=(d_qkv,),
            micros=1,
        )
        order = (got_up, down_grad)
    last_terms = call(
        functools.partial(last_grad_kernel, rows),
        grad_outs(3 * share + SPARE),
        *x,
        d_qkv,
        grads2,
        grads1,
        hidden0,
        hidden1,
        after=order,
        micros=2,
    )
    part, sent = call(
        input_grad_kernel,
        (shape((mine, width), F32), shape((mine, width), BF)),
        d_qkv,
        qkv_weight,
        after=(last_terms[-1],),
        micros=1,
    )
    if cube:
        summed = call(
            sum_up_kernel,
            shape((4, 4 * rows, width + share), BF),
            up_terms[0],
            got_up,
            output_terms[0],
            got_output,
            after=(last_terms[-1],),
            micros=1,
        )
        up_got = to_owners(summed, rows)
        got = lax.ppermute(last_terms[1], "dp", XSWAP)
        summed = call(
            sum_one_kernel, shape((4, 4 * rows, 3 * share + SPARE), BF), last_terms[0], got, micros=1
        )
        last_got = to_owners(summed, rows)
    else:
        up_got = to_owners_any(jnp.concatenate([up_terms[0], output_terms[0]], axis=1), rows)
        last_got = to_owners_any(last_terms[0], rows)
        down_grad = lax.psum_scatter(down_terms[0], "dp", scatter_dimension=0, tiled=True)
    got = lax.ppermute(sent, "head", CORE)
    part, sent = call(
        input_add_kernel,
        (shape((tok, width), F32), shape((tok, width), BF)),
        part,
        got,
        d_first,
        micros=1,
    )
    far = lax.ppermute(sent, "head", CHIP)
    input_grad = call(input_end_kernel, shape((tok, width), BF), part, far, micros=1)

    up_grad, output_grad = call(
        functools.partial(finish_up_kernel, rows),
        (shape((rows, 4 * width), F32), shape((rows, width), F32)),
        up_got,
    )
    query_grad, key_grad, value_grad, *bias_out = call(
        finish_last_kernel,
        (shape((rows, width), F32),) * 3 + (shape((rows,), F32),) * 8 + (shape((4 * rows,), F32),),
        last_got,
    )

    return (
        layer_output,
        input_grad,
        query_grad,
        key_grad,
        value_grad,
        bias_out[0],
        bias_out[1],
        output_grad,
        bias_out[2],
        bias_out[3],
        bias_out[4],
        up_grad,
        bias_out[8],
        down_grad,
        bias_out[5],
        bias_out[6],
        bias_out[7],
    )


def input_add_kernel(part, got, d_first, kept, sent):
    tok = kept.shape[0]
    total = part[...] + got[...].astype(F32)
    kept[...] = total[:tok] + d_first[...]
    sent[...] = total[tok:].astype(BF)


def input_end_kernel(kept, far, out):
    out[...] = (kept[...] + far[...].astype(F32)).astype(BF)


def input_grad_kernel(d_qkv, weight, part, sent):
    mine = part.shape[0]
    share = weight.shape[1] // 3
    d = d_qkv[...]
    total = dot(d, weight[...], NT)
    part[...] = total[:mine]
    sent[...] = total[mine:].astype(BF)


def solution(mesh):
    matrix = P(ALL, None)
    vector = P(ALL)
    placed = (
        matrix, P("dp"), matrix, matrix, matrix, matrix, vector, vector, matrix,
        vector, vector, vector, matrix, vector, matrix, vector, vector, vector,
    )
    given = (
        matrix, matrix, matrix, matrix, matrix, vector, vector, matrix, vector,
        vector, vector, matrix, vector, matrix, vector, vector, vector,
    )
    return jax.shard_map(body, mesh=mesh, in_specs=placed, out_specs=given, check_vma=False)
```

time: 324 us -> 212 us (0.65)
  local copies, waits for them, and re-layouts: 65.2 us -> 6.88 us
  other arithmetic: 32.9 us -> 0 us
  Pallas kernels: 0 us -> 28 us
  matrix products: 24 us -> 0 us
  starting transfers between devices: 61.9 us -> 49.8 us
  waiting for transfers between devices: 135 us -> 126 us
    pallas_call x0 -> x30, Pallas kernels: none -> 28 us  [the longest x26 25.6 us: call(): pl.pallas_call(run, out_shape=outs, in_specs=[spec] * count + [pl.BlockSp...]
    dot_general x36 -> x0, matrix products: 24 us -> none  [dot(): return jnp.dot(left, right, preferred_element_type=F32)]
    unnamed x233 -> x30, local copies, waits for them, and re-layouts: 24.1 us -> 6.88 us
    ppermute x42 -> x39, waiting for transfers between devices: 127 us -> 115 us  [the longest x4 28 us: body(): parts = found + [lax.ppermute(part, 'dp', XSWAP) for part in found]]
    ppermute x42 -> x39, starting transfers between devices: 47.8 us -> 39 us  [the longest x4 5.07 us: body(): parts += [lax.ppermute(part, 'dp', XSWAP) for part in parts]]
    concatenate x10 -> x0, other arithmetic: 8.54 us -> none  [the longest x1 1.86 us: body(): jnp.concatenate([up_grad, output_grad], axis=1)]
    gather x6 -> x0, local copies, waits for them, and re-layouts: 7.96 us -> none  [the longest x5 7.4 us: gather_dp(): jnp.take(found, order, axis=0).reshape(8 * piece.shape[0], piece.shape[1])]
    reduce_sum x15 -> x0, other arithmetic: 7.5 us -> none  [the longest x1 1.47 us: body(): last = jnp.sum(last.reshape(dp_count, heads, rows, 3 * share + 128), axis=0)]
  transfers between devices with their start and end apart: 47 -> 42, of which waited for: 23 -> 26; matrix products, arithmetic and copies ran while one was open for 25% -> 0% of each run, Pallas kernels for 0% -> 9%
where the time goes in v2:
time: 212 us
  waiting for transfers between devices  126 us (59%)
  starting transfers between devices  49.8 us (23%)
  Pallas kernels  28 us (13%)
  local copies, waits for them, and re-layouts  6.88 us (3%)
    ppermute x4, waiting for transfers between devices, body(): parts = found + [lax.ppermute(part, 'dp', XSWAP) for part in found]  28 us
    pallas_call x26, Pallas kernels, call(): pl.pallas_call(run, out_shape=outs, in_specs=[spec] * count + [pl.BlockSp...  25.6 us
    ppermute x3, waiting for transfers between devices, body(): parts += [lax.ppermute(parts[0], 'dp', zshift(k)) for k in (1, 2, 3)]  15.4 us
    ppermute x1, waiting for transfers between devices, body(): got = lax.ppermute(last_terms[1], 'dp', XSWAP)  11.5 us
    ppermute x2, waiting for transfers between devices, pair_sum(): return (kept, lax.ppermute(low, 'head', CHIP))  9.82 us
    ppermute x1, waiting for transfers between devices, body(): got_down = lax.ppermute(down_terms[1], 'dp', XSWAP)  9.52 us
    all_to_all x2, starting transfers between devices, to_owners(): lax.all_to_all(summed.reshape(16 * rows, columns), ALL, 0, 0, tiled=True,...  9.2 us
    ppermute x1, waiting for transfers between devices, body(): far = lax.ppermute(sent, 'head', CHIP)  9.19 us
  transfers between devices with their start and end apart: 42, of which 26 were waited for; matrix products, arithmetic and copies ran while one was open for 0% of the time, Pallas kernels for 9%

profile of v2, /device:TPU:0, one launch (start us, length us, event | category | flops | bytes accessed | tf_op | source)
XLA Modules:
  0.0 211.8 jit_solution(18317578719111936898)
XLA Ops:
  0.7 2.4 %shard_map.305 = (bf16[24,1792]{1,0:T(8,128)(2,1)}, bf16[24,1792]{1,0:T(8,128)(2,1)}, bf16[24,1792]{1,0:T(8,128)(2,1)}, bf16[24,1792]{1,0:T(8,128)(2,1)}, bf16[4,24,768]{2,1,0:T(8,128)(2,1)}) custom-call(f32[24,768]{1,0:T(8,128)} %query.1, f32[24,768]{1,0:T(8,128)} %key.1, f32[24,768]{1,0:T(8,128)} %value.1, f32[24,768]{1,0:T(8,128)} %output.1, ...), custom_call_target="tpu_custom_call" | custom-call | tf_op jit(solution)/shard_map/pallas_call | solution.py:145
  3.6 2.6 %collective-permute-start.4 = (bf16[24,1792]{1,0:T(8,128)(2,1)}, bf16[24,1792]{1,0:T(8,128)(2,1)S(1)}, u32[]{:S(2)}, u32[]{:S(2)}) collective-permute-start(bf16[24,1792]{1,0:T(8,128)(2,1)} %get-tuple-element.93), channel_id=1, source_target_pairs={{0,2},{1,3},{2,0},{3,1},{4,6},{5,7},{6,4},{7,5},{8,10},{9,11},{10,... | collective-permute-start | bytes 258056 | tf_op jit(solution)/shard_map/ppermute | solution.py:569
  6.3 3.3 %collective-permute-done.4.refs_2_ = bf16[24,1792]{1,0:T(8,128)(2,1)S(1)} collective-permute-done((bf16[24,1792]{1,0:T(8,128)(2,1)}, bf16[24,1792]{1,0:T(8,128)(2,1)S(1)}, u32[]{:S(2)}, u32[]{:S(2)}) %collective-permute-start.4) | collective-permute-done | bytes 86048 | tf_op jit(solution)/shard_map/ppermute | solution.py:569
  9.6 1.6 collective-permute-done.5.refs_3_
  13.0 1.7 collective-permute-start.13
  14.7 2.2 %collective-permute-start.8 = (bf16[96,640]{1,0:T(8,128)(2,1)S(1)}, bf16[96,640]{1,0:T(8,128)(2,1)S(1)}, u32[]{:S(2)}, u32[]{:S(2)}) collective-permute-start(bf16[96,640]{1,0:T(8,128)(2,1)S(1)} %bitcast.13), channel_id=1, source_target_pairs={{0,24},{4,28},{8,0},{12,4},{16,8},{20,12},{24,16},{28,20},{1,25},{... | collective-permute-start | bytes 368648 | tf_op jit(solution)/shard_map/ppermute | solution.py:582
  17.8 1.6 collective-permute-start.6
  20.8 7.0 %collective-permute-done.8.refs_3_ = bf16[96,640]{1,0:T(8,128)(2,1)S(1)} collective-permute-done((bf16[96,640]{1,0:T(8,128)(2,1)S(1)}, bf16[96,640]{1,0:T(8,128)(2,1)S(1)}, u32[]{:S(2)}, u32[]{:S(2)}) %collective-permute-start.8) | collective-permute-done | bytes 122912 | tf_op jit(solution)/shard_map/ppermute | solution.py:582
  27.8 8.5 %collective-permute-done.7.refs_2_ = bf16[96,640]{1,0:T(8,128)(2,1)S(1)} collective-permute-done((bf16[96,640]{1,0:T(8,128)(2,1)S(1)}, bf16[96,640]{1,0:T(8,128)(2,1)S(1)}, u32[]{:S(2)}, u32[]{:S(2)}) %collective-permute-start.7) | collective-permute-done | bytes 122912 | tf_op jit(solution)/shard_map/ppermute | solution.py:582
  36.3 1.6 collective-permute-start.9
  38.4 1.5 collective-permute-start.11
  39.9 2.7 %collective-permute-done.9.refs_4_ = bf16[96,640]{1,0:T(8,128)(2,1)S(1)} collective-permute-done((bf16[96,640]{1,0:T(8,128)(2,1)S(1)}, bf16[96,640]{1,0:T(8,128)(2,1)S(1)}, u32[]{:S(2)}, u32[]{:S(2)}) %collective-permute-start.9) | collective-permute-done | bytes 122912 | tf_op jit(solution)/shard_map/ppermute | solution.py:583
  42.6 1.5 collective-permute-start.14
  45.2 1.7 collective-permute-done.11.refs_6_
  46.9 1.5 collective-permute-start.10
  48.4 3.4 %collective-permute-done.10.refs_5_ = bf16[96,640]{1,0:T(8,128)(2,1)S(1)} collective-permute-done((bf16[96,640]{1,0:T(8,128)(2,1)S(1)}, bf16[96,640]{1,0:T(8,128)(2,1)S(1)}, u32[]{:S(2)}, u32[]{:S(2)}) %collective-permute-start.10) | collective-permute-done | bytes 122912 | tf_op jit(solution)/shard_map/ppermute | solution.py:583
  52.0 5.0 %shard_map.309 = (bf16[512,576]{1,0:T(8,128)(2,1)S(1)}, f32[3,512,512]{2,1,0:T(8,128)S(1)}, bf16[512,192]{1,0:T(8,128)(2,1)S(1)}, f32[16,768]{1,0:T(8,128)S(1)}) custom-call(s32[4,128]{1,0:T(4,128)S(1)} %bitcast.18, bf16[128,768]{1,0:T(8,128)(2,1)S(1)} %copy-done.1, bf16[128,768]{1,0:T(8,128)(2,1)S(1)} %collective-permute-done.refs_2_.refs_1_, ...), custom_call_target="tpu_custom_call" | custom-call | flops 100000000 | bytes 500000 | tf_op jit(solution)/shard_map/pallas_call | solution.py:39
  57.1 1.6 collective-permute-start.15
  59.0 4.5 %collective-permute-done.15.refs_3_.refs_1_ = bf16[512,192]{1,0:T(8,128)(2,1)S(1)} collective-permute-done((bf16[512,192]{1,0:T(8,128)(2,1)S(1)}, bf16[512,192]{1,0:T(8,128)(2,1)S(1)}, u32[]{:S(2)}, u32[]{:S(2)}) %collective-permute-start.15) | collective-permute-done | bytes 196640 | tf_op jit(solution)/shard_map/ppermute | solution.py:609
  67.0 1.7 collective-permute-done.19.refs_0_
  70.2 4.7 %collective-permute-done.20.refs_4_ = bf16[96,1920]{1,0:T(8,128)(2,1)S(1)} collective-permute-done((bf16[96,1920]{1,0:T(8,128)(2,1)S(1)}, bf16[96,1920]{1,0:T(8,128)(2,1)S(1)}, u32[]{:S(2)}, u32[]{:S(2)}) %collective-permute-start.20) | collective-permute-done | bytes 368672 | tf_op jit(solution)/shard_map/ppermute | solution.py:616
  74.9 7.9 %collective-permute-done.21.refs_5_ = bf16[96,1920]{1,0:T(8,128)(2,1)S(1)} collective-permute-done((bf16[96,1920]{1,0:T(8,128)(2,1)S(1)}, bf16[96,1920]{1,0:T(8,128)(2,1)S(1)}, u32[]{:S(2)}, u32[]{:S(2)}) %collective-permute-start.21) | collective-permute-done | bytes 368672 | tf_op jit(solution)/shard_map/ppermute | solution.py:616
  82.8 7.9 %collective-permute-done.22.refs_6_ = bf16[96,1920]{1,0:T(8,128)(2,1)S(1)} collective-permute-done((bf16[96,1920]{1,0:T(8,128)(2,1)S(1)}, bf16[96,1920]{1,0:T(8,128)(2,1)S(1)}, u32[]{:S(2)}, u32[]{:S(2)}) %collective-permute-start.22) | collective-permute-done | bytes 368672 | tf_op jit(solution)/shard_map/ppermute | solution.py:616
  90.7 7.5 %collective-permute-done.23.refs_7_ = bf16[96,1920]{1,0:T(8,128)(2,1)S(1)} collective-permute-done((bf16[96,1920]{1,0:T(8,128)(2,1)S(1)}, bf16[96,1920]{1,0:T(8,128)(2,1)S(1)}, u32[]{:S(2)}, u32[]{:S(2)}) %collective-permute-start.23) | collective-permute-done | bytes 368672 | tf_op jit(solution)/shard_map/ppermute | solution.py:616
  99.0 1.9 collective-permute-done.16.refs_4_.refs_2_
  100.9 1.9 shard_map.314
  103.0 1.9 shard_map.313
  105.0 1.6 collective-permute-start.26
  106.7 9.8 %collective-permute-done.26.refs_1_ = bf16[256,768]{1,0:T(8,128)(2,1)S(1)} collective-permute-done((bf16[256,768]{1,0:T(8,128)(2,1)S(1)}, bf16[256,768]{1,0:T(8,128)(2,1)S(1)}, u32[]{:S(2)}, u32[]{:S(2)}) %collective-permute-start.26) | collective-permute-done | bytes 393248 | tf_op jit(solution)/shard_map/ppermute | solution.py:653
  117.6 1.7 collective-permute-done.27.refs_3_.refs_0_
  121.3 1.5 collective-permute-start.30
  123.9 1.6 collective-permute-start.29
  127.9 9.5 %collective-permute-done.30.refs_7_.refs_1_ = bf16[4,96,768]{2,1,0:T(8,128)(2,1)S(1)} collective-permute-done((bf16[4,96,768]{2,1,0:T(8,128)(2,1)S(1)}, bf16[4,96,768]{2,1,0:T(8,128)(2,1)S(1)}, u32[]{:S(2)}, u32[]{:S(2)}) %collective-permute-start.30) | collective-permute-done | bytes 589856 | tf_op jit(solution)/shard_map/ppermute | solution.py:704
  138.3 3.5 %collective-permute-start.35 = (bf16[96,768]{1,0:T(8,128)(2,1)S(1)}, bf16[96,768]{1,0:T(8,128)(2,1)S(1)}, u32[]{:S(2)}, u32[]{:S(2)}) collective-permute-start(bf16[96,768]{1,0:T(8,128)(2,1)S(1)} %get-tuple-element.141), channel_id=1, source_target_pairs={{0,24},{4,28},{8,0},{12,4},{16,8},{20,12},{24,16},{28,20},{1,25},{... | collective-permute-start | bytes 442376 | tf_op jit(solution)/shard_map/ppermute | solution.py:729
  142.3 1.7 shard_map.324
  144.0 3.0 %shard_map.325.refs_4_.refs_0_ = bf16[512,576]{1,0:T(8,128)(2,1)S(1)} custom-call(bf16[256,768]{1,0:T(8,128)(2,1)S(1)} %get-tuple-element.129.refs_2_.refs_4_.refs_0_, bf16[256,768]{1,0:T(8,128)(2,1)S(1)} %collective-permute-done.31.refs_5_.refs_1_, bf16[768,384]{1,0:T(8,128)(2,1)S(1)} %get-tuple-element.101.refs_6_.refs_2_, ...), custom_call_target="tpu_custom_call" | custom-call | flops 80000000 | bytes 400000 | tf_op jit(solution)/shard_map/pallas_call | solution.py:39
  147.0 2.0 collective-permute-done.34.refs_2_
  149.0 3.7 %collective-permute-done.33.refs_1_ = bf16[96,768]{1,0:T(8,128)(2,1)S(1)} collective-permute-done((bf16[96,768]{1,0:T(8,128)(2,1)S(1)}, bf16[96,768]{1,0:T(8,128)(2,1)S(1)}, u32[]{:S(2)}, u32[]{:S(2)}) %collective-permute-start.33) | collective-permute-done | bytes 147488 | tf_op jit(solution)/shard_map/ppermute | solution.py:729
  155.3 1.6 collective-permute-start.38
  156.8 11.5 %collective-permute-done.38.refs_1_ = bf16[4,96,640]{2,1,0:T(8,128)(2,1)S(1)} collective-permute-done((bf16[4,96,640]{2,1,0:T(8,128)(2,1)S(1)}, bf16[4,96,640]{2,1,0:T(8,128)(2,1)S(1)}, u32[]{:S(2)}, u32[]{:S(2)}) %collective-permute-start.38) | collective-permute-done | bytes 491552 | tf_op jit(solution)/shard_map/ppermute | solution.py:797
  169.2 5.1 %all-to-all-start = ((bf16[16,24,640]{2,1,0:T(8,128)(2,1)}), bf16[16,24,640]{2,1,0:T(8,128)(2,1)S(1)}, u32[]{:S(2)}, u32[]{:S(2)}) async-start(bf16[16,24,640]{2,1,0:T(8,128)(2,1)} %bitcast.9), calls=%async_computation | async-start | bytes 983040 | tf_op jit(solution)/shard_map/all_to_all | solution.py:498
  174.3 1.5 collective-permute-start.39
  175.8 5.8 %collective-permute-done.39.refs_3_ = bf16[4,96,192]{2,1,0:T(8,128)(2,1)S(1)} collective-permute-done((bf16[4,96,192]{2,1,0:T(8,128)(2,1)S(1)}, bf16[4,96,192]{2,1,0:T(8,128)(2,1)S(1)}, u32[]{:S(2)}, u32[]{:S(2)}) %collective-permute-start.39) | collective-permute-done | bytes 147488 | tf_op jit(solution)/shard_map/ppermute | solution.py:755
  184.9 3.2 %all-to-all-done = bf16[16,24,640]{2,1,0:T(8,128)(2,1)S(1)} async-done(((bf16[16,24,640]{2,1,0:T(8,128)(2,1)}), bf16[16,24,640]{2,1,0:T(8,128)(2,1)S(1)}, u32[]{:S(2)}, u32[]{:S(2)}) %all-to-all-start) | async-done | bytes 491552 | tf_op jit(solution)/shard_map/all_to_all | solution.py:498
  188.1 4.1 %all-to-all-start.1 = ((bf16[16,24,960]{2,1,0:T(8,128)(2,1)}), bf16[16,24,960]{2,1,0:T(8,128)(2,1)S(1)}, u32[]{:S(2)}, u32[]{:S(2)}) async-start(bf16[16,24,960]{2,1,0:T(8,128)(2,1)} %bitcast.5), calls=%async_computation.1 | async-start | bytes 1572864 | tf_op jit(solution)/shard_map/all_to_all | solution.py:498
  194.9 2.0 collective-permute-start.37
  196.9 9.2 %collective-permute-done.37.refs_1_ = bf16[128,768]{1,0:T(8,128)(2,1)S(1)} collective-permute-done((bf16[128,768]{1,0:T(8,128)(2,1)S(1)}, bf16[128,768]{1,0:T(8,128)(2,1)S(1)}, u32[]{:S(2)}, u32[]{:S(2)}) %collective-permute-start.37) | collective-permute-done | bytes 196640 | tf_op jit(solution)/shard_map/ppermute | solution.py:815
  207.6 3.2 %all-to-all-done.1 = bf16[16,24,960]{2,1,0:T(8,128)(2,1)S(1)} async-done(((bf16[16,24,960]{2,1,0:T(8,128)(2,1)}), bf16[16,24,960]{2,1,0:T(8,128)(2,1)S(1)}, u32[]{:S(2)}, u32[]{:S(2)}) %all-to-all-start.1) | async-done | bytes 737312 | tf_op jit(solution)/shard_map/all_to_all | solution.py:498
  (96 shorter events, 33.0 us)
Async XLA Ops:
  0.7 18.7 %copy-start.1 = (bf16[128,768]{1,0:T(8,128)(2,1)S(1)}, bf16[128,768]{1,0:T(8,128)(2,1)}, u32[]{:S(2)}) copy-start(bf16[128,768]{1,0:T(8,128)(2,1)} %refs_0_.5) | copy-start | bytes 589828
  0.7 41.9 %copy-start.11 = (bf16[128,768]{1,0:T(8,128)(2,1)S(1)}, bf16[128,768]{1,0:T(8,128)(2,1)}, u32[]{:S(2)}) copy-start(bf16[128,768]{1,0:T(8,128)(2,1)} %refs_3_.3) | copy-start | bytes 589828
  3.1 3.2 %collective-permute-start.3 = (bf16[24,1792]{1,0:T(8,128)(2,1)}, bf16[24,1792]{1,0:T(8,128)(2,1)S(1)}, u32[]{:S(2)}, u32[]{:S(2)}) collective-permute-start(bf16[24,1792]{1,0:T(8,128)(2,1)} %get-tuple-element.92), channel_id=1, source_target_pairs={{0,1},{1,0},{2,3},{3,2},{4,5},{5,4},{6,7},{7,6},{8,9},{9,8},{10,11... | collective-permute-start | bytes 258056 | tf_op jit(solution)/shard_map/ppermute | solution.py:569
  3.6 6.0 %collective-permute-start.4 = (bf16[24,1792]{1,0:T(8,128)(2,1)}, bf16[24,1792]{1,0:T(8,128)(2,1)S(1)}, u32[]{:S(2)}, u32[]{:S(2)}) collective-permute-start(bf16[24,1792]{1,0:T(8,128)(2,1)} %get-tuple-element.93), channel_id=1, source_target_pairs={{0,2},{1,3},{2,0},{3,1},{4,6},{5,7},{6,4},{7,5},{8,10},{9,11},{10,... | collective-permute-start | bytes 258056 | tf_op jit(solution)/shard_map/ppermute | solution.py:569
  6.2 5.0 %collective-permute-start.5 = (bf16[24,1792]{1,0:T(8,128)(2,1)}, bf16[24,1792]{1,0:T(8,128)(2,1)S(1)}, u32[]{:S(2)}, u32[]{:S(2)}) collective-permute-start(bf16[24,1792]{1,0:T(8,128)(2,1)} %get-tuple-element.94), channel_id=1, source_target_pairs={{0,3},{1,2},{2,1},{3,0},{4,7},{5,6},{6,5},{7,4},{8,11},{9,10},{10,... | collective-permute-start | bytes 258056 | tf_op jit(solution)/shard_map/ppermute | solution.py:569
  13.0 23.2 %collective-permute-start.13 = (bf16[96,1920]{1,0:T(8,128)(2,1)S(1)}, bf16[96,1920]{1,0:T(8,128)(2,1)S(1)}, u32[]{:S(2)}, u32[]{:S(2)}) collective-permute-start(bf16[96,1920]{1,0:T(8,128)(2,1)S(1)} %bitcast.10), channel_id=1, source_target_pairs={{0,8},{4,12},{8,16},{12,20},{16,24},{20,28},{24,0},{28,4},{1,9},{5... | collective-permute-start | bytes 1105928 | tf_op jit(solution)/shard_map/ppermute | solution.py:584
  14.7 37.3 %copy-start.14 = (s32[512]{0:T(512)S(1)}, s32[512]{0:T(512)}, u32[]{:S(2)}) copy-start(s32[512]{0:T(512)} %param.19) | copy-start | bytes 6148
  14.7 13.1 %collective-permute-start.8 = (bf16[96,640]{1,0:T(8,128)(2,1)S(1)}, bf16[96,640]{1,0:T(8,128)(2,1)S(1)}, u32[]{:S(2)}, u32[]{:S(2)}) collective-permute-start(bf16[96,640]{1,0:T(8,128)(2,1)S(1)} %bitcast.13), channel_id=1, source_target_pairs={{0,24},{4,28},{8,0},{12,4},{16,8},{20,12},{24,16},{28,20},{1,25},{... | collective-permute-start | bytes 368648 | tf_op jit(solution)/shard_map/ppermute | solution.py:582
  16.9 19.3 %collective-permute-start.7 = (bf16[96,640]{1,0:T(8,128)(2,1)S(1)}, bf16[96,640]{1,0:T(8,128)(2,1)S(1)}, u32[]{:S(2)}, u32[]{:S(2)}) collective-permute-start(bf16[96,640]{1,0:T(8,128)(2,1)S(1)} %bitcast.14), channel_id=1, source_target_pairs={{0,16},{4,20},{8,24},{12,28},{16,0},{20,4},{24,8},{28,12},{1,17},{... | collective-permute-start | bytes 368648 | tf_op jit(solution)/shard_map/ppermute | solution.py:582
  17.8 18.5 %collective-permute-start.6 = (bf16[96,640]{1,0:T(8,128)(2,1)S(1)}, bf16[96,640]{1,0:T(8,128)(2,1)S(1)}, u32[]{:S(2)}, u32[]{:S(2)}) collective-permute-start(bf16[96,640]{1,0:T(8,128)(2,1)S(1)} %bitcast.15), channel_id=1, source_target_pairs={{0,8},{4,12},{8,16},{12,20},{16,24},{20,28},{24,0},{28,4},{1,9},{5... | collective-permute-start | bytes 368648 | tf_op jit(solution)/shard_map/ppermute | solution.py:582
  19.3 20.6 %collective-permute-start = (bf16[128,768]{1,0:T(8,128)(2,1)S(1)}, bf16[128,768]{1,0:T(8,128)(2,1)S(1)}, u32[]{:S(2)}, u32[]{:S(2)}) collective-permute-start(bf16[128,768]{1,0:T(8,128)(2,1)S(1)} %copy-done.1), channel_id=1, source_target_pairs={{0,2},{1,3},{2,0},{3,1},{4,6},{5,7},{6,4},{7,5},{8,10},{9,11},{10,... | collective-permute-start | bytes 589832 | tf_op jit(solution)/shard_map/ppermute | solution.py:548
  36.2 22.4 %collective-permute-start.18 = (bf16[96,1920]{1,0:T(8,128)(2,1)S(1)}, bf16[96,1920]{1,0:T(8,128)(2,1)S(1)}, u32[]{:S(2)}, u32[]{:S(2)}) collective-permute-start(bf16[96,1920]{1,0:T(8,128)(2,1)S(1)} %shard_map.307.refs_8_.refs_1_), channel_id=1, source_target_pairs={{0,8},{4,12},{8,16},{12,20},{16,24},{20,28},{24,0},{28,4},{1,9},{5... | collective-permute-start | bytes 1105928 | tf_op jit(solution)/shard_map/ppermute | solution.py:614
  36.3 6.2 %collective-permute-start.9 = (bf16[96,640]{1,0:T(8,128)(2,1)S(1)}, bf16[96,640]{1,0:T(8,128)(2,1)S(1)}, u32[]{:S(2)}, u32[]{:S(2)}) collective-permute-start(bf16[96,640]{1,0:T(8,128)(2,1)S(1)} %bitcast.16), channel_id=1, source_target_pairs={{0,4},{4,0},{8,12},{12,8},{16,20},{20,16},{24,28},{28,24},{1,5},{5... | collective-permute-start | bytes 368648 | tf_op jit(solution)/shard_map/ppermute | solution.py:583
  37.9 7.3 %collective-permute-start.12 = (bf16[96,640]{1,0:T(8,128)(2,1)S(1)}, bf16[96,640]{1,0:T(8,128)(2,1)S(1)}, u32[]{:S(2)}, u32[]{:S(2)}) collective-permute-start(bf16[96,640]{1,0:T(8,128)(2,1)S(1)} %collective-permute-done.8.refs_3_), channel_id=1, source_target_pairs={{0,4},{4,0},{8,12},{12,8},{16,20},{20,16},{24,28},{28,24},{1,5},{5... | collective-permute-start | bytes 368648 | tf_op jit(solution)/shard_map/ppermute | solution.py:583
  38.4 8.5 %collective-permute-start.11 = (bf16[96,640]{1,0:T(8,128)(2,1)S(1)}, bf16[96,640]{1,0:T(8,128)(2,1)S(1)}, u32[]{:S(2)}, u32[]{:S(2)}) collective-permute-start(bf16[96,640]{1,0:T(8,128)(2,1)S(1)} %collective-permute-done.7.refs_2_), channel_id=1, source_target_pairs={{0,4},{4,0},{8,12},{12,8},{16,20},{20,16},{24,28},{28,24},{1,5},{5... | collective-permute-start | bytes 368648 | tf_op jit(solution)/shard_map/ppermute | solution.py:583
  39.9 12.1 %collective-permute-start.1 = (bf16[128,768]{1,0:T(8,128)(2,1)S(1)}, bf16[128,768]{1,0:T(8,128)(2,1)S(1)}, u32[]{:S(2)}, u32[]{:S(2)}) collective-permute-start(bf16[128,768]{1,0:T(8,128)(2,1)S(1)} %copy-done.1), channel_id=1, source_target_pairs={{0,1},{1,0},{2,3},{3,2},{4,5},{5,4},{6,7},{7,6},{8,9},{9,8},{10,11... | collective-permute-start | bytes 589832 | tf_op jit(solution)/shard_map/ppermute | solution.py:549
  42.6 9.4 %collective-permute-start.14 = (bf16[128,768]{1,0:T(8,128)(2,1)S(1)}, bf16[128,768]{1,0:T(8,128)(2,1)S(1)}, u32[]{:S(2)}, u32[]{:S(2)}) collective-permute-start(bf16[128,768]{1,0:T(8,128)(2,1)S(1)} %copy-done.11), channel_id=1, source_target_pairs={{0,2},{1,3},{2,0},{3,1},{4,6},{5,7},{6,4},{7,5},{8,10},{9,11},{10,... | collective-permute-start | bytes 589832 | tf_op jit(solution)/shard_map/ppermute | solution.py:553
  45.2 6.8 %collective-permute-start.2 = (bf16[128,768]{1,0:T(8,128)(2,1)S(1)}, bf16[128,768]{1,0:T(8,128)(2,1)S(1)}, u32[]{:S(2)}, u32[]{:S(2)}) collective-permute-start(bf16[128,768]{1,0:T(8,128)(2,1)S(1)} %collective-permute-done.refs_2_.refs_1_), channel_id=1, source_target_pairs={{0,1},{1,0},{2,3},{3,2},{4,5},{5,4},{6,7},{7,6},{8,9},{9,8},{10,11... | collective-permute-start | bytes 589832 | tf_op jit(solution)/shard_map/ppermute | solution.py:550
  46.9 4.9 %collective-permute-start.10 = (bf16[96,640]{1,0:T(8,128)(2,1)S(1)}, bf16[96,640]{1,0:T(8,128)(2,1)S(1)}, u32[]{:S(2)}, u32[]{:S(2)}) collective-permute-start(bf16[96,640]{1,0:T(8,128)(2,1)S(1)} %collective-permute-done.6.refs_1_), channel_id=1, source_target_pairs={{0,4},{4,0},{8,12},{12,8},{16,20},{20,16},{24,28},{28,24},{1,5},{5... | collective-permute-start | bytes 368648 | tf_op jit(solution)/shard_map/ppermute | solution.py:583
  57.1 6.4 %collective-permute-start.15 = (bf16[512,192]{1,0:T(8,128)(2,1)S(1)}, bf16[512,192]{1,0:T(8,128)(2,1)S(1)}, u32[]{:S(2)}, u32[]{:S(2)}) collective-permute-start(bf16[512,192]{1,0:T(8,128)(2,1)S(1)} %get-tuple-element.100.refs_1_.refs_2_.refs_0_), channel_id=1, source_target_pairs={{0,2},{1,3},{2,0},{3,1},{4,6},{5,7},{6,4},{7,5},{8,10},{9,11},{10,... | collective-permute-start | bytes 589832 | tf_op jit(solution)/shard_map/ppermute | solution.py:609
  58.7 10.0 %collective-permute-start.19 = (bf16[96,1920]{1,0:T(8,128)(2,1)S(1)}, bf16[96,1920]{1,0:T(8,128)(2,1)S(1)}, u32[]{:S(2)}, u32[]{:S(2)}) collective-permute-start(bf16[96,1920]{1,0:T(8,128)(2,1)S(1)} %shard_map.310.refs_2_), channel_id=1, source_target_pairs={{0,8},{4,12},{8,16},{12,20},{16,24},{20,28},{24,0},{28,4},{1,9},{5... | collective-permute-start | bytes 1105928 | tf_op jit(solution)/shard_map/ppermute | solution.py:615
  63.5 3.5 %collective-permute-start.17 = (bf16[512,192]{1,0:T(8,128)(2,1)S(1)}, bf16[512,192]{1,0:T(8,128)(2,1)S(1)}, u32[]{:S(2)}, u32[]{:S(2)}) collective-permute-start(bf16[512,192]{1,0:T(8,128)(2,1)S(1)} %collective-permute-done.15.refs_3_.refs_1_), channel_id=1, source_target_pairs={{0,1},{1,0},{2,3},{3,2},{4,5},{5,4},{6,7},{7,6},{8,9},{9,8},{10,11... | collective-permute-start | bytes 589832 | tf_op jit(solution)/shard_map/ppermute | solution.py:611
  63.5 11.4 %collective-permute-start.20 = (bf16[96,1920]{1,0:T(8,128)(2,1)S(1)}, bf16[96,1920]{1,0:T(8,128)(2,1)S(1)}, u32[]{:S(2)}, u32[]{:S(2)}) collective-permute-start(bf16[96,1920]{1,0:T(8,128)(2,1)S(1)} %bitcast.11), channel_id=1, source_target_pairs={{0,4},{4,0},{8,12},{12,8},{16,20},{20,16},{24,28},{28,24},{1,5},{5... | collective-permute-start | bytes 1105928 | tf_op jit(solution)/shard_map/ppermute | solution.py:616
  65.0 17.8 %collective-permute-start.21 = (bf16[96,1920]{1,0:T(8,128)(2,1)S(1)}, bf16[96,1920]{1,0:T(8,128)(2,1)S(1)}, u32[]{:S(2)}, u32[]{:S(2)}) collective-permute-start(bf16[96,1920]{1,0:T(8,128)(2,1)S(1)} %shard_map.307.refs_8_.refs_1_), channel_id=1, source_target_pairs={{0,4},{4,0},{8,12},{12,8},{16,20},{20,16},{24,28},{28,24},{1,5},{5... | collective-permute-start | bytes 1105928 | tf_op jit(solution)/shard_map/ppermute | solution.py:616
  65.5 25.2 %collective-permute-start.22 = (bf16[96,1920]{1,0:T(8,128)(2,1)S(1)}, bf16[96,1920]{1,0:T(8,128)(2,1)S(1)}, u32[]{:S(2)}, u32[]{:S(2)}) collective-permute-start(bf16[96,1920]{1,0:T(8,128)(2,1)S(1)} %shard_map.310.refs_2_), channel_id=1, source_target_pairs={{0,4},{4,0},{8,12},{12,8},{16,20},{20,16},{24,28},{28,24},{1,5},{5... | collective-permute-start | bytes 1105928 | tf_op jit(solution)/shard_map/ppermute | solution.py:616
  68.7 29.5 %collective-permute-start.23 = (bf16[96,1920]{1,0:T(8,128)(2,1)S(1)}, bf16[96,1920]{1,0:T(8,128)(2,1)S(1)}, u32[]{:S(2)}, u32[]{:S(2)}) collective-permute-start(bf16[96,1920]{1,0:T(8,128)(2,1)S(1)} %shard_map.311.refs_3_), channel_id=1, source_target_pairs={{0,4},{4,0},{8,12},{12,8},{16,20},{20,16},{24,28},{28,24},{1,5},{5... | collective-permute-start | bytes 1105928 | tf_op jit(solution)/shard_map/ppermute | solution.py:616
  98.4 2.4 %collective-permute-start.24 = (bf16[768,384]{1,0:T(8,128)(2,1)S(1)}, bf16[768,384]{1,0:T(8,128)(2,1)S(1)}, u32[]{:S(2)}, u32[]{:S(2)}) collective-permute-start(bf16[768,384]{1,0:T(8,128)(2,1)S(1)} %get-tuple-element.101.refs_6_.refs_2_), channel_id=1, source_target_pairs={{0,1},{1,0},{2,3},{3,2},{4,5},{5,4},{6,7},{7,6},{8,9},{9,8},{10,11... | collective-permute-start | bytes 1769480 | tf_op jit(solution)/shard_map/ppermute | solution.py:624
  98.5 2.4 %collective-permute-start.16 = (bf16[512,192]{1,0:T(8,128)(2,1)S(1)}, bf16[512,192]{1,0:T(8,128)(2,1)S(1)}, u32[]{:S(2)}, u32[]{:S(2)}) collective-permute-start(bf16[512,192]{1,0:T(8,128)(2,1)S(1)} %get-tuple-element.100.refs_1_.refs_2_.refs_0_), channel_id=1, source_target_pairs={{0,1},{1,0},{2,3},{3,2},{4,5},{5,4},{6,7},{7,6},{8,9},{9,8},{10,11... | collective-permute-start | bytes 589832 | tf_op jit(solution)/shard_map/ppermute | solution.py:610
  102.8 2.1 collective-permute-start.25
  105.0 11.5 %collective-permute-start.26 = (bf16[256,768]{1,0:T(8,128)(2,1)S(1)}, bf16[256,768]{1,0:T(8,128)(2,1)S(1)}, u32[]{:S(2)}, u32[]{:S(2)}) collective-permute-start(bf16[256,768]{1,0:T(8,128)(2,1)S(1)} %get-tuple-element.108), channel_id=1, source_target_pairs={{0,2},{1,3},{2,0},{3,1},{4,6},{5,7},{6,4},{7,5},{8,10},{9,11},{10,... | collective-permute-start | bytes 1179656 | tf_op jit(solution)/shard_map/ppermute | solution.py:653
  117.6 1.7 collective-permute-start.27
  121.1 2.6 %collective-permute-start.28 = (bf16[256,768]{1,0:T(8,128)(2,1)S(1)}, bf16[256,768]{1,0:T(8,128)(2,1)S(1)}, u32[]{:S(2)}, u32[]{:S(2)}) collective-permute-start(bf16[256,768]{1,0:T(8,128)(2,1)S(1)} %get-tuple-element.118), channel_id=1, source_target_pairs={{0,1},{1,0},{2,3},{3,2},{4,5},{5,4},{6,7},{7,6},{8,9},{9,8},{10,11... | collective-permute-start | bytes 1179656 | tf_op jit(solution)/shard_map/ppermute | solution.py:649
  121.3 16.2 %collective-permute-start.30 = (bf16[4,96,768]{2,1,0:T(8,128)(2,1)S(1)}, bf16[4,96,768]{2,1,0:T(8,128)(2,1)S(1)}, u32[]{:S(2)}, u32[]{:S(2)}) collective-permute-start(bf16[4,96,768]{2,1,0:T(8,128)(2,1)S(1)} %get-tuple-element.115.refs_4_), channel_id=1, source_target_pairs={{0,4},{4,0},{8,12},{12,8},{16,20},{20,16},{24,28},{28,24},{1,5},{5... | collective-permute-start | bytes 1769480 | tf_op jit(solution)/shard_map/ppermute | solution.py:704
  123.9 13.6 %collective-permute-start.29 = (bf16[256,768]{1,0:T(8,128)(2,1)S(1)}, bf16[256,768]{1,0:T(8,128)(2,1)S(1)}, u32[]{:S(2)}, u32[]{:S(2)}) collective-permute-start(bf16[256,768]{1,0:T(8,128)(2,1)S(1)} %get-tuple-element.120), channel_id=1, source_target_pairs={{0,2},{1,3},{2,0},{3,1},{4,6},{5,7},{6,4},{7,5},{8,10},{9,11},{10,... | collective-permute-start | bytes 1179656 | tf_op jit(solution)/shard_map/ppermute | solution.py:653
  127.3 26.1 %collective-permute-start.32 = (bf16[4,96,768]{2,1,0:T(8,128)(2,1)S(1)}, bf16[4,96,768]{2,1,0:T(8,128)(2,1)S(1)}, u32[]{:S(2)}, u32[]{:S(2)}) collective-permute-start(bf16[4,96,768]{2,1,0:T(8,128)(2,1)S(1)} %get-tuple-element.128.refs_6_), channel_id=1, source_target_pairs={{0,4},{4,0},{8,12},{12,8},{16,20},{20,16},{24,28},{28,24},{1,5},{5... | collective-permute-start | bytes 1769480 | tf_op jit(solution)/shard_map/ppermute | solution.py:754
  138.0 4.3 %copy-start.7 = (f32[128,768]{1,0:T(8,128)}, f32[128,768]{1,0:T(8,128)S(1)}, u32[]{:S(2)}) copy-start(f32[128,768]{1,0:T(8,128)S(1)} %get-tuple-element.145.refs_2_) | copy-start | bytes 1179652
  138.0 4.3 %collective-permute-start.31 = (bf16[256,768]{1,0:T(8,128)(2,1)S(1)}, bf16[256,768]{1,0:T(8,128)(2,1)S(1)}, u32[]{:S(2)}, u32[]{:S(2)}) collective-permute-start(bf16[256,768]{1,0:T(8,128)(2,1)S(1)} %get-tuple-element.129.refs_2_.refs_4_.refs_0_), channel_id=1, source_target_pairs={{0,1},{1,0},{2,3},{3,2},{4,5},{5,4},{6,7},{7,6},{8,9},{9,8},{10,11... | collective-permute-start | bytes 1179656 | tf_op jit(solution)/shard_map/ppermute | solution.py:718
  138.2 10.8 %collective-permute-start.34 = (bf16[96,768]{1,0:T(8,128)(2,1)S(1)}, bf16[96,768]{1,0:T(8,128)(2,1)S(1)}, u32[]{:S(2)}, u32[]{:S(2)}) collective-permute-start(bf16[96,768]{1,0:T(8,128)(2,1)S(1)} %get-tuple-element.140), channel_id=1, source_target_pairs={{0,16},{4,20},{8,24},{12,28},{16,0},{20,4},{24,8},{28,12},{1,17},{... | collective-permute-start | bytes 442376 | tf_op jit(solution)/shard_map/ppermute | solution.py:729
  138.3 10.7 %collective-permute-start.35 = (bf16[96,768]{1,0:T(8,128)(2,1)S(1)}, bf16[96,768]{1,0:T(8,128)(2,1)S(1)}, u32[]{:S(2)}, u32[]{:S(2)}) collective-permute-start(bf16[96,768]{1,0:T(8,128)(2,1)S(1)} %get-tuple-element.141), channel_id=1, source_target_pairs={{0,24},{4,28},{8,0},{12,4},{16,8},{20,12},{24,16},{28,20},{1,25},{... | collective-permute-start | bytes 442376 | tf_op jit(solution)/shard_map/ppermute | solution.py:729
  141.8 10.9 %collective-permute-start.33 = (bf16[96,768]{1,0:T(8,128)(2,1)S(1)}, bf16[96,768]{1,0:T(8,128)(2,1)S(1)}, u32[]{:S(2)}, u32[]{:S(2)}) collective-permute-start(bf16[96,768]{1,0:T(8,128)(2,1)S(1)} %get-tuple-element.133.refs_6_), channel_id=1, source_target_pairs={{0,8},{4,12},{8,16},{12,20},{16,24},{20,28},{24,0},{28,4},{1,9},{5... | collective-permute-start | bytes 442376 | tf_op jit(solution)/shard_map/ppermute | solution.py:729
  144.0 3.0 %copy-start.9 = (bf16[4,96,192]{2,1,0:T(8,128)(2,1)}, bf16[4,96,192]{2,1,0:T(8,128)(2,1)S(1)}, u32[]{:S(2)}) copy-start(bf16[4,96,192]{2,1,0:T(8,128)(2,1)S(1)} %get-tuple-element.134.refs_6_) | copy-start | bytes 442372
  155.3 13.0 %collective-permute-start.38 = (bf16[4,96,640]{2,1,0:T(8,128)(2,1)S(1)}, bf16[4,96,640]{2,1,0:T(8,128)(2,1)S(1)}, u32[]{:S(2)}, u32[]{:S(2)}) collective-permute-start(bf16[4,96,640]{2,1,0:T(8,128)(2,1)S(1)} %get-tuple-element.142.refs_2_.refs_4_), channel_id=1, source_target_pairs={{0,4},{4,0},{8,12},{12,8},{16,20},{20,16},{24,28},{28,24},{1,5},{5... | collective-permute-start | bytes 1474568 | tf_op jit(solution)/shard_map/ppermute | solution.py:797
  168.3 6.0 %copy-start.10 = (bf16[4,96,192]{2,1,0:T(8,128)(2,1)S(1)}, bf16[4,96,192]{2,1,0:T(8,128)(2,1)}, u32[]{:S(2)}) copy-start(bf16[4,96,192]{2,1,0:T(8,128)(2,1)} %copy-done.9) | copy-start | bytes 442372
  169.2 18.9 %all-to-all-start = ((bf16[16,24,640]{2,1,0:T(8,128)(2,1)}), bf16[16,24,640]{2,1,0:T(8,128)(2,1)S(1)}, u32[]{:S(2)}, u32[]{:S(2)}) async-start(bf16[16,24,640]{2,1,0:T(8,128)(2,1)} %bitcast.9), calls=%async_computation | async-start | bytes 983040 | tf_op jit(solution)/shard_map/all_to_all | solution.py:498
  174.3 7.3 %collective-permute-start.39 = (bf16[4,96,192]{2,1,0:T(8,128)(2,1)S(1)}, bf16[4,96,192]{2,1,0:T(8,128)(2,1)S(1)}, u32[]{:S(2)}, u32[]{:S(2)}) collective-permute-start(bf16[4,96,192]{2,1,0:T(8,128)(2,1)S(1)} %copy-done.10), channel_id=1, source_target_pairs={{0,4},{4,0},{8,12},{12,8},{16,20},{20,16},{24,28},{28,24},{1,5},{5... | collective-permute-start | bytes 442376 | tf_op jit(solution)/shard_map/ppermute | solution.py:755
  188.1 22.8 %all-to-all-start.1 = ((bf16[16,24,960]{2,1,0:T(8,128)(2,1)}), bf16[16,24,960]{2,1,0:T(8,128)(2,1)S(1)}, u32[]{:S(2)}, u32[]{:S(2)}) async-start(bf16[16,24,960]{2,1,0:T(8,128)(2,1)} %bitcast.5), calls=%async_computation.1 | async-start | bytes 1572864 | tf_op jit(solution)/shard_map/all_to_all | solution.py:498
  193.0 1.8 collective-permute-start.36
  194.9 11.1 %collective-permute-start.37 = (bf16[128,768]{1,0:T(8,128)(2,1)S(1)}, bf16[128,768]{1,0:T(8,128)(2,1)S(1)}, u32[]{:S(2)}, u32[]{:S(2)}) collective-permute-start(bf16[128,768]{1,0:T(8,128)(2,1)S(1)} %get-tuple-element.147), channel_id=1, source_target_pairs={{0,2},{1,3},{2,0},{3,1},{4,6},{5,7},{6,4},{7,5},{8,10},{9,11},{10,... | collective-permute-start | bytes 589832 | tf_op jit(solution)/shard_map/ppermute | solution.py:815
  (9 other events, 12.5 us)

commit v3 on v2

--- a/solution.py
+++ b/solution.py
@@ -29,23 +29,26 @@
     return jax.ShapeDtypeStruct(dims, kind)
 
 
-def call(kernel, outs, *args, after=(), micros=2, limit=8):
+def call(kernel, outs, *args, after=(), micros=0.05, limit=8, scratch=()):
     spec = pl.BlockSpec(memory_space=pltpu.VMEM)
     count, extra = len(args), len(after)
 
     def run(*refs):
         kernel(*refs[:count], *refs[count + extra :])
 
-    return pl.pallas_call(
-        run,
-        out_shape=outs,
-        in_specs=[spec] * count + [pl.BlockSpec(memory_space=pl.ANY)] * extra,
-        out_specs=jax.tree.map(lambda _: spec, outs),
-        compiler_params=pltpu.CompilerParams(vmem_limit_bytes=limit << 20),
-        cost_estimate=pl.CostEstimate(
-            flops=int(micros * 2e7), bytes_accessed=int(micros * 1e5), transcendentals=0
-        ),
-    )(*args, *after)
+    named = getattr(kernel, "func", kernel).__name__.removesuffix("_kernel")
+    with jax.named_scope(named):
+        return pl.pallas_call(
+            run,
+            out_shape=outs,
+            in_specs=[spec] * count + [pl.BlockSpec(memory_space=pl.ANY)] * extra,
+            scratch_shapes=list(scratch),
+            out_specs=jax.tree.map(lambda _: spec, outs),
+            compiler_params=pltpu.CompilerParams(vmem_limit_bytes=limit << 20),
+            cost_estimate=pl.CostEstimate(
+                flops=int(micros * SCALE * 1e9), bytes_accessed=int(micros * SCALE * 3e6), transcendentals=0
+            ),
+        )(*args, *after)
 
 
 def later(value, *after):
@@ -92,6 +95,36 @@
 
 
 SPARE = 64
+RINGS = 1
+R3CTX = 1
+X3CHIP = 1
+R1Z = 0
+BFIRST = 1
+XW1 = 1
+DOWNFIRST = 0
+ROWSLATE = 1
+INFIRST = 0
+HOLDUP = 1
+OEARLY = 1
+Z1FIRST = 1
+HOLDDOWN = 1
+C_MERGE = 0.3
+C_JOIN = 0.6
+C_ATT = 5
+C_FFN = 1.9
+C_ADD = 0.2
+C_FIN = 1.2
+C_WG = 0.8
+C_FB = 1.0
+C_FIRST = 0.5
+C_ROWS = 0.3
+C_OUT = 1.7
+C_AB = 3.0
+C_LG = 0.9
+C_IN = 0.8
+C_LAST = 10
+C_SUM = 0.5
+SCALE = 0.3
 
 
 def pack_kernel(query, key, value, output, up, down, *refs):
@@ -181,14 +214,25 @@
     return jnp.split(every, cuts, axis=1)
 
 
-def merge_kernel(own, core, chip, far, third, first_out, second_out):
+def merge_first_kernel(own, core, chip, far, out):
     here = lax.axis_index("head")
-    cut = first_out.shape[2]
-    rest = own.shape[1] - cut
     for flip, piece in ((0, own), (1, core), (2, chip), (3, far)):
-        first_out[here ^ flip] = piece[:, :cut]
-        second_out[here ^ flip, :, :rest] = piece[:, cut:]
-    second_out[:, :, rest:] = third[...]
+        out[here ^ flip] = piece[:, : out.shape[2]]
+
+
+def merge_rest_kernel(own, core, chip, far, out):
+    here = lax.axis_index("head")
+    rest = out.shape[2]
+    for flip, piece in ((0, own), (1, core), (2, chip), (3, far)):
+        out[here ^ flip] = piece[:, piece.shape[1] - rest :]
+
+
+def merge_kernel(own, core, chip, far, third, out):
+    here = lax.axis_index("head")
+    rest = out.shape[2] - third.shape[2]
+    for flip, piece in ((0, own), (1, core), (2, chip), (3, far)):
+        out[here ^ flip, :, :rest] = piece[:, piece.shape[1] - rest :]
+    out[:, :, rest:] = third[...]
 
 
 def join_kernel(splits, *refs):
@@ -390,8 +434,8 @@
     d_qkv_out[...] = jnp.concatenate(parts[0] + parts[1] + parts[2], axis=1).astype(BF)
 
 
-def output_grad_kernel(ctx, ctx_chip, ctx_core, ctx_far, low0, low1, *outs):
-    out, kept, *sent = outs[-1:] + outs[:-1]
+def output_grad_kernel(ctx, ctx_chip, ctx_core, ctx_far, low0, low1, kept, *rest):
+    *sent, out = rest
     share = ctx.shape[1]
     width = low0.shape[1]
     tok = ctx.shape[0] // 4
@@ -445,25 +489,30 @@
     split_rows(kept, sent[0] if sent else None, jnp.concatenate([weights, columns], axis=1))
 
 
-def finish_up_kernel(rows, got, up_out, output_out):
-    depth, _, _, columns = got.shape
-    width = output_out.shape[1]
-    share = width // 4
-    piece = 4 * rows
-    sums = []
-    for h in range(4):
-        total = got[0, h].astype(F32)
-        for z in range(1, depth):
-            total = total + got[z, h].astype(F32)
-        sums.append(total)
-    output_out[...] = jnp.concatenate([t[:, width : width + share] for t in sums], axis=1)
-    up_out[...] = jnp.concatenate(
-        [sums[h][:, j * piece : (j + 1) * piece] for j in range(width // piece) for h in range(4)],
+def finish_up_kernel(relative, p0, p1, p2, p3, out):
+    width = p0.shape[1]
+    piece = out.shape[1] // width * p0.shape[0]
+    given = [p[...].astype(F32) for p in (p0, p1, p2, p3)]
+    if relative:
+        given = by_rank(given)
+    out[...] = jnp.concatenate(
+        [given[h][:, j * piece : (j + 1) * piece] for j in range(width // piece) for h in range(4)],
         axis=1,
     )
 
 
-def finish_last_kernel(got, query_out, key_out, value_out, *bias_outs):
+def by_rank(given):
+    here = lax.axis_index("head")
+    chosen = []
+    for i in range(4):
+        value = given[i]
+        for h in range(1, 4):
+            value = jnp.where(here == h, given[h ^ i], value)
+        chosen.append(value)
+    return chosen
+
+
+def finish_last_kernel(got, query_out, key_out, value_out, output_out, *bias_outs):
     depth, _, rows, columns = got.shape
     share = query_out.shape[1] // 4
     sums = []
@@ -475,7 +524,8 @@
     for i, out in enumerate((query_out, key_out, value_out)):
         out[...] = jnp.concatenate([t[:, i * share : (i + 1) * share] for t in sums], axis=1)
     every = sums[0] + sums[1] + sums[2] + sums[3]
-    every = jnp.concatenate([every[:, 3 * share :], jnp.zeros((rows, 128 - SPARE), F32)], axis=1)
+    output_out[...] = jnp.concatenate([t[:, 3 * share + SPARE :] for t in sums], axis=1)
+    every = jnp.concatenate([every[:, 3 * share : 3 * share + SPARE], jnp.zeros((rows, 128 - SPARE), F32)], axis=1)
     every = jnp.concatenate([every, jnp.zeros((128 - rows, 128), F32)], axis=0).T
     for i in range(8):
         bias_outs[i][...] = every[i : i + 1, :rows].reshape(rows)
@@ -483,14 +533,10 @@
     bias_outs[8][...] = long.reshape(4 * rows)
 
 
-def sum_up_kernel(kept0, got0, kept1, got1, out):
+def sum_two_kernel(kept0, got0, kept1, got1, out):
     cut = kept0.shape[2]
     out[:, :, :cut] = (kept0[...] + got0[...].astype(F32)).astype(BF)
     out[:, :, cut:] = (kept1[...] + got1[...].astype(F32)).astype(BF)
-
-
-def sum_one_kernel(kept, got, out):
-    out[...] = (kept[...] + got[...].astype(F32)).astype(BF)
 
 
 def to_owners(summed, rows):
@@ -504,6 +550,32 @@
 def to_owners_any(whole, rows):
     part = lax.psum_scatter(whole, "dp", scatter_dimension=0, tiled=True).astype(BF)
     return lax.all_to_all(part, "head", 0, 0, tiled=True).reshape(1, 4, rows, -1)
+
+
+def z_grad_kernel(left0, left1, right0, right1, whole, sent):
+    grad = dot(left0[...], right0[...], TN) + dot(left1[...], right1[...], TN)
+    whole[...] = grad.reshape(whole.shape)
+    sent[...] = whole[lax.rem(lax.axis_index("dp") // 2 + 3, 4)].astype(BF)
+
+
+def z_step_kernel(step, whole, got, sent):
+    at = lax.rem(lax.axis_index("dp") // 2 + 4 - step, 4)
+    sent[...] = (whole[at] + got[...].astype(F32)).astype(BF)
+
+
+def z_sum_kernel(whole, got, kept, sent):
+    place = lax.axis_index("dp")
+    x = place & 1
+    total = whole.at[place // 2]
+    kept[...] = total[x] + got[x].astype(F32)
+    sent[...] = (total[1 - x] + got[1 - x].astype(F32)).astype(BF)
+
+
+def heads_kernel(kept, got, *outs):
+    rows = outs[0].shape[0]
+    total = kept[...] + got[...].astype(F32)
+    for out, value in zip(outs, by_rank([total[h * rows : (h + 1) * rows] for h in range(4)])):
+        out[...] = value.astype(BF)
 
 
 def rows_kernel(kept, got, mine, *sent):
@@ -567,27 +639,48 @@
         *pieces, third = pack(matrices, biases)
         for flip in (3, 2, 1):
             pieces[flip] = lax.ppermute(pieces[flip], "head", [(i, i ^ flip) for i in range(4)])
-        narrow, wide = call(
-            merge_kernel,
-            (
-                shape((4, rows, 3 * share + SPARE), BF),
-                shape((4, rows, 2 * width + width // 2), BF),
-            ),
-            *pieces,
-            third,
-            micros=1,
-        )
-        wide = wide.reshape(4 * rows, -1)
+        narrow = call(
+            merge_first_kernel, shape((4, rows, 3 * share + SPARE), BF), *pieces, micros=C_MERGE
+        )
         parts = [narrow.reshape(4 * rows, -1)]
         parts += [lax.ppermute(parts[0], "dp", zshift(k)) for k in (1, 2, 3)]
         parts += [lax.ppermute(part, "dp", XSWAP) for part in parts]
-        found = [wide, later(lax.ppermute(wide, "dp", zshift(1)), *parts[1:4])]
+        if RINGS == 1:
+            rings = [
+                call(
+                    merge_kernel,
+                    shape((4, rows, 2 * width + width // 2), BF),
+                    *pieces,
+                    third,
+                    after=(narrow,),
+                    micros=C_MERGE,
+                )
+            ]
+        else:
+            rings = [
+                call(
+                    merge_rest_kernel,
+                    shape((4, rows, width + width // 2), BF),
+                    *pieces,
+                    after=(narrow,),
+                    micros=C_MERGE,
+                ),
+                third,
+            ]
+            if BFIRST:
+                rings = rings[::-1]
+        rings = [ring.reshape(4 * rows, -1) for ring in rings]
+        found = [
+            [ring, lax.ppermute(later(ring, *parts[1:4]) if R1Z else ring, "dp", zshift(1))]
+            for ring in rings
+        ]
+        crossed = [[lax.ppermute(ring, "dp", XSWAP)] for ring in rings]
         qkv_weight, columns = call(
             functools.partial(join_kernel, (3 * share, SPARE)),
             (shape((width, 3 * share), BF), shape((width, SPARE), BF)),
             *parts,
-            after=(found[1],),
-            micros=1,
+            after=tuple(c[0] for c in crossed),
+            micros=C_JOIN,
         )
     else:
         qkv_weight, columns, up_full, near, down_full = gather_any(matrices, biases)
@@ -603,24 +696,46 @@
         *x,
         qkv_weight,
         columns,
-        after=(up1,),
-        micros=5,
+        micros=C_ATT,
     )
     ctx_chip = lax.ppermute(ctx, "head", CHIP)
     ctx_core = lax.ppermute(ctx, "head", CORE)
     ctx_far = lax.ppermute(ctx_chip, "head", CORE)
     contexts = (ctx, ctx_chip, ctx_core, ctx_far)
     if cube:
-        found.append(later(lax.ppermute(found[1], "dp", zshift(1)), ctx))
-        found.append(later(lax.ppermute(found[2], "dp", zshift(1)), ctx_far))
-        parts = found + [lax.ppermute(part, "dp", XSWAP) for part in found]
-        splits = (width, width // 2, width)
-        up_full, near, down_full = call(
-            functools.partial(join_kernel, splits),
-            tuple(shape((width, s), BF) for s in splits),
-            *parts,
-            micros=1,
-        )
+        joined = []
+        for ring, (have, swapped) in enumerate(zip(found, crossed)):
+            swapped.append(lax.ppermute(have[1], "dp", XSWAP))
+            have.append(lax.ppermute(have[1], "dp", zshift(1)))
+            swapped.append(lax.ppermute(have[2], "dp", XSWAP))
+            hold = have[2]
+            if R3CTX:
+                hold = later(hold, ctx, *swapped[1 : 1 + XW1])
+            have.append(lax.ppermute(hold, "dp", zshift(1)))
+            hold = have[3]
+            if X3CHIP:
+                hold = later(hold, ctx_chip, *swapped[2 : 2 + XW1])
+            swapped.append(lax.ppermute(hold, "dp", XSWAP))
+            columns_of = have[0].shape[1]
+            splits = {
+                5 * width // 2: (width, width // 2, width),
+                3 * width // 2: (width, width // 2),
+                width: (width,),
+            }[columns_of]
+            joined.append(
+                call(
+                    functools.partial(join_kernel, splits),
+                    tuple(shape((width, s), BF) for s in splits),
+                    *have,
+                    *swapped,
+                    after=(ctx_far, up1),
+                    micros=C_JOIN,
+                )
+            )
+        if RINGS == 1:
+            up_full, near, down_full = joined[0]
+        else:
+            (down_full,), (up_full, near) = joined if BFIRST else joined[::-1]
     other = lax.ppermute(near, "head", CORE)
 
     def ffn(half):
@@ -642,13 +757,13 @@
             up_full,
             down_full,
             bias,
-            micros=3,
+            micros=C_FFN,
         )
 
     def pair_sum(part, sent):
         got = lax.ppermute(sent, "head", CORE)
         kept, low = call(
-            add_kernel, (shape((mine, width), F32), shape((mine, width), BF)), part, got, micros=1
+            add_kernel, (shape((mine, width), F32), shape((mine, width), BF)), part, got, micros=C_ADD
         )
         return kept, lax.ppermute(low, "head", CHIP)
 
@@ -669,7 +784,8 @@
         upstream,
         up1,
         bias,
-    )
+ micros=C_FIN,
+)
     ds1 = lax.ppermute(ds0, "head", CORE)
 
     def grad_outs(columns):
@@ -687,22 +803,48 @@
             up_full,
             down_full,
             after=after,
-            micros=1,
-        )
-
-    down_terms = call(
-        weight_grad_kernel, grad_outs(width), act0, act1, ds0, ds1, micros=1
-    )
-    dh1, sent, hidden1 = ffn_back(ds1, slope1, BF, (down_terms[-1],))
-    dh0, part, hidden0 = ffn_back(ds0, slope0, F32, (down_terms[-1],))
+            micros=C_FB,
+        )
+
+    down_first = DOWNFIRST or not cube
+    if down_first:
+        down_terms = call(
+            weight_grad_kernel, grad_outs(width), act0, act1, ds0, ds1, micros=C_WG
+        )
+    order = (down_terms[-1],) if down_first else ()
+    dh1, sent, hidden1 = ffn_back(ds1, slope1, BF, order)
+    dh0, part, hidden0 = ffn_back(ds0, slope0, F32, order)
     part, far = pair_sum(part, sent)
-    up_terms = call(
-        weight_grad_kernel, grad_outs(width), nl0, nl1, dh0, dh1, after=(part,), micros=1
-    )
-    order = (up_terms[-1],)
     if cube:
+        up_whole, up_run = call(
+            z_grad_kernel,
+            (shape((4, 2, 4 * rows, width), F32), shape((2, 4 * rows, width), BF)),
+            nl0,
+            nl1,
+            dh0,
+            dh1,
+            after=(part,),
+            micros=C_WG,
+        )
+        up_got = [lax.ppermute(up_run, "dp", zshift(1))]
+        if not down_first:
+            down_terms = call(
+                weight_grad_kernel,
+                grad_outs(width),
+                act0,
+                act1,
+                ds0,
+                ds1,
+                after=(up_run,),
+                micros=C_WG,
+            )
+        order = (down_terms[-1],) + ((up_got[0],) if Z1FIRST else ())
         got_down = lax.ppermute(down_terms[1], "dp", XSWAP)
-        order += (got_down,)
+    else:
+        up_terms = call(
+            weight_grad_kernel, grad_outs(width), nl0, nl1, dh0, dh1, after=(part,), micros=C_WG
+        )
+        order = (up_terms[-1],)
     d_first, df0, grads1 = call(
         first_back_kernel,
         (shape((tok, width), F32), shape((mine, width), BF), shape((8, width), F32)),
@@ -713,30 +855,32 @@
         rate1,
         bias,
         after=order,
-        micros=1,
+        micros=C_FIRST,
     )
     df1 = lax.ppermute(df0, "head", CORE)
-    order = ()
-    if cube:
-        down_kept, *down_sent = call(
-            rows_kernel,
-            (shape((4 * rows, width), F32),) + (shape((4 * rows, width), BF),) * 3,
-            down_terms[0],
-            got_down,
-            after=(df0,),
-            micros=1,
-        )
-        down_got = [lax.ppermute(o, "dp", zshift(k)) for k, o in zip((1, 2, 3), down_sent)]
-        order = (down_sent[0],)
+    def next_step(step, after):
+        run = call(
+            functools.partial(z_step_kernel, step),
+            shape((2, 4 * rows, width), BF),
+            up_whole,
+            up_got[-1],
+            after=after,
+            micros=0.3,
+        )
+        up_got.append(lax.ppermute(run, "dp", zshift(1)))
+        return run
+
+    order = (next_step(2, (df0,)),) if cube else ()
     output_terms = call(
         output_grad_kernel,
-        grad_outs(share) + (shape((width, share), F32),),
+        grad_outs(share),
         *contexts,
         df0,
         df1,
         after=order,
-        micros=1,
-    )[:-1]
+        scratch=(pltpu.VMEM((width, share), F32),),
+        micros=C_OUT,
+    )
     d_qkv = call(
         attend_back_kernel,
         shape((4 * tok, 3 * share), BF),
@@ -747,21 +891,21 @@
         qkv,
         probs,
         after=(output_terms[-1],),
-        micros=4,
-    )
+        micros=C_AB,
+    )
+    last_columns = 4 * share + SPARE
     order = ()
     if cube:
-        got_up = lax.ppermute(up_terms[1], "dp", XSWAP)
-        got_output = lax.ppermute(output_terms[1], "dp", XSWAP)
-        down_grad = call(
-            sum_kernel,
-            shape((4 * rows, width), F32),
-            down_kept,
-            *down_got,
-            after=(d_qkv,),
-            micros=1,
-        )
-        order = (got_up, down_grad)
+        down_kept, *down_sent = call(
+            rows_kernel,
+            (shape((4 * rows, width), F32),) + (shape((4 * rows, width), BF),) * 3,
+            down_terms[0],
+            got_down,
+            after=(d_qkv,) if ROWSLATE else (df0,),
+            micros=C_ROWS,
+        )
+        down_got = [lax.ppermute(o, "dp", zshift(k)) for k, o in zip((1, 2, 3), down_sent)]
+        order = (down_sent[0],)
     last_terms = call(
         functools.partial(last_grad_kernel, rows),
         grad_outs(3 * share + SPARE),
@@ -772,57 +916,87 @@
         hidden0,
         hidden1,
         after=order,
-        micros=2,
-    )
+        micros=C_LG,
+    )
+    order = (last_terms[-1],)
+    if cube:
+        got_last = lax.ppermute(last_terms[1], "dp", XSWAP)
+        got_output = lax.ppermute(output_terms[1], "dp", XSWAP)
+        order = (next_step(3, order),)
     part, sent = call(
         input_grad_kernel,
         (shape((mine, width), F32), shape((mine, width), BF)),
         d_qkv,
         qkv_weight,
-        after=(last_terms[-1],),
-        micros=1,
-    )
+        after=order,
+        micros=C_IN,
+    )
+    got = lax.ppermute(sent, "head", CORE)
     if cube:
-        summed = call(
-            sum_up_kernel,
-            shape((4, 4 * rows, width + share), BF),
-            up_terms[0],
-            got_up,
-            output_terms[0],
-            got_output,
-            after=(last_terms[-1],),
-            micros=1,
-        )
-        up_got = to_owners(summed, rows)
-        got = lax.ppermute(last_terms[1], "dp", XSWAP)
-        summed = call(
-            sum_one_kernel, shape((4, 4 * rows, 3 * share + SPARE), BF), last_terms[0], got, micros=1
-        )
-        last_got = to_owners(summed, rows)
-    else:
-        up_got = to_owners_any(jnp.concatenate([up_terms[0], output_terms[0]], axis=1), rows)
-        last_got = to_owners_any(last_terms[0], rows)
-        down_grad = lax.psum_scatter(down_terms[0], "dp", scatter_dimension=0, tiled=True)
-    got = lax.ppermute(sent, "head", CORE)
+        up_kept, up_cross = call(
+            z_sum_kernel,
+            (shape((4 * rows, width), F32), shape((4 * rows, width), BF)),
+            up_whole,
+            up_got[-1],
+            after=order + ((sent,) if INFIRST else ()),
+            micros=C_SUM,
+        )
     part, sent = call(
         input_add_kernel,
         (shape((tok, width), F32), shape((tok, width), BF)),
         part,
         got,
         d_first,
-        micros=1,
+        micros=0.4,
     )
     far = lax.ppermute(sent, "head", CHIP)
-    input_grad = call(input_end_kernel, shape((tok, width), BF), part, far, micros=1)
-
-    up_grad, output_grad = call(
-        functools.partial(finish_up_kernel, rows),
-        (shape((rows, 4 * width), F32), shape((rows, width), F32)),
-        up_got,
-    )
-    query_grad, key_grad, value_grad, *bias_out = call(
+    input_grad = call(input_end_kernel, shape((tok, width), BF), part, far, micros=0.3)
+    if cube:
+        up_pieces = list(
+            call(
+                heads_kernel,
+                (shape((rows, width), BF),) * 4,
+                up_kept,
+                lax.ppermute(up_cross, "dp", XSWAP),
+                micros=C_SUM,
+            )
+        )
+        for flip in (1, 2, 3):
+            up_pieces[flip] = lax.ppermute(up_pieces[flip], "head", [(i, i ^ flip) for i in range(4)])
+        down_grad = call(
+            sum_kernel,
+            shape((4 * rows, width), F32),
+            down_kept,
+            *down_got,
+            after=(got_output,) if OEARLY else (),
+            micros=C_SUM,
+        )
+    else:
+        up_pieces = to_owners_any(up_terms[0], rows)
+        up_pieces = [up_pieces[0, h] for h in range(4)]
+        down_grad = lax.psum_scatter(down_terms[0], "dp", scatter_dimension=0, tiled=True)
+    up_grad = call(
+        functools.partial(finish_up_kernel, cube),
+        shape((rows, 4 * width), F32),
+        *up_pieces,
+    )
+    if cube:
+        summed = call(
+            sum_two_kernel,
+            shape((4, 4 * rows, last_columns), BF),
+            last_terms[0],
+            got_last,
+            output_terms[0],
+            got_output,
+            micros=C_LAST,
+        )
+        hold = ((up_kept,) if HOLDUP else ()) + ((down_grad,) if HOLDDOWN else ())
+        last_got = to_owners(later(summed, *hold) if hold else summed, rows)
+    else:
+        last_got = to_owners_any(jnp.concatenate([last_terms[0], output_terms[0]], axis=1), rows)
+    query_grad, key_grad, value_grad, output_grad, *bias_out = call(
         finish_last_kernel,
-        (shape((rows, width), F32),) * 3 + (shape((rows,), F32),) * 8 + (shape((4 * rows,), F32),),
+        (shape((rows, width), F32),) * 4 + (shape((rows,), F32),) * 8 + (shape((4 * rows,), F32),),
         last_got,
     )
 

time: 212 us -> 169 us (0.80)
  waiting for transfers between devices: 126 us -> 90.9 us
  local copies, waits for them, and re-layouts: 6.88 us -> 1.98 us
  starting transfers between devices: 49.8 us -> 46.8 us
    ppermute x9 -> x15, waiting for transfers between devices: 41.2 us -> 30.9 us  [the longest x1 9.18 us: body(): have.append(lax.ppermute(hold, 'dp', zshift(1)))]
    ppermute x1, waiting for transfers between devices: 9.52 us -> 0.01 us  [body(): got_down = lax.ppermute(down_terms[1], 'dp', XSWAP)]
    ppermute x1, waiting for transfers between devices: 9.19 us -> 0.01 us  [body(): far = lax.ppermute(sent, 'head', CHIP)]
    all_to_all x2 -> x1, waiting for transfers between devices: 6.43 us -> 1.02 us  [to_owners(): lax.all_to_all(summed.reshape(16 * rows, columns), ALL, 0, 0, tiled=True,...]
    all_to_all x2 -> x1, starting transfers between devices: 9.2 us -> 4.14 us  [to_owners(): lax.all_to_all(summed.reshape(16 * rows, columns), ALL, 0, 0, tiled=True,...]
    unnamed x30 -> x18, local copies, waits for them, and re-layouts: 6.88 us -> 1.98 us
    ppermute x1, waiting for transfers between devices: 4.47 us -> 0.01 us  [body(): ctx_chip = lax.ppermute(ctx, 'head', CHIP)]
    ppermute x1, waiting for transfers between devices: 0.01 us -> 4.08 us  [body(): up1 = lax.ppermute(upstream, 'head', CHIP)]
  transfers between devices with their start and end apart: 42 -> 47, of which waited for: 26 -> 25; matrix products, arithmetic and copies ran while one was open for 0% -> 0% of each run, Pallas kernels for 9% -> 11%
where the time goes in v3:
time: 169 us; the launch traced here: 168 us
  waiting for transfers between devices  90.9 us (54%)
  starting transfers between devices  46.8 us (28%)
  Pallas kernels  27.4 us (16%)
  local copies, waits for them, and re-layouts  1.98 us (1%)
    pallas_call x30, Pallas kernels, call(): pl.pallas_call(run, out_shape=outs, in_specs=[spec] * count + [pl.BlockSp...  25 us
    ppermute x3, waiting for transfers between devices, body(): parts += [lax.ppermute(parts[0], 'dp', zshift(k)) for k in (1, 2, 3)]  13.7 us
    ppermute x2, waiting for transfers between devices, pair_sum(): return (kept, lax.ppermute(low, 'head', CHIP))  9.78 us
    ppermute x1, waiting for transfers between devices, body(): have.append(lax.ppermute(hold, 'dp', zshift(1)))  9.18 us
    ppermute x1, waiting for transfers between devices, body(): got_output = lax.ppermute(output_terms[1], 'dp', XSWAP)  8.64 us
    ppermute x1, waiting for transfers between devices, body(): up_got = [lax.ppermute(up_run, 'dp', zshift(1))]  8.24 us
    ppermute x3, waiting for transfers between devices, body(): lax.ppermute(o, 'dp', zshift(k))  7.63 us
    ppermute x4, waiting for transfers between devices, body(): parts += [lax.ppermute(part, 'dp', XSWAP) for part in parts]  5.21 us
  transfers between devices with their start and end apart: 47, of which 25 were waited for; matrix products, arithmetic and copies ran while one was open for 0% of the time, Pallas kernels for 11%

profile of v3, /device:TPU:0, one launch (start us, length us, event | category | flops | bytes accessed | tf_op | source)
XLA Modules:
  0.0 168.3 jit_solution(17710051191701240142)
XLA Ops:
  0.7 2.4 %shard_map.305 = (bf16[24,1792]{1,0:T(8,128)(2,1)}, bf16[24,1792]{1,0:T(8,128)(2,1)}, bf16[24,1792]{1,0:T(8,128)(2,1)}, bf16[24,1792]{1,0:T(8,128)(2,1)}, bf16[4,24,768]{2,1,0:T(8,128)(2,1)}) custom-call(f32[24,768]{1,0:T(8,128)} %query.1, f32[24,768]{1,0:T(8,128)} %key.1, f32[24,768]{1,0:T(8,128)} %value.1, f32[24,768]{1,0:T(8,128)} %output.1, ...), custom_call_target="tpu_custom_call" | custom-call | tf_op jit(solution)/shard_map/pallas_call | solution.py:178
  3.6 2.6 %collective-permute-start.4 = (bf16[24,1792]{1,0:T(8,128)(2,1)}, bf16[24,1792]{1,0:T(8,128)(2,1)S(1)}, u32[]{:S(2)}, u32[]{:S(2)}) collective-permute-start(bf16[24,1792]{1,0:T(8,128)(2,1)} %get-tuple-element.96), channel_id=1, source_target_pairs={{0,2},{1,3},{2,0},{3,1},{4,6},{5,7},{6,4},{7,5},{8,10},{9,11},{10,... | collective-permute-start | bytes 258056 | tf_op jit(solution)/shard_map/ppermute | solution.py:641
  6.3 1.7 %collective-permute-start = (bf16[128,768]{1,0:T(8,128)(2,1)}, bf16[128,768]{1,0:T(8,128)(2,1)S(1)}, u32[]{:S(2)}, u32[]{:S(2)}) collective-permute-start(bf16[128,768]{1,0:T(8,128)(2,1)} %refs_0_.5), channel_id=1, source_target_pairs={{0,2},{1,3},{2,0},{3,1},{4,6},{5,7},{6,4},{7,5},{8,10},{9,11},{10,... | collective-permute-start | bytes 589832 | tf_op jit(solution)/shard_map/ppermute | solution.py:620
  8.0 1.6 collective-permute-done.4.refs_2_
  9.6 1.6 collective-permute-done.5.refs_3_
  13.1 1.6 collective-permute-start.17
  14.7 1.5 collective-permute-start.9
  16.2 2.2 %collective-permute-start.8 = (bf16[96,640]{1,0:T(8,128)(2,1)S(1)}, bf16[96,640]{1,0:T(8,128)(2,1)S(1)}, u32[]{:S(2)}, u32[]{:S(2)}) collective-permute-start(bf16[96,640]{1,0:T(8,128)(2,1)S(1)} %bitcast.10), channel_id=1, source_target_pairs={{0,24},{4,28},{8,0},{12,4},{16,8},{20,12},{24,16},{28,20},{1,25},{... | collective-permute-start | bytes 368648 | tf_op jit(solution)/shard_map/ppermute | solution.py:646
  19.3 1.6 collective-permute-start.6
  21.8 7.0 %collective-permute-done.8.refs_3_ = bf16[96,640]{1,0:T(8,128)(2,1)S(1)} collective-permute-done((bf16[96,640]{1,0:T(8,128)(2,1)S(1)}, bf16[96,640]{1,0:T(8,128)(2,1)S(1)}, u32[]{:S(2)}, u32[]{:S(2)}) %collective-permute-start.8) | collective-permute-done | bytes 122912 | tf_op jit(solution)/shard_map/ppermute | solution.py:646
  28.7 1.2 collective-permute-start.12
  29.9 6.7 %collective-permute-done.7.refs_2_ = bf16[96,640]{1,0:T(8,128)(2,1)S(1)} collective-permute-done((bf16[96,640]{1,0:T(8,128)(2,1)S(1)}, bf16[96,640]{1,0:T(8,128)(2,1)S(1)}, u32[]{:S(2)}, u32[]{:S(2)}) %collective-permute-start.7) | collective-permute-done | bytes 122912 | tf_op jit(solution)/shard_map/ppermute | solution.py:646
  36.6 1.5 collective-permute-start.11
  38.7 1.6 collective-permute-start.19
  40.2 2.6 %collective-permute-done.11.refs_6_ = bf16[96,640]{1,0:T(8,128)(2,1)S(1)} collective-permute-done((bf16[96,640]{1,0:T(8,128)(2,1)S(1)}, bf16[96,640]{1,0:T(8,128)(2,1)S(1)}, u32[]{:S(2)}, u32[]{:S(2)}) %collective-permute-start.11) | collective-permute-done | bytes 122912 | tf_op jit(solution)/shard_map/ppermute | solution.py:647
  42.8 2.6 %collective-permute-done.10.refs_5_ = bf16[96,640]{1,0:T(8,128)(2,1)S(1)} collective-permute-done((bf16[96,640]{1,0:T(8,128)(2,1)S(1)}, bf16[96,640]{1,0:T(8,128)(2,1)S(1)}, u32[]{:S(2)}, u32[]{:S(2)}) %collective-permute-start.10) | collective-permute-done | bytes 122912 | tf_op jit(solution)/shard_map/ppermute | solution.py:647
  45.7 1.2 collective-permute-done.2.refs_4_.refs_1_.refs_3_
  46.9 5.0 %attend.1 = (bf16[512,576]{1,0:T(8,128)(2,1)S(1)}, f32[3,512,512]{2,1,0:T(8,128)S(1)}, bf16[512,192]{1,0:T(8,128)(2,1)S(1)}, f32[16,768]{1,0:T(8,128)S(1)}) custom-call(s32[4,128]{1,0:T(4,128)S(1)} %bitcast.14, bf16[128,768]{1,0:T(8,128)(2,1)S(1)} %copy-done.1, bf16[128,768]{1,0:T(8,128)(2,1)S(1)} %collective-permute-done.refs_2_.refs_1_, ...), custom_call_target="tpu_custom_call" | custom-call | flops 1500000000 | bytes 4500000 | tf_op jit(solution)/shard_map/attend/pallas_call | solution.py:41
  52.4 1.5 collective-permute-start.21
  53.9 1.6 collective-permute-start.14
  55.5 9.2 %collective-permute-done.20.refs_3_ = bf16[96,1920]{1,0:T(8,128)(2,1)S(1)} collective-permute-done((bf16[96,1920]{1,0:T(8,128)(2,1)S(1)}, bf16[96,1920]{1,0:T(8,128)(2,1)S(1)}, u32[]{:S(2)}, u32[]{:S(2)}) %collective-permute-start.20) | collective-permute-done | bytes 368672 | tf_op jit(solution)/shard_map/ppermute | solution.py:714
  64.7 1.5 collective-permute-start.22
  66.3 1.6 collective-permute-start.23
  67.9 4.1 %collective-permute-done.23.refs_9_.refs_4_ = bf16[128,768]{1,0:T(8,128)(2,1)S(1)} collective-permute-done((bf16[128,768]{1,0:T(8,128)(2,1)S(1)}, bf16[128,768]{1,0:T(8,128)(2,1)S(1)}, u32[]{:S(2)}, u32[]{:S(2)}) %collective-permute-start.23) | collective-permute-done | bytes 196640 | tf_op jit(solution)/shard_map/ppermute | solution.py:625
  72.0 2.5 %collective-permute-done.22.refs_7_ = bf16[96,1920]{1,0:T(8,128)(2,1)S(1)} collective-permute-done((bf16[96,1920]{1,0:T(8,128)(2,1)S(1)}, bf16[96,1920]{1,0:T(8,128)(2,1)S(1)}, u32[]{:S(2)}, u32[]{:S(2)}) %collective-permute-start.22) | collective-permute-done | bytes 368672 | tf_op jit(solution)/shard_map/ppermute | solution.py:718
  75.2 1.9 %collective-permute-done.15.refs_4_.refs_2_ = bf16[512,192]{1,0:T(8,128)(2,1)S(1)} collective-permute-done((bf16[512,192]{1,0:T(8,128)(2,1)S(1)}, bf16[512,192]{1,0:T(8,128)(2,1)S(1)}, u32[]{:S(2)}, u32[]{:S(2)}) %collective-permute-start.15) | collective-permute-done | bytes 196640 | tf_op jit(solution)/shard_map/ppermute | solution.py:702
  77.1 1.9 %ffn.3 = (bf16[256,768]{1,0:T(8,128)(2,1)S(1)}, bf16[256,768]{1,0:T(8,128)(2,1)S(1)}, f32[256,768]{1,0:T(8,128)S(1)}, bf16[256,768]{1,0:T(8,128)(2,1)S(1)}) custom-call(bf16[128,768]{1,0:T(8,128)(2,1)S(1)} %collective-permute-done.1.refs_3_.refs_0_.refs_2_, bf16[128,768]{1,0:T(8,128)(2,1)S(1)} %collective-permute-done.2.refs_4_.refs_1_.refs_3_, ...), custom_call_target="tpu_custom_call" | custom-call | flops 570000000 | bytes 1709999 | tf_op jit(solution)/shard_map/ffn/pallas_call | solution.py:41
  79.2 1.9 %ffn.2 = (bf16[256,768]{1,0:T(8,128)(2,1)S(1)}, bf16[256,768]{1,0:T(8,128)(2,1)S(1)}, f32[256,768]{1,0:T(8,128)S(1)}, f32[256,768]{1,0:T(8,128)S(1)}, f32[256,76...) custom-call(bf16[128,768]{1,0:T(8,128)(2,1)S(1)} %copy-done.1, ...), custom_call_target="tpu_custom_call" | custom-call | flops 570000000 | bytes 1709999 | tf_op jit(solution)/shard_map/ffn/pallas_call | solution.py:41
  81.3 1.7 collective-permute-start.26
  82.9 9.8 %collective-permute-done.26.refs_1_ = bf16[256,768]{1,0:T(8,128)(2,1)S(1)} collective-permute-done((bf16[256,768]{1,0:T(8,128)(2,1)S(1)}, bf16[256,768]{1,0:T(8,128)(2,1)S(1)}, u32[]{:S(2)}, u32[]{:S(2)}) %collective-permute-start.26) | collective-permute-done | bytes 393248 | tf_op jit(solution)/shard_map/ppermute | solution.py:768
  93.9 1.7 %collective-permute-done.27.refs_0_.refs_3_ = bf16[256,768]{1,0:T(8,128)(2,1)S(1)} collective-permute-done((bf16[256,768]{1,0:T(8,128)(2,1)S(1)}, bf16[256,768]{1,0:T(8,128)(2,1)S(1)}, u32[]{:S(2)}, u32[]{:S(2)}) %collective-permute-start.27) | collective-permute-done | bytes 393248 | tf_op jit(solution)/shard_map/ppermute | solution.py:789
  98.4 1.7 collective-permute-start.29
  101.9 1.5 collective-permute-start.33
  103.4 8.2 %collective-permute-done.30.refs_7_.refs_1_ = bf16[2,96,768]{2,1,0:T(8,128)(2,1)S(1)} collective-permute-done((bf16[2,96,768]{2,1,0:T(8,128)(2,1)S(1)}, bf16[2,96,768]{2,1,0:T(8,128)(2,1)S(1)}, u32[]{:S(2)}, u32[]{:S(2)}) %collective-permute-start.30) | collective-permute-done | bytes 294944 | tf_op jit(solution)/shard_map/ppermute | solution.py:829
  112.6 1.3 collective-permute-done.31.refs_5_.refs_1_
  114.8 3.0 %attend_back.1.refs_2_.refs_4_.refs_0_ = bf16[512,576]{1,0:T(8,128)(2,1)S(1)} custom-call(bf16[256,768]{1,0:T(8,128)(2,1)S(1)} %get-tuple-element.130.refs_2_.refs_4_.refs_0_, bf16[256,768]{1,0:T(8,128)(2,1)S(1)} %collective-permute-done.31.refs_5_.refs_1_, bf16[768,384]{1,0:T(8,128)(2,1)S(1)} %get-tuple-element.102.refs_6_.refs_2_, ...), custom_call_target="tpu_custom_call" | custom-call | flops 900000000 | bytes 2699999 | tf_op jit(solution)/shard_map/attend_back/pallas_call | solution.py:41
  118.8 1.5 collective-permute-start.36
  120.9 2.9 %collective-permute-done.32.refs_1_ = bf16[2,96,768]{2,1,0:T(8,128)(2,1)S(1)} collective-permute-done((bf16[2,96,768]{2,1,0:T(8,128)(2,1)S(1)}, bf16[2,96,768]{2,1,0:T(8,128)(2,1)S(1)}, u32[]{:S(2)}, u32[]{:S(2)}) %collective-permute-start.32) | collective-permute-done | bytes 294944 | tf_op jit(solution)/shard_map/ppermute | solution.py:870
  124.3 3.4 %collective-permute-start.41 = (bf16[96,768]{1,0:T(8,128)(2,1)S(1)}, bf16[96,768]{1,0:T(8,128)(2,1)S(1)}, u32[]{:S(2)}, u32[]{:S(2)}) collective-permute-start(bf16[96,768]{1,0:T(8,128)(2,1)S(1)} %get-tuple-element.152), channel_id=1, source_target_pairs={{0,24},{4,28},{8,0},{12,4},{16,8},{20,12},{24,16},{28,20},{1,25},{... | collective-permute-start | bytes 442376 | tf_op jit(solution)/shard_map/ppermute | solution.py:907
  127.7 8.6 %collective-permute-done.37.refs_3_.refs_4_ = bf16[4,96,192]{2,1,0:T(8,128)(2,1)S(1)} collective-permute-done((bf16[4,96,192]{2,1,0:T(8,128)(2,1)S(1)}, bf16[4,96,192]{2,1,0:T(8,128)(2,1)S(1)}, u32[]{:S(2)}, u32[]{:S(2)}) %collective-permute-start.37) | collective-permute-done | bytes 147488 | tf_op jit(solution)/shard_map/ppermute | solution.py:924
  136.4 5.1 %collective-permute-done.40.refs_2_ = bf16[96,768]{1,0:T(8,128)(2,1)S(1)} collective-permute-done((bf16[96,768]{1,0:T(8,128)(2,1)S(1)}, bf16[96,768]{1,0:T(8,128)(2,1)S(1)}, u32[]{:S(2)}, u32[]{:S(2)}) %collective-permute-start.40) | collective-permute-done | bytes 147488 | tf_op jit(solution)/shard_map/ppermute | solution.py:907
  141.4 2.6 %collective-permute-done.39.refs_1_ = bf16[96,768]{1,0:T(8,128)(2,1)S(1)} collective-permute-done((bf16[96,768]{1,0:T(8,128)(2,1)S(1)}, bf16[96,768]{1,0:T(8,128)(2,1)S(1)}, u32[]{:S(2)}, u32[]{:S(2)}) %collective-permute-start.39) | collective-permute-done | bytes 147488 | tf_op jit(solution)/shard_map/ppermute | solution.py:907
  146.0 4.1 %all-to-all-start = ((bf16[16,24,832]{2,1,0:T(8,128)(2,1)}), bf16[16,24,832]{2,1,0:T(8,128)(2,1)S(1)}, u32[]{:S(2)}, u32[]{:S(2)}) async-start(bf16[16,24,832]{2,1,0:T(8,128)(2,1)} %bitcast.3), calls=%async_computation | async-start | bytes 1376256 | tf_op jit(solution)/shard_map/all_to_all | solution.py:544
  151.4 1.4 collective-permute-start.42
  152.9 1.9 %collective-permute-start.35 = (bf16[128,768]{1,0:T(8,128)(2,1)S(1)}, bf16[128,768]{1,0:T(8,128)(2,1)S(1)}, u32[]{:S(2)}, u32[]{:S(2)}) collective-permute-start(bf16[128,768]{1,0:T(8,128)(2,1)S(1)} %get-tuple-element.146), channel_id=1, source_target_pairs={{0,2},{1,3},{2,0},{3,1},{4,6},{5,7},{6,4},{7,5},{8,10},{9,11},{10,... | collective-permute-start | bytes 589832 | tf_op jit(solution)/shard_map/ppermute | solution.py:952
  154.8 2.5 %collective-permute-done.42.refs_1_ = bf16[96,768]{1,0:T(8,128)(2,1)S(1)} collective-permute-done((bf16[96,768]{1,0:T(8,128)(2,1)S(1)}, bf16[96,768]{1,0:T(8,128)(2,1)S(1)}, u32[]{:S(2)}, u32[]{:S(2)}) %collective-permute-start.42) | collective-permute-done | bytes 147488 | tf_op jit(solution)/shard_map/ppermute | solution.py:960
  157.4 2.0 %collective-permute-start.44 = (bf16[24,768]{1,0:T(8,128)(2,1)S(1)}, bf16[24,768]{1,0:T(8,128)(2,1)S(1)}, u32[]{:S(2)}, u32[]{:S(2)}) collective-permute-start(bf16[24,768]{1,0:T(8,128)(2,1)S(1)} %get-tuple-element.165), channel_id=1, source_target_pairs={{0,2},{1,3},{2,0},{3,1},{4,6},{5,7},{6,4},{7,5},{8,10},{9,11},{10,... | collective-permute-start | bytes 110600 | tf_op jit(solution)/shard_map/ppermute | solution.py:965
  159.5 4.7 %collective-permute-done.44.refs_2_ = bf16[24,768]{1,0:T(8,128)(2,1)S(1)} collective-permute-done((bf16[24,768]{1,0:T(8,128)(2,1)S(1)}, bf16[24,768]{1,0:T(8,128)(2,1)S(1)}, u32[]{:S(2)}, u32[]{:S(2)}) %collective-permute-start.44) | collective-permute-done | bytes 36896 | tf_op jit(solution)/shard_map/ppermute | solution.py:965
  (98 shorter events, 23.6 us)
Async XLA Ops:
  0.7 42.1 %copy-start.1 = (bf16[128,768]{1,0:T(8,128)(2,1)S(1)}, bf16[128,768]{1,0:T(8,128)(2,1)}, u32[]{:S(2)}) copy-start(bf16[128,768]{1,0:T(8,128)(2,1)} %refs_0_.5) | copy-start | bytes 589828
  3.1 4.9 %collective-permute-start.3 = (bf16[24,1792]{1,0:T(8,128)(2,1)}, bf16[24,1792]{1,0:T(8,128)(2,1)S(1)}, u32[]{:S(2)}, u32[]{:S(2)}) collective-permute-start(bf16[24,1792]{1,0:T(8,128)(2,1)} %get-tuple-element.95), channel_id=1, source_target_pairs={{0,1},{1,0},{2,3},{3,2},{4,5},{5,4},{6,7},{7,6},{8,9},{9,8},{10,11... | collective-permute-start | bytes 258056 | tf_op jit(solution)/shard_map/ppermute | solution.py:641
  3.6 6.0 %collective-permute-start.4 = (bf16[24,1792]{1,0:T(8,128)(2,1)}, bf16[24,1792]{1,0:T(8,128)(2,1)S(1)}, u32[]{:S(2)}, u32[]{:S(2)}) collective-permute-start(bf16[24,1792]{1,0:T(8,128)(2,1)} %get-tuple-element.96), channel_id=1, source_target_pairs={{0,2},{1,3},{2,0},{3,1},{4,6},{5,7},{6,4},{7,5},{8,10},{9,11},{10,... | collective-permute-start | bytes 258056 | tf_op jit(solution)/shard_map/ppermute | solution.py:641
  6.2 5.0 %collective-permute-start.5 = (bf16[24,1792]{1,0:T(8,128)(2,1)}, bf16[24,1792]{1,0:T(8,128)(2,1)S(1)}, u32[]{:S(2)}, u32[]{:S(2)}) collective-permute-start(bf16[24,1792]{1,0:T(8,128)(2,1)} %get-tuple-element.97), channel_id=1, source_target_pairs={{0,3},{1,2},{2,1},{3,0},{4,7},{5,6},{6,5},{7,4},{8,11},{9,10},{10,... | collective-permute-start | bytes 258056 | tf_op jit(solution)/shard_map/ppermute | solution.py:641
  6.3 13.0 %collective-permute-start = (bf16[128,768]{1,0:T(8,128)(2,1)}, bf16[128,768]{1,0:T(8,128)(2,1)S(1)}, u32[]{:S(2)}, u32[]{:S(2)}) collective-permute-start(bf16[128,768]{1,0:T(8,128)(2,1)} %refs_0_.5), channel_id=1, source_target_pairs={{0,2},{1,3},{2,0},{3,1},{4,6},{5,7},{6,4},{7,5},{8,10},{9,11},{10,... | collective-permute-start | bytes 589832 | tf_op jit(solution)/shard_map/ppermute | solution.py:620
  13.1 25.6 %collective-permute-start.17 = (bf16[96,1920]{1,0:T(8,128)(2,1)S(1)}, bf16[96,1920]{1,0:T(8,128)(2,1)S(1)}, u32[]{:S(2)}, u32[]{:S(2)}) collective-permute-start(bf16[96,1920]{1,0:T(8,128)(2,1)S(1)} %bitcast.6), channel_id=1, source_target_pairs={{0,8},{4,12},{8,16},{12,20},{16,24},{20,28},{24,0},{28,4},{1,9},{5... | collective-permute-start | bytes 1105928 | tf_op jit(solution)/shard_map/ppermute | solution.py:674
  14.7 6.1 %collective-permute-start.9 = (bf16[96,640]{1,0:T(8,128)(2,1)S(1)}, bf16[96,640]{1,0:T(8,128)(2,1)S(1)}, u32[]{:S(2)}, u32[]{:S(2)}) collective-permute-start(bf16[96,640]{1,0:T(8,128)(2,1)S(1)} %bitcast.9), channel_id=1, source_target_pairs={{0,4},{4,0},{8,12},{12,8},{16,20},{20,16},{24,28},{28,24},{1,5},{5... | collective-permute-start | bytes 368648 | tf_op jit(solution)/shard_map/ppermute | solution.py:647
  16.2 12.5 %collective-permute-start.8 = (bf16[96,640]{1,0:T(8,128)(2,1)S(1)}, bf16[96,640]{1,0:T(8,128)(2,1)S(1)}, u32[]{:S(2)}, u32[]{:S(2)}) collective-permute-start(bf16[96,640]{1,0:T(8,128)(2,1)S(1)} %bitcast.10), channel_id=1, source_target_pairs={{0,24},{4,28},{8,0},{12,4},{16,8},{20,12},{24,16},{28,20},{1,25},{... | collective-permute-start | bytes 368648 | tf_op jit(solution)/shard_map/ppermute | solution.py:646
  18.5 18.2 %collective-permute-start.7 = (bf16[96,640]{1,0:T(8,128)(2,1)S(1)}, bf16[96,640]{1,0:T(8,128)(2,1)S(1)}, u32[]{:S(2)}, u32[]{:S(2)}) collective-permute-start(bf16[96,640]{1,0:T(8,128)(2,1)S(1)} %bitcast.11), channel_id=1, source_target_pairs={{0,16},{4,20},{8,24},{12,28},{16,0},{20,4},{24,8},{28,12},{1,17},{... | collective-permute-start | bytes 368648 | tf_op jit(solution)/shard_map/ppermute | solution.py:646
  19.3 18.9 %collective-permute-start.6 = (bf16[96,640]{1,0:T(8,128)(2,1)S(1)}, bf16[96,640]{1,0:T(8,128)(2,1)S(1)}, u32[]{:S(2)}, u32[]{:S(2)}) collective-permute-start(bf16[96,640]{1,0:T(8,128)(2,1)S(1)} %bitcast.12), channel_id=1, source_target_pairs={{0,8},{4,12},{8,16},{12,20},{16,24},{20,28},{24,0},{28,4},{1,9},{5... | collective-permute-start | bytes 368648 | tf_op jit(solution)/shard_map/ppermute | solution.py:646
  20.8 24.6 %collective-permute-start.13 = (bf16[96,1920]{1,0:T(8,128)(2,1)S(1)}, bf16[96,1920]{1,0:T(8,128)(2,1)S(1)}, u32[]{:S(2)}, u32[]{:S(2)}) collective-permute-start(bf16[96,1920]{1,0:T(8,128)(2,1)S(1)} %bitcast.7), channel_id=1, source_target_pairs={{0,4},{4,0},{8,12},{12,8},{16,20},{20,16},{24,28},{28,24},{1,5},{5... | collective-permute-start | bytes 1105928 | tf_op jit(solution)/shard_map/ppermute | solution.py:677
  28.7 9.9 %collective-permute-start.12 = (bf16[96,640]{1,0:T(8,128)(2,1)S(1)}, bf16[96,640]{1,0:T(8,128)(2,1)S(1)}, u32[]{:S(2)}, u32[]{:S(2)}) collective-permute-start(bf16[96,640]{1,0:T(8,128)(2,1)S(1)} %collective-permute-done.8.refs_3_), channel_id=1, source_target_pairs={{0,4},{4,0},{8,12},{12,8},{16,20},{20,16},{24,28},{28,24},{1,5},{5... | collective-permute-start | bytes 368648 | tf_op jit(solution)/shard_map/ppermute | solution.py:647
  36.6 6.2 %collective-permute-start.11 = (bf16[96,640]{1,0:T(8,128)(2,1)S(1)}, bf16[96,640]{1,0:T(8,128)(2,1)S(1)}, u32[]{:S(2)}, u32[]{:S(2)}) collective-permute-start(bf16[96,640]{1,0:T(8,128)(2,1)S(1)} %collective-permute-done.7.refs_2_), channel_id=1, source_target_pairs={{0,4},{4,0},{8,12},{12,8},{16,20},{20,16},{24,28},{28,24},{1,5},{5... | collective-permute-start | bytes 368648 | tf_op jit(solution)/shard_map/ppermute | solution.py:647
  38.1 7.3 %collective-permute-start.10 = (bf16[96,640]{1,0:T(8,128)(2,1)S(1)}, bf16[96,640]{1,0:T(8,128)(2,1)S(1)}, u32[]{:S(2)}, u32[]{:S(2)}) collective-permute-start(bf16[96,640]{1,0:T(8,128)(2,1)S(1)} %collective-permute-done.6.refs_1_), channel_id=1, source_target_pairs={{0,4},{4,0},{8,12},{12,8},{16,20},{20,16},{24,28},{28,24},{1,5},{5... | collective-permute-start | bytes 368648 | tf_op jit(solution)/shard_map/ppermute | solution.py:647
  38.7 13.3 %collective-permute-start.18 = (bf16[96,1920]{1,0:T(8,128)(2,1)S(1)}, bf16[96,1920]{1,0:T(8,128)(2,1)S(1)}, u32[]{:S(2)}, u32[]{:S(2)}) collective-permute-start(bf16[96,1920]{1,0:T(8,128)(2,1)S(1)} %collective-permute-done.17.refs_1_), channel_id=1, source_target_pairs={{0,8},{4,12},{8,16},{12,20},{16,24},{20,28},{24,0},{28,4},{1,9},{5... | collective-permute-start | bytes 1105928 | tf_op jit(solution)/shard_map/ppermute | solution.py:709
  38.7 13.7 %collective-permute-start.19 = (bf16[96,1920]{1,0:T(8,128)(2,1)S(1)}, bf16[96,1920]{1,0:T(8,128)(2,1)S(1)}, u32[]{:S(2)}, u32[]{:S(2)}) collective-permute-start(bf16[96,1920]{1,0:T(8,128)(2,1)S(1)} %collective-permute-done.17.refs_1_), channel_id=1, source_target_pairs={{0,4},{4,0},{8,12},{12,8},{16,20},{20,16},{24,28},{28,24},{1,5},{5... | collective-permute-start | bytes 1105928 | tf_op jit(solution)/shard_map/ppermute | solution.py:708
  42.8 2.8 %collective-permute-start.1 = (bf16[128,768]{1,0:T(8,128)(2,1)S(1)}, bf16[128,768]{1,0:T(8,128)(2,1)S(1)}, u32[]{:S(2)}, u32[]{:S(2)}) collective-permute-start(bf16[128,768]{1,0:T(8,128)(2,1)S(1)} %copy-done.1), channel_id=1, source_target_pairs={{0,1},{1,0},{2,3},{3,2},{4,5},{5,4},{6,7},{7,6},{8,9},{9,8},{10,11... | collective-permute-start | bytes 589832 | tf_op jit(solution)/shard_map/ppermute | solution.py:621
  45.4 1.4 collective-permute-start.2
  52.4 12.3 %collective-permute-start.20 = (bf16[96,1920]{1,0:T(8,128)(2,1)S(1)}, bf16[96,1920]{1,0:T(8,128)(2,1)S(1)}, u32[]{:S(2)}, u32[]{:S(2)}) collective-permute-start(bf16[96,1920]{1,0:T(8,128)(2,1)S(1)} %shard_map.306), channel_id=1, source_target_pairs={{0,8},{4,12},{8,16},{12,20},{16,24},{20,28},{24,0},{28,4},{1,9},{5... | collective-permute-start | bytes 1105928 | tf_op jit(solution)/shard_map/ppermute | solution.py:714
  52.4 12.3 %collective-permute-start.21 = (bf16[96,1920]{1,0:T(8,128)(2,1)S(1)}, bf16[96,1920]{1,0:T(8,128)(2,1)S(1)}, u32[]{:S(2)}, u32[]{:S(2)}) collective-permute-start(bf16[96,1920]{1,0:T(8,128)(2,1)S(1)} %collective-permute-done.18.refs_2_), channel_id=1, source_target_pairs={{0,4},{4,0},{8,12},{12,8},{16,20},{20,16},{24,28},{28,24},{1,5},{5... | collective-permute-start | bytes 1105928 | tf_op jit(solution)/shard_map/ppermute | solution.py:710
  53.9 10.8 %collective-permute-start.14 = (bf16[512,192]{1,0:T(8,128)(2,1)S(1)}, bf16[512,192]{1,0:T(8,128)(2,1)S(1)}, u32[]{:S(2)}, u32[]{:S(2)}) collective-permute-start(bf16[512,192]{1,0:T(8,128)(2,1)S(1)} %get-tuple-element.101.refs_1_.refs_2_.refs_0_), channel_id=1, source_target_pairs={{0,2},{1,3},{2,0},{3,1},{4,6},{5,7},{6,4},{7,5},{8,10},{9,11},{10,... | collective-permute-start | bytes 589832 | tf_op jit(solution)/shard_map/ppermute | solution.py:701
  64.7 9.7 %collective-permute-start.22 = (bf16[96,1920]{1,0:T(8,128)(2,1)S(1)}, bf16[96,1920]{1,0:T(8,128)(2,1)S(1)}, u32[]{:S(2)}, u32[]{:S(2)}) collective-permute-start(bf16[96,1920]{1,0:T(8,128)(2,1)S(1)} %shard_map.307), channel_id=1, source_target_pairs={{0,4},{4,0},{8,12},{12,8},{16,20},{20,16},{24,28},{28,24},{1,5},{5... | collective-permute-start | bytes 1105928 | tf_op jit(solution)/shard_map/ppermute | solution.py:718
  66.3 5.7 %collective-permute-start.23 = (bf16[128,768]{1,0:T(8,128)(2,1)S(1)}, bf16[128,768]{1,0:T(8,128)(2,1)S(1)}, u32[]{:S(2)}, u32[]{:S(2)}) collective-permute-start(bf16[128,768]{1,0:T(8,128)(2,1)S(1)} %copy-done.5), channel_id=1, source_target_pairs={{0,2},{1,3},{2,0},{3,1},{4,6},{5,7},{6,4},{7,5},{8,10},{9,11},{10,... | collective-permute-start | bytes 589832 | tf_op jit(solution)/shard_map/ppermute | solution.py:625
  67.9 4.1 %collective-permute-start.16 = (bf16[512,192]{1,0:T(8,128)(2,1)S(1)}, bf16[512,192]{1,0:T(8,128)(2,1)S(1)}, u32[]{:S(2)}, u32[]{:S(2)}) collective-permute-start(bf16[512,192]{1,0:T(8,128)(2,1)S(1)} %collective-permute-done.14.refs_1_.refs_3_), channel_id=1, source_target_pairs={{0,1},{1,0},{2,3},{3,2},{4,5},{5,4},{6,7},{7,6},{8,9},{9,8},{10,11... | collective-permute-start | bytes 589832 | tf_op jit(solution)/shard_map/ppermute | solution.py:703
  74.7 2.4 %collective-permute-start.24 = (bf16[768,384]{1,0:T(8,128)(2,1)S(1)}, bf16[768,384]{1,0:T(8,128)(2,1)S(1)}, u32[]{:S(2)}, u32[]{:S(2)}) collective-permute-start(bf16[768,384]{1,0:T(8,128)(2,1)S(1)} %get-tuple-element.102.refs_6_.refs_2_), channel_id=1, source_target_pairs={{0,1},{1,0},{2,3},{3,2},{4,5},{5,4},{6,7},{7,6},{8,9},{9,8},{10,11... | collective-permute-start | bytes 1769480 | tf_op jit(solution)/shard_map/ppermute | solution.py:739
  74.7 2.4 %collective-permute-start.15 = (bf16[512,192]{1,0:T(8,128)(2,1)S(1)}, bf16[512,192]{1,0:T(8,128)(2,1)S(1)}, u32[]{:S(2)}, u32[]{:S(2)}) collective-permute-start(bf16[512,192]{1,0:T(8,128)(2,1)S(1)} %get-tuple-element.101.refs_1_.refs_2_.refs_0_), channel_id=1, source_target_pairs={{0,1},{1,0},{2,3},{3,2},{4,5},{5,4},{6,7},{7,6},{8,9},{9,8},{10,11... | collective-permute-start | bytes 589832 | tf_op jit(solution)/shard_map/ppermute | solution.py:702
  79.0 2.1 %collective-permute-start.25 = (bf16[256,768]{1,0:T(8,128)(2,1)S(1)}, bf16[256,768]{1,0:T(8,128)(2,1)S(1)}, u32[]{:S(2)}, u32[]{:S(2)}) collective-permute-start(bf16[256,768]{1,0:T(8,128)(2,1)S(1)} %get-tuple-element.107), channel_id=1, source_target_pairs={{0,1},{1,0},{2,3},{3,2},{4,5},{5,4},{6,7},{7,6},{8,9},{9,8},{10,11... | collective-permute-start | bytes 1179656 | tf_op jit(solution)/shard_map/ppermute | solution.py:764
  81.3 11.5 %collective-permute-start.26 = (bf16[256,768]{1,0:T(8,128)(2,1)S(1)}, bf16[256,768]{1,0:T(8,128)(2,1)S(1)}, u32[]{:S(2)}, u32[]{:S(2)}) collective-permute-start(bf16[256,768]{1,0:T(8,128)(2,1)S(1)} %get-tuple-element.109), channel_id=1, source_target_pairs={{0,2},{1,3},{2,0},{3,1},{4,6},{5,7},{6,4},{7,5},{8,10},{9,11},{10,... | collective-permute-start | bytes 1179656 | tf_op jit(solution)/shard_map/ppermute | solution.py:768
  93.9 1.7 %collective-permute-start.27 = (bf16[256,768]{1,0:T(8,128)(2,1)S(1)}, bf16[256,768]{1,0:T(8,128)(2,1)S(1)}, u32[]{:S(2)}, u32[]{:S(2)}) collective-permute-start(bf16[256,768]{1,0:T(8,128)(2,1)S(1)} %get-tuple-element.112.refs_0_.refs_2_), channel_id=1, source_target_pairs={{0,1},{1,0},{2,3},{3,2},{4,5},{5,4},{6,7},{7,6},{8,9},{9,8},{10,11... | collective-permute-start | bytes 1179656 | tf_op jit(solution)/shard_map/ppermute | solution.py:789
  96.5 1.8 %collective-permute-start.28 = (bf16[256,768]{1,0:T(8,128)(2,1)S(1)}, bf16[256,768]{1,0:T(8,128)(2,1)S(1)}, u32[]{:S(2)}, u32[]{:S(2)}) collective-permute-start(bf16[256,768]{1,0:T(8,128)(2,1)S(1)} %get-tuple-element.116), channel_id=1, source_target_pairs={{0,1},{1,0},{2,3},{3,2},{4,5},{5,4},{6,7},{7,6},{8,9},{9,8},{10,11... | collective-permute-start | bytes 1179656 | tf_op jit(solution)/shard_map/ppermute | solution.py:764
  98.4 13.2 %collective-permute-start.29 = (bf16[256,768]{1,0:T(8,128)(2,1)S(1)}, bf16[256,768]{1,0:T(8,128)(2,1)S(1)}, u32[]{:S(2)}, u32[]{:S(2)}) collective-permute-start(bf16[256,768]{1,0:T(8,128)(2,1)S(1)} %get-tuple-element.118), channel_id=1, source_target_pairs={{0,2},{1,3},{2,0},{3,1},{4,6},{5,7},{6,4},{7,5},{8,10},{9,11},{10,... | collective-permute-start | bytes 1179656 | tf_op jit(solution)/shard_map/ppermute | solution.py:768
  101.0 10.6 %collective-permute-start.30 = (bf16[2,96,768]{2,1,0:T(8,128)(2,1)S(1)}, bf16[2,96,768]{2,1,0:T(8,128)(2,1)S(1)}, u32[]{:S(2)}, u32[]{:S(2)}) collective-permute-start(bf16[2,96,768]{2,1,0:T(8,128)(2,1)S(1)} %get-tuple-element.128.refs_4_), channel_id=1, source_target_pairs={{0,8},{4,12},{8,16},{12,20},{16,24},{20,28},{24,0},{28,4},{1,9},{5... | collective-permute-start | bytes 884744 | tf_op jit(solution)/shard_map/ppermute | solution.py:829
  101.9 15.9 %collective-permute-start.33 = (bf16[4,96,768]{2,1,0:T(8,128)(2,1)S(1)}, bf16[4,96,768]{2,1,0:T(8,128)(2,1)S(1)}, u32[]{:S(2)}, u32[]{:S(2)}) collective-permute-start(bf16[4,96,768]{2,1,0:T(8,128)(2,1)S(1)} %get-tuple-element.129.refs_6_), channel_id=1, source_target_pairs={{0,4},{4,0},{8,12},{12,8},{16,20},{20,16},{24,28},{28,24},{1,5},{5... | collective-permute-start | bytes 1769480 | tf_op jit(solution)/shard_map/ppermute | solution.py:842
  112.1 1.8 %collective-permute-start.31 = (bf16[256,768]{1,0:T(8,128)(2,1)S(1)}, bf16[256,768]{1,0:T(8,128)(2,1)S(1)}, u32[]{:S(2)}, u32[]{:S(2)}) collective-permute-start(bf16[256,768]{1,0:T(8,128)(2,1)S(1)} %get-tuple-element.130.refs_2_.refs_4_.refs_0_), channel_id=1, source_target_pairs={{0,1},{1,0},{2,3},{3,2},{4,5},{5,4},{6,7},{7,6},{8,9},{9,8},{10,11... | collective-permute-start | bytes 1179656 | tf_op jit(solution)/shard_map/ppermute | solution.py:860
  112.3 11.5 %collective-permute-start.32 = (bf16[2,96,768]{2,1,0:T(8,128)(2,1)S(1)}, bf16[2,96,768]{2,1,0:T(8,128)(2,1)S(1)}, u32[]{:S(2)}, u32[]{:S(2)}) collective-permute-start(bf16[2,96,768]{2,1,0:T(8,128)(2,1)S(1)} %z_step.2.refs_6_), channel_id=1, source_target_pairs={{0,8},{4,12},{8,16},{12,20},{16,24},{20,28},{24,0},{28,4},{1,9},{5... | collective-permute-start | bytes 884744 | tf_op jit(solution)/shard_map/ppermute | solution.py:870
  118.8 26.0 %collective-permute-start.36 = (bf16[4,96,640]{2,1,0:T(8,128)(2,1)S(1)}, bf16[4,96,640]{2,1,0:T(8,128)(2,1)S(1)}, u32[]{:S(2)}, u32[]{:S(2)}) collective-permute-start(bf16[4,96,640]{2,1,0:T(8,128)(2,1)S(1)} %get-tuple-element.141.refs_2_), channel_id=1, source_target_pairs={{0,4},{4,0},{8,12},{12,8},{16,20},{20,16},{24,28},{28,24},{1,5},{5... | collective-permute-start | bytes 1474568 | tf_op jit(solution)/shard_map/ppermute | solution.py:923
  120.3 16.0 %collective-permute-start.37 = (bf16[4,96,192]{2,1,0:T(8,128)(2,1)S(1)}, bf16[4,96,192]{2,1,0:T(8,128)(2,1)S(1)}, u32[]{:S(2)}, u32[]{:S(2)}) collective-permute-start(bf16[4,96,192]{2,1,0:T(8,128)(2,1)S(1)} %get-tuple-element.134.refs_6_), channel_id=1, source_target_pairs={{0,4},{4,0},{8,12},{12,8},{16,20},{20,16},{24,28},{28,24},{1,5},{5... | collective-permute-start | bytes 442376 | tf_op jit(solution)/shard_map/ppermute | solution.py:924
  123.8 20.9 %collective-permute-start.38 = (bf16[2,96,768]{2,1,0:T(8,128)(2,1)S(1)}, bf16[2,96,768]{2,1,0:T(8,128)(2,1)S(1)}, u32[]{:S(2)}, u32[]{:S(2)}) collective-permute-start(bf16[2,96,768]{2,1,0:T(8,128)(2,1)S(1)} %z_step.3.refs_2_), channel_id=1, source_target_pairs={{0,8},{4,12},{8,16},{12,20},{16,24},{20,28},{24,0},{28,4},{1,9},{5... | collective-permute-start | bytes 884744 | tf_op jit(solution)/shard_map/ppermute | solution.py:870
  123.9 17.5 %collective-permute-start.40 = (bf16[96,768]{1,0:T(8,128)(2,1)S(1)}, bf16[96,768]{1,0:T(8,128)(2,1)S(1)}, u32[]{:S(2)}, u32[]{:S(2)}) collective-permute-start(bf16[96,768]{1,0:T(8,128)(2,1)S(1)} %get-tuple-element.151), channel_id=1, source_target_pairs={{0,16},{4,20},{8,24},{12,28},{16,0},{20,4},{24,8},{28,12},{1,17},{... | collective-permute-start | bytes 442376 | tf_op jit(solution)/shard_map/ppermute | solution.py:907
  124.3 17.1 %collective-permute-start.41 = (bf16[96,768]{1,0:T(8,128)(2,1)S(1)}, bf16[96,768]{1,0:T(8,128)(2,1)S(1)}, u32[]{:S(2)}, u32[]{:S(2)}) collective-permute-start(bf16[96,768]{1,0:T(8,128)(2,1)S(1)} %get-tuple-element.152), channel_id=1, source_target_pairs={{0,24},{4,28},{8,0},{12,4},{16,8},{20,12},{24,16},{28,20},{1,25},{... | collective-permute-start | bytes 442376 | tf_op jit(solution)/shard_map/ppermute | solution.py:907
  136.4 7.6 %collective-permute-start.39 = (bf16[96,768]{1,0:T(8,128)(2,1)S(1)}, bf16[96,768]{1,0:T(8,128)(2,1)S(1)}, u32[]{:S(2)}, u32[]{:S(2)}) collective-permute-start(bf16[96,768]{1,0:T(8,128)(2,1)S(1)} %get-tuple-element.140.refs_9_), channel_id=1, source_target_pairs={{0,8},{4,12},{8,16},{12,20},{16,24},{20,28},{24,0},{28,4},{1,9},{5... | collective-permute-start | bytes 442376 | tf_op jit(solution)/shard_map/ppermute | solution.py:907
  146.0 21.3 %all-to-all-start = ((bf16[16,24,832]{2,1,0:T(8,128)(2,1)}), bf16[16,24,832]{2,1,0:T(8,128)(2,1)S(1)}, u32[]{:S(2)}, u32[]{:S(2)}) async-start(bf16[16,24,832]{2,1,0:T(8,128)(2,1)} %bitcast.3), calls=%async_computation | async-start | bytes 1376256 | tf_op jit(solution)/shard_map/all_to_all | solution.py:544
  151.0 1.9 %collective-permute-start.34 = (bf16[256,768]{1,0:T(8,128)(2,1)S(1)}, bf16[256,768]{1,0:T(8,128)(2,1)S(1)}, u32[]{:S(2)}, u32[]{:S(2)}) collective-permute-start(bf16[256,768]{1,0:T(8,128)(2,1)S(1)} %get-tuple-element.143), channel_id=1, source_target_pairs={{0,1},{1,0},{2,3},{3,2},{4,5},{5,4},{6,7},{7,6},{8,9},{9,8},{10,11... | collective-permute-start | bytes 1179656 | tf_op jit(solution)/shard_map/ppermute | solution.py:934
  151.4 5.9 %collective-permute-start.42 = (bf16[96,768]{1,0:T(8,128)(2,1)S(1)}, bf16[96,768]{1,0:T(8,128)(2,1)S(1)}, u32[]{:S(2)}, u32[]{:S(2)}) collective-permute-start(bf16[96,768]{1,0:T(8,128)(2,1)S(1)} %get-tuple-element.162), channel_id=1, source_target_pairs={{0,4},{4,0},{8,12},{12,8},{16,20},{20,16},{24,28},{28,24},{1,5},{5... | collective-permute-start | bytes 442376 | tf_op jit(solution)/shard_map/ppermute | solution.py:960
  152.9 12.6 %collective-permute-start.35 = (bf16[128,768]{1,0:T(8,128)(2,1)S(1)}, bf16[128,768]{1,0:T(8,128)(2,1)S(1)}, u32[]{:S(2)}, u32[]{:S(2)}) collective-permute-start(bf16[128,768]{1,0:T(8,128)(2,1)S(1)} %get-tuple-element.146), channel_id=1, source_target_pairs={{0,2},{1,3},{2,0},{3,1},{4,6},{5,7},{6,4},{7,5},{8,10},{9,11},{10,... | collective-permute-start | bytes 589832 | tf_op jit(solution)/shard_map/ppermute | solution.py:952
  157.3 2.1 %collective-permute-start.43 = (bf16[24,768]{1,0:T(8,128)(2,1)S(1)}, bf16[24,768]{1,0:T(8,128)(2,1)S(1)}, u32[]{:S(2)}, u32[]{:S(2)}) collective-permute-start(bf16[24,768]{1,0:T(8,128)(2,1)S(1)} %get-tuple-element.164), channel_id=1, source_target_pairs={{0,1},{1,0},{2,3},{3,2},{4,5},{5,4},{6,7},{7,6},{8,9},{9,8},{10,11... | collective-permute-start | bytes 110600 | tf_op jit(solution)/shard_map/ppermute | solution.py:965
  157.4 6.8 %collective-permute-start.44 = (bf16[24,768]{1,0:T(8,128)(2,1)S(1)}, bf16[24,768]{1,0:T(8,128)(2,1)S(1)}, u32[]{:S(2)}, u32[]{:S(2)}) collective-permute-start(bf16[24,768]{1,0:T(8,128)(2,1)S(1)} %get-tuple-element.165), channel_id=1, source_target_pairs={{0,2},{1,3},{2,0},{3,1},{4,6},{5,7},{6,4},{7,5},{8,10},{9,11},{10,... | collective-permute-start | bytes 110600 | tf_op jit(solution)/shard_map/ppermute | solution.py:965
  159.4 5.3 %collective-permute-start.45 = (bf16[24,768]{1,0:T(8,128)(2,1)S(1)}, bf16[24,768]{1,0:T(8,128)(2,1)S(1)}, u32[]{:S(2)}, u32[]{:S(2)}) collective-permute-start(bf16[24,768]{1,0:T(8,128)(2,1)S(1)} %get-tuple-element.166), channel_id=1, source_target_pairs={{0,3},{1,2},{2,1},{3,0},{4,7},{5,6},{6,5},{7,4},{8,11},{9,10},{10,... | collective-permute-start | bytes 110600 | tf_op jit(solution)/shard_map/ppermute | solution.py:965
  (7 other events, 58.1 us)

commit v4 on v3

--- a/solution.py
+++ b/solution.py
@@ -95,12 +95,20 @@
 
 
 SPARE = 64
-RINGS = 1
-R3CTX = 1
-X3CHIP = 1
-R1Z = 0
-BFIRST = 1
+R3CTX = 0
+HOLD1 = 0
+HOLDX0 = 1
+R2FIRST = 1
+X3CHIP = 0
 XW1 = 1
+X1R3 = 0
+MERGE2 = 0
+HOLDB1 = 0
+B2FIRST = 0
+B3CTX = 0
+HOLDB3 = 1
+UP1CTX = 1
+AFTERY = 0
 DOWNFIRST = 0
 ROWSLATE = 1
 INFIRST = 0
@@ -128,8 +136,8 @@
 
 
 def pack_kernel(query, key, value, output, up, down, *refs):
-    biases, outs, scratch = refs[:9], refs[9:14], refs[14:]
-    second, third = outs[:4], outs[4]
+    biases, outs, scratch = refs[:9], refs[9:15], refs[15:]
+    first, second, third = outs[0], outs[1:5], outs[5]
     matrices, vectors, square, sems = scratch[:6], scratch[6:15], scratch[15], scratch[16]
     pairs = list(zip((query, key, value, output, up, down) + biases, matrices + vectors))
     copies = [pltpu.make_async_copy(a, b, sems.at[i]) for i, (a, b) in enumerate(pairs)]
@@ -151,12 +159,15 @@
     columns = square[...].T[:rows, :SPARE]
     slabs = []
     for h in range(4):
+        slab = jnp.concatenate(
+            [w[:, h * share : (h + 1) * share] for w in (query, key, value)] + [columns], axis=1
+        ).astype(BF)
+        for z in range(4):
+            first[z, h] = slab
         half = (h % 2) * (width // 2)
         slabs.append(
             jnp.concatenate(
-                [w[:, h * share : (h + 1) * share] for w in (query, key, value)]
-                + [columns]
-                + [up[:, piece * (4 * j + h) : piece * (4 * j + h + 1)] for j in range(width // piece)]
+                [up[:, piece * (4 * j + h) : piece * (4 * j + h + 1)] for j in range(width // piece)]
                 + [output[:, half : half + width // 2]],
                 axis=1,
             )
@@ -177,10 +188,11 @@
     vmem = pl.BlockSpec(memory_space=pltpu.VMEM)
     return pl.pallas_call(
         pack_kernel,
-        out_shape=(shape((rows, 3 * share + SPARE + width + width // 2), BF),) * 4
+        out_shape=(shape((4, 4, rows, 3 * share + SPARE), BF),)
+        + (shape((rows, width + width // 2), BF),) * 4
         + (shape((4, rows, width), BF),),
         in_specs=[hbm] * 15,
-        out_specs=(vmem,) * 5,
+        out_specs=(vmem,) * 6,
         scratch_shapes=[pltpu.VMEM(v.shape, F32) for v in matrices + biases]
         + [pltpu.VMEM((128, 128), F32), pltpu.SemaphoreType.DMA((15,))],
         compiler_params=pltpu.CompilerParams(vmem_limit_bytes=56 << 20),
@@ -214,25 +226,35 @@
     return jnp.split(every, cuts, axis=1)
 
 
-def merge_first_kernel(own, core, chip, far, out):
+def join_first_kernel(mine, theirs, weight, columns):
+    rows = mine.shape[1]
+    cut = weight.shape[1]
+    x = lax.axis_index("dp") & 1
+    for z in range(4):
+        for flip, ref in ((0, mine), (1, theirs)):
+            at = pl.ds(pl.multiple_of((2 * z + (x ^ flip)) * rows, 16), rows)
+            weight[at, :] = ref[z, :, :cut]
+            columns[at, :] = ref[z, :, cut:]
+
+
+def merge_rest_kernel(own, core, chip, far, out):
     here = lax.axis_index("head")
     for flip, piece in ((0, own), (1, core), (2, chip), (3, far)):
-        out[here ^ flip] = piece[:, : out.shape[2]]
-
-
-def merge_rest_kernel(own, core, chip, far, out):
-    here = lax.axis_index("head")
-    rest = out.shape[2]
-    for flip, piece in ((0, own), (1, core), (2, chip), (3, far)):
-        out[here ^ flip] = piece[:, piece.shape[1] - rest :]
-
-
-def merge_kernel(own, core, chip, far, third, out):
-    here = lax.axis_index("head")
-    rest = out.shape[2] - third.shape[2]
-    for flip, piece in ((0, own), (1, core), (2, chip), (3, far)):
-        out[here ^ flip, :, :rest] = piece[:, piece.shape[1] - rest :]
-    out[:, :, rest:] = third[...]
+        out[here ^ flip] = piece[...]
+
+
+def pair_kernel(own, other, out):
+    out[0] = own[...]
+    out[1] = other[...]
+
+
+def join_pairs_kernel(p0, p1, p2, p3, out):
+    rows = p0.shape[1]
+    place = lax.axis_index("dp")
+    for i, piece in enumerate((p0, p1, p2, p3)):
+        for flip in range(2):
+            owner = lax.rem(place + 8 - 2 * i, 8) ^ flip
+            out[pl.ds(pl.multiple_of(owner * rows, 16), rows), :] = piece[flip]
 
 
 def join_kernel(splits, *refs):
@@ -636,50 +658,45 @@
         up_bias,
     )
     if cube:
-        *pieces, third = pack(matrices, biases)
+        first, *pieces, third = pack(matrices, biases)
         for flip in (3, 2, 1):
             pieces[flip] = lax.ppermute(pieces[flip], "head", [(i, i ^ flip) for i in range(4)])
-        narrow = call(
-            merge_first_kernel, shape((4, rows, 3 * share + SPARE), BF), *pieces, micros=C_MERGE
-        )
-        parts = [narrow.reshape(4 * rows, -1)]
-        parts += [lax.ppermute(parts[0], "dp", zshift(k)) for k in (1, 2, 3)]
-        parts += [lax.ppermute(part, "dp", XSWAP) for part in parts]
-        if RINGS == 1:
-            rings = [
-                call(
-                    merge_kernel,
-                    shape((4, rows, 2 * width + width // 2), BF),
-                    *pieces,
-                    third,
-                    after=(narrow,),
-                    micros=C_MERGE,
-                )
-            ]
-        else:
-            rings = [
-                call(
-                    merge_rest_kernel,
-                    shape((4, rows, width + width // 2), BF),
-                    *pieces,
-                    after=(narrow,),
-                    micros=C_MERGE,
-                ),
-                third,
-            ]
-            if BFIRST:
-                rings = rings[::-1]
-        rings = [ring.reshape(4 * rows, -1) for ring in rings]
-        found = [
-            [ring, lax.ppermute(later(ring, *parts[1:4]) if R1Z else ring, "dp", zshift(1))]
-            for ring in rings
-        ]
-        crossed = [[lax.ppermute(ring, "dp", XSWAP)] for ring in rings]
+        first = first.reshape(4, 4 * rows, 3 * share + SPARE)
+        if AFTERY == 4:
+            first = later(first, *pieces[1:])
+        elif AFTERY:
+            first = later(first, pieces[AFTERY])
+        first = to_owners(first, rows).reshape(4, 4 * rows, 3 * share + SPARE)
+        low = third.reshape(4 * rows, width)
+        both = call(
+            pair_kernel,
+            shape((2, 4 * rows, width), BF),
+            low,
+            lax.ppermute(low, "dp", XSWAP),
+            micros=C_MERGE,
+        )
+        wide = call(
+            merge_rest_kernel,
+            shape((4, rows, width + width // 2), BF),
+            *pieces,
+            after=(both,) if MERGE2 else (),
+            micros=C_MERGE,
+        ).reshape(4 * rows, -1)
+        have = [wide, lax.ppermute(wide, "dp", zshift(1))]
+        pairs = [both, lax.ppermute(both, "dp", zshift(1))]
+        swapped = [lax.ppermute(wide, "dp", XSWAP)]
+        hold = ((have[1],) if HOLD1 else ()) + ((swapped[0],) if HOLDX0 else ())
+        hold += (pairs[1],) if HOLDB1 else ()
+        theirs = lax.ppermute(later(first, *hold) if hold else first, "dp", XSWAP)
+        have.append(lax.ppermute(have[1], "dp", zshift(1)))
+        pairs.append(lax.ppermute(pairs[1], "dp", zshift(1)))
+        hold = ((have[2],) if R2FIRST else ()) + ((pairs[2],) if B2FIRST else ())
         qkv_weight, columns = call(
-            functools.partial(join_kernel, (3 * share, SPARE)),
+            join_first_kernel,
             (shape((width, 3 * share), BF), shape((width, SPARE), BF)),
-            *parts,
-            after=tuple(c[0] for c in crossed),
+            first,
+            theirs,
+            after=hold,
             micros=C_JOIN,
         )
     else:
@@ -698,44 +715,36 @@
         columns,
         micros=C_ATT,
     )
-    ctx_chip = lax.ppermute(ctx, "head", CHIP)
+    ctx_chip = lax.ppermute(later(ctx, up1) if UP1CTX else ctx, "head", CHIP)
     ctx_core = lax.ppermute(ctx, "head", CORE)
-    ctx_far = lax.ppermute(ctx_chip, "head", CORE)
+    if cube:
+        swapped.append(lax.ppermute(have[1], "dp", XSWAP))
+        swapped.append(lax.ppermute(have[2], "dp", XSWAP))
+        hold = ((ctx,) if R3CTX else ()) + ((swapped[1],) if X1R3 else ())
+        have.append(lax.ppermute(later(have[2], *hold) if hold else have[2], "dp", zshift(1)))
+        hold = ((ctx_chip,) if X3CHIP else ()) + ((swapped[2],) if XW1 else ())
+        swapped.append(lax.ppermute(later(have[3], *hold) if hold else have[3], "dp", XSWAP))
+        pairs.append(lax.ppermute(later(pairs[2], ctx) if B3CTX else pairs[2], "dp", zshift(1)))
+        ctx_far = lax.ppermute(later(ctx_chip, pairs[3]) if HOLDB3 else ctx_chip, "head", CORE)
+        down_full = call(
+            join_pairs_kernel,
+            shape((width, width), BF),
+            *pairs,
+            after=(ctx_far,),
+            micros=C_JOIN,
+        )
+        splits = (width, width // 2)
+        up_full, near = call(
+            functools.partial(join_kernel, splits),
+            tuple(shape((width, s), BF) for s in splits),
+            *have,
+            *swapped,
+            after=(ctx_far, up1),
+            micros=C_JOIN,
+        )
+    else:
+        ctx_far = lax.ppermute(ctx_chip, "head", CORE)
     contexts = (ctx, ctx_chip, ctx_core, ctx_far)
-    if cube:
-        joined = []
-        for ring, (have, swapped) in enumerate(zip(found, crossed)):
-            swapped.append(lax.ppermute(have[1], "dp", XSWAP))
-            have.append(lax.ppermute(have[1], "dp", zshift(1)))
-            swapped.append(lax.ppermute(have[2], "dp", XSWAP))
-            hold = have[2]
-            if R3CTX:
-                hold = later(hold, ctx, *swapped[1 : 1 + XW1])
-            have.append(lax.ppermute(hold, "dp", zshift(1)))
-            hold = have[3]
-            if X3CHIP:
-                hold = later(hold, ctx_chip, *swapped[2 : 2 + XW1])
-            swapped.append(lax.ppermute(hold, "dp", XSWAP))
-            columns_of = have[0].shape[1]
-            splits = {
-                5 * width // 2: (width, width // 2, width),
-                3 * width // 2: (width, width // 2),
-                width: (width,),
-            }[columns_of]
-            joined.append(
-                call(
-                    functools.partial(join_kernel, splits),
-                    tuple(shape((width, s), BF) for s in splits),
-                    *have,
-                    *swapped,
-                    after=(ctx_far, up1),
-                    micros=C_JOIN,
-                )
-            )
-        if RINGS == 1:
-            up_full, near, down_full = joined[0]
-        else:
-            (down_full,), (up_full, near) = joined if BFIRST else joined[::-1]
     other = lax.ppermute(near, "head", CORE)
 
     def ffn(half):

time: 169 us -> 164 us (0.970)
  waiting for transfers between devices: 90.9 us -> 85.2 us
    ppermute x13 -> x11, waiting for transfers between devices: 30.6 us -> 17.9 us  [the longest x1 5.28 us: body(): have = [wide, lax.ppermute(wide, 'dp', zshift(1))]]
    ppermute x1, waiting for transfers between devices: 0.01 us -> 10.3 us  [body(): have.append(lax.ppermute(have[1], 'dp', zshift(1)))]
    all_to_all x1 -> x2, starting transfers between devices: 4.14 us -> 11.7 us  [to_owners(): lax.all_to_all(summed.reshape(16 * rows, columns), ALL, 0, 0, tiled=True,...]
    ppermute x1, waiting for transfers between devices: 4.08 us -> 0.01 us  [body(): up1 = lax.ppermute(upstream, 'head', CHIP)]
    ppermute x13 -> x11, starting transfers between devices: 15 us -> 11.1 us  [the longest x1 1.56 us: body(): swapped = [lax.ppermute(wide, 'dp', XSWAP)]]
    pallas_call x30 -> x31, Pallas kernels: 25 us -> 25.3 us  [call(): pl.pallas_call(run, out_shape=outs, in_specs=[spec] * count + [pl.BlockSp...]
  transfers between devices with their start and end apart: 47 -> 46, of which waited for: 25 -> 26; matrix products, arithmetic and copies ran while one was open for 0% -> 0% of each run, Pallas kernels for 11% -> 12%
where the time goes in v4:
time: 164 us; the launch traced here: 163 us
  waiting for transfers between devices  85.2 us (52%)
  starting transfers between devices  47.8 us (29%)
  Pallas kernels  27.8 us (17%)
    pallas_call x31, Pallas kernels, call(): pl.pallas_call(run, out_shape=outs, in_specs=[spec] * count + [pl.BlockSp...  25.3 us
    all_to_all x2, starting transfers between devices, to_owners(): lax.all_to_all(summed.reshape(16 * rows, columns), ALL, 0, 0, tiled=True,...  11.7 us
    ppermute x1, waiting for transfers between devices, body(): have.append(lax.ppermute(have[1], 'dp', zshift(1)))  10.3 us
    ppermute x2, waiting for transfers between devices, pair_sum(): return (kept, lax.ppermute(low, 'head', CHIP))  9.78 us
    ppermute x1, waiting for transfers between devices, body(): got_output = lax.ppermute(output_terms[1], 'dp', XSWAP)  8.78 us
    ppermute x1, waiting for transfers between devices, body(): up_got = [lax.ppermute(up_run, 'dp', zshift(1))]  7.67 us
    ppermute x3, waiting for transfers between devices, body(): lax.ppermute(o, 'dp', zshift(k))  6.66 us
    ppermute x1, waiting for transfers between devices, body(): have = [wide, lax.ppermute(wide, 'dp', zshift(1))]  5.28 us
  transfers between devices with their start and end apart: 46, of which 26 were waited for; matrix products, arithmetic and copies ran while one was open for 0% of the time, Pallas kernels for 12%

profile of v4, /device:TPU:0, one launch (start us, length us, event | category | flops | bytes accessed | tf_op | source)
XLA Modules:
  0.0 163.1 jit_solution(3554991436739296177)
XLA Ops:
  0.7 2.5 %shard_map.305 = (bf16[4,4,24,640]{3,2,1,0:T(8,128)(2,1)}, bf16[24,1152]{1,0:T(8,128)(2,1)}, bf16[24,1152]{1,0:T(8,128)(2,1)}, bf16[24,1152]{1,0:T(8,128)(2,1)},...) custom-call(f32[24,768]{1,0:T(8,128)} %query.1, f32[24,768]{1,0:T(8,128)} %key.1, f32[24,768]{1,0:T(8,128)} %value.1, ...), custom_call_target="tpu_custom_call" | custom-call | tf_op jit(solution)/shard_map/pallas_call | solution.py:189
  3.2 7.5 %all-to-all-start = ((bf16[16,24,640]{2,1,0:T(8,128)(2,1)}), bf16[16,24,640]{2,1,0:T(8,128)(2,1)S(1)}, u32[]{:S(2)}, u32[]{:S(2)}) async-start(bf16[16,24,640]{2,1,0:T(8,128)(2,1)} %bitcast.16), calls=%async_computation | async-start | bytes 983040 | tf_op jit(solution)/shard_map/all_to_all | solution.py:566
  11.1 1.7 %collective-permute-start.4 = (bf16[24,1152]{1,0:T(8,128)(2,1)}, bf16[24,1152]{1,0:T(8,128)(2,1)S(1)}, u32[]{:S(2)}, u32[]{:S(2)}) collective-permute-start(bf16[24,1152]{1,0:T(8,128)(2,1)} %get-tuple-element.97), channel_id=1, source_target_pairs={{0,2},{1,3},{2,0},{3,1},{4,6},{5,7},{6,4},{7,5},{8,10},{9,11},{10,... | collective-permute-start | bytes 165896 | tf_op jit(solution)/shard_map/ppermute | solution.py:663
  12.8 1.5 collective-permute-start.13
  14.3 4.5 %collective-permute-done.4.refs_2_ = bf16[24,1152]{1,0:T(8,128)(2,1)S(1)} collective-permute-done((bf16[24,1152]{1,0:T(8,128)(2,1)}, bf16[24,1152]{1,0:T(8,128)(2,1)S(1)}, u32[]{:S(2)}, u32[]{:S(2)}) %collective-permute-start.4) | collective-permute-done | bytes 55328 | tf_op jit(solution)/shard_map/ppermute | solution.py:663
  19.9 1.6 collective-permute-start.6
  21.5 1.4 collective-permute-start.14
  22.9 1.6 all-to-all-done
  24.6 3.4 %collective-permute-done.6.refs_1_.refs_4_ = bf16[96,1152]{1,0:T(8,128)(2,1)S(1)} collective-permute-done((bf16[96,1152]{1,0:T(8,128)(2,1)S(1)}, bf16[96,1152]{1,0:T(8,128)(2,1)S(1)}, u32[]{:S(2)}, u32[]{:S(2)}) %collective-permute-start.6) | collective-permute-done | bytes 221216 | tf_op jit(solution)/shard_map/ppermute | solution.py:687
  28.0 1.5 collective-permute-start.7
  29.4 1.3 collective-permute-start.8
  30.8 2.5 %collective-permute-done.14.refs_1_ = bf16[2,96,768]{2,1,0:T(8,128)(2,1)S(1)} collective-permute-done((bf16[2,96,768]{2,1,0:T(8,128)(2,1)S(1)}, bf16[2,96,768]{2,1,0:T(8,128)(2,1)S(1)}, u32[]{:S(2)}, u32[]{:S(2)}) %collective-permute-start.14) | collective-permute-done | bytes 294944 | tf_op jit(solution)/shard_map/ppermute | solution.py:686
  33.2 5.3 %collective-permute-done.8.refs_1_ = bf16[96,1152]{1,0:T(8,128)(2,1)S(1)} collective-permute-done((bf16[96,1152]{1,0:T(8,128)(2,1)S(1)}, bf16[96,1152]{1,0:T(8,128)(2,1)S(1)}, u32[]{:S(2)}, u32[]{:S(2)}) %collective-permute-start.8) | collective-permute-done | bytes 221216 | tf_op jit(solution)/shard_map/ppermute | solution.py:685
  39.0 10.3 %collective-permute-done.9.refs_2_ = bf16[96,1152]{1,0:T(8,128)(2,1)S(1)} collective-permute-done((bf16[96,1152]{1,0:T(8,128)(2,1)S(1)}, bf16[96,1152]{1,0:T(8,128)(2,1)S(1)}, u32[]{:S(2)}, u32[]{:S(2)}) %collective-permute-start.9) | collective-permute-done | bytes 221216 | tf_op jit(solution)/shard_map/ppermute | solution.py:691
  51.1 1.2 collective-permute-start.16
  52.3 5.1 %attend.1 = (bf16[512,576]{1,0:T(8,128)(2,1)S(1)}, f32[3,512,512]{2,1,0:T(8,128)S(1)}, bf16[512,192]{1,0:T(8,128)(2,1)S(1)}, f32[16,768]{1,0:T(8,128)S(1)}) custom-call(s32[4,128]{1,0:T(4,128)S(1)} %bitcast.15, bf16[128,768]{1,0:T(8,128)(2,1)S(1)} %copy-done.1, bf16[128,768]{1,0:T(8,128)(2,1)S(1)} %collective-permute-done.refs_2_.refs_1_, ...), custom_call_target="tpu_custom_call" | custom-call | flops 1500000000 | bytes 4500000 | tf_op jit(solution)/shard_map/attend/pallas_call | solution.py:41
  57.4 1.1 collective-permute-start.11
  58.5 1.5 collective-permute-start.19
  60.0 1.2 collective-permute-done.18.refs_3_
  61.2 1.4 collective-permute-start.21
  62.7 2.5 %collective-permute-done.11.refs_3_.refs_1_ = bf16[512,192]{1,0:T(8,128)(2,1)S(1)} collective-permute-done((bf16[512,192]{1,0:T(8,128)(2,1)S(1)}, bf16[512,192]{1,0:T(8,128)(2,1)S(1)}, u32[]{:S(2)}, u32[]{:S(2)}) %collective-permute-start.11) | collective-permute-done | bytes 196640 | tf_op jit(solution)/shard_map/ppermute | solution.py:718
  66.8 2.4 %collective-permute-done.21.refs_7_ = bf16[96,1152]{1,0:T(8,128)(2,1)S(1)} collective-permute-done((bf16[96,1152]{1,0:T(8,128)(2,1)S(1)}, bf16[96,1152]{1,0:T(8,128)(2,1)S(1)}, u32[]{:S(2)}, u32[]{:S(2)}) %collective-permute-start.21) | collective-permute-done | bytes 221216 | tf_op jit(solution)/shard_map/ppermute | solution.py:726
  70.0 1.8 %collective-permute-done.12.refs_4_.refs_2_ = bf16[512,192]{1,0:T(8,128)(2,1)S(1)} collective-permute-done((bf16[512,192]{1,0:T(8,128)(2,1)S(1)}, bf16[512,192]{1,0:T(8,128)(2,1)S(1)}, u32[]{:S(2)}, u32[]{:S(2)}) %collective-permute-start.12) | collective-permute-done | bytes 196640 | tf_op jit(solution)/shard_map/ppermute | solution.py:719
  71.8 1.9 %ffn.3 = (bf16[256,768]{1,0:T(8,128)(2,1)S(1)}, bf16[256,768]{1,0:T(8,128)(2,1)S(1)}, f32[256,768]{1,0:T(8,128)S(1)}, bf16[256,768]{1,0:T(8,128)(2,1)S(1)}) custom-call(bf16[128,768]{1,0:T(8,128)(2,1)S(1)} %collective-permute-done.1.refs_3_.refs_0_.refs_2_, bf16[128,768]{1,0:T(8,128)(2,1)S(1)} %collective-permute-done.2.refs_4_.refs_1_.refs_3_, ...), custom_call_target="tpu_custom_call" | custom-call | flops 570000000 | bytes 1709999 | tf_op jit(solution)/shard_map/ffn/pallas_call | solution.py:41
  73.9 1.9 %ffn.2 = (bf16[256,768]{1,0:T(8,128)(2,1)S(1)}, bf16[256,768]{1,0:T(8,128)(2,1)S(1)}, f32[256,768]{1,0:T(8,128)S(1)}, f32[256,768]{1,0:T(8,128)S(1)}, f32[256,76...) custom-call(bf16[128,768]{1,0:T(8,128)(2,1)S(1)} %copy-done.1, ...), custom_call_target="tpu_custom_call" | custom-call | flops 570000000 | bytes 1709999 | tf_op jit(solution)/shard_map/ffn/pallas_call | solution.py:41
  76.0 1.7 %collective-permute-start.24 = (bf16[256,768]{1,0:T(8,128)(2,1)S(1)}, bf16[256,768]{1,0:T(8,128)(2,1)S(1)}, u32[]{:S(2)}, u32[]{:S(2)}) collective-permute-start(bf16[256,768]{1,0:T(8,128)(2,1)S(1)} %get-tuple-element.109), channel_id=1, source_target_pairs={{0,2},{1,3},{2,0},{3,1},{4,6},{5,7},{6,4},{7,5},{8,10},{9,11},{10,... | collective-permute-start | bytes 1179656 | tf_op jit(solution)/shard_map/ppermute | solution.py:777
  77.7 9.8 %collective-permute-done.24.refs_1_ = bf16[256,768]{1,0:T(8,128)(2,1)S(1)} collective-permute-done((bf16[256,768]{1,0:T(8,128)(2,1)S(1)}, bf16[256,768]{1,0:T(8,128)(2,1)S(1)}, u32[]{:S(2)}, u32[]{:S(2)}) %collective-permute-start.24) | collective-permute-done | bytes 393248 | tf_op jit(solution)/shard_map/ppermute | solution.py:777
  87.4 1.1 final.1
  88.6 1.7 %collective-permute-done.25.refs_0_.refs_3_ = bf16[256,768]{1,0:T(8,128)(2,1)S(1)} collective-permute-done((bf16[256,768]{1,0:T(8,128)(2,1)S(1)}, bf16[256,768]{1,0:T(8,128)(2,1)S(1)}, u32[]{:S(2)}, u32[]{:S(2)}) %collective-permute-start.25) | collective-permute-done | bytes 393248 | tf_op jit(solution)/shard_map/ppermute | solution.py:798
  93.2 1.7 %collective-permute-start.27 = (bf16[256,768]{1,0:T(8,128)(2,1)S(1)}, bf16[256,768]{1,0:T(8,128)(2,1)S(1)}, u32[]{:S(2)}, u32[]{:S(2)}) collective-permute-start(bf16[256,768]{1,0:T(8,128)(2,1)S(1)} %get-tuple-element.118), channel_id=1, source_target_pairs={{0,2},{1,3},{2,0},{3,1},{4,6},{5,7},{6,4},{7,5},{8,10},{9,11},{10,... | collective-permute-start | bytes 1179656 | tf_op jit(solution)/shard_map/ppermute | solution.py:777
  97.2 1.6 collective-permute-start.31
  98.7 7.7 %collective-permute-done.28.refs_7_.refs_1_ = bf16[2,96,768]{2,1,0:T(8,128)(2,1)S(1)} collective-permute-done((bf16[2,96,768]{2,1,0:T(8,128)(2,1)S(1)}, bf16[2,96,768]{2,1,0:T(8,128)(2,1)S(1)}, u32[]{:S(2)}, u32[]{:S(2)}) %collective-permute-start.28) | collective-permute-done | bytes 294944 | tf_op jit(solution)/shard_map/ppermute | solution.py:838
  107.4 1.3 collective-permute-done.29.refs_5_.refs_1_
  109.6 3.1 %attend_back.1.refs_2_.refs_4_.refs_0_ = bf16[512,576]{1,0:T(8,128)(2,1)S(1)} custom-call(bf16[256,768]{1,0:T(8,128)(2,1)S(1)} %get-tuple-element.130.refs_2_.refs_4_.refs_0_, bf16[256,768]{1,0:T(8,128)(2,1)S(1)} %collective-permute-done.29.refs_5_.refs_1_, bf16[768,384]{1,0:T(8,128)(2,1)S(1)} %get-tuple-element.103.refs_6_.refs_2_, ...), custom_call_target="tpu_custom_call" | custom-call | flops 900000000 | bytes 2699999 | tf_op jit(solution)/shard_map/attend_back/pallas_call | solution.py:41
  113.7 1.5 collective-permute-start.34
  115.8 2.7 %collective-permute-done.30.refs_1_ = bf16[2,96,768]{2,1,0:T(8,128)(2,1)S(1)} collective-permute-done((bf16[2,96,768]{2,1,0:T(8,128)(2,1)S(1)}, bf16[2,96,768]{2,1,0:T(8,128)(2,1)S(1)}, u32[]{:S(2)}, u32[]{:S(2)}) %collective-permute-start.30) | collective-permute-done | bytes 294944 | tf_op jit(solution)/shard_map/ppermute | solution.py:879
  119.1 3.4 %collective-permute-start.39 = (bf16[96,768]{1,0:T(8,128)(2,1)S(1)}, bf16[96,768]{1,0:T(8,128)(2,1)S(1)}, u32[]{:S(2)}, u32[]{:S(2)}) collective-permute-start(bf16[96,768]{1,0:T(8,128)(2,1)S(1)} %get-tuple-element.152), channel_id=1, source_target_pairs={{0,24},{4,28},{8,0},{12,4},{16,8},{20,12},{24,16},{28,20},{1,25},{... | collective-permute-start | bytes 442376 | tf_op jit(solution)/shard_map/ppermute | solution.py:916
  122.5 8.8 %collective-permute-done.35.refs_3_.refs_4_ = bf16[4,96,192]{2,1,0:T(8,128)(2,1)S(1)} collective-permute-done((bf16[4,96,192]{2,1,0:T(8,128)(2,1)S(1)}, bf16[4,96,192]{2,1,0:T(8,128)(2,1)S(1)}, u32[]{:S(2)}, u32[]{:S(2)}) %collective-permute-start.35) | collective-permute-done | bytes 147488 | tf_op jit(solution)/shard_map/ppermute | solution.py:933
  132.1 4.0 %collective-permute-done.38.refs_2_ = bf16[96,768]{1,0:T(8,128)(2,1)S(1)} collective-permute-done((bf16[96,768]{1,0:T(8,128)(2,1)S(1)}, bf16[96,768]{1,0:T(8,128)(2,1)S(1)}, u32[]{:S(2)}, u32[]{:S(2)}) %collective-permute-start.38) | collective-permute-done | bytes 147488 | tf_op jit(solution)/shard_map/ppermute | solution.py:916
  136.1 2.7 %collective-permute-done.37.refs_1_ = bf16[96,768]{1,0:T(8,128)(2,1)S(1)} collective-permute-done((bf16[96,768]{1,0:T(8,128)(2,1)S(1)}, bf16[96,768]{1,0:T(8,128)(2,1)S(1)}, u32[]{:S(2)}, u32[]{:S(2)}) %collective-permute-start.37) | collective-permute-done | bytes 147488 | tf_op jit(solution)/shard_map/ppermute | solution.py:916
  139.6 1.0 sum_two.1.refs_0_
  140.8 4.1 %all-to-all-start.1 = ((bf16[16,24,832]{2,1,0:T(8,128)(2,1)}), bf16[16,24,832]{2,1,0:T(8,128)(2,1)S(1)}, u32[]{:S(2)}, u32[]{:S(2)}) async-start(bf16[16,24,832]{2,1,0:T(8,128)(2,1)} %bitcast.5), calls=%async_computation.1 | async-start | bytes 1376256 | tf_op jit(solution)/shard_map/all_to_all | solution.py:566
  146.2 1.5 collective-permute-start.40
  147.8 1.8 %collective-permute-start.33 = (bf16[128,768]{1,0:T(8,128)(2,1)S(1)}, bf16[128,768]{1,0:T(8,128)(2,1)S(1)}, u32[]{:S(2)}, u32[]{:S(2)}) collective-permute-start(bf16[128,768]{1,0:T(8,128)(2,1)S(1)} %get-tuple-element.146), channel_id=1, source_target_pairs={{0,2},{1,3},{2,0},{3,1},{4,6},{5,7},{6,4},{7,5},{8,10},{9,11},{10,... | collective-permute-start | bytes 589832 | tf_op jit(solution)/shard_map/ppermute | solution.py:961
  149.6 2.5 %collective-permute-done.40.refs_1_ = bf16[96,768]{1,0:T(8,128)(2,1)S(1)} collective-permute-done((bf16[96,768]{1,0:T(8,128)(2,1)S(1)}, bf16[96,768]{1,0:T(8,128)(2,1)S(1)}, u32[]{:S(2)}, u32[]{:S(2)}) %collective-permute-start.40) | collective-permute-done | bytes 147488 | tf_op jit(solution)/shard_map/ppermute | solution.py:969
  152.2 2.0 %collective-permute-start.42 = (bf16[24,768]{1,0:T(8,128)(2,1)S(1)}, bf16[24,768]{1,0:T(8,128)(2,1)S(1)}, u32[]{:S(2)}, u32[]{:S(2)}) collective-permute-start(bf16[24,768]{1,0:T(8,128)(2,1)S(1)} %get-tuple-element.165), channel_id=1, source_target_pairs={{0,2},{1,3},{2,0},{3,1},{4,6},{5,7},{6,4},{7,5},{8,10},{9,11},{10,... | collective-permute-start | bytes 110600 | tf_op jit(solution)/shard_map/ppermute | solution.py:974
  154.3 4.7 %collective-permute-done.42.refs_2_ = bf16[24,768]{1,0:T(8,128)(2,1)S(1)} collective-permute-done((bf16[24,768]{1,0:T(8,128)(2,1)S(1)}, bf16[24,768]{1,0:T(8,128)(2,1)S(1)}, u32[]{:S(2)}, u32[]{:S(2)}) %collective-permute-start.42) | collective-permute-done | bytes 36896 | tf_op jit(solution)/shard_map/ppermute | solution.py:974
  161.0 1.0 all-to-all-done.1
  (101 shorter events, 21.9 us)
Async XLA Ops:
  3.2 21.3 %all-to-all-start = ((bf16[16,24,640]{2,1,0:T(8,128)(2,1)}), bf16[16,24,640]{2,1,0:T(8,128)(2,1)S(1)}, u32[]{:S(2)}, u32[]{:S(2)}) async-start(bf16[16,24,640]{2,1,0:T(8,128)(2,1)} %bitcast.16), calls=%async_computation | async-start | bytes 983040 | tf_op jit(solution)/shard_map/all_to_all | solution.py:566
  10.7 3.6 %collective-permute-start.3 = (bf16[24,1152]{1,0:T(8,128)(2,1)}, bf16[24,1152]{1,0:T(8,128)(2,1)S(1)}, u32[]{:S(2)}, u32[]{:S(2)}) collective-permute-start(bf16[24,1152]{1,0:T(8,128)(2,1)} %get-tuple-element.96), channel_id=1, source_target_pairs={{0,1},{1,0},{2,3},{3,2},{4,5},{5,4},{6,7},{7,6},{8,9},{9,8},{10,11... | collective-permute-start | bytes 165896 | tf_op jit(solution)/shard_map/ppermute | solution.py:663
  11.1 7.7 %collective-permute-start.4 = (bf16[24,1152]{1,0:T(8,128)(2,1)}, bf16[24,1152]{1,0:T(8,128)(2,1)S(1)}, u32[]{:S(2)}, u32[]{:S(2)}) collective-permute-start(bf16[24,1152]{1,0:T(8,128)(2,1)} %get-tuple-element.97), channel_id=1, source_target_pairs={{0,2},{1,3},{2,0},{3,1},{4,6},{5,7},{6,4},{7,5},{8,10},{9,11},{10,... | collective-permute-start | bytes 165896 | tf_op jit(solution)/shard_map/ppermute | solution.py:663
  12.8 6.2 %collective-permute-start.5 = (bf16[24,1152]{1,0:T(8,128)(2,1)}, bf16[24,1152]{1,0:T(8,128)(2,1)S(1)}, u32[]{:S(2)}, u32[]{:S(2)}) collective-permute-start(bf16[24,1152]{1,0:T(8,128)(2,1)} %get-tuple-element.98), channel_id=1, source_target_pairs={{0,3},{1,2},{2,1},{3,0},{4,7},{5,6},{6,5},{7,4},{8,11},{9,10},{10,... | collective-permute-start | bytes 165896 | tf_op jit(solution)/shard_map/ppermute | solution.py:663
  12.8 8.6 %collective-permute-start.13 = (bf16[96,768]{1,0:T(8,128)(2,1)}, bf16[96,768]{1,0:T(8,128)(2,1)S(1)}, u32[]{:S(2)}, u32[]{:S(2)}) collective-permute-start(bf16[96,768]{1,0:T(8,128)(2,1)} %bitcast.13), channel_id=1, source_target_pairs={{0,4},{4,0},{8,12},{12,8},{16,20},{20,16},{24,28},{28,24},{1,5},{5... | collective-permute-start | bytes 442376 | tf_op jit(solution)/shard_map/ppermute | solution.py:675
  19.9 8.1 %collective-permute-start.6 = (bf16[96,1152]{1,0:T(8,128)(2,1)S(1)}, bf16[96,1152]{1,0:T(8,128)(2,1)S(1)}, u32[]{:S(2)}, u32[]{:S(2)}) collective-permute-start(bf16[96,1152]{1,0:T(8,128)(2,1)S(1)} %bitcast.10), channel_id=1, source_target_pairs={{0,4},{4,0},{8,12},{12,8},{16,20},{20,16},{24,28},{28,24},{1,5},{5... | collective-permute-start | bytes 663560 | tf_op jit(solution)/shard_map/ppermute | solution.py:687
  21.5 27.8 %copy-start.4 = (bf16[128,768]{1,0:T(8,128)(2,1)S(1)}, bf16[128,768]{1,0:T(8,128)(2,1)}, u32[]{:S(2)}) copy-start(bf16[128,768]{1,0:T(8,128)(2,1)} %refs_3_.3) | copy-start | bytes 589828
  21.5 11.8 %collective-permute-start.14 = (bf16[2,96,768]{2,1,0:T(8,128)(2,1)S(1)}, bf16[2,96,768]{2,1,0:T(8,128)(2,1)S(1)}, u32[]{:S(2)}, u32[]{:S(2)}) collective-permute-start(bf16[2,96,768]{2,1,0:T(8,128)(2,1)S(1)} %pair.1.refs_0_), channel_id=1, source_target_pairs={{0,8},{4,12},{8,16},{12,20},{16,24},{20,28},{24,0},{28,4},{1,9},{5... | collective-permute-start | bytes 884744 | tf_op jit(solution)/shard_map/ppermute | solution.py:686
  24.5 27.7 %copy-start.7 = (s32[512]{0:T(512)S(1)}, s32[512]{0:T(512)}, u32[]{:S(2)}) copy-start(s32[512]{0:T(512)} %param.19) | copy-start | bytes 6148
  28.0 22.1 %collective-permute-start.7 = (bf16[4,96,640]{2,1,0:T(8,128)(2,1)S(1)}, bf16[4,96,640]{2,1,0:T(8,128)(2,1)S(1)}, u32[]{:S(2)}, u32[]{:S(2)}) collective-permute-start(bf16[4,96,640]{2,1,0:T(8,128)(2,1)S(1)} %shard_map.306), channel_id=1, source_target_pairs={{0,4},{4,0},{8,12},{12,8},{16,20},{20,16},{24,28},{28,24},{1,5},{5... | collective-permute-start | bytes 1474568 | tf_op jit(solution)/shard_map/ppermute | solution.py:690
  29.4 9.1 %collective-permute-start.8 = (bf16[96,1152]{1,0:T(8,128)(2,1)S(1)}, bf16[96,1152]{1,0:T(8,128)(2,1)S(1)}, u32[]{:S(2)}, u32[]{:S(2)}) collective-permute-start(bf16[96,1152]{1,0:T(8,128)(2,1)S(1)} %bitcast.11), channel_id=1, source_target_pairs={{0,8},{4,12},{8,16},{12,20},{16,24},{20,28},{24,0},{28,4},{1,9},{5... | collective-permute-start | bytes 663560 | tf_op jit(solution)/shard_map/ppermute | solution.py:685
  30.7 7.8 %collective-permute-start = (bf16[128,768]{1,0:T(8,128)(2,1)S(1)}, bf16[128,768]{1,0:T(8,128)(2,1)S(1)}, u32[]{:S(2)}, u32[]{:S(2)}) collective-permute-start(bf16[128,768]{1,0:T(8,128)(2,1)S(1)} %copy-done.1), channel_id=1, source_target_pairs={{0,2},{1,3},{2,0},{3,1},{4,6},{5,7},{6,4},{7,5},{8,10},{9,11},{10,... | collective-permute-start | bytes 589832 | tf_op jit(solution)/shard_map/ppermute | solution.py:642
  33.2 17.8 %collective-permute-start.15 = (bf16[2,96,768]{2,1,0:T(8,128)(2,1)S(1)}, bf16[2,96,768]{2,1,0:T(8,128)(2,1)S(1)}, u32[]{:S(2)}, u32[]{:S(2)}) collective-permute-start(bf16[2,96,768]{2,1,0:T(8,128)(2,1)S(1)} %collective-permute-done.14.refs_1_), channel_id=1, source_target_pairs={{0,8},{4,12},{8,16},{12,20},{16,24},{20,28},{24,0},{28,4},{1,9},{5... | collective-permute-start | bytes 884744 | tf_op jit(solution)/shard_map/ppermute | solution.py:692
  38.5 10.8 %collective-permute-start.9 = (bf16[96,1152]{1,0:T(8,128)(2,1)S(1)}, bf16[96,1152]{1,0:T(8,128)(2,1)S(1)}, u32[]{:S(2)}, u32[]{:S(2)}) collective-permute-start(bf16[96,1152]{1,0:T(8,128)(2,1)S(1)} %collective-permute-done.8.refs_1_), channel_id=1, source_target_pairs={{0,8},{4,12},{8,16},{12,20},{16,24},{20,28},{24,0},{28,4},{1,9},{5... | collective-permute-start | bytes 663560 | tf_op jit(solution)/shard_map/ppermute | solution.py:691
  38.5 12.4 %collective-permute-start.1 = (bf16[128,768]{1,0:T(8,128)(2,1)S(1)}, bf16[128,768]{1,0:T(8,128)(2,1)S(1)}, u32[]{:S(2)}, u32[]{:S(2)}) collective-permute-start(bf16[128,768]{1,0:T(8,128)(2,1)S(1)} %copy-done.1), channel_id=1, source_target_pairs={{0,1},{1,0},{2,3},{3,2},{4,5},{5,4},{6,7},{7,6},{8,9},{9,8},{10,11... | collective-permute-start | bytes 589832 | tf_op jit(solution)/shard_map/ppermute | solution.py:643
  38.5 13.7 %collective-permute-start.2 = (bf16[128,768]{1,0:T(8,128)(2,1)S(1)}, bf16[128,768]{1,0:T(8,128)(2,1)S(1)}, u32[]{:S(2)}, u32[]{:S(2)}) collective-permute-start(bf16[128,768]{1,0:T(8,128)(2,1)S(1)} %collective-permute-done.refs_2_.refs_1_), channel_id=1, source_target_pairs={{0,1},{1,0},{2,3},{3,2},{4,5},{5,4},{6,7},{7,6},{8,9},{9,8},{10,11... | collective-permute-start | bytes 589832 | tf_op jit(solution)/shard_map/ppermute | solution.py:644
  49.3 8.0 %collective-permute-start.10 = (bf16[128,768]{1,0:T(8,128)(2,1)S(1)}, bf16[128,768]{1,0:T(8,128)(2,1)S(1)}, u32[]{:S(2)}, u32[]{:S(2)}) collective-permute-start(bf16[128,768]{1,0:T(8,128)(2,1)S(1)} %copy-done.4), channel_id=1, source_target_pairs={{0,2},{1,3},{2,0},{3,1},{4,6},{5,7},{6,4},{7,5},{8,10},{9,11},{10,... | collective-permute-start | bytes 589832 | tf_op jit(solution)/shard_map/ppermute | solution.py:647
  50.1 11.1 %collective-permute-start.20 = (bf16[96,1152]{1,0:T(8,128)(2,1)S(1)}, bf16[96,1152]{1,0:T(8,128)(2,1)S(1)}, u32[]{:S(2)}, u32[]{:S(2)}) collective-permute-start(bf16[96,1152]{1,0:T(8,128)(2,1)S(1)} %collective-permute-done.9.refs_2_), channel_id=1, source_target_pairs={{0,4},{4,0},{8,12},{12,8},{16,20},{20,16},{24,28},{28,24},{1,5},{5... | collective-permute-start | bytes 663560 | tf_op jit(solution)/shard_map/ppermute | solution.py:722
  51.0 10.2 %collective-permute-start.18 = (bf16[96,1152]{1,0:T(8,128)(2,1)S(1)}, bf16[96,1152]{1,0:T(8,128)(2,1)S(1)}, u32[]{:S(2)}, u32[]{:S(2)}) collective-permute-start(bf16[96,1152]{1,0:T(8,128)(2,1)S(1)} %collective-permute-done.9.refs_2_), channel_id=1, source_target_pairs={{0,8},{4,12},{8,16},{12,20},{16,24},{20,28},{24,0},{28,4},{1,9},{5... | collective-permute-start | bytes 663560 | tf_op jit(solution)/shard_map/ppermute | solution.py:724
  51.1 14.9 %collective-permute-start.16 = (bf16[2,96,768]{2,1,0:T(8,128)(2,1)S(1)}, bf16[2,96,768]{2,1,0:T(8,128)(2,1)S(1)}, u32[]{:S(2)}, u32[]{:S(2)}) collective-permute-start(bf16[2,96,768]{2,1,0:T(8,128)(2,1)S(1)} %collective-permute-done.15.refs_2_), channel_id=1, source_target_pairs={{0,8},{4,12},{8,16},{12,20},{16,24},{20,28},{24,0},{28,4},{1,9},{5... | collective-permute-start | bytes 884744 | tf_op jit(solution)/shard_map/ppermute | solution.py:727
  57.4 7.8 %collective-permute-start.11 = (bf16[512,192]{1,0:T(8,128)(2,1)S(1)}, bf16[512,192]{1,0:T(8,128)(2,1)S(1)}, u32[]{:S(2)}, u32[]{:S(2)}) collective-permute-start(bf16[512,192]{1,0:T(8,128)(2,1)S(1)} %shard_map.307), channel_id=1, source_target_pairs={{0,2},{1,3},{2,0},{3,1},{4,6},{5,7},{6,4},{7,5},{8,10},{9,11},{10,... | collective-permute-start | bytes 589832 | tf_op jit(solution)/shard_map/ppermute | solution.py:718
  58.5 8.3 %collective-permute-start.19 = (bf16[96,1152]{1,0:T(8,128)(2,1)S(1)}, bf16[96,1152]{1,0:T(8,128)(2,1)S(1)}, u32[]{:S(2)}, u32[]{:S(2)}) collective-permute-start(bf16[96,1152]{1,0:T(8,128)(2,1)S(1)} %collective-permute-done.8.refs_1_), channel_id=1, source_target_pairs={{0,4},{4,0},{8,12},{12,8},{16,20},{20,16},{24,28},{28,24},{1,5},{5... | collective-permute-start | bytes 663560 | tf_op jit(solution)/shard_map/ppermute | solution.py:721
  61.2 7.9 %collective-permute-start.21 = (bf16[96,1152]{1,0:T(8,128)(2,1)S(1)}, bf16[96,1152]{1,0:T(8,128)(2,1)S(1)}, u32[]{:S(2)}, u32[]{:S(2)}) collective-permute-start(bf16[96,1152]{1,0:T(8,128)(2,1)S(1)} %shard_map.309), channel_id=1, source_target_pairs={{0,4},{4,0},{8,12},{12,8},{16,20},{20,16},{24,28},{28,24},{1,5},{5... | collective-permute-start | bytes 663560 | tf_op jit(solution)/shard_map/ppermute | solution.py:726
  65.9 3.3 %collective-permute-start.17 = (bf16[512,192]{1,0:T(8,128)(2,1)S(1)}, bf16[512,192]{1,0:T(8,128)(2,1)S(1)}, u32[]{:S(2)}, u32[]{:S(2)}) collective-permute-start(bf16[512,192]{1,0:T(8,128)(2,1)S(1)} %shard_map.308), channel_id=1, source_target_pairs={{0,1},{1,0},{2,3},{3,2},{4,5},{5,4},{6,7},{7,6},{8,9},{9,8},{10,11... | collective-permute-start | bytes 589832 | tf_op jit(solution)/shard_map/ppermute | solution.py:728
  69.3 2.4 %collective-permute-start.22 = (bf16[768,384]{1,0:T(8,128)(2,1)S(1)}, bf16[768,384]{1,0:T(8,128)(2,1)S(1)}, u32[]{:S(2)}, u32[]{:S(2)}) collective-permute-start(bf16[768,384]{1,0:T(8,128)(2,1)S(1)} %get-tuple-element.103.refs_6_.refs_2_), channel_id=1, source_target_pairs={{0,1},{1,0},{2,3},{3,2},{4,5},{5,4},{6,7},{7,6},{8,9},{9,8},{10,11... | collective-permute-start | bytes 1769480 | tf_op jit(solution)/shard_map/ppermute | solution.py:748
  69.4 2.4 %collective-permute-start.12 = (bf16[512,192]{1,0:T(8,128)(2,1)S(1)}, bf16[512,192]{1,0:T(8,128)(2,1)S(1)}, u32[]{:S(2)}, u32[]{:S(2)}) collective-permute-start(bf16[512,192]{1,0:T(8,128)(2,1)S(1)} %get-tuple-element.101.refs_2_.refs_0_), channel_id=1, source_target_pairs={{0,1},{1,0},{2,3},{3,2},{4,5},{5,4},{6,7},{7,6},{8,9},{9,8},{10,11... | collective-permute-start | bytes 589832 | tf_op jit(solution)/shard_map/ppermute | solution.py:719
  73.7 2.2 %collective-permute-start.23 = (bf16[256,768]{1,0:T(8,128)(2,1)S(1)}, bf16[256,768]{1,0:T(8,128)(2,1)S(1)}, u32[]{:S(2)}, u32[]{:S(2)}) collective-permute-start(bf16[256,768]{1,0:T(8,128)(2,1)S(1)} %get-tuple-element.107), channel_id=1, source_target_pairs={{0,1},{1,0},{2,3},{3,2},{4,5},{5,4},{6,7},{7,6},{8,9},{9,8},{10,11... | collective-permute-start | bytes 1179656 | tf_op jit(solution)/shard_map/ppermute | solution.py:773
  76.0 11.5 %collective-permute-start.24 = (bf16[256,768]{1,0:T(8,128)(2,1)S(1)}, bf16[256,768]{1,0:T(8,128)(2,1)S(1)}, u32[]{:S(2)}, u32[]{:S(2)}) collective-permute-start(bf16[256,768]{1,0:T(8,128)(2,1)S(1)} %get-tuple-element.109), channel_id=1, source_target_pairs={{0,2},{1,3},{2,0},{3,1},{4,6},{5,7},{6,4},{7,5},{8,10},{9,11},{10,... | collective-permute-start | bytes 1179656 | tf_op jit(solution)/shard_map/ppermute | solution.py:777
  88.6 1.7 %collective-permute-start.25 = (bf16[256,768]{1,0:T(8,128)(2,1)S(1)}, bf16[256,768]{1,0:T(8,128)(2,1)S(1)}, u32[]{:S(2)}, u32[]{:S(2)}) collective-permute-start(bf16[256,768]{1,0:T(8,128)(2,1)S(1)} %get-tuple-element.112.refs_0_.refs_2_), channel_id=1, source_target_pairs={{0,1},{1,0},{2,3},{3,2},{4,5},{5,4},{6,7},{7,6},{8,9},{9,8},{10,11... | collective-permute-start | bytes 1179656 | tf_op jit(solution)/shard_map/ppermute | solution.py:798
  91.3 1.8 %collective-permute-start.26 = (bf16[256,768]{1,0:T(8,128)(2,1)S(1)}, bf16[256,768]{1,0:T(8,128)(2,1)S(1)}, u32[]{:S(2)}, u32[]{:S(2)}) collective-permute-start(bf16[256,768]{1,0:T(8,128)(2,1)S(1)} %get-tuple-element.116), channel_id=1, source_target_pairs={{0,1},{1,0},{2,3},{3,2},{4,5},{5,4},{6,7},{7,6},{8,9},{9,8},{10,11... | collective-permute-start | bytes 1179656 | tf_op jit(solution)/shard_map/ppermute | solution.py:773
  93.2 13.2 %collective-permute-start.27 = (bf16[256,768]{1,0:T(8,128)(2,1)S(1)}, bf16[256,768]{1,0:T(8,128)(2,1)S(1)}, u32[]{:S(2)}, u32[]{:S(2)}) collective-permute-start(bf16[256,768]{1,0:T(8,128)(2,1)S(1)} %get-tuple-element.118), channel_id=1, source_target_pairs={{0,2},{1,3},{2,0},{3,1},{4,6},{5,7},{6,4},{7,5},{8,10},{9,11},{10,... | collective-permute-start | bytes 1179656 | tf_op jit(solution)/shard_map/ppermute | solution.py:777
  95.8 10.6 %collective-permute-start.28 = (bf16[2,96,768]{2,1,0:T(8,128)(2,1)S(1)}, bf16[2,96,768]{2,1,0:T(8,128)(2,1)S(1)}, u32[]{:S(2)}, u32[]{:S(2)}) collective-permute-start(bf16[2,96,768]{2,1,0:T(8,128)(2,1)S(1)} %get-tuple-element.128.refs_4_), channel_id=1, source_target_pairs={{0,8},{4,12},{8,16},{12,20},{16,24},{20,28},{24,0},{28,4},{1,9},{5... | collective-permute-start | bytes 884744 | tf_op jit(solution)/shard_map/ppermute | solution.py:838
  97.2 15.6 %collective-permute-start.31 = (bf16[4,96,768]{2,1,0:T(8,128)(2,1)S(1)}, bf16[4,96,768]{2,1,0:T(8,128)(2,1)S(1)}, u32[]{:S(2)}, u32[]{:S(2)}) collective-permute-start(bf16[4,96,768]{2,1,0:T(8,128)(2,1)S(1)} %get-tuple-element.129.refs_6_), channel_id=1, source_target_pairs={{0,4},{4,0},{8,12},{12,8},{16,20},{20,16},{24,28},{28,24},{1,5},{5... | collective-permute-start | bytes 1769480 | tf_op jit(solution)/shard_map/ppermute | solution.py:851
  106.9 1.8 %collective-permute-start.29 = (bf16[256,768]{1,0:T(8,128)(2,1)S(1)}, bf16[256,768]{1,0:T(8,128)(2,1)S(1)}, u32[]{:S(2)}, u32[]{:S(2)}) collective-permute-start(bf16[256,768]{1,0:T(8,128)(2,1)S(1)} %get-tuple-element.130.refs_2_.refs_4_.refs_0_), channel_id=1, source_target_pairs={{0,1},{1,0},{2,3},{3,2},{4,5},{5,4},{6,7},{7,6},{8,9},{9,8},{10,11... | collective-permute-start | bytes 1179656 | tf_op jit(solution)/shard_map/ppermute | solution.py:869
  107.1 11.5 %collective-permute-start.30 = (bf16[2,96,768]{2,1,0:T(8,128)(2,1)S(1)}, bf16[2,96,768]{2,1,0:T(8,128)(2,1)S(1)}, u32[]{:S(2)}, u32[]{:S(2)}) collective-permute-start(bf16[2,96,768]{2,1,0:T(8,128)(2,1)S(1)} %z_step.2.refs_6_), channel_id=1, source_target_pairs={{0,8},{4,12},{8,16},{12,20},{16,24},{20,28},{24,0},{28,4},{1,9},{5... | collective-permute-start | bytes 884744 | tf_op jit(solution)/shard_map/ppermute | solution.py:879
  113.7 25.9 %collective-permute-start.34 = (bf16[4,96,640]{2,1,0:T(8,128)(2,1)S(1)}, bf16[4,96,640]{2,1,0:T(8,128)(2,1)S(1)}, u32[]{:S(2)}, u32[]{:S(2)}) collective-permute-start(bf16[4,96,640]{2,1,0:T(8,128)(2,1)S(1)} %get-tuple-element.141.refs_2_), channel_id=1, source_target_pairs={{0,4},{4,0},{8,12},{12,8},{16,20},{20,16},{24,28},{28,24},{1,5},{5... | collective-permute-start | bytes 1474568 | tf_op jit(solution)/shard_map/ppermute | solution.py:932
  115.3 16.0 %collective-permute-start.35 = (bf16[4,96,192]{2,1,0:T(8,128)(2,1)S(1)}, bf16[4,96,192]{2,1,0:T(8,128)(2,1)S(1)}, u32[]{:S(2)}, u32[]{:S(2)}) collective-permute-start(bf16[4,96,192]{2,1,0:T(8,128)(2,1)S(1)} %get-tuple-element.134.refs_6_), channel_id=1, source_target_pairs={{0,4},{4,0},{8,12},{12,8},{16,20},{20,16},{24,28},{28,24},{1,5},{5... | collective-permute-start | bytes 442376 | tf_op jit(solution)/shard_map/ppermute | solution.py:933
  118.6 20.9 %collective-permute-start.36 = (bf16[2,96,768]{2,1,0:T(8,128)(2,1)S(1)}, bf16[2,96,768]{2,1,0:T(8,128)(2,1)S(1)}, u32[]{:S(2)}, u32[]{:S(2)}) collective-permute-start(bf16[2,96,768]{2,1,0:T(8,128)(2,1)S(1)} %z_step.3.refs_2_), channel_id=1, source_target_pairs={{0,8},{4,12},{8,16},{12,20},{16,24},{20,28},{24,0},{28,4},{1,9},{5... | collective-permute-start | bytes 884744 | tf_op jit(solution)/shard_map/ppermute | solution.py:879
  118.7 17.4 %collective-permute-start.38 = (bf16[96,768]{1,0:T(8,128)(2,1)S(1)}, bf16[96,768]{1,0:T(8,128)(2,1)S(1)}, u32[]{:S(2)}, u32[]{:S(2)}) collective-permute-start(bf16[96,768]{1,0:T(8,128)(2,1)S(1)} %get-tuple-element.151), channel_id=1, source_target_pairs={{0,16},{4,20},{8,24},{12,28},{16,0},{20,4},{24,8},{28,12},{1,17},{... | collective-permute-start | bytes 442376 | tf_op jit(solution)/shard_map/ppermute | solution.py:916
  119.1 17.0 %collective-permute-start.39 = (bf16[96,768]{1,0:T(8,128)(2,1)S(1)}, bf16[96,768]{1,0:T(8,128)(2,1)S(1)}, u32[]{:S(2)}, u32[]{:S(2)}) collective-permute-start(bf16[96,768]{1,0:T(8,128)(2,1)S(1)} %get-tuple-element.152), channel_id=1, source_target_pairs={{0,24},{4,28},{8,0},{12,4},{16,8},{20,12},{24,16},{28,20},{1,25},{... | collective-permute-start | bytes 442376 | tf_op jit(solution)/shard_map/ppermute | solution.py:916
  131.3 7.5 %collective-permute-start.37 = (bf16[96,768]{1,0:T(8,128)(2,1)S(1)}, bf16[96,768]{1,0:T(8,128)(2,1)S(1)}, u32[]{:S(2)}, u32[]{:S(2)}) collective-permute-start(bf16[96,768]{1,0:T(8,128)(2,1)S(1)} %get-tuple-element.140.refs_9_), channel_id=1, source_target_pairs={{0,8},{4,12},{8,16},{12,20},{16,24},{20,28},{24,0},{28,4},{1,9},{5... | collective-permute-start | bytes 442376 | tf_op jit(solution)/shard_map/ppermute | solution.py:916
  140.8 21.3 %all-to-all-start.1 = ((bf16[16,24,832]{2,1,0:T(8,128)(2,1)}), bf16[16,24,832]{2,1,0:T(8,128)(2,1)S(1)}, u32[]{:S(2)}, u32[]{:S(2)}) async-start(bf16[16,24,832]{2,1,0:T(8,128)(2,1)} %bitcast.5), calls=%async_computation.1 | async-start | bytes 1376256 | tf_op jit(solution)/shard_map/all_to_all | solution.py:566
  145.7 2.0 %collective-permute-start.32 = (bf16[256,768]{1,0:T(8,128)(2,1)S(1)}, bf16[256,768]{1,0:T(8,128)(2,1)S(1)}, u32[]{:S(2)}, u32[]{:S(2)}) collective-permute-start(bf16[256,768]{1,0:T(8,128)(2,1)S(1)} %get-tuple-element.143), channel_id=1, source_target_pairs={{0,1},{1,0},{2,3},{3,2},{4,5},{5,4},{6,7},{7,6},{8,9},{9,8},{10,11... | collective-permute-start | bytes 1179656 | tf_op jit(solution)/shard_map/ppermute | solution.py:943
  146.2 5.9 %collective-permute-start.40 = (bf16[96,768]{1,0:T(8,128)(2,1)S(1)}, bf16[96,768]{1,0:T(8,128)(2,1)S(1)}, u32[]{:S(2)}, u32[]{:S(2)}) collective-permute-start(bf16[96,768]{1,0:T(8,128)(2,1)S(1)} %get-tuple-element.162), channel_id=1, source_target_pairs={{0,4},{4,0},{8,12},{12,8},{16,20},{20,16},{24,28},{28,24},{1,5},{5... | collective-permute-start | bytes 442376 | tf_op jit(solution)/shard_map/ppermute | solution.py:969
  147.8 12.5 %collective-permute-start.33 = (bf16[128,768]{1,0:T(8,128)(2,1)S(1)}, bf16[128,768]{1,0:T(8,128)(2,1)S(1)}, u32[]{:S(2)}, u32[]{:S(2)}) collective-permute-start(bf16[128,768]{1,0:T(8,128)(2,1)S(1)} %get-tuple-element.146), channel_id=1, source_target_pairs={{0,2},{1,3},{2,0},{3,1},{4,6},{5,7},{6,4},{7,5},{8,10},{9,11},{10,... | collective-permute-start | bytes 589832 | tf_op jit(solution)/shard_map/ppermute | solution.py:961
  152.1 2.1 %collective-permute-start.41 = (bf16[24,768]{1,0:T(8,128)(2,1)S(1)}, bf16[24,768]{1,0:T(8,128)(2,1)S(1)}, u32[]{:S(2)}, u32[]{:S(2)}) collective-permute-start(bf16[24,768]{1,0:T(8,128)(2,1)S(1)} %get-tuple-element.164), channel_id=1, source_target_pairs={{0,1},{1,0},{2,3},{3,2},{4,5},{5,4},{6,7},{7,6},{8,9},{9,8},{10,11... | collective-permute-start | bytes 110600 | tf_op jit(solution)/shard_map/ppermute | solution.py:974
  152.2 6.8 %collective-permute-start.42 = (bf16[24,768]{1,0:T(8,128)(2,1)S(1)}, bf16[24,768]{1,0:T(8,128)(2,1)S(1)}, u32[]{:S(2)}, u32[]{:S(2)}) collective-permute-start(bf16[24,768]{1,0:T(8,128)(2,1)S(1)} %get-tuple-element.165), channel_id=1, source_target_pairs={{0,2},{1,3},{2,0},{3,1},{4,6},{5,7},{6,4},{7,5},{8,10},{9,11},{10,... | collective-permute-start | bytes 110600 | tf_op jit(solution)/shard_map/ppermute | solution.py:974
  154.2 5.3 %collective-permute-start.43 = (bf16[24,768]{1,0:T(8,128)(2,1)S(1)}, bf16[24,768]{1,0:T(8,128)(2,1)S(1)}, u32[]{:S(2)}, u32[]{:S(2)}) collective-permute-start(bf16[24,768]{1,0:T(8,128)(2,1)S(1)} %get-tuple-element.166), channel_id=1, source_target_pairs={{0,3},{1,2},{2,1},{3,0},{4,7},{5,6},{6,5},{7,4},{8,11},{9,10},{10,... | collective-permute-start | bytes 110600 | tf_op jit(solution)/shard_map/ppermute | solution.py:974
  (6 other events, 36.9 us)

commit v5 on v4

--- a/solution.py
+++ b/solution.py
@@ -112,8 +112,14 @@
 DOWNFIRST = 0
 ROWSLATE = 1
 INFIRST = 0
-HOLDUP = 1
+HOLDUP = 0
+INHEADS = 0
+INFIN = 1
 OEARLY = 1
+OSTEP = 1
+ZLATE = 0
+C_FUP = 26
+CUT = 384
 Z1FIRST = 1
 HOLDDOWN = 1
 C_MERGE = 0.3
@@ -402,7 +408,7 @@
 
 
 def split_rows(kept, sent, values):
-    if sent is None:
+    if not sent:
         kept[...] = values
         return
     rows = kept.shape[1]
@@ -411,12 +417,16 @@
     for z in range(4):
         even, odd = pieces[z, 0], pieces[z, 1]
         kept[z] = jnp.where(mine == 0, even, odd)
-        sent[z] = jnp.where(mine == 0, odd, even).astype(BF)
+        leaving = jnp.where(mine == 0, odd, even).astype(BF)
+        column = 0
+        for out in sent:
+            out[z] = leaving[:, column : column + out.shape[2]]
+            column += out.shape[2]
 
 
 def weight_grad_kernel(left0, left1, right0, right1, kept, *sent):
     grad = dot(left0[...], right0[...], TN) + dot(left1[...], right1[...], TN)
-    split_rows(kept, sent[0] if sent else None, grad)
+    split_rows(kept, sent, grad)
 
 
 def first_back_kernel(part, far, d_second, unit, rate, bias, d_first_out, low_out, grads):
@@ -476,7 +486,7 @@
     ):
         at = pl.multiple_of((here ^ flip) * share, 64)
         out[pl.ds(at, share), :] = dot(pick(ref, order), low, TN)
-    split_rows(kept, sent[0] if sent else None, out[...])
+    split_rows(kept, sent, out[...])
 
 
 def last_grad_kernel(rows, x0, x1, x2, x3, d_qkv, grads2, grads1, sum0, sum1, kept, *sent):
@@ -508,7 +518,7 @@
     every = jnp.concatenate([two[:2], g1[0:3], g2[0:3]] + ups, axis=0)
     every = jnp.concatenate([every, jnp.zeros((4, width), F32)], axis=0)
     columns = transpose_wide(every)[:, :SPARE]
-    split_rows(kept, sent[0] if sent else None, jnp.concatenate([weights, columns], axis=1))
+    split_rows(kept, sent, jnp.concatenate([weights, columns], axis=1))
 
 
 def finish_up_kernel(relative, p0, p1, p2, p3, out):
@@ -555,10 +565,14 @@
     bias_outs[8][...] = long.reshape(4 * rows)
 
 
-def sum_two_kernel(kept0, got0, kept1, got1, out):
-    cut = kept0.shape[2]
-    out[:, :, :cut] = (kept0[...] + got0[...].astype(F32)).astype(BF)
-    out[:, :, cut:] = (kept1[...] + got1[...].astype(F32)).astype(BF)
+def sum_two_kernel(kept0, kept1, *refs):
+    *gots, out = refs
+    cut, column = kept0.shape[2], 0
+    for got in gots[:-1]:
+        part = slice(column, column + got.shape[2])
+        out[:, :, part] = (kept0[:, :, part] + got[...].astype(F32)).astype(BF)
+        column = part.stop
+    out[:, :, cut:] = (kept1[...] + gots[-1][...].astype(F32)).astype(BF)
 
 
 def to_owners(summed, rows):
@@ -797,10 +811,10 @@
 )
     ds1 = lax.ppermute(ds0, "head", CORE)
 
-    def grad_outs(columns):
+    def grad_outs(columns, cuts=None):
         if cube:
-            dims = (4, width // 8, columns)
-            return (shape(dims, F32), shape(dims, BF))
+            kept = shape((4, width // 8, columns), F32)
+            return (kept,) + tuple(shape((4, width // 8, c), BF) for c in cuts or (columns,))
         return (shape((width, columns), F32),)
 
     def ffn_back(low, slope, kind, after):
@@ -913,11 +927,10 @@
             after=(d_qkv,) if ROWSLATE else (df0,),
             micros=C_ROWS,
         )
-        down_got = [lax.ppermute(o, "dp", zshift(k)) for k, o in zip((1, 2, 3), down_sent)]
         order = (down_sent[0],)
     last_terms = call(
         functools.partial(last_grad_kernel, rows),
-        grad_outs(3 * share + SPARE),
+        grad_outs(3 * share + SPARE, (CUT, 3 * share + SPARE - CUT) if CUT else None),
         *x,
         d_qkv,
         grads2,
@@ -929,9 +942,13 @@
     )
     order = (last_terms[-1],)
     if cube:
-        got_last = lax.ppermute(last_terms[1], "dp", XSWAP)
+        got_last = [lax.ppermute(term, "dp", XSWAP) for term in last_terms[1:]]
         got_output = lax.ppermute(output_terms[1], "dp", XSWAP)
-        order = (next_step(3, order),)
+        order = (next_step(3, order + ((got_output,) if OSTEP else ())),)
+        down_got = [
+            lax.ppermute(later(o, *order) if ZLATE == k else o, "dp", zshift(k))
+            for k, o in zip((1, 2, 3), down_sent)
+        ]
     part, sent = call(
         input_grad_kernel,
         (shape((mine, width), F32), shape((mine, width), BF)),
@@ -967,6 +984,7 @@
                 (shape((rows, width), BF),) * 4,
                 up_kept,
                 lax.ppermute(up_cross, "dp", XSWAP),
+                after=(input_grad,) if INHEADS else (),
                 micros=C_SUM,
             )
         )
@@ -988,14 +1006,16 @@
         functools.partial(finish_up_kernel, cube),
         shape((rows, 4 * width), F32),
         *up_pieces,
+        after=(input_grad,) if INFIN else (),
+        micros=C_FUP,
     )
     if cube:
         summed = call(
             sum_two_kernel,
             shape((4, 4 * rows, last_columns), BF),
             last_terms[0],
-            got_last,
             output_terms[0],
+            *got_last,
             got_output,
             micros=C_LAST,
         )

time: 164 us -> 159 us (0.970)
  waiting for transfers between devices: 85.2 us -> 71.5 us
  local copies, waits for them, and re-layouts: 1.06 us -> 5.52 us
  Pallas kernels: 27.8 us -> 30.2 us
  starting transfers between devices: 47.8 us -> 49.8 us
    ppermute x1, waiting for transfers between devices: 8.78 us -> 0.01 us  [body(): got_output = lax.ppermute(output_terms[1], 'dp', XSWAP)]
    unnamed x20 -> x26, local copies, waits for them, and re-layouts: 1.06 us -> 5.52 us
    ppermute x2, waiting for transfers between devices: 2.71 us -> 0.01 us  [next_step(): up_got.append(lax.ppermute(run, 'dp', zshift(1)))]
    ppermute x1, waiting for transfers between devices: 2.46 us -> 5.08 us  [body(): lax.ppermute(up_cross, 'dp', XSWAP)]
    pallas_call x31, Pallas kernels: 25.3 us -> 27.7 us  [call(): pl.pallas_call(run, out_shape=outs, in_specs=[spec] * count + [pl.BlockSp...]
    ppermute x3, waiting for transfers between devices: 5.18 us -> 3.39 us  [body(): lax.ppermute(up_pieces[flip], 'head', [(i, i ^ flip) for i in range(4)])]
    all_to_all x2, starting transfers between devices: 11.7 us -> 13.4 us  [to_owners(): lax.all_to_all(summed.reshape(16 * rows, columns), ALL, 0, 0, tiled=True,...]
    ppermute x4 -> x5, waiting for transfers between devices: 6.66 us -> 5.03 us  [the longest x3 5.03 us: body(): lax.ppermute(later(o, *order) if ZLATE == k else o, 'dp', zshift(k))]
  transfers between devices with their start and end apart: 46 -> 47, of which waited for: 26 -> 23; matrix products, arithmetic and copies ran while one was open for 0% -> 0% of each run, Pallas kernels for 12% -> 14%
where the time goes in v5:
time: 159 us; the launch traced here: 158 us
  waiting for transfers between devices  71.5 us (45%)
  starting transfers between devices  49.8 us (31%)
  Pallas kernels  30.2 us (19%)
  local copies, waits for them, and re-layouts  5.52 us (3%)
    pallas_call x31, Pallas kernels, call(): pl.pallas_call(run, out_shape=outs, in_specs=[spec] * count + [pl.BlockSp...  27.7 us
    all_to_all x2, starting transfers between devices, to_owners(): lax.all_to_all(summed.reshape(16 * rows, columns), ALL, 0, 0, tiled=True,...  13.4 us
    ppermute x1, waiting for transfers between devices, body(): have.append(lax.ppermute(have[1], 'dp', zshift(1)))  10.3 us
    ppermute x2, waiting for transfers between devices, pair_sum(): return (kept, lax.ppermute(low, 'head', CHIP))  9.75 us
    ppermute x1, waiting for transfers between devices, body(): up_got = [lax.ppermute(up_run, 'dp', zshift(1))]  7.69 us
    unnamed x26, local copies, waits for them, and re-layouts  5.52 us
    ppermute x1, waiting for transfers between devices, body(): have = [wide, lax.ppermute(wide, 'dp', zshift(1))]  5.28 us
    ppermute x1, waiting for transfers between devices, body(): lax.ppermute(up_cross, 'dp', XSWAP)  5.08 us
  transfers between devices with their start and end apart: 47, of which 23 were waited for; matrix products, arithmetic and copies ran while one was open for 0% of the time, Pallas kernels for 14%

profile of v5, /device:TPU:0, one launch (start us, length us, event | category | flops | bytes accessed | tf_op | source)
XLA Modules:
  0.0 158.3 jit_solution(1340150184463756686)
XLA Ops:
  0.7 2.5 %shard_map.305 = (bf16[4,4,24,640]{3,2,1,0:T(8,128)(2,1)}, bf16[24,1152]{1,0:T(8,128)(2,1)}, bf16[24,1152]{1,0:T(8,128)(2,1)}, bf16[24,1152]{1,0:T(8,128)(2,1)},...) custom-call(f32[24,768]{1,0:T(8,128)} %query.1, f32[24,768]{1,0:T(8,128)} %key.1, f32[24,768]{1,0:T(8,128)} %value.1, ...), custom_call_target="tpu_custom_call" | custom-call | tf_op jit(solution)/shard_map/pallas_call | solution.py:195
  3.2 7.5 %all-to-all-start = ((bf16[16,24,640]{2,1,0:T(8,128)(2,1)}), bf16[16,24,640]{2,1,0:T(8,128)(2,1)S(1)}, u32[]{:S(2)}, u32[]{:S(2)}) async-start(bf16[16,24,640]{2,1,0:T(8,128)(2,1)} %bitcast.16), calls=%async_computation | async-start | bytes 983040 | tf_op jit(solution)/shard_map/all_to_all | solution.py:580
  11.1 1.7 %collective-permute-start.4 = (bf16[24,1152]{1,0:T(8,128)(2,1)}, bf16[24,1152]{1,0:T(8,128)(2,1)S(1)}, u32[]{:S(2)}, u32[]{:S(2)}) collective-permute-start(bf16[24,1152]{1,0:T(8,128)(2,1)} %get-tuple-element.98), channel_id=1, source_target_pairs={{0,2},{1,3},{2,0},{3,1},{4,6},{5,7},{6,4},{7,5},{8,10},{9,11},{10,... | collective-permute-start | bytes 165896 | tf_op jit(solution)/shard_map/ppermute | solution.py:677
  12.8 1.5 collective-permute-start.13
  14.3 4.5 %collective-permute-done.4.refs_2_ = bf16[24,1152]{1,0:T(8,128)(2,1)S(1)} collective-permute-done((bf16[24,1152]{1,0:T(8,128)(2,1)}, bf16[24,1152]{1,0:T(8,128)(2,1)S(1)}, u32[]{:S(2)}, u32[]{:S(2)}) %collective-permute-start.4) | collective-permute-done | bytes 55328 | tf_op jit(solution)/shard_map/ppermute | solution.py:677
  19.9 1.6 collective-permute-start.6
  21.5 1.4 collective-permute-start.14
  22.9 1.6 %all-to-all-done = bf16[16,24,640]{2,1,0:T(8,128)(2,1)S(1)} async-done(((bf16[16,24,640]{2,1,0:T(8,128)(2,1)}), bf16[16,24,640]{2,1,0:T(8,128)(2,1)S(1)}, u32[]{:S(2)}, u32[]{:S(2)}) %all-to-all-start) | async-done | bytes 491552 | tf_op jit(solution)/shard_map/all_to_all | solution.py:580
  24.6 3.4 %collective-permute-done.6.refs_1_.refs_4_ = bf16[96,1152]{1,0:T(8,128)(2,1)S(1)} collective-permute-done((bf16[96,1152]{1,0:T(8,128)(2,1)S(1)}, bf16[96,1152]{1,0:T(8,128)(2,1)S(1)}, u32[]{:S(2)}, u32[]{:S(2)}) %collective-permute-start.6) | collective-permute-done | bytes 221216 | tf_op jit(solution)/shard_map/ppermute | solution.py:701
  28.0 1.5 collective-permute-start.7
  29.5 1.3 collective-permute-start.8
  30.8 2.5 %collective-permute-done.14.refs_1_ = bf16[2,96,768]{2,1,0:T(8,128)(2,1)S(1)} collective-permute-done((bf16[2,96,768]{2,1,0:T(8,128)(2,1)S(1)}, bf16[2,96,768]{2,1,0:T(8,128)(2,1)S(1)}, u32[]{:S(2)}, u32[]{:S(2)}) %collective-permute-start.14) | collective-permute-done | bytes 294944 | tf_op jit(solution)/shard_map/ppermute | solution.py:700
  33.2 5.3 %collective-permute-done.8.refs_1_ = bf16[96,1152]{1,0:T(8,128)(2,1)S(1)} collective-permute-done((bf16[96,1152]{1,0:T(8,128)(2,1)S(1)}, bf16[96,1152]{1,0:T(8,128)(2,1)S(1)}, u32[]{:S(2)}, u32[]{:S(2)}) %collective-permute-start.8) | collective-permute-done | bytes 221216 | tf_op jit(solution)/shard_map/ppermute | solution.py:699
  39.1 10.3 %collective-permute-done.9.refs_2_ = bf16[96,1152]{1,0:T(8,128)(2,1)S(1)} collective-permute-done((bf16[96,1152]{1,0:T(8,128)(2,1)S(1)}, bf16[96,1152]{1,0:T(8,128)(2,1)S(1)}, u32[]{:S(2)}, u32[]{:S(2)}) %collective-permute-start.9) | collective-permute-done | bytes 221216 | tf_op jit(solution)/shard_map/ppermute | solution.py:705
  51.1 1.2 collective-permute-start.16
  52.3 5.0 %attend.1 = (bf16[512,576]{1,0:T(8,128)(2,1)S(1)}, f32[3,512,512]{2,1,0:T(8,128)S(1)}, bf16[512,192]{1,0:T(8,128)(2,1)S(1)}, f32[16,768]{1,0:T(8,128)S(1)}) custom-call(s32[4,128]{1,0:T(4,128)S(1)} %bitcast.15, bf16[128,768]{1,0:T(8,128)(2,1)S(1)} %copy-done.1, bf16[128,768]{1,0:T(8,128)(2,1)S(1)} %collective-permute-done.refs_2_.refs_1_, ...), custom_call_target="tpu_custom_call" | custom-call | flops 1500000000 | bytes 4500000 | tf_op jit(solution)/shard_map/attend/pallas_call | solution.py:41
  57.4 1.2 collective-permute-start.11
  58.5 1.5 collective-permute-start.19
  60.0 1.2 collective-permute-done.18.refs_3_
  61.2 1.4 collective-permute-start.21
  62.7 2.5 %collective-permute-done.11.refs_3_.refs_1_ = bf16[512,192]{1,0:T(8,128)(2,1)S(1)} collective-permute-done((bf16[512,192]{1,0:T(8,128)(2,1)S(1)}, bf16[512,192]{1,0:T(8,128)(2,1)S(1)}, u32[]{:S(2)}, u32[]{:S(2)}) %collective-permute-start.11) | collective-permute-done | bytes 196640 | tf_op jit(solution)/shard_map/ppermute | solution.py:732
  66.8 2.4 %collective-permute-done.21.refs_7_ = bf16[96,1152]{1,0:T(8,128)(2,1)S(1)} collective-permute-done((bf16[96,1152]{1,0:T(8,128)(2,1)S(1)}, bf16[96,1152]{1,0:T(8,128)(2,1)S(1)}, u32[]{:S(2)}, u32[]{:S(2)}) %collective-permute-start.21) | collective-permute-done | bytes 221216 | tf_op jit(solution)/shard_map/ppermute | solution.py:740
  70.0 1.8 %collective-permute-done.12.refs_4_.refs_2_ = bf16[512,192]{1,0:T(8,128)(2,1)S(1)} collective-permute-done((bf16[512,192]{1,0:T(8,128)(2,1)S(1)}, bf16[512,192]{1,0:T(8,128)(2,1)S(1)}, u32[]{:S(2)}, u32[]{:S(2)}) %collective-permute-start.12) | collective-permute-done | bytes 196640 | tf_op jit(solution)/shard_map/ppermute | solution.py:733
  71.7 1.9 %ffn.3 = (bf16[256,768]{1,0:T(8,128)(2,1)S(1)}, bf16[256,768]{1,0:T(8,128)(2,1)S(1)}, f32[256,768]{1,0:T(8,128)S(1)}, bf16[256,768]{1,0:T(8,128)(2,1)S(1)}) custom-call(bf16[128,768]{1,0:T(8,128)(2,1)S(1)} %collective-permute-done.1.refs_3_.refs_0_.refs_2_, bf16[128,768]{1,0:T(8,128)(2,1)S(1)} %collective-permute-done.2.refs_4_.refs_1_.refs_3_, ...), custom_call_target="tpu_custom_call" | custom-call | flops 570000000 | bytes 1709999 | tf_op jit(solution)/shard_map/ffn/pallas_call | solution.py:41
  73.8 1.9 %ffn.2 = (bf16[256,768]{1,0:T(8,128)(2,1)S(1)}, bf16[256,768]{1,0:T(8,128)(2,1)S(1)}, f32[256,768]{1,0:T(8,128)S(1)}, f32[256,768]{1,0:T(8,128)S(1)}, f32[256,76...) custom-call(bf16[128,768]{1,0:T(8,128)(2,1)S(1)} %copy-done.1, ...), custom_call_target="tpu_custom_call" | custom-call | flops 570000000 | bytes 1709999 | tf_op jit(solution)/shard_map/ffn/pallas_call | solution.py:41
  75.9 1.7 %collective-permute-start.24 = (bf16[256,768]{1,0:T(8,128)(2,1)S(1)}, bf16[256,768]{1,0:T(8,128)(2,1)S(1)}, u32[]{:S(2)}, u32[]{:S(2)}) collective-permute-start(bf16[256,768]{1,0:T(8,128)(2,1)S(1)} %get-tuple-element.110), channel_id=1, source_target_pairs={{0,2},{1,3},{2,0},{3,1},{4,6},{5,7},{6,4},{7,5},{8,10},{9,11},{10,... | collective-permute-start | bytes 1179656 | tf_op jit(solution)/shard_map/ppermute | solution.py:791
  77.6 9.8 %collective-permute-done.24.refs_1_ = bf16[256,768]{1,0:T(8,128)(2,1)S(1)} collective-permute-done((bf16[256,768]{1,0:T(8,128)(2,1)S(1)}, bf16[256,768]{1,0:T(8,128)(2,1)S(1)}, u32[]{:S(2)}, u32[]{:S(2)}) %collective-permute-start.24) | collective-permute-done | bytes 393248 | tf_op jit(solution)/shard_map/ppermute | solution.py:791
  87.3 1.2 final.1
  88.5 1.7 %collective-permute-done.25.refs_0_.refs_3_ = bf16[256,768]{1,0:T(8,128)(2,1)S(1)} collective-permute-done((bf16[256,768]{1,0:T(8,128)(2,1)S(1)}, bf16[256,768]{1,0:T(8,128)(2,1)S(1)}, u32[]{:S(2)}, u32[]{:S(2)}) %collective-permute-start.25) | collective-permute-done | bytes 393248 | tf_op jit(solution)/shard_map/ppermute | solution.py:812
  93.1 1.7 %collective-permute-start.27 = (bf16[256,768]{1,0:T(8,128)(2,1)S(1)}, bf16[256,768]{1,0:T(8,128)(2,1)S(1)}, u32[]{:S(2)}, u32[]{:S(2)}) collective-permute-start(bf16[256,768]{1,0:T(8,128)(2,1)S(1)} %get-tuple-element.119), channel_id=1, source_target_pairs={{0,2},{1,3},{2,0},{3,1},{4,6},{5,7},{6,4},{7,5},{8,10},{9,11},{10,... | collective-permute-start | bytes 1179656 | tf_op jit(solution)/shard_map/ppermute | solution.py:791
  97.1 1.5 collective-permute-start.31
  98.6 7.7 %collective-permute-done.28.refs_7_.refs_1_ = bf16[2,96,768]{2,1,0:T(8,128)(2,1)S(1)} collective-permute-done((bf16[2,96,768]{2,1,0:T(8,128)(2,1)S(1)}, bf16[2,96,768]{2,1,0:T(8,128)(2,1)S(1)}, u32[]{:S(2)}, u32[]{:S(2)}) %collective-permute-start.28) | collective-permute-done | bytes 294944 | tf_op jit(solution)/shard_map/ppermute | solution.py:852
  107.6 1.0 collective-permute-done.29.refs_5_.refs_1_
  109.5 1.5 collective-permute-start.32
  111.1 3.0 %attend_back.1.refs_2_.refs_4_.refs_0_ = bf16[512,576]{1,0:T(8,128)(2,1)S(1)} custom-call(bf16[256,768]{1,0:T(8,128)(2,1)S(1)} %get-tuple-element.131.refs_2_.refs_4_.refs_0_, bf16[256,768]{1,0:T(8,128)(2,1)S(1)} %collective-permute-done.29.refs_5_.refs_1_, bf16[768,384]{1,0:T(8,128)(2,1)S(1)} %get-tuple-element.104.refs_6_.refs_2_, ...), custom_call_target="tpu_custom_call" | custom-call | flops 900000000 | bytes 2699999 | tf_op jit(solution)/shard_map/attend_back/pallas_call | solution.py:41
  115.7 1.5 collective-permute-start.36
  117.1 1.4 collective-permute-start.38
  118.5 2.7 %collective-permute-start.39 = (bf16[96,768]{1,0:T(8,128)(2,1)S(1)}, bf16[96,768]{1,0:T(8,128)(2,1)S(1)}, u32[]{:S(2)}, u32[]{:S(2)}) collective-permute-start(bf16[96,768]{1,0:T(8,128)(2,1)S(1)} %get-tuple-element.153), channel_id=1, source_target_pairs={{0,24},{4,28},{8,0},{12,4},{16,8},{20,12},{24,16},{28,20},{1,25},{... | collective-permute-start | bytes 442376 | tf_op jit(solution)/shard_map/ppermute | solution.py:949
  121.3 1.6 input_grad.1
  123.8 4.3 %collective-permute-done.38.refs_2_ = bf16[96,768]{1,0:T(8,128)(2,1)S(1)} collective-permute-done((bf16[96,768]{1,0:T(8,128)(2,1)S(1)}, bf16[96,768]{1,0:T(8,128)(2,1)S(1)}, u32[]{:S(2)}, u32[]{:S(2)}) %collective-permute-start.38) | collective-permute-done | bytes 147488 | tf_op jit(solution)/shard_map/ppermute | solution.py:949
  130.5 1.0 sum_two.1.refs_0_
  131.6 5.9 %all-to-all-start.1 = ((bf16[16,24,832]{2,1,0:T(8,128)(2,1)}), bf16[16,24,832]{2,1,0:T(8,128)(2,1)S(1)}, u32[]{:S(2)}, u32[]{:S(2)}) async-start(bf16[16,24,832]{2,1,0:T(8,128)(2,1)} %bitcast.5), calls=%async_computation.1 | async-start | bytes 1376256 | tf_op jit(solution)/shard_map/all_to_all | solution.py:580
  137.5 1.1 copy-done.3
  139.6 1.1 input_add.1
  140.7 2.0 %collective-permute-start.34 = (bf16[128,768]{1,0:T(8,128)(2,1)S(1)}, bf16[128,768]{1,0:T(8,128)(2,1)S(1)}, u32[]{:S(2)}, u32[]{:S(2)}) collective-permute-start(bf16[128,768]{1,0:T(8,128)(2,1)S(1)} %get-tuple-element.147), channel_id=1, source_target_pairs={{0,2},{1,3},{2,0},{3,1},{4,6},{5,7},{6,4},{7,5},{8,10},{9,11},{10,... | collective-permute-start | bytes 589832 | tf_op jit(solution)/shard_map/ppermute | solution.py:978
  144.3 5.1 %collective-permute-done.41.refs_1_ = bf16[96,768]{1,0:T(8,128)(2,1)S(1)} collective-permute-done((bf16[96,768]{1,0:T(8,128)(2,1)S(1)}, bf16[96,768]{1,0:T(8,128)(2,1)S(1)}, u32[]{:S(2)}, u32[]{:S(2)}) %collective-permute-start.41) | collective-permute-done | bytes 147488 | tf_op jit(solution)/shard_map/ppermute | solution.py:986
  150.0 1.4 collective-permute-start.44
  152.1 3.2 %collective-permute-done.43.refs_2_ = bf16[24,768]{1,0:T(8,128)(2,1)S(1)} collective-permute-done((bf16[24,768]{1,0:T(8,128)(2,1)S(1)}, bf16[24,768]{1,0:T(8,128)(2,1)S(1)}, u32[]{:S(2)}, u32[]{:S(2)}) %collective-permute-start.43) | collective-permute-done | bytes 36896 | tf_op jit(solution)/shard_map/ppermute | solution.py:992
  (109 shorter events, 25.6 us)
Async XLA Ops:
  3.2 21.3 %all-to-all-start = ((bf16[16,24,640]{2,1,0:T(8,128)(2,1)}), bf16[16,24,640]{2,1,0:T(8,128)(2,1)S(1)}, u32[]{:S(2)}, u32[]{:S(2)}) async-start(bf16[16,24,640]{2,1,0:T(8,128)(2,1)} %bitcast.16), calls=%async_computation | async-start | bytes 983040 | tf_op jit(solution)/shard_map/all_to_all | solution.py:580
  10.7 3.6 %collective-permute-start.3 = (bf16[24,1152]{1,0:T(8,128)(2,1)}, bf16[24,1152]{1,0:T(8,128)(2,1)S(1)}, u32[]{:S(2)}, u32[]{:S(2)}) collective-permute-start(bf16[24,1152]{1,0:T(8,128)(2,1)} %get-tuple-element.97), channel_id=1, source_target_pairs={{0,1},{1,0},{2,3},{3,2},{4,5},{5,4},{6,7},{7,6},{8,9},{9,8},{10,11... | collective-permute-start | bytes 165896 | tf_op jit(solution)/shard_map/ppermute | solution.py:677
  11.1 7.7 %collective-permute-start.4 = (bf16[24,1152]{1,0:T(8,128)(2,1)}, bf16[24,1152]{1,0:T(8,128)(2,1)S(1)}, u32[]{:S(2)}, u32[]{:S(2)}) collective-permute-start(bf16[24,1152]{1,0:T(8,128)(2,1)} %get-tuple-element.98), channel_id=1, source_target_pairs={{0,2},{1,3},{2,0},{3,1},{4,6},{5,7},{6,4},{7,5},{8,10},{9,11},{10,... | collective-permute-start | bytes 165896 | tf_op jit(solution)/shard_map/ppermute | solution.py:677
  12.8 6.2 %collective-permute-start.5 = (bf16[24,1152]{1,0:T(8,128)(2,1)}, bf16[24,1152]{1,0:T(8,128)(2,1)S(1)}, u32[]{:S(2)}, u32[]{:S(2)}) collective-permute-start(bf16[24,1152]{1,0:T(8,128)(2,1)} %get-tuple-element.99), channel_id=1, source_target_pairs={{0,3},{1,2},{2,1},{3,0},{4,7},{5,6},{6,5},{7,4},{8,11},{9,10},{10,... | collective-permute-start | bytes 165896 | tf_op jit(solution)/shard_map/ppermute | solution.py:677
  12.8 8.6 %collective-permute-start.13 = (bf16[96,768]{1,0:T(8,128)(2,1)}, bf16[96,768]{1,0:T(8,128)(2,1)S(1)}, u32[]{:S(2)}, u32[]{:S(2)}) collective-permute-start(bf16[96,768]{1,0:T(8,128)(2,1)} %bitcast.13), channel_id=1, source_target_pairs={{0,4},{4,0},{8,12},{12,8},{16,20},{20,16},{24,28},{28,24},{1,5},{5... | collective-permute-start | bytes 442376 | tf_op jit(solution)/shard_map/ppermute | solution.py:689
  19.9 8.1 %collective-permute-start.6 = (bf16[96,1152]{1,0:T(8,128)(2,1)S(1)}, bf16[96,1152]{1,0:T(8,128)(2,1)S(1)}, u32[]{:S(2)}, u32[]{:S(2)}) collective-permute-start(bf16[96,1152]{1,0:T(8,128)(2,1)S(1)} %bitcast.10), channel_id=1, source_target_pairs={{0,4},{4,0},{8,12},{12,8},{16,20},{20,16},{24,28},{28,24},{1,5},{5... | collective-permute-start | bytes 663560 | tf_op jit(solution)/shard_map/ppermute | solution.py:701
  21.5 27.8 %copy-start.6 = (bf16[128,768]{1,0:T(8,128)(2,1)S(1)}, bf16[128,768]{1,0:T(8,128)(2,1)}, u32[]{:S(2)}) copy-start(bf16[128,768]{1,0:T(8,128)(2,1)} %refs_3_.3) | copy-start | bytes 589828
  21.5 11.8 %collective-permute-start.14 = (bf16[2,96,768]{2,1,0:T(8,128)(2,1)S(1)}, bf16[2,96,768]{2,1,0:T(8,128)(2,1)S(1)}, u32[]{:S(2)}, u32[]{:S(2)}) collective-permute-start(bf16[2,96,768]{2,1,0:T(8,128)(2,1)S(1)} %pair.1.refs_0_), channel_id=1, source_target_pairs={{0,8},{4,12},{8,16},{12,20},{16,24},{20,28},{24,0},{28,4},{1,9},{5... | collective-permute-start | bytes 884744 | tf_op jit(solution)/shard_map/ppermute | solution.py:700
  28.0 22.1 %collective-permute-start.7 = (bf16[4,96,640]{2,1,0:T(8,128)(2,1)S(1)}, bf16[4,96,640]{2,1,0:T(8,128)(2,1)S(1)}, u32[]{:S(2)}, u32[]{:S(2)}) collective-permute-start(bf16[4,96,640]{2,1,0:T(8,128)(2,1)S(1)} %shard_map.306), channel_id=1, source_target_pairs={{0,4},{4,0},{8,12},{12,8},{16,20},{20,16},{24,28},{28,24},{1,5},{5... | collective-permute-start | bytes 1474568 | tf_op jit(solution)/shard_map/ppermute | solution.py:704
  29.5 9.1 %collective-permute-start.8 = (bf16[96,1152]{1,0:T(8,128)(2,1)S(1)}, bf16[96,1152]{1,0:T(8,128)(2,1)S(1)}, u32[]{:S(2)}, u32[]{:S(2)}) collective-permute-start(bf16[96,1152]{1,0:T(8,128)(2,1)S(1)} %bitcast.11), channel_id=1, source_target_pairs={{0,8},{4,12},{8,16},{12,20},{16,24},{20,28},{24,0},{28,4},{1,9},{5... | collective-permute-start | bytes 663560 | tf_op jit(solution)/shard_map/ppermute | solution.py:699
  30.7 7.8 %collective-permute-start = (bf16[128,768]{1,0:T(8,128)(2,1)S(1)}, bf16[128,768]{1,0:T(8,128)(2,1)S(1)}, u32[]{:S(2)}, u32[]{:S(2)}) collective-permute-start(bf16[128,768]{1,0:T(8,128)(2,1)S(1)} %copy-done.1), channel_id=1, source_target_pairs={{0,2},{1,3},{2,0},{3,1},{4,6},{5,7},{6,4},{7,5},{8,10},{9,11},{10,... | collective-permute-start | bytes 589832 | tf_op jit(solution)/shard_map/ppermute | solution.py:656
  33.2 17.8 %collective-permute-start.15 = (bf16[2,96,768]{2,1,0:T(8,128)(2,1)S(1)}, bf16[2,96,768]{2,1,0:T(8,128)(2,1)S(1)}, u32[]{:S(2)}, u32[]{:S(2)}) collective-permute-start(bf16[2,96,768]{2,1,0:T(8,128)(2,1)S(1)} %collective-permute-done.14.refs_1_), channel_id=1, source_target_pairs={{0,8},{4,12},{8,16},{12,20},{16,24},{20,28},{24,0},{28,4},{1,9},{5... | collective-permute-start | bytes 884744 | tf_op jit(solution)/shard_map/ppermute | solution.py:706
  38.5 10.8 %collective-permute-start.9 = (bf16[96,1152]{1,0:T(8,128)(2,1)S(1)}, bf16[96,1152]{1,0:T(8,128)(2,1)S(1)}, u32[]{:S(2)}, u32[]{:S(2)}) collective-permute-start(bf16[96,1152]{1,0:T(8,128)(2,1)S(1)} %collective-permute-done.8.refs_1_), channel_id=1, source_target_pairs={{0,8},{4,12},{8,16},{12,20},{16,24},{20,28},{24,0},{28,4},{1,9},{5... | collective-permute-start | bytes 663560 | tf_op jit(solution)/shard_map/ppermute | solution.py:705
  38.5 12.4 %collective-permute-start.1 = (bf16[128,768]{1,0:T(8,128)(2,1)S(1)}, bf16[128,768]{1,0:T(8,128)(2,1)S(1)}, u32[]{:S(2)}, u32[]{:S(2)}) collective-permute-start(bf16[128,768]{1,0:T(8,128)(2,1)S(1)} %copy-done.1), channel_id=1, source_target_pairs={{0,1},{1,0},{2,3},{3,2},{4,5},{5,4},{6,7},{7,6},{8,9},{9,8},{10,11... | collective-permute-start | bytes 589832 | tf_op jit(solution)/shard_map/ppermute | solution.py:657
  38.5 13.7 %collective-permute-start.2 = (bf16[128,768]{1,0:T(8,128)(2,1)S(1)}, bf16[128,768]{1,0:T(8,128)(2,1)S(1)}, u32[]{:S(2)}, u32[]{:S(2)}) collective-permute-start(bf16[128,768]{1,0:T(8,128)(2,1)S(1)} %collective-permute-done.refs_2_.refs_1_), channel_id=1, source_target_pairs={{0,1},{1,0},{2,3},{3,2},{4,5},{5,4},{6,7},{7,6},{8,9},{9,8},{10,11... | collective-permute-start | bytes 589832 | tf_op jit(solution)/shard_map/ppermute | solution.py:658
  49.3 8.0 %collective-permute-start.10 = (bf16[128,768]{1,0:T(8,128)(2,1)S(1)}, bf16[128,768]{1,0:T(8,128)(2,1)S(1)}, u32[]{:S(2)}, u32[]{:S(2)}) collective-permute-start(bf16[128,768]{1,0:T(8,128)(2,1)S(1)} %copy-done.6), channel_id=1, source_target_pairs={{0,2},{1,3},{2,0},{3,1},{4,6},{5,7},{6,4},{7,5},{8,10},{9,11},{10,... | collective-permute-start | bytes 589832 | tf_op jit(solution)/shard_map/ppermute | solution.py:661
  50.1 11.1 %collective-permute-start.20 = (bf16[96,1152]{1,0:T(8,128)(2,1)S(1)}, bf16[96,1152]{1,0:T(8,128)(2,1)S(1)}, u32[]{:S(2)}, u32[]{:S(2)}) collective-permute-start(bf16[96,1152]{1,0:T(8,128)(2,1)S(1)} %collective-permute-done.9.refs_2_), channel_id=1, source_target_pairs={{0,4},{4,0},{8,12},{12,8},{16,20},{20,16},{24,28},{28,24},{1,5},{5... | collective-permute-start | bytes 663560 | tf_op jit(solution)/shard_map/ppermute | solution.py:736
  51.0 10.2 %collective-permute-start.18 = (bf16[96,1152]{1,0:T(8,128)(2,1)S(1)}, bf16[96,1152]{1,0:T(8,128)(2,1)S(1)}, u32[]{:S(2)}, u32[]{:S(2)}) collective-permute-start(bf16[96,1152]{1,0:T(8,128)(2,1)S(1)} %collective-permute-done.9.refs_2_), channel_id=1, source_target_pairs={{0,8},{4,12},{8,16},{12,20},{16,24},{20,28},{24,0},{28,4},{1,9},{5... | collective-permute-start | bytes 663560 | tf_op jit(solution)/shard_map/ppermute | solution.py:738
  51.1 14.9 %collective-permute-start.16 = (bf16[2,96,768]{2,1,0:T(8,128)(2,1)S(1)}, bf16[2,96,768]{2,1,0:T(8,128)(2,1)S(1)}, u32[]{:S(2)}, u32[]{:S(2)}) collective-permute-start(bf16[2,96,768]{2,1,0:T(8,128)(2,1)S(1)} %collective-permute-done.15.refs_2_), channel_id=1, source_target_pairs={{0,8},{4,12},{8,16},{12,20},{16,24},{20,28},{24,0},{28,4},{1,9},{5... | collective-permute-start | bytes 884744 | tf_op jit(solution)/shard_map/ppermute | solution.py:741
  57.4 7.8 %collective-permute-start.11 = (bf16[512,192]{1,0:T(8,128)(2,1)S(1)}, bf16[512,192]{1,0:T(8,128)(2,1)S(1)}, u32[]{:S(2)}, u32[]{:S(2)}) collective-permute-start(bf16[512,192]{1,0:T(8,128)(2,1)S(1)} %shard_map.307), channel_id=1, source_target_pairs={{0,2},{1,3},{2,0},{3,1},{4,6},{5,7},{6,4},{7,5},{8,10},{9,11},{10,... | collective-permute-start | bytes 589832 | tf_op jit(solution)/shard_map/ppermute | solution.py:732
  58.5 8.2 %collective-permute-start.19 = (bf16[96,1152]{1,0:T(8,128)(2,1)S(1)}, bf16[96,1152]{1,0:T(8,128)(2,1)S(1)}, u32[]{:S(2)}, u32[]{:S(2)}) collective-permute-start(bf16[96,1152]{1,0:T(8,128)(2,1)S(1)} %collective-permute-done.8.refs_1_), channel_id=1, source_target_pairs={{0,4},{4,0},{8,12},{12,8},{16,20},{20,16},{24,28},{28,24},{1,5},{5... | collective-permute-start | bytes 663560 | tf_op jit(solution)/shard_map/ppermute | solution.py:735
  61.2 7.9 %collective-permute-start.21 = (bf16[96,1152]{1,0:T(8,128)(2,1)S(1)}, bf16[96,1152]{1,0:T(8,128)(2,1)S(1)}, u32[]{:S(2)}, u32[]{:S(2)}) collective-permute-start(bf16[96,1152]{1,0:T(8,128)(2,1)S(1)} %shard_map.309), channel_id=1, source_target_pairs={{0,4},{4,0},{8,12},{12,8},{16,20},{20,16},{24,28},{28,24},{1,5},{5... | collective-permute-start | bytes 663560 | tf_op jit(solution)/shard_map/ppermute | solution.py:740
  65.9 3.2 %collective-permute-start.17 = (bf16[512,192]{1,0:T(8,128)(2,1)S(1)}, bf16[512,192]{1,0:T(8,128)(2,1)S(1)}, u32[]{:S(2)}, u32[]{:S(2)}) collective-permute-start(bf16[512,192]{1,0:T(8,128)(2,1)S(1)} %shard_map.308), channel_id=1, source_target_pairs={{0,1},{1,0},{2,3},{3,2},{4,5},{5,4},{6,7},{7,6},{8,9},{9,8},{10,11... | collective-permute-start | bytes 589832 | tf_op jit(solution)/shard_map/ppermute | solution.py:742
  69.3 2.4 %collective-permute-start.22 = (bf16[768,384]{1,0:T(8,128)(2,1)S(1)}, bf16[768,384]{1,0:T(8,128)(2,1)S(1)}, u32[]{:S(2)}, u32[]{:S(2)}) collective-permute-start(bf16[768,384]{1,0:T(8,128)(2,1)S(1)} %get-tuple-element.104.refs_6_.refs_2_), channel_id=1, source_target_pairs={{0,1},{1,0},{2,3},{3,2},{4,5},{5,4},{6,7},{7,6},{8,9},{9,8},{10,11... | collective-permute-start | bytes 1769480 | tf_op jit(solution)/shard_map/ppermute | solution.py:762
  69.4 2.4 %collective-permute-start.12 = (bf16[512,192]{1,0:T(8,128)(2,1)S(1)}, bf16[512,192]{1,0:T(8,128)(2,1)S(1)}, u32[]{:S(2)}, u32[]{:S(2)}) collective-permute-start(bf16[512,192]{1,0:T(8,128)(2,1)S(1)} %get-tuple-element.102.refs_2_.refs_0_), channel_id=1, source_target_pairs={{0,1},{1,0},{2,3},{3,2},{4,5},{5,4},{6,7},{7,6},{8,9},{9,8},{10,11... | collective-permute-start | bytes 589832 | tf_op jit(solution)/shard_map/ppermute | solution.py:733
  73.6 2.1 %collective-permute-start.23 = (bf16[256,768]{1,0:T(8,128)(2,1)S(1)}, bf16[256,768]{1,0:T(8,128)(2,1)S(1)}, u32[]{:S(2)}, u32[]{:S(2)}) collective-permute-start(bf16[256,768]{1,0:T(8,128)(2,1)S(1)} %get-tuple-element.108), channel_id=1, source_target_pairs={{0,1},{1,0},{2,3},{3,2},{4,5},{5,4},{6,7},{7,6},{8,9},{9,8},{10,11... | collective-permute-start | bytes 1179656 | tf_op jit(solution)/shard_map/ppermute | solution.py:787
  75.9 11.5 %collective-permute-start.24 = (bf16[256,768]{1,0:T(8,128)(2,1)S(1)}, bf16[256,768]{1,0:T(8,128)(2,1)S(1)}, u32[]{:S(2)}, u32[]{:S(2)}) collective-permute-start(bf16[256,768]{1,0:T(8,128)(2,1)S(1)} %get-tuple-element.110), channel_id=1, source_target_pairs={{0,2},{1,3},{2,0},{3,1},{4,6},{5,7},{6,4},{7,5},{8,10},{9,11},{10,... | collective-permute-start | bytes 1179656 | tf_op jit(solution)/shard_map/ppermute | solution.py:791
  88.5 1.7 %collective-permute-start.25 = (bf16[256,768]{1,0:T(8,128)(2,1)S(1)}, bf16[256,768]{1,0:T(8,128)(2,1)S(1)}, u32[]{:S(2)}, u32[]{:S(2)}) collective-permute-start(bf16[256,768]{1,0:T(8,128)(2,1)S(1)} %get-tuple-element.113.refs_0_.refs_2_), channel_id=1, source_target_pairs={{0,1},{1,0},{2,3},{3,2},{4,5},{5,4},{6,7},{7,6},{8,9},{9,8},{10,11... | collective-permute-start | bytes 1179656 | tf_op jit(solution)/shard_map/ppermute | solution.py:812
  91.2 1.8 %collective-permute-start.26 = (bf16[256,768]{1,0:T(8,128)(2,1)S(1)}, bf16[256,768]{1,0:T(8,128)(2,1)S(1)}, u32[]{:S(2)}, u32[]{:S(2)}) collective-permute-start(bf16[256,768]{1,0:T(8,128)(2,1)S(1)} %get-tuple-element.117), channel_id=1, source_target_pairs={{0,1},{1,0},{2,3},{3,2},{4,5},{5,4},{6,7},{7,6},{8,9},{9,8},{10,11... | collective-permute-start | bytes 1179656 | tf_op jit(solution)/shard_map/ppermute | solution.py:787
  93.1 13.3 %collective-permute-start.27 = (bf16[256,768]{1,0:T(8,128)(2,1)S(1)}, bf16[256,768]{1,0:T(8,128)(2,1)S(1)}, u32[]{:S(2)}, u32[]{:S(2)}) collective-permute-start(bf16[256,768]{1,0:T(8,128)(2,1)S(1)} %get-tuple-element.119), channel_id=1, source_target_pairs={{0,2},{1,3},{2,0},{3,1},{4,6},{5,7},{6,4},{7,5},{8,10},{9,11},{10,... | collective-permute-start | bytes 1179656 | tf_op jit(solution)/shard_map/ppermute | solution.py:791
  95.7 10.6 %collective-permute-start.28 = (bf16[2,96,768]{2,1,0:T(8,128)(2,1)S(1)}, bf16[2,96,768]{2,1,0:T(8,128)(2,1)S(1)}, u32[]{:S(2)}, u32[]{:S(2)}) collective-permute-start(bf16[2,96,768]{2,1,0:T(8,128)(2,1)S(1)} %get-tuple-element.129.refs_4_), channel_id=1, source_target_pairs={{0,8},{4,12},{8,16},{12,20},{16,24},{20,28},{24,0},{28,4},{1,9},{5... | collective-permute-start | bytes 884744 | tf_op jit(solution)/shard_map/ppermute | solution.py:852
  97.1 17.0 %collective-permute-start.31 = (bf16[4,96,768]{2,1,0:T(8,128)(2,1)S(1)}, bf16[4,96,768]{2,1,0:T(8,128)(2,1)S(1)}, u32[]{:S(2)}, u32[]{:S(2)}) collective-permute-start(bf16[4,96,768]{2,1,0:T(8,128)(2,1)S(1)} %get-tuple-element.130.refs_6_), channel_id=1, source_target_pairs={{0,4},{4,0},{8,12},{12,8},{16,20},{20,16},{24,28},{28,24},{1,5},{5... | collective-permute-start | bytes 1769480 | tf_op jit(solution)/shard_map/ppermute | solution.py:865
  106.8 1.8 %collective-permute-start.29 = (bf16[256,768]{1,0:T(8,128)(2,1)S(1)}, bf16[256,768]{1,0:T(8,128)(2,1)S(1)}, u32[]{:S(2)}, u32[]{:S(2)}) collective-permute-start(bf16[256,768]{1,0:T(8,128)(2,1)S(1)} %get-tuple-element.131.refs_2_.refs_4_.refs_0_), channel_id=1, source_target_pairs={{0,1},{1,0},{2,3},{3,2},{4,5},{5,4},{6,7},{7,6},{8,9},{9,8},{10,11... | collective-permute-start | bytes 1179656 | tf_op jit(solution)/shard_map/ppermute | solution.py:883
  107.6 11.0 %collective-permute-start.30 = (bf16[2,96,768]{2,1,0:T(8,128)(2,1)S(1)}, bf16[2,96,768]{2,1,0:T(8,128)(2,1)S(1)}, u32[]{:S(2)}, u32[]{:S(2)}) collective-permute-start(bf16[2,96,768]{2,1,0:T(8,128)(2,1)S(1)} %z_step.2.refs_6_), channel_id=1, source_target_pairs={{0,8},{4,12},{8,16},{12,20},{16,24},{20,28},{24,0},{28,4},{1,9},{5... | collective-permute-start | bytes 884744 | tf_op jit(solution)/shard_map/ppermute | solution.py:893
  109.5 11.7 %collective-permute-start.32 = (bf16[4,96,192]{2,1,0:T(8,128)(2,1)S(1)}, bf16[4,96,192]{2,1,0:T(8,128)(2,1)S(1)}, u32[]{:S(2)}, u32[]{:S(2)}) collective-permute-start(bf16[4,96,192]{2,1,0:T(8,128)(2,1)S(1)} %get-tuple-element.135.refs_6_), channel_id=1, source_target_pairs={{0,4},{4,0},{8,12},{12,8},{16,20},{20,16},{24,28},{28,24},{1,5},{5... | collective-permute-start | bytes 442376 | tf_op jit(solution)/shard_map/ppermute | solution.py:946
  115.0 15.5 %collective-permute-start.35 = (bf16[4,96,384]{2,1,0:T(8,128)(2,1)S(1)}, bf16[4,96,384]{2,1,0:T(8,128)(2,1)S(1)}, u32[]{:S(2)}, u32[]{:S(2)}) collective-permute-start(bf16[4,96,384]{2,1,0:T(8,128)(2,1)S(1)} %get-tuple-element.150), channel_id=1, source_target_pairs={{0,4},{4,0},{8,12},{12,8},{16,20},{20,16},{24,28},{28,24},{1,5},{5... | collective-permute-start | bytes 884744 | tf_op jit(solution)/shard_map/ppermute | solution.py:945
  115.7 14.9 %collective-permute-start.36 = (bf16[4,96,256]{2,1,0:T(8,128)(2,1)S(1)}, bf16[4,96,256]{2,1,0:T(8,128)(2,1)S(1)}, u32[]{:S(2)}, u32[]{:S(2)}) collective-permute-start(bf16[4,96,256]{2,1,0:T(8,128)(2,1)S(1)} %get-tuple-element.142.refs_2_), channel_id=1, source_target_pairs={{0,4},{4,0},{8,12},{12,8},{16,20},{20,16},{24,28},{28,24},{1,5},{5... | collective-permute-start | bytes 589832 | tf_op jit(solution)/shard_map/ppermute | solution.py:945
  117.1 11.0 %collective-permute-start.38 = (bf16[96,768]{1,0:T(8,128)(2,1)S(1)}, bf16[96,768]{1,0:T(8,128)(2,1)S(1)}, u32[]{:S(2)}, u32[]{:S(2)}) collective-permute-start(bf16[96,768]{1,0:T(8,128)(2,1)S(1)} %get-tuple-element.152), channel_id=1, source_target_pairs={{0,16},{4,20},{8,24},{12,28},{16,0},{20,4},{24,8},{28,12},{1,17},{... | collective-permute-start | bytes 442376 | tf_op jit(solution)/shard_map/ppermute | solution.py:949
  118.5 10.5 %collective-permute-start.39 = (bf16[96,768]{1,0:T(8,128)(2,1)S(1)}, bf16[96,768]{1,0:T(8,128)(2,1)S(1)}, u32[]{:S(2)}, u32[]{:S(2)}) collective-permute-start(bf16[96,768]{1,0:T(8,128)(2,1)S(1)} %get-tuple-element.153), channel_id=1, source_target_pairs={{0,24},{4,28},{8,0},{12,4},{16,8},{20,12},{24,16},{28,20},{1,25},{... | collective-permute-start | bytes 442376 | tf_op jit(solution)/shard_map/ppermute | solution.py:949
  121.3 8.5 %collective-permute-start.37 = (bf16[96,768]{1,0:T(8,128)(2,1)S(1)}, bf16[96,768]{1,0:T(8,128)(2,1)S(1)}, u32[]{:S(2)}, u32[]{:S(2)}) collective-permute-start(bf16[96,768]{1,0:T(8,128)(2,1)S(1)} %get-tuple-element.141.refs_9_), channel_id=1, source_target_pairs={{0,8},{4,12},{8,16},{12,20},{16,24},{20,28},{24,0},{28,4},{1,9},{5... | collective-permute-start | bytes 442376 | tf_op jit(solution)/shard_map/ppermute | solution.py:949
  128.1 14.6 %collective-permute-start.40 = (bf16[2,96,768]{2,1,0:T(8,128)(2,1)S(1)}, bf16[2,96,768]{2,1,0:T(8,128)(2,1)}, u32[]{:S(2)}, u32[]{:S(2)}) collective-permute-start(bf16[2,96,768]{2,1,0:T(8,128)(2,1)S(1)} %z_step.3.refs_2_), channel_id=1, source_target_pairs={{0,8},{4,12},{8,16},{12,20},{16,24},{20,28},{24,0},{28,4},{1,9},{5... | collective-permute-start | bytes 884744 | tf_op jit(solution)/shard_map/ppermute | solution.py:893
  129.0 8.5 %collective-permute-start.33 = (bf16[256,768]{1,0:T(8,128)(2,1)}, bf16[256,768]{1,0:T(8,128)(2,1)}, u32[]{:S(2)}, u32[]{:S(2)}) collective-permute-start(bf16[256,768]{1,0:T(8,128)(2,1)} %get-tuple-element.144), channel_id=1, source_target_pairs={{0,1},{1,0},{2,3},{3,2},{4,5},{5,4},{6,7},{7,6},{8,9},{9,8},{10,11... | collective-permute-start | bytes 1179656 | tf_op jit(solution)/shard_map/ppermute | solution.py:960
  131.6 25.7 %all-to-all-start.1 = ((bf16[16,24,832]{2,1,0:T(8,128)(2,1)}), bf16[16,24,832]{2,1,0:T(8,128)(2,1)S(1)}, u32[]{:S(2)}, u32[]{:S(2)}) async-start(bf16[16,24,832]{2,1,0:T(8,128)(2,1)} %bitcast.5), calls=%async_computation.1 | async-start | bytes 1376256 | tf_op jit(solution)/shard_map/all_to_all | solution.py:580
  140.7 10.7 %collective-permute-start.34 = (bf16[128,768]{1,0:T(8,128)(2,1)S(1)}, bf16[128,768]{1,0:T(8,128)(2,1)S(1)}, u32[]{:S(2)}, u32[]{:S(2)}) collective-permute-start(bf16[128,768]{1,0:T(8,128)(2,1)S(1)} %get-tuple-element.147), channel_id=1, source_target_pairs={{0,2},{1,3},{2,0},{3,1},{4,6},{5,7},{6,4},{7,5},{8,10},{9,11},{10,... | collective-permute-start | bytes 589832 | tf_op jit(solution)/shard_map/ppermute | solution.py:978
  143.7 5.7 %collective-permute-start.41 = (bf16[96,768]{1,0:T(8,128)(2,1)S(1)}, bf16[96,768]{1,0:T(8,128)(2,1)S(1)}, u32[]{:S(2)}, u32[]{:S(2)}) collective-permute-start(bf16[96,768]{1,0:T(8,128)(2,1)S(1)} %get-tuple-element.164), channel_id=1, source_target_pairs={{0,4},{4,0},{8,12},{12,8},{16,20},{20,16},{24,28},{28,24},{1,5},{5... | collective-permute-start | bytes 442376 | tf_op jit(solution)/shard_map/ppermute | solution.py:986
  149.4 2.7 %collective-permute-start.42 = (bf16[24,768]{1,0:T(8,128)(2,1)S(1)}, bf16[24,768]{1,0:T(8,128)(2,1)S(1)}, u32[]{:S(2)}, u32[]{:S(2)}) collective-permute-start(bf16[24,768]{1,0:T(8,128)(2,1)S(1)} %get-tuple-element.166), channel_id=1, source_target_pairs={{0,1},{1,0},{2,3},{3,2},{4,5},{5,4},{6,7},{7,6},{8,9},{9,8},{10,11... | collective-permute-start | bytes 110600 | tf_op jit(solution)/shard_map/ppermute | solution.py:992
  149.5 5.8 %collective-permute-start.43 = (bf16[24,768]{1,0:T(8,128)(2,1)S(1)}, bf16[24,768]{1,0:T(8,128)(2,1)S(1)}, u32[]{:S(2)}, u32[]{:S(2)}) collective-permute-start(bf16[24,768]{1,0:T(8,128)(2,1)S(1)} %get-tuple-element.167), channel_id=1, source_target_pairs={{0,2},{1,3},{2,0},{3,1},{4,6},{5,7},{6,4},{7,5},{8,10},{9,11},{10,... | collective-permute-start | bytes 110600 | tf_op jit(solution)/shard_map/ppermute | solution.py:992
  150.0 5.5 %collective-permute-start.44 = (bf16[24,768]{1,0:T(8,128)(2,1)S(1)}, bf16[24,768]{1,0:T(8,128)(2,1)S(1)}, u32[]{:S(2)}, u32[]{:S(2)}) collective-permute-start(bf16[24,768]{1,0:T(8,128)(2,1)S(1)} %get-tuple-element.168), channel_id=1, source_target_pairs={{0,3},{1,2},{2,1},{3,0},{4,7},{5,6},{6,5},{7,4},{8,11},{9,10},{10,... | collective-permute-start | bytes 110600 | tf_op jit(solution)/shard_map/ppermute | solution.py:992
  (10 other events, 61.8 us)

commit v6 on v5

--- a/solution.py
+++ b/solution.py
@@ -107,7 +107,7 @@
 B2FIRST = 0
 B3CTX = 0
 HOLDB3 = 1
-UP1CTX = 1
+UP1CTX = 0
 AFTERY = 0
 DOWNFIRST = 0
 ROWSLATE = 1
@@ -115,6 +115,8 @@
 HOLDUP = 0
 INHEADS = 0
 INFIN = 1
+ZSUMFIRST = 1
+COREFIRST = 0
 OEARLY = 1
 OSTEP = 1
 ZLATE = 0
@@ -739,7 +741,7 @@
         hold = ((ctx_chip,) if X3CHIP else ()) + ((swapped[2],) if XW1 else ())
         swapped.append(lax.ppermute(later(have[3], *hold) if hold else have[3], "dp", XSWAP))
         pairs.append(lax.ppermute(later(pairs[2], ctx) if B3CTX else pairs[2], "dp", zshift(1)))
-        ctx_far = lax.ppermute(later(ctx_chip, pairs[3]) if HOLDB3 else ctx_chip, "head", CORE)
+        ctx_far = lax.ppermute(later(ctx_chip, pairs[3], *((ctx_core,) if COREFIRST else ())) if HOLDB3 else ctx_chip, "head", CORE)
         down_full = call(
             join_pairs_kernel,
             shape((width, width), BF),
@@ -973,6 +975,7 @@
         part,
         got,
         d_first,
+        after=(up_cross,) if ZSUMFIRST and cube else (),
         micros=0.4,
     )
     far = lax.ppermute(sent, "head", CHIP)

time: 159 us -> 156 us (0.981)
  local copies, waits for them, and re-layouts: 5.52 us -> 3.39 us
  starting transfers between devices: 49.8 us -> 48.2 us
    ppermute x3, waiting for transfers between devices: 3.39 us -> 0.35 us  [body(): lax.ppermute(up_pieces[flip], 'head', [(i, i ^ flip) for i in range(4)])]
    ppermute x1, waiting for transfers between devices: 0.01 us -> 2.32 us  [body(): up1 = lax.ppermute(upstream, 'head', CHIP)]
    unnamed x26 -> x25, local copies, waits for them, and re-layouts: 5.52 us -> 3.39 us
    ppermute x2, starting transfers between devices: 3.4 us -> 1.44 us  [pair_sum(): return (kept, lax.ppermute(low, 'head', CHIP))]
  transfers between devices with their start and end apart: 47 -> 47, of which waited for: 23 -> 24; matrix products, arithmetic and copies ran while one was open for 0% -> 0% of each run, Pallas kernels for 14% -> 15%
where the time goes in v6:
time: 156 us; the launch traced here: 155 us
  waiting for transfers between devices  72 us (46%)
  starting transfers between devices  48.2 us (31%)
  Pallas kernels  30.3 us (19%)
  local copies, waits for them, and re-layouts  3.39 us (2%)
    pallas_call x31, Pallas kernels, call(): pl.pallas_call(run, out_shape=outs, in_specs=[spec] * count + [pl.BlockSp...  27.7 us
    all_to_all x2, starting transfers between devices, to_owners(): lax.all_to_all(summed.reshape(16 * rows, columns), ALL, 0, 0, tiled=True,...  14 us
    ppermute x2, waiting for transfers between devices, pair_sum(): return (kept, lax.ppermute(low, 'head', CHIP))  10.7 us
    ppermute x1, waiting for transfers between devices, body(): have.append(lax.ppermute(have[1], 'dp', zshift(1)))  10.3 us
    ppermute x1, waiting for transfers between devices, body(): up_got = [lax.ppermute(up_run, 'dp', zshift(1))]  7.88 us
    ppermute x1, waiting for transfers between devices, body(): have = [wide, lax.ppermute(wide, 'dp', zshift(1))]  5.3 us
    ppermute x3, starting transfers between devices, body(): lax.ppermute(later(o, *order) if ZLATE == k else o, 'dp', zshift(k))  4.99 us
    ppermute x1, waiting for transfers between devices, body(): lax.ppermute(up_cross, 'dp', XSWAP)  4.86 us
  transfers between devices with their start and end apart: 47, of which 24 were waited for; matrix products, arithmetic and copies ran while one was open for 0% of the time, Pallas kernels for 15%

profile of v6, /device:TPU:0, one launch (start us, length us, event | category | flops | bytes accessed | tf_op | source)
XLA Modules:
  0.0 155.1 jit_solution(15143252048482434606)
XLA Ops:
  0.7 2.5 %shard_map.305 = (bf16[4,4,24,640]{3,2,1,0:T(8,128)(2,1)}, bf16[24,1152]{1,0:T(8,128)(2,1)}, bf16[24,1152]{1,0:T(8,128)(2,1)}, bf16[24,1152]{1,0:T(8,128)(2,1)},...) custom-call(f32[24,768]{1,0:T(8,128)} %query.1, f32[24,768]{1,0:T(8,128)} %key.1, f32[24,768]{1,0:T(8,128)} %value.1, ...), custom_call_target="tpu_custom_call" | custom-call | tf_op jit(solution)/shard_map/pallas_call | solution.py:197
  3.2 7.5 %all-to-all-start = ((bf16[16,24,640]{2,1,0:T(8,128)(2,1)}), bf16[16,24,640]{2,1,0:T(8,128)(2,1)S(1)}, u32[]{:S(2)}, u32[]{:S(2)}) async-start(bf16[16,24,640]{2,1,0:T(8,128)(2,1)} %bitcast.16), calls=%async_computation | async-start | bytes 983040 | tf_op jit(solution)/shard_map/all_to_all | solution.py:582
  11.1 1.7 %collective-permute-start.4 = (bf16[24,1152]{1,0:T(8,128)(2,1)}, bf16[24,1152]{1,0:T(8,128)(2,1)S(1)}, u32[]{:S(2)}, u32[]{:S(2)}) collective-permute-start(bf16[24,1152]{1,0:T(8,128)(2,1)} %get-tuple-element.98), channel_id=1, source_target_pairs={{0,2},{1,3},{2,0},{3,1},{4,6},{5,7},{6,4},{7,5},{8,10},{9,11},{10,... | collective-permute-start | bytes 165896 | tf_op jit(solution)/shard_map/ppermute | solution.py:679
  12.8 1.5 collective-permute-start.12
  14.3 4.5 %collective-permute-done.4.refs_2_ = bf16[24,1152]{1,0:T(8,128)(2,1)S(1)} collective-permute-done((bf16[24,1152]{1,0:T(8,128)(2,1)}, bf16[24,1152]{1,0:T(8,128)(2,1)S(1)}, u32[]{:S(2)}, u32[]{:S(2)}) %collective-permute-start.4) | collective-permute-done | bytes 55328 | tf_op jit(solution)/shard_map/ppermute | solution.py:679
  19.9 1.6 %collective-permute-start.6 = (bf16[96,1152]{1,0:T(8,128)(2,1)S(1)}, bf16[96,1152]{1,0:T(8,128)(2,1)S(1)}, u32[]{:S(2)}, u32[]{:S(2)}) collective-permute-start(bf16[96,1152]{1,0:T(8,128)(2,1)S(1)} %bitcast.10), channel_id=1, source_target_pairs={{0,4},{4,0},{8,12},{12,8},{16,20},{20,16},{24,28},{28,24},{1,5},{5... | collective-permute-start | bytes 663560 | tf_op jit(solution)/shard_map/ppermute | solution.py:703
  21.5 1.4 collective-permute-start.13
  22.9 1.6 %all-to-all-done = bf16[16,24,640]{2,1,0:T(8,128)(2,1)S(1)} async-done(((bf16[16,24,640]{2,1,0:T(8,128)(2,1)}), bf16[16,24,640]{2,1,0:T(8,128)(2,1)S(1)}, u32[]{:S(2)}, u32[]{:S(2)}) %all-to-all-start) | async-done | bytes 491552 | tf_op jit(solution)/shard_map/all_to_all | solution.py:582
  24.6 3.4 %collective-permute-done.6.refs_1_.refs_4_ = bf16[96,1152]{1,0:T(8,128)(2,1)S(1)} collective-permute-done((bf16[96,1152]{1,0:T(8,128)(2,1)S(1)}, bf16[96,1152]{1,0:T(8,128)(2,1)S(1)}, u32[]{:S(2)}, u32[]{:S(2)}) %collective-permute-start.6) | collective-permute-done | bytes 221216 | tf_op jit(solution)/shard_map/ppermute | solution.py:703
  28.0 1.5 collective-permute-start.7
  29.5 1.3 collective-permute-start.8
  30.8 2.5 %collective-permute-done.13.refs_1_ = bf16[2,96,768]{2,1,0:T(8,128)(2,1)S(1)} collective-permute-done((bf16[2,96,768]{2,1,0:T(8,128)(2,1)S(1)}, bf16[2,96,768]{2,1,0:T(8,128)(2,1)S(1)}, u32[]{:S(2)}, u32[]{:S(2)}) %collective-permute-start.13) | collective-permute-done | bytes 294944 | tf_op jit(solution)/shard_map/ppermute | solution.py:702
  33.2 5.3 %collective-permute-done.8.refs_1_ = bf16[96,1152]{1,0:T(8,128)(2,1)S(1)} collective-permute-done((bf16[96,1152]{1,0:T(8,128)(2,1)S(1)}, bf16[96,1152]{1,0:T(8,128)(2,1)S(1)}, u32[]{:S(2)}, u32[]{:S(2)}) %collective-permute-start.8) | collective-permute-done | bytes 221216 | tf_op jit(solution)/shard_map/ppermute | solution.py:701
  39.1 10.3 %collective-permute-done.9.refs_2_ = bf16[96,1152]{1,0:T(8,128)(2,1)S(1)} collective-permute-done((bf16[96,1152]{1,0:T(8,128)(2,1)S(1)}, bf16[96,1152]{1,0:T(8,128)(2,1)S(1)}, u32[]{:S(2)}, u32[]{:S(2)}) %collective-permute-start.9) | collective-permute-done | bytes 221216 | tf_op jit(solution)/shard_map/ppermute | solution.py:707
  50.0 1.0 collective-permute-start.15
  51.3 5.1 %attend.1 = (bf16[512,576]{1,0:T(8,128)(2,1)S(1)}, f32[3,512,512]{2,1,0:T(8,128)S(1)}, bf16[512,192]{1,0:T(8,128)(2,1)S(1)}, f32[16,768]{1,0:T(8,128)S(1)}) custom-call(s32[4,128]{1,0:T(4,128)S(1)} %bitcast.15, bf16[128,768]{1,0:T(8,128)(2,1)S(1)} %copy-done.1, bf16[128,768]{1,0:T(8,128)(2,1)S(1)} %collective-permute-done.refs_2_.refs_1_, ...), custom_call_target="tpu_custom_call" | custom-call | flops 1500000000 | bytes 4500000 | tf_op jit(solution)/shard_map/attend/pallas_call | solution.py:41
  56.3 1.0 collective-permute-start.10
  57.3 1.5 collective-permute-start.18
  58.9 1.3 collective-permute-done.17.refs_3_
  60.2 1.5 collective-permute-start.20
  62.3 3.1 %collective-permute-done.10.refs_3_.refs_1_ = bf16[512,192]{1,0:T(8,128)(2,1)S(1)} collective-permute-done((bf16[512,192]{1,0:T(8,128)(2,1)S(1)}, bf16[512,192]{1,0:T(8,128)(2,1)S(1)}, u32[]{:S(2)}, u32[]{:S(2)}) %collective-permute-start.10) | collective-permute-done | bytes 196640 | tf_op jit(solution)/shard_map/ppermute | solution.py:734
  65.5 2.3 %collective-permute-done.21.refs_9_.refs_4_ = bf16[128,768]{1,0:T(8,128)(2,1)S(1)} collective-permute-done((bf16[128,768]{1,0:T(8,128)(2,1)S(1)}, bf16[128,768]{1,0:T(8,128)(2,1)S(1)}, u32[]{:S(2)}, u32[]{:S(2)}) %collective-permute-start.21) | collective-permute-done | bytes 196640 | tf_op jit(solution)/shard_map/ppermute | solution.py:663
  67.8 1.1 collective-permute-done.20.refs_7_
  69.8 1.8 %collective-permute-done.11.refs_4_.refs_2_ = bf16[512,192]{1,0:T(8,128)(2,1)S(1)} collective-permute-done((bf16[512,192]{1,0:T(8,128)(2,1)S(1)}, bf16[512,192]{1,0:T(8,128)(2,1)S(1)}, u32[]{:S(2)}, u32[]{:S(2)}) %collective-permute-start.11) | collective-permute-done | bytes 196640 | tf_op jit(solution)/shard_map/ppermute | solution.py:735
  71.5 1.9 %ffn.3 = (bf16[256,768]{1,0:T(8,128)(2,1)S(1)}, bf16[256,768]{1,0:T(8,128)(2,1)S(1)}, f32[256,768]{1,0:T(8,128)S(1)}, bf16[256,768]{1,0:T(8,128)(2,1)S(1)}) custom-call(bf16[128,768]{1,0:T(8,128)(2,1)S(1)} %collective-permute-done.1.refs_3_.refs_0_.refs_2_, bf16[128,768]{1,0:T(8,128)(2,1)S(1)} %collective-permute-done.2.refs_4_.refs_1_.refs_3_, ...), custom_call_target="tpu_custom_call" | custom-call | flops 570000000 | bytes 1709999 | tf_op jit(solution)/shard_map/ffn/pallas_call | solution.py:41
  73.6 1.9 %ffn.2 = (bf16[256,768]{1,0:T(8,128)(2,1)S(1)}, bf16[256,768]{1,0:T(8,128)(2,1)S(1)}, f32[256,768]{1,0:T(8,128)S(1)}, f32[256,768]{1,0:T(8,128)S(1)}, f32[256,76...) custom-call(bf16[128,768]{1,0:T(8,128)(2,1)S(1)} %copy-done.1, ...), custom_call_target="tpu_custom_call" | custom-call | flops 570000000 | bytes 1709999 | tf_op jit(solution)/shard_map/ffn/pallas_call | solution.py:41
  76.4 10.7 %collective-permute-done.24.refs_1_ = bf16[256,768]{1,0:T(8,128)(2,1)S(1)} collective-permute-done((bf16[256,768]{1,0:T(8,128)(2,1)S(1)}, bf16[256,768]{1,0:T(8,128)(2,1)S(1)}, u32[]{:S(2)}, u32[]{:S(2)}) %collective-permute-start.24) | collective-permute-done | bytes 393248 | tf_op jit(solution)/shard_map/ppermute | solution.py:793
  87.1 1.2 final.1
  88.3 1.7 %collective-permute-done.25.refs_0_.refs_3_ = bf16[256,768]{1,0:T(8,128)(2,1)S(1)} collective-permute-done((bf16[256,768]{1,0:T(8,128)(2,1)S(1)}, bf16[256,768]{1,0:T(8,128)(2,1)S(1)}, u32[]{:S(2)}, u32[]{:S(2)}) %collective-permute-start.25) | collective-permute-done | bytes 393248 | tf_op jit(solution)/shard_map/ppermute | solution.py:814
  93.6 0.9 z_grad.1
  95.7 1.6 %collective-permute-start.31 = (bf16[4,96,768]{2,1,0:T(8,128)(2,1)S(1)}, bf16[4,96,768]{2,1,0:T(8,128)(2,1)S(1)}, u32[]{:S(2)}, u32[]{:S(2)}) collective-permute-start(bf16[4,96,768]{2,1,0:T(8,128)(2,1)S(1)} %get-tuple-element.130.refs_6_), channel_id=1, source_target_pairs={{0,4},{4,0},{8,12},{12,8},{16,20},{20,16},{24,28},{28,24},{1,5},{5... | collective-permute-start | bytes 1769480 | tf_op jit(solution)/shard_map/ppermute | solution.py:867
  97.3 7.9 %collective-permute-done.28.refs_7_.refs_1_ = bf16[2,96,768]{2,1,0:T(8,128)(2,1)S(1)} collective-permute-done((bf16[2,96,768]{2,1,0:T(8,128)(2,1)S(1)}, bf16[2,96,768]{2,1,0:T(8,128)(2,1)S(1)}, u32[]{:S(2)}, u32[]{:S(2)}) %collective-permute-start.28) | collective-permute-done | bytes 294944 | tf_op jit(solution)/shard_map/ppermute | solution.py:854
  106.4 1.0 collective-permute-done.29.refs_5_.refs_1_
  108.3 1.5 collective-permute-start.32
  109.9 3.0 %attend_back.1.refs_2_.refs_4_.refs_0_ = bf16[512,576]{1,0:T(8,128)(2,1)S(1)} custom-call(bf16[256,768]{1,0:T(8,128)(2,1)S(1)} %get-tuple-element.131.refs_2_.refs_4_.refs_0_, bf16[256,768]{1,0:T(8,128)(2,1)S(1)} %collective-permute-done.29.refs_5_.refs_1_, bf16[768,384]{1,0:T(8,128)(2,1)S(1)} %get-tuple-element.104.refs_6_.refs_2_, ...), custom_call_target="tpu_custom_call" | custom-call | flops 900000000 | bytes 2699999 | tf_op jit(solution)/shard_map/attend_back/pallas_call | solution.py:41
  114.5 1.5 collective-permute-start.37
  116.0 2.2 %collective-permute-start.39 = (bf16[96,768]{1,0:T(8,128)(2,1)S(1)}, bf16[96,768]{1,0:T(8,128)(2,1)S(1)}, u32[]{:S(2)}, u32[]{:S(2)}) collective-permute-start(bf16[96,768]{1,0:T(8,128)(2,1)S(1)} %get-tuple-element.153), channel_id=1, source_target_pairs={{0,16},{4,20},{8,24},{12,28},{16,0},{20,4},{24,8},{28,12},{1,17},{... | collective-permute-start | bytes 442376 | tf_op jit(solution)/shard_map/ppermute | solution.py:951
  118.1 2.8 %collective-permute-start.40 = (bf16[96,768]{1,0:T(8,128)(2,1)S(1)}, bf16[96,768]{1,0:T(8,128)(2,1)S(1)}, u32[]{:S(2)}, u32[]{:S(2)}) collective-permute-start(bf16[96,768]{1,0:T(8,128)(2,1)S(1)} %get-tuple-element.154), channel_id=1, source_target_pairs={{0,24},{4,28},{8,0},{12,4},{16,8},{20,12},{24,16},{28,20},{1,25},{... | collective-permute-start | bytes 442376 | tf_op jit(solution)/shard_map/ppermute | solution.py:951
  121.0 1.6 %input_grad.1 = (f32[256,768]{1,0:T(8,128)S(1)}, bf16[256,768]{1,0:T(8,128)(2,1)}) custom-call(bf16[512,576]{1,0:T(8,128)(2,1)S(1)} %attend_back.1.refs_2_.refs_4_.refs_0_, bf16[768,576]{1,0:T(8,128)(2,1)S(1)} %get-tuple-element.100.refs_5_.refs_1_, bf16[2,96,768]{2,1,0:T(8,128)(2,1)S(1)} %z_step.3.refs_2_), custom_call_target="tpu_custom_call" | custom-call | flops 240000000 | bytes 720000 | tf_op jit(solution)/shard_map/input_grad/pallas_call | solution.py:41
  123.5 3.4 %collective-permute-done.39.refs_2_ = bf16[96,768]{1,0:T(8,128)(2,1)S(1)} collective-permute-done((bf16[96,768]{1,0:T(8,128)(2,1)S(1)}, bf16[96,768]{1,0:T(8,128)(2,1)S(1)}, u32[]{:S(2)}, u32[]{:S(2)}) %collective-permute-start.39) | collective-permute-done | bytes 147488 | tf_op jit(solution)/shard_map/ppermute | solution.py:951
  129.4 1.0 sum_two.1.refs_0_
  130.4 6.5 %all-to-all-start.1 = ((bf16[16,24,832]{2,1,0:T(8,128)(2,1)}), bf16[16,24,832]{2,1,0:T(8,128)(2,1)S(1)}, u32[]{:S(2)}, u32[]{:S(2)}) async-start(bf16[16,24,832]{2,1,0:T(8,128)(2,1)} %bitcast.5), calls=%async_computation.1 | async-start | bytes 1376256 | tf_op jit(solution)/shard_map/all_to_all | solution.py:582
  137.9 1.0 z_sum.1
  138.9 1.1 input_add.1
  140.0 1.4 collective-permute-start.35
  142.1 4.9 %collective-permute-done.41.refs_1_ = bf16[96,768]{1,0:T(8,128)(2,1)S(1)} collective-permute-done((bf16[96,768]{1,0:T(8,128)(2,1)S(1)}, bf16[96,768]{1,0:T(8,128)(2,1)S(1)}, u32[]{:S(2)}, u32[]{:S(2)}) %collective-permute-start.41) | collective-permute-done | bytes 147488 | tf_op jit(solution)/shard_map/ppermute | solution.py:989
  147.5 1.4 collective-permute-start.44
  148.9 1.4 collective-permute-done.35.refs_1_
  (107 shorter events, 24.2 us)
Async XLA Ops:
  3.2 21.3 %all-to-all-start = ((bf16[16,24,640]{2,1,0:T(8,128)(2,1)}), bf16[16,24,640]{2,1,0:T(8,128)(2,1)S(1)}, u32[]{:S(2)}, u32[]{:S(2)}) async-start(bf16[16,24,640]{2,1,0:T(8,128)(2,1)} %bitcast.16), calls=%async_computation | async-start | bytes 983040 | tf_op jit(solution)/shard_map/all_to_all | solution.py:582
  10.7 3.6 %collective-permute-start.3 = (bf16[24,1152]{1,0:T(8,128)(2,1)}, bf16[24,1152]{1,0:T(8,128)(2,1)S(1)}, u32[]{:S(2)}, u32[]{:S(2)}) collective-permute-start(bf16[24,1152]{1,0:T(8,128)(2,1)} %get-tuple-element.97), channel_id=1, source_target_pairs={{0,1},{1,0},{2,3},{3,2},{4,5},{5,4},{6,7},{7,6},{8,9},{9,8},{10,11... | collective-permute-start | bytes 165896 | tf_op jit(solution)/shard_map/ppermute | solution.py:679
  11.1 7.7 %collective-permute-start.4 = (bf16[24,1152]{1,0:T(8,128)(2,1)}, bf16[24,1152]{1,0:T(8,128)(2,1)S(1)}, u32[]{:S(2)}, u32[]{:S(2)}) collective-permute-start(bf16[24,1152]{1,0:T(8,128)(2,1)} %get-tuple-element.98), channel_id=1, source_target_pairs={{0,2},{1,3},{2,0},{3,1},{4,6},{5,7},{6,4},{7,5},{8,10},{9,11},{10,... | collective-permute-start | bytes 165896 | tf_op jit(solution)/shard_map/ppermute | solution.py:679
  12.8 6.2 %collective-permute-start.5 = (bf16[24,1152]{1,0:T(8,128)(2,1)}, bf16[24,1152]{1,0:T(8,128)(2,1)S(1)}, u32[]{:S(2)}, u32[]{:S(2)}) collective-permute-start(bf16[24,1152]{1,0:T(8,128)(2,1)} %get-tuple-element.99), channel_id=1, source_target_pairs={{0,3},{1,2},{2,1},{3,0},{4,7},{5,6},{6,5},{7,4},{8,11},{9,10},{10,... | collective-permute-start | bytes 165896 | tf_op jit(solution)/shard_map/ppermute | solution.py:679
  12.8 8.6 %collective-permute-start.12 = (bf16[96,768]{1,0:T(8,128)(2,1)}, bf16[96,768]{1,0:T(8,128)(2,1)S(1)}, u32[]{:S(2)}, u32[]{:S(2)}) collective-permute-start(bf16[96,768]{1,0:T(8,128)(2,1)} %bitcast.13), channel_id=1, source_target_pairs={{0,4},{4,0},{8,12},{12,8},{16,20},{20,16},{24,28},{28,24},{1,5},{5... | collective-permute-start | bytes 442376 | tf_op jit(solution)/shard_map/ppermute | solution.py:691
  19.9 8.1 %collective-permute-start.6 = (bf16[96,1152]{1,0:T(8,128)(2,1)S(1)}, bf16[96,1152]{1,0:T(8,128)(2,1)S(1)}, u32[]{:S(2)}, u32[]{:S(2)}) collective-permute-start(bf16[96,1152]{1,0:T(8,128)(2,1)S(1)} %bitcast.10), channel_id=1, source_target_pairs={{0,4},{4,0},{8,12},{12,8},{16,20},{20,16},{24,28},{28,24},{1,5},{5... | collective-permute-start | bytes 663560 | tf_op jit(solution)/shard_map/ppermute | solution.py:703
  21.5 11.8 %collective-permute-start.13 = (bf16[2,96,768]{2,1,0:T(8,128)(2,1)S(1)}, bf16[2,96,768]{2,1,0:T(8,128)(2,1)S(1)}, u32[]{:S(2)}, u32[]{:S(2)}) collective-permute-start(bf16[2,96,768]{2,1,0:T(8,128)(2,1)S(1)} %pair.1.refs_0_), channel_id=1, source_target_pairs={{0,8},{4,12},{8,16},{12,20},{16,24},{20,28},{24,0},{28,4},{1,9},{5... | collective-permute-start | bytes 884744 | tf_op jit(solution)/shard_map/ppermute | solution.py:702
  24.6 26.7 %copy-start.10 = (s32[512]{0:T(512)S(1)}, s32[512]{0:T(512)}, u32[]{:S(2)}) copy-start(s32[512]{0:T(512)} %param.19) | copy-start | bytes 6148
  28.0 22.0 %collective-permute-start.7 = (bf16[4,96,640]{2,1,0:T(8,128)(2,1)S(1)}, bf16[4,96,640]{2,1,0:T(8,128)(2,1)S(1)}, u32[]{:S(2)}, u32[]{:S(2)}) collective-permute-start(bf16[4,96,640]{2,1,0:T(8,128)(2,1)S(1)} %shard_map.306), channel_id=1, source_target_pairs={{0,4},{4,0},{8,12},{12,8},{16,20},{20,16},{24,28},{28,24},{1,5},{5... | collective-permute-start | bytes 1474568 | tf_op jit(solution)/shard_map/ppermute | solution.py:706
  29.5 9.1 %collective-permute-start.8 = (bf16[96,1152]{1,0:T(8,128)(2,1)S(1)}, bf16[96,1152]{1,0:T(8,128)(2,1)S(1)}, u32[]{:S(2)}, u32[]{:S(2)}) collective-permute-start(bf16[96,1152]{1,0:T(8,128)(2,1)S(1)} %bitcast.11), channel_id=1, source_target_pairs={{0,8},{4,12},{8,16},{12,20},{16,24},{20,28},{24,0},{28,4},{1,9},{5... | collective-permute-start | bytes 663560 | tf_op jit(solution)/shard_map/ppermute | solution.py:701
  30.7 7.8 %collective-permute-start = (bf16[128,768]{1,0:T(8,128)(2,1)S(1)}, bf16[128,768]{1,0:T(8,128)(2,1)S(1)}, u32[]{:S(2)}, u32[]{:S(2)}) collective-permute-start(bf16[128,768]{1,0:T(8,128)(2,1)S(1)} %copy-done.1), channel_id=1, source_target_pairs={{0,2},{1,3},{2,0},{3,1},{4,6},{5,7},{6,4},{7,5},{8,10},{9,11},{10,... | collective-permute-start | bytes 589832 | tf_op jit(solution)/shard_map/ppermute | solution.py:658
  33.2 16.8 %collective-permute-start.14 = (bf16[2,96,768]{2,1,0:T(8,128)(2,1)S(1)}, bf16[2,96,768]{2,1,0:T(8,128)(2,1)S(1)}, u32[]{:S(2)}, u32[]{:S(2)}) collective-permute-start(bf16[2,96,768]{2,1,0:T(8,128)(2,1)S(1)} %collective-permute-done.13.refs_1_), channel_id=1, source_target_pairs={{0,8},{4,12},{8,16},{12,20},{16,24},{20,28},{24,0},{28,4},{1,9},{5... | collective-permute-start | bytes 884744 | tf_op jit(solution)/shard_map/ppermute | solution.py:708
  38.5 10.9 %collective-permute-start.9 = (bf16[96,1152]{1,0:T(8,128)(2,1)S(1)}, bf16[96,1152]{1,0:T(8,128)(2,1)S(1)}, u32[]{:S(2)}, u32[]{:S(2)}) collective-permute-start(bf16[96,1152]{1,0:T(8,128)(2,1)S(1)} %collective-permute-done.8.refs_1_), channel_id=1, source_target_pairs={{0,8},{4,12},{8,16},{12,20},{16,24},{20,28},{24,0},{28,4},{1,9},{5... | collective-permute-start | bytes 663560 | tf_op jit(solution)/shard_map/ppermute | solution.py:707
  38.5 12.7 %collective-permute-start.1 = (bf16[128,768]{1,0:T(8,128)(2,1)S(1)}, bf16[128,768]{1,0:T(8,128)(2,1)S(1)}, u32[]{:S(2)}, u32[]{:S(2)}) collective-permute-start(bf16[128,768]{1,0:T(8,128)(2,1)S(1)} %copy-done.1), channel_id=1, source_target_pairs={{0,1},{1,0},{2,3},{3,2},{4,5},{5,4},{6,7},{7,6},{8,9},{9,8},{10,11... | collective-permute-start | bytes 589832 | tf_op jit(solution)/shard_map/ppermute | solution.py:659
  38.5 12.7 %collective-permute-start.2 = (bf16[128,768]{1,0:T(8,128)(2,1)S(1)}, bf16[128,768]{1,0:T(8,128)(2,1)S(1)}, u32[]{:S(2)}, u32[]{:S(2)}) collective-permute-start(bf16[128,768]{1,0:T(8,128)(2,1)S(1)} %collective-permute-done.refs_2_.refs_1_), channel_id=1, source_target_pairs={{0,1},{1,0},{2,3},{3,2},{4,5},{5,4},{6,7},{7,6},{8,9},{9,8},{10,11... | collective-permute-start | bytes 589832 | tf_op jit(solution)/shard_map/ppermute | solution.py:660
  49.4 10.8 %collective-permute-start.19 = (bf16[96,1152]{1,0:T(8,128)(2,1)S(1)}, bf16[96,1152]{1,0:T(8,128)(2,1)S(1)}, u32[]{:S(2)}, u32[]{:S(2)}) collective-permute-start(bf16[96,1152]{1,0:T(8,128)(2,1)S(1)} %collective-permute-done.9.refs_2_), channel_id=1, source_target_pairs={{0,4},{4,0},{8,12},{12,8},{16,20},{20,16},{24,28},{28,24},{1,5},{5... | collective-permute-start | bytes 663560 | tf_op jit(solution)/shard_map/ppermute | solution.py:738
  50.0 10.1 %collective-permute-start.17 = (bf16[96,1152]{1,0:T(8,128)(2,1)S(1)}, bf16[96,1152]{1,0:T(8,128)(2,1)S(1)}, u32[]{:S(2)}, u32[]{:S(2)}) collective-permute-start(bf16[96,1152]{1,0:T(8,128)(2,1)S(1)} %collective-permute-done.9.refs_2_), channel_id=1, source_target_pairs={{0,8},{4,12},{8,16},{12,20},{16,24},{20,28},{24,0},{28,4},{1,9},{5... | collective-permute-start | bytes 663560 | tf_op jit(solution)/shard_map/ppermute | solution.py:740
  50.0 15.4 %collective-permute-start.15 = (bf16[2,96,768]{2,1,0:T(8,128)(2,1)S(1)}, bf16[2,96,768]{2,1,0:T(8,128)(2,1)S(1)}, u32[]{:S(2)}, u32[]{:S(2)}) collective-permute-start(bf16[2,96,768]{2,1,0:T(8,128)(2,1)S(1)} %collective-permute-done.14.refs_2_), channel_id=1, source_target_pairs={{0,8},{4,12},{8,16},{12,20},{16,24},{20,28},{24,0},{28,4},{1,9},{5... | collective-permute-start | bytes 884744 | tf_op jit(solution)/shard_map/ppermute | solution.py:743
  56.3 9.0 %collective-permute-start.10 = (bf16[512,192]{1,0:T(8,128)(2,1)S(1)}, bf16[512,192]{1,0:T(8,128)(2,1)S(1)}, u32[]{:S(2)}, u32[]{:S(2)}) collective-permute-start(bf16[512,192]{1,0:T(8,128)(2,1)S(1)} %get-tuple-element.102.refs_2_.refs_0_), channel_id=1, source_target_pairs={{0,2},{1,3},{2,0},{3,1},{4,6},{5,7},{6,4},{7,5},{8,10},{9,11},{10,... | collective-permute-start | bytes 589832 | tf_op jit(solution)/shard_map/ppermute | solution.py:734
  57.3 10.5 %collective-permute-start.18 = (bf16[96,1152]{1,0:T(8,128)(2,1)S(1)}, bf16[96,1152]{1,0:T(8,128)(2,1)S(1)}, u32[]{:S(2)}, u32[]{:S(2)}) collective-permute-start(bf16[96,1152]{1,0:T(8,128)(2,1)S(1)} %collective-permute-done.8.refs_1_), channel_id=1, source_target_pairs={{0,4},{4,0},{8,12},{12,8},{16,20},{20,16},{24,28},{28,24},{1,5},{5... | collective-permute-start | bytes 663560 | tf_op jit(solution)/shard_map/ppermute | solution.py:737
  60.2 8.8 %collective-permute-start.20 = (bf16[96,1152]{1,0:T(8,128)(2,1)S(1)}, bf16[96,1152]{1,0:T(8,128)(2,1)S(1)}, u32[]{:S(2)}, u32[]{:S(2)}) collective-permute-start(bf16[96,1152]{1,0:T(8,128)(2,1)S(1)} %shard_map.308), channel_id=1, source_target_pairs={{0,4},{4,0},{8,12},{12,8},{16,20},{20,16},{24,28},{28,24},{1,5},{5... | collective-permute-start | bytes 663560 | tf_op jit(solution)/shard_map/ppermute | solution.py:742
  61.6 6.2 %collective-permute-start.21 = (bf16[128,768]{1,0:T(8,128)(2,1)S(1)}, bf16[128,768]{1,0:T(8,128)(2,1)S(1)}, u32[]{:S(2)}, u32[]{:S(2)}) collective-permute-start(bf16[128,768]{1,0:T(8,128)(2,1)S(1)} %copy-done.6), channel_id=1, source_target_pairs={{0,2},{1,3},{2,0},{3,1},{4,6},{5,7},{6,4},{7,5},{8,10},{9,11},{10,... | collective-permute-start | bytes 589832 | tf_op jit(solution)/shard_map/ppermute | solution.py:663
  65.4 3.5 %collective-permute-start.16 = (bf16[512,192]{1,0:T(8,128)(2,1)S(1)}, bf16[512,192]{1,0:T(8,128)(2,1)S(1)}, u32[]{:S(2)}, u32[]{:S(2)}) collective-permute-start(bf16[512,192]{1,0:T(8,128)(2,1)S(1)} %shard_map.307), channel_id=1, source_target_pairs={{0,1},{1,0},{2,3},{3,2},{4,5},{5,4},{6,7},{7,6},{8,9},{9,8},{10,11... | collective-permute-start | bytes 589832 | tf_op jit(solution)/shard_map/ppermute | solution.py:744
  69.1 2.4 %collective-permute-start.22 = (bf16[768,384]{1,0:T(8,128)(2,1)S(1)}, bf16[768,384]{1,0:T(8,128)(2,1)S(1)}, u32[]{:S(2)}, u32[]{:S(2)}) collective-permute-start(bf16[768,384]{1,0:T(8,128)(2,1)S(1)} %get-tuple-element.104.refs_6_.refs_2_), channel_id=1, source_target_pairs={{0,1},{1,0},{2,3},{3,2},{4,5},{5,4},{6,7},{7,6},{8,9},{9,8},{10,11... | collective-permute-start | bytes 1769480 | tf_op jit(solution)/shard_map/ppermute | solution.py:764
  69.2 2.4 %collective-permute-start.11 = (bf16[512,192]{1,0:T(8,128)(2,1)S(1)}, bf16[512,192]{1,0:T(8,128)(2,1)S(1)}, u32[]{:S(2)}, u32[]{:S(2)}) collective-permute-start(bf16[512,192]{1,0:T(8,128)(2,1)S(1)} %get-tuple-element.102.refs_2_.refs_0_), channel_id=1, source_target_pairs={{0,1},{1,0},{2,3},{3,2},{4,5},{5,4},{6,7},{7,6},{8,9},{9,8},{10,11... | collective-permute-start | bytes 589832 | tf_op jit(solution)/shard_map/ppermute | solution.py:735
  73.4 2.1 %collective-permute-start.23 = (bf16[256,768]{1,0:T(8,128)(2,1)S(1)}, bf16[256,768]{1,0:T(8,128)(2,1)S(1)}, u32[]{:S(2)}, u32[]{:S(2)}) collective-permute-start(bf16[256,768]{1,0:T(8,128)(2,1)S(1)} %get-tuple-element.108), channel_id=1, source_target_pairs={{0,1},{1,0},{2,3},{3,2},{4,5},{5,4},{6,7},{7,6},{8,9},{9,8},{10,11... | collective-permute-start | bytes 1179656 | tf_op jit(solution)/shard_map/ppermute | solution.py:789
  75.7 11.5 %collective-permute-start.24 = (bf16[256,768]{1,0:T(8,128)(2,1)S(1)}, bf16[256,768]{1,0:T(8,128)(2,1)S(1)}, u32[]{:S(2)}, u32[]{:S(2)}) collective-permute-start(bf16[256,768]{1,0:T(8,128)(2,1)S(1)} %get-tuple-element.110), channel_id=1, source_target_pairs={{0,2},{1,3},{2,0},{3,1},{4,6},{5,7},{6,4},{7,5},{8,10},{9,11},{10,... | collective-permute-start | bytes 1179656 | tf_op jit(solution)/shard_map/ppermute | solution.py:793
  88.3 1.7 %collective-permute-start.25 = (bf16[256,768]{1,0:T(8,128)(2,1)S(1)}, bf16[256,768]{1,0:T(8,128)(2,1)S(1)}, u32[]{:S(2)}, u32[]{:S(2)}) collective-permute-start(bf16[256,768]{1,0:T(8,128)(2,1)S(1)} %get-tuple-element.113.refs_0_.refs_2_), channel_id=1, source_target_pairs={{0,1},{1,0},{2,3},{3,2},{4,5},{5,4},{6,7},{7,6},{8,9},{9,8},{10,11... | collective-permute-start | bytes 1179656 | tf_op jit(solution)/shard_map/ppermute | solution.py:814
  91.0 1.8 %collective-permute-start.26 = (bf16[256,768]{1,0:T(8,128)(2,1)S(1)}, bf16[256,768]{1,0:T(8,128)(2,1)S(1)}, u32[]{:S(2)}, u32[]{:S(2)}) collective-permute-start(bf16[256,768]{1,0:T(8,128)(2,1)S(1)} %get-tuple-element.117), channel_id=1, source_target_pairs={{0,1},{1,0},{2,3},{3,2},{4,5},{5,4},{6,7},{7,6},{8,9},{9,8},{10,11... | collective-permute-start | bytes 1179656 | tf_op jit(solution)/shard_map/ppermute | solution.py:789
  92.9 12.3 %collective-permute-start.27 = (bf16[256,768]{1,0:T(8,128)(2,1)S(1)}, bf16[256,768]{1,0:T(8,128)(2,1)S(1)}, u32[]{:S(2)}, u32[]{:S(2)}) collective-permute-start(bf16[256,768]{1,0:T(8,128)(2,1)S(1)} %get-tuple-element.119), channel_id=1, source_target_pairs={{0,2},{1,3},{2,0},{3,1},{4,6},{5,7},{6,4},{7,5},{8,10},{9,11},{10,... | collective-permute-start | bytes 1179656 | tf_op jit(solution)/shard_map/ppermute | solution.py:793
  94.5 10.6 %collective-permute-start.28 = (bf16[2,96,768]{2,1,0:T(8,128)(2,1)S(1)}, bf16[2,96,768]{2,1,0:T(8,128)(2,1)S(1)}, u32[]{:S(2)}, u32[]{:S(2)}) collective-permute-start(bf16[2,96,768]{2,1,0:T(8,128)(2,1)S(1)} %get-tuple-element.129.refs_4_), channel_id=1, source_target_pairs={{0,8},{4,12},{8,16},{12,20},{16,24},{20,28},{24,0},{28,4},{1,9},{5... | collective-permute-start | bytes 884744 | tf_op jit(solution)/shard_map/ppermute | solution.py:854
  95.7 17.1 %collective-permute-start.31 = (bf16[4,96,768]{2,1,0:T(8,128)(2,1)S(1)}, bf16[4,96,768]{2,1,0:T(8,128)(2,1)S(1)}, u32[]{:S(2)}, u32[]{:S(2)}) collective-permute-start(bf16[4,96,768]{2,1,0:T(8,128)(2,1)S(1)} %get-tuple-element.130.refs_6_), channel_id=1, source_target_pairs={{0,4},{4,0},{8,12},{12,8},{16,20},{20,16},{24,28},{28,24},{1,5},{5... | collective-permute-start | bytes 1769480 | tf_op jit(solution)/shard_map/ppermute | solution.py:867
  105.7 1.8 %collective-permute-start.29 = (bf16[256,768]{1,0:T(8,128)(2,1)S(1)}, bf16[256,768]{1,0:T(8,128)(2,1)S(1)}, u32[]{:S(2)}, u32[]{:S(2)}) collective-permute-start(bf16[256,768]{1,0:T(8,128)(2,1)S(1)} %get-tuple-element.131.refs_2_.refs_4_.refs_0_), channel_id=1, source_target_pairs={{0,1},{1,0},{2,3},{3,2},{4,5},{5,4},{6,7},{7,6},{8,9},{9,8},{10,11... | collective-permute-start | bytes 1179656 | tf_op jit(solution)/shard_map/ppermute | solution.py:885
  106.4 11.7 %collective-permute-start.30 = (bf16[2,96,768]{2,1,0:T(8,128)(2,1)S(1)}, bf16[2,96,768]{2,1,0:T(8,128)(2,1)S(1)}, u32[]{:S(2)}, u32[]{:S(2)}) collective-permute-start(bf16[2,96,768]{2,1,0:T(8,128)(2,1)S(1)} %z_step.2.refs_6_), channel_id=1, source_target_pairs={{0,8},{4,12},{8,16},{12,20},{16,24},{20,28},{24,0},{28,4},{1,9},{5... | collective-permute-start | bytes 884744 | tf_op jit(solution)/shard_map/ppermute | solution.py:895
  108.3 12.6 %collective-permute-start.32 = (bf16[4,96,192]{2,1,0:T(8,128)(2,1)S(1)}, bf16[4,96,192]{2,1,0:T(8,128)(2,1)S(1)}, u32[]{:S(2)}, u32[]{:S(2)}) collective-permute-start(bf16[4,96,192]{2,1,0:T(8,128)(2,1)S(1)} %get-tuple-element.135.refs_6_), channel_id=1, source_target_pairs={{0,4},{4,0},{8,12},{12,8},{16,20},{20,16},{24,28},{28,24},{1,5},{5... | collective-permute-start | bytes 442376 | tf_op jit(solution)/shard_map/ppermute | solution.py:948
  113.9 15.5 %collective-permute-start.36 = (bf16[4,96,384]{2,1,0:T(8,128)(2,1)S(1)}, bf16[4,96,384]{2,1,0:T(8,128)(2,1)S(1)}, u32[]{:S(2)}, u32[]{:S(2)}) collective-permute-start(bf16[4,96,384]{2,1,0:T(8,128)(2,1)S(1)} %get-tuple-element.151), channel_id=1, source_target_pairs={{0,4},{4,0},{8,12},{12,8},{16,20},{20,16},{24,28},{28,24},{1,5},{5... | collective-permute-start | bytes 884744 | tf_op jit(solution)/shard_map/ppermute | solution.py:947
  114.5 14.9 %collective-permute-start.37 = (bf16[4,96,256]{2,1,0:T(8,128)(2,1)S(1)}, bf16[4,96,256]{2,1,0:T(8,128)(2,1)S(1)}, u32[]{:S(2)}, u32[]{:S(2)}) collective-permute-start(bf16[4,96,256]{2,1,0:T(8,128)(2,1)S(1)} %get-tuple-element.142.refs_2_), channel_id=1, source_target_pairs={{0,4},{4,0},{8,12},{12,8},{16,20},{20,16},{24,28},{28,24},{1,5},{5... | collective-permute-start | bytes 589832 | tf_op jit(solution)/shard_map/ppermute | solution.py:947
  116.0 10.9 %collective-permute-start.39 = (bf16[96,768]{1,0:T(8,128)(2,1)S(1)}, bf16[96,768]{1,0:T(8,128)(2,1)S(1)}, u32[]{:S(2)}, u32[]{:S(2)}) collective-permute-start(bf16[96,768]{1,0:T(8,128)(2,1)S(1)} %get-tuple-element.153), channel_id=1, source_target_pairs={{0,16},{4,20},{8,24},{12,28},{16,0},{20,4},{24,8},{28,12},{1,17},{... | collective-permute-start | bytes 442376 | tf_op jit(solution)/shard_map/ppermute | solution.py:951
  118.1 9.7 %collective-permute-start.40 = (bf16[96,768]{1,0:T(8,128)(2,1)S(1)}, bf16[96,768]{1,0:T(8,128)(2,1)S(1)}, u32[]{:S(2)}, u32[]{:S(2)}) collective-permute-start(bf16[96,768]{1,0:T(8,128)(2,1)S(1)} %get-tuple-element.154), channel_id=1, source_target_pairs={{0,24},{4,28},{8,0},{12,4},{16,8},{20,12},{24,16},{28,20},{1,25},{... | collective-permute-start | bytes 442376 | tf_op jit(solution)/shard_map/ppermute | solution.py:951
  121.0 7.6 %collective-permute-start.38 = (bf16[96,768]{1,0:T(8,128)(2,1)S(1)}, bf16[96,768]{1,0:T(8,128)(2,1)S(1)}, u32[]{:S(2)}, u32[]{:S(2)}) collective-permute-start(bf16[96,768]{1,0:T(8,128)(2,1)S(1)} %get-tuple-element.141.refs_9_), channel_id=1, source_target_pairs={{0,8},{4,12},{8,16},{12,20},{16,24},{20,28},{24,0},{28,4},{1,9},{5... | collective-permute-start | bytes 442376 | tf_op jit(solution)/shard_map/ppermute | solution.py:951
  126.9 11.0 %collective-permute-start.34 = (bf16[2,96,768]{2,1,0:T(8,128)(2,1)S(1)}, bf16[2,96,768]{2,1,0:T(8,128)(2,1)}, u32[]{:S(2)}, u32[]{:S(2)}) collective-permute-start(bf16[2,96,768]{2,1,0:T(8,128)(2,1)S(1)} %z_step.3.refs_2_), channel_id=1, source_target_pairs={{0,8},{4,12},{8,16},{12,20},{16,24},{20,28},{24,0},{28,4},{1,9},{5... | collective-permute-start | bytes 884744 | tf_op jit(solution)/shard_map/ppermute | solution.py:895
  127.8 11.1 %collective-permute-start.33 = (bf16[256,768]{1,0:T(8,128)(2,1)}, bf16[256,768]{1,0:T(8,128)(2,1)}, u32[]{:S(2)}, u32[]{:S(2)}) collective-permute-start(bf16[256,768]{1,0:T(8,128)(2,1)} %get-tuple-element.144), channel_id=1, source_target_pairs={{0,1},{1,0},{2,3},{3,2},{4,5},{5,4},{6,7},{7,6},{8,9},{9,8},{10,11... | collective-permute-start | bytes 1179656 | tf_op jit(solution)/shard_map/ppermute | solution.py:962
  130.4 23.6 %all-to-all-start.1 = ((bf16[16,24,832]{2,1,0:T(8,128)(2,1)}), bf16[16,24,832]{2,1,0:T(8,128)(2,1)S(1)}, u32[]{:S(2)}, u32[]{:S(2)}) async-start(bf16[16,24,832]{2,1,0:T(8,128)(2,1)} %bitcast.5), calls=%async_computation.1 | async-start | bytes 1376256 | tf_op jit(solution)/shard_map/all_to_all | solution.py:582
  140.0 10.3 %collective-permute-start.35 = (bf16[128,768]{1,0:T(8,128)(2,1)S(1)}, bf16[128,768]{1,0:T(8,128)(2,1)S(1)}, u32[]{:S(2)}, u32[]{:S(2)}) collective-permute-start(bf16[128,768]{1,0:T(8,128)(2,1)S(1)} %get-tuple-element.148), channel_id=1, source_target_pairs={{0,2},{1,3},{2,0},{3,1},{4,6},{5,7},{6,4},{7,5},{8,10},{9,11},{10,... | collective-permute-start | bytes 589832 | tf_op jit(solution)/shard_map/ppermute | solution.py:981
  141.4 5.5 %collective-permute-start.41 = (bf16[96,768]{1,0:T(8,128)(2,1)S(1)}, bf16[96,768]{1,0:T(8,128)(2,1)S(1)}, u32[]{:S(2)}, u32[]{:S(2)}) collective-permute-start(bf16[96,768]{1,0:T(8,128)(2,1)S(1)} %get-tuple-element.146.refs_3_), channel_id=1, source_target_pairs={{0,4},{4,0},{8,12},{12,8},{16,20},{20,16},{24,28},{28,24},{1,5},{5... | collective-permute-start | bytes 442376 | tf_op jit(solution)/shard_map/ppermute | solution.py:989
  147.0 4.0 %collective-permute-start.42 = (bf16[24,768]{1,0:T(8,128)(2,1)S(1)}, bf16[24,768]{1,0:T(8,128)(2,1)S(1)}, u32[]{:S(2)}, u32[]{:S(2)}) collective-permute-start(bf16[24,768]{1,0:T(8,128)(2,1)S(1)} %get-tuple-element.166), channel_id=1, source_target_pairs={{0,1},{1,0},{2,3},{3,2},{4,5},{5,4},{6,7},{7,6},{8,9},{9,8},{10,11... | collective-permute-start | bytes 110600 | tf_op jit(solution)/shard_map/ppermute | solution.py:995
  147.1 4.3 %collective-permute-start.43 = (bf16[24,768]{1,0:T(8,128)(2,1)S(1)}, bf16[24,768]{1,0:T(8,128)(2,1)S(1)}, u32[]{:S(2)}, u32[]{:S(2)}) collective-permute-start(bf16[24,768]{1,0:T(8,128)(2,1)S(1)} %get-tuple-element.167), channel_id=1, source_target_pairs={{0,2},{1,3},{2,0},{3,1},{4,6},{5,7},{6,4},{7,5},{8,10},{9,11},{10,... | collective-permute-start | bytes 110600 | tf_op jit(solution)/shard_map/ppermute | solution.py:995
  147.5 3.9 %collective-permute-start.44 = (bf16[24,768]{1,0:T(8,128)(2,1)S(1)}, bf16[24,768]{1,0:T(8,128)(2,1)S(1)}, u32[]{:S(2)}, u32[]{:S(2)}) collective-permute-start(bf16[24,768]{1,0:T(8,128)(2,1)S(1)} %get-tuple-element.168), channel_id=1, source_target_pairs={{0,3},{1,2},{2,1},{3,0},{4,7},{5,6},{6,5},{7,4},{8,11},{9,10},{10,... | collective-permute-start | bytes 110600 | tf_op jit(solution)/shard_map/ppermute | solution.py:995
  (10 other events, 46.3 us)

commit v7 on v6

--- a/solution.py
+++ b/solution.py
@@ -337,7 +337,7 @@
     here = lax.axis_index("head")
     o_bias, a_gain, a_shift, u_bias = [bias[i : i + 1, :] for i in (2, 3, 4, 8)]
     total = jnp.concatenate([x0[...], x1[...]], axis=0).astype(F32) + o_bias
-    sums = [jnp.zeros((mine, near.shape[1]), F32)] * 2
+    parts, spots = [], []
 
     def pick(ref, order):
         order = order[2 * half : 2 * half + 2]
@@ -350,8 +350,12 @@
         (3, ctx_far, (3, 2, 1, 0)),
     ):
         at = pl.multiple_of((here ^ flip) * share, 64)
-        part = pick(ref, order)
-        sums = [t + dot(part, w[pl.ds(at, share), :]) for t, w in zip(sums, (near, other))]
+        parts.append(pick(ref, order))
+        spots.append(pl.ds(at, share))
+    part = jnp.concatenate(parts, axis=1)
+    sums = [
+        dot(part, jnp.concatenate([w[spot, :] for spot in spots], axis=0)) for w in (near, other)
+    ]
     total = total + jnp.concatenate(in_order(*sums), axis=1)
     unit, rate = norm_stats(total)
     normed = unit * a_gain + a_shift

time: 156 us -> 155 us (level)
  transfers between devices with their start and end apart: 47 -> 47, of which waited for: 24 -> 23; matrix products, arithmetic and copies ran while one was open for 0% -> 0% of each run, Pallas kernels for 15% -> 14%
where the time goes in v7:
time: 155 us
  waiting for transfers between devices  72.9 us (47%)
  starting transfers between devices  47.3 us (31%)
  Pallas kernels  30.1 us (19%)
  local copies, waits for them, and re-layouts  3.39 us (2%)
    pallas_call x31, Pallas kernels, call(): pl.pallas_call(run, out_shape=outs, in_specs=[spec] * count + [pl.BlockSp...  27.5 us
    all_to_all x2, starting transfers between devices, to_owners(): lax.all_to_all(summed.reshape(16 * rows, columns), ALL, 0, 0, tiled=True,...  14 us
    ppermute x2, waiting for transfers between devices, pair_sum(): return (kept, lax.ppermute(low, 'head', CHIP))  10.7 us
    ppermute x1, waiting for transfers between devices, body(): have.append(lax.ppermute(have[1], 'dp', zshift(1)))  10.3 us
    ppermute x1, waiting for transfers between devices, body(): up_got = [lax.ppermute(up_run, 'dp', zshift(1))]  7.87 us
    ppermute x1, waiting for transfers between devices, body(): have = [wide, lax.ppermute(wide, 'dp', zshift(1))]  5.3 us
    ppermute x3, starting transfers between devices, body(): lax.ppermute(later(o, *order) if ZLATE == k else o, 'dp', zshift(k))  4.99 us
    ppermute x3, waiting for transfers between devices, body(): lax.ppermute(later(o, *order) if ZLATE == k else o, 'dp', zshift(k))  4.89 us
  transfers between devices with their start and end apart: 47, of which 23 were waited for; matrix products, arithmetic and copies ran while one was open for 0% of the time, Pallas kernels for 14%

profile of v7, /device:TPU:0, one launch (start us, length us, event | category | flops | bytes accessed | tf_op | source)
XLA Modules:
  0.0 154.9 jit_solution(9709527551750917334)
XLA Ops:
  0.7 2.5 %shard_map.305 = (bf16[4,4,24,640]{3,2,1,0:T(8,128)(2,1)}, bf16[24,1152]{1,0:T(8,128)(2,1)}, bf16[24,1152]{1,0:T(8,128)(2,1)}, bf16[24,1152]{1,0:T(8,128)(2,1)},...) custom-call(f32[24,768]{1,0:T(8,128)} %query.1, f32[24,768]{1,0:T(8,128)} %key.1, f32[24,768]{1,0:T(8,128)} %value.1, ...), custom_call_target="tpu_custom_call" | custom-call | tf_op jit(solution)/shard_map/pallas_call | solution.py:197
  3.2 7.5 %all-to-all-start = ((bf16[16,24,640]{2,1,0:T(8,128)(2,1)}), bf16[16,24,640]{2,1,0:T(8,128)(2,1)S(1)}, u32[]{:S(2)}, u32[]{:S(2)}) async-start(bf16[16,24,640]{2,1,0:T(8,128)(2,1)} %bitcast.16), calls=%async_computation | async-start | bytes 983040 | tf_op jit(solution)/shard_map/all_to_all | solution.py:586
  11.1 1.7 %collective-permute-start.4 = (bf16[24,1152]{1,0:T(8,128)(2,1)}, bf16[24,1152]{1,0:T(8,128)(2,1)S(1)}, u32[]{:S(2)}, u32[]{:S(2)}) collective-permute-start(bf16[24,1152]{1,0:T(8,128)(2,1)} %get-tuple-element.98), channel_id=1, source_target_pairs={{0,2},{1,3},{2,0},{3,1},{4,6},{5,7},{6,4},{7,5},{8,10},{9,11},{10,... | collective-permute-start | bytes 165896 | tf_op jit(solution)/shard_map/ppermute | solution.py:683
  12.8 1.5 collective-permute-start.12
  14.3 4.5 %collective-permute-done.4.refs_2_ = bf16[24,1152]{1,0:T(8,128)(2,1)S(1)} collective-permute-done((bf16[24,1152]{1,0:T(8,128)(2,1)}, bf16[24,1152]{1,0:T(8,128)(2,1)S(1)}, u32[]{:S(2)}, u32[]{:S(2)}) %collective-permute-start.4) | collective-permute-done | bytes 55328 | tf_op jit(solution)/shard_map/ppermute | solution.py:683
  19.9 1.6 %collective-permute-start.6 = (bf16[96,1152]{1,0:T(8,128)(2,1)S(1)}, bf16[96,1152]{1,0:T(8,128)(2,1)S(1)}, u32[]{:S(2)}, u32[]{:S(2)}) collective-permute-start(bf16[96,1152]{1,0:T(8,128)(2,1)S(1)} %bitcast.10), channel_id=1, source_target_pairs={{0,4},{4,0},{8,12},{12,8},{16,20},{20,16},{24,28},{28,24},{1,5},{5... | collective-permute-start | bytes 663560 | tf_op jit(solution)/shard_map/ppermute | solution.py:707
  21.5 1.4 collective-permute-start.13
  22.9 1.6 %all-to-all-done = bf16[16,24,640]{2,1,0:T(8,128)(2,1)S(1)} async-done(((bf16[16,24,640]{2,1,0:T(8,128)(2,1)}), bf16[16,24,640]{2,1,0:T(8,128)(2,1)S(1)}, u32[]{:S(2)}, u32[]{:S(2)}) %all-to-all-start) | async-done | bytes 491552 | tf_op jit(solution)/shard_map/all_to_all | solution.py:586
  24.6 3.4 %collective-permute-done.6.refs_1_.refs_4_ = bf16[96,1152]{1,0:T(8,128)(2,1)S(1)} collective-permute-done((bf16[96,1152]{1,0:T(8,128)(2,1)S(1)}, bf16[96,1152]{1,0:T(8,128)(2,1)S(1)}, u32[]{:S(2)}, u32[]{:S(2)}) %collective-permute-start.6) | collective-permute-done | bytes 221216 | tf_op jit(solution)/shard_map/ppermute | solution.py:707
  28.0 1.5 collective-permute-start.7
  29.5 1.3 collective-permute-start.8
  30.8 2.5 %collective-permute-done.13.refs_1_ = bf16[2,96,768]{2,1,0:T(8,128)(2,1)S(1)} collective-permute-done((bf16[2,96,768]{2,1,0:T(8,128)(2,1)S(1)}, bf16[2,96,768]{2,1,0:T(8,128)(2,1)S(1)}, u32[]{:S(2)}, u32[]{:S(2)}) %collective-permute-start.13) | collective-permute-done | bytes 294944 | tf_op jit(solution)/shard_map/ppermute | solution.py:706
  33.2 5.3 %collective-permute-done.8.refs_1_ = bf16[96,1152]{1,0:T(8,128)(2,1)S(1)} collective-permute-done((bf16[96,1152]{1,0:T(8,128)(2,1)S(1)}, bf16[96,1152]{1,0:T(8,128)(2,1)S(1)}, u32[]{:S(2)}, u32[]{:S(2)}) %collective-permute-start.8) | collective-permute-done | bytes 221216 | tf_op jit(solution)/shard_map/ppermute | solution.py:705
  39.1 10.3 %collective-permute-done.9.refs_2_ = bf16[96,1152]{1,0:T(8,128)(2,1)S(1)} collective-permute-done((bf16[96,1152]{1,0:T(8,128)(2,1)S(1)}, bf16[96,1152]{1,0:T(8,128)(2,1)S(1)}, u32[]{:S(2)}, u32[]{:S(2)}) %collective-permute-start.9) | collective-permute-done | bytes 221216 | tf_op jit(solution)/shard_map/ppermute | solution.py:711
  50.0 1.0 collective-permute-start.15
  51.3 5.1 %attend.1 = (bf16[512,576]{1,0:T(8,128)(2,1)S(1)}, f32[3,512,512]{2,1,0:T(8,128)S(1)}, bf16[512,192]{1,0:T(8,128)(2,1)S(1)}, f32[16,768]{1,0:T(8,128)S(1)}) custom-call(s32[4,128]{1,0:T(4,128)S(1)} %bitcast.15, bf16[128,768]{1,0:T(8,128)(2,1)S(1)} %copy-done.1, bf16[128,768]{1,0:T(8,128)(2,1)S(1)} %collective-permute-done.refs_2_.refs_1_, ...), custom_call_target="tpu_custom_call" | custom-call | flops 1500000000 | bytes 4500000 | tf_op jit(solution)/shard_map/attend/pallas_call | solution.py:41
  56.3 1.0 collective-permute-start.10
  57.3 1.5 collective-permute-start.18
  58.9 1.3 collective-permute-done.17.refs_3_
  60.2 1.5 collective-permute-start.20
  62.3 3.1 %collective-permute-done.10.refs_3_.refs_1_ = bf16[512,192]{1,0:T(8,128)(2,1)S(1)} collective-permute-done((bf16[512,192]{1,0:T(8,128)(2,1)S(1)}, bf16[512,192]{1,0:T(8,128)(2,1)S(1)}, u32[]{:S(2)}, u32[]{:S(2)}) %collective-permute-start.10) | collective-permute-done | bytes 196640 | tf_op jit(solution)/shard_map/ppermute | solution.py:738
  65.5 2.3 %collective-permute-done.21.refs_9_.refs_4_ = bf16[128,768]{1,0:T(8,128)(2,1)S(1)} collective-permute-done((bf16[128,768]{1,0:T(8,128)(2,1)S(1)}, bf16[128,768]{1,0:T(8,128)(2,1)S(1)}, u32[]{:S(2)}, u32[]{:S(2)}) %collective-permute-start.21) | collective-permute-done | bytes 196640 | tf_op jit(solution)/shard_map/ppermute | solution.py:667
  67.8 1.1 collective-permute-done.20.refs_7_
  69.8 1.8 %collective-permute-done.11.refs_4_.refs_2_ = bf16[512,192]{1,0:T(8,128)(2,1)S(1)} collective-permute-done((bf16[512,192]{1,0:T(8,128)(2,1)S(1)}, bf16[512,192]{1,0:T(8,128)(2,1)S(1)}, u32[]{:S(2)}, u32[]{:S(2)}) %collective-permute-start.11) | collective-permute-done | bytes 196640 | tf_op jit(solution)/shard_map/ppermute | solution.py:739
  71.5 1.8 %ffn.3 = (bf16[256,768]{1,0:T(8,128)(2,1)S(1)}, bf16[256,768]{1,0:T(8,128)(2,1)S(1)}, f32[256,768]{1,0:T(8,128)S(1)}, bf16[256,768]{1,0:T(8,128)(2,1)S(1)}) custom-call(bf16[128,768]{1,0:T(8,128)(2,1)S(1)} %collective-permute-done.1.refs_3_.refs_0_.refs_2_, bf16[128,768]{1,0:T(8,128)(2,1)S(1)} %collective-permute-done.2.refs_4_.refs_1_.refs_3_, ...), custom_call_target="tpu_custom_call" | custom-call | flops 570000000 | bytes 1709999 | tf_op jit(solution)/shard_map/ffn/pallas_call | solution.py:41
  73.5 1.8 %ffn.2 = (bf16[256,768]{1,0:T(8,128)(2,1)S(1)}, bf16[256,768]{1,0:T(8,128)(2,1)S(1)}, f32[256,768]{1,0:T(8,128)S(1)}, f32[256,768]{1,0:T(8,128)S(1)}, f32[256,76...) custom-call(bf16[128,768]{1,0:T(8,128)(2,1)S(1)} %copy-done.1, ...), custom_call_target="tpu_custom_call" | custom-call | flops 570000000 | bytes 1709999 | tf_op jit(solution)/shard_map/ffn/pallas_call | solution.py:41
  76.2 10.7 %collective-permute-done.24.refs_1_ = bf16[256,768]{1,0:T(8,128)(2,1)S(1)} collective-permute-done((bf16[256,768]{1,0:T(8,128)(2,1)S(1)}, bf16[256,768]{1,0:T(8,128)(2,1)S(1)}, u32[]{:S(2)}, u32[]{:S(2)}) %collective-permute-start.24) | collective-permute-done | bytes 393248 | tf_op jit(solution)/shard_map/ppermute | solution.py:797
  86.9 1.2 final.1
  88.1 1.7 %collective-permute-done.25.refs_0_.refs_3_ = bf16[256,768]{1,0:T(8,128)(2,1)S(1)} collective-permute-done((bf16[256,768]{1,0:T(8,128)(2,1)S(1)}, bf16[256,768]{1,0:T(8,128)(2,1)S(1)}, u32[]{:S(2)}, u32[]{:S(2)}) %collective-permute-start.25) | collective-permute-done | bytes 393248 | tf_op jit(solution)/shard_map/ppermute | solution.py:818
  95.7 1.6 %collective-permute-start.31 = (bf16[4,96,768]{2,1,0:T(8,128)(2,1)S(1)}, bf16[4,96,768]{2,1,0:T(8,128)(2,1)S(1)}, u32[]{:S(2)}, u32[]{:S(2)}) collective-permute-start(bf16[4,96,768]{2,1,0:T(8,128)(2,1)S(1)} %get-tuple-element.130.refs_6_), channel_id=1, source_target_pairs={{0,4},{4,0},{8,12},{12,8},{16,20},{20,16},{24,28},{28,24},{1,5},{5... | collective-permute-start | bytes 1769480 | tf_op jit(solution)/shard_map/ppermute | solution.py:871
  97.3 7.9 %collective-permute-done.28.refs_7_.refs_1_ = bf16[2,96,768]{2,1,0:T(8,128)(2,1)S(1)} collective-permute-done((bf16[2,96,768]{2,1,0:T(8,128)(2,1)S(1)}, bf16[2,96,768]{2,1,0:T(8,128)(2,1)S(1)}, u32[]{:S(2)}, u32[]{:S(2)}) %collective-permute-start.28) | collective-permute-done | bytes 294944 | tf_op jit(solution)/shard_map/ppermute | solution.py:858
  106.4 1.0 collective-permute-done.29.refs_5_.refs_1_
  108.3 1.5 collective-permute-start.32
  109.9 3.0 %attend_back.1.refs_2_.refs_4_.refs_0_ = bf16[512,576]{1,0:T(8,128)(2,1)S(1)} custom-call(bf16[256,768]{1,0:T(8,128)(2,1)S(1)} %get-tuple-element.131.refs_2_.refs_4_.refs_0_, bf16[256,768]{1,0:T(8,128)(2,1)S(1)} %collective-permute-done.29.refs_5_.refs_1_, bf16[768,384]{1,0:T(8,128)(2,1)S(1)} %get-tuple-element.104.refs_6_.refs_2_, ...), custom_call_target="tpu_custom_call" | custom-call | flops 900000000 | bytes 2699999 | tf_op jit(solution)/shard_map/attend_back/pallas_call | solution.py:41
  114.5 1.5 collective-permute-start.37
  115.9 2.2 %collective-permute-start.39 = (bf16[96,768]{1,0:T(8,128)(2,1)S(1)}, bf16[96,768]{1,0:T(8,128)(2,1)S(1)}, u32[]{:S(2)}, u32[]{:S(2)}) collective-permute-start(bf16[96,768]{1,0:T(8,128)(2,1)S(1)} %get-tuple-element.153), channel_id=1, source_target_pairs={{0,16},{4,20},{8,24},{12,28},{16,0},{20,4},{24,8},{28,12},{1,17},{... | collective-permute-start | bytes 442376 | tf_op jit(solution)/shard_map/ppermute | solution.py:955
  118.1 2.8 %collective-permute-start.40 = (bf16[96,768]{1,0:T(8,128)(2,1)S(1)}, bf16[96,768]{1,0:T(8,128)(2,1)S(1)}, u32[]{:S(2)}, u32[]{:S(2)}) collective-permute-start(bf16[96,768]{1,0:T(8,128)(2,1)S(1)} %get-tuple-element.154), channel_id=1, source_target_pairs={{0,24},{4,28},{8,0},{12,4},{16,8},{20,12},{24,16},{28,20},{1,25},{... | collective-permute-start | bytes 442376 | tf_op jit(solution)/shard_map/ppermute | solution.py:955
  121.0 1.6 %input_grad.1 = (f32[256,768]{1,0:T(8,128)S(1)}, bf16[256,768]{1,0:T(8,128)(2,1)}) custom-call(bf16[512,576]{1,0:T(8,128)(2,1)S(1)} %attend_back.1.refs_2_.refs_4_.refs_0_, bf16[768,576]{1,0:T(8,128)(2,1)S(1)} %get-tuple-element.100.refs_5_.refs_1_, bf16[2,96,768]{2,1,0:T(8,128)(2,1)S(1)} %z_step.3.refs_2_), custom_call_target="tpu_custom_call" | custom-call | flops 240000000 | bytes 720000 | tf_op jit(solution)/shard_map/input_grad/pallas_call | solution.py:41
  123.5 4.9 %collective-permute-done.39.refs_2_ = bf16[96,768]{1,0:T(8,128)(2,1)S(1)} collective-permute-done((bf16[96,768]{1,0:T(8,128)(2,1)S(1)}, bf16[96,768]{1,0:T(8,128)(2,1)S(1)}, u32[]{:S(2)}, u32[]{:S(2)}) %collective-permute-start.39) | collective-permute-done | bytes 147488 | tf_op jit(solution)/shard_map/ppermute | solution.py:955
  129.2 1.0 sum_two.1.refs_0_
  130.2 6.5 %all-to-all-start.1 = ((bf16[16,24,832]{2,1,0:T(8,128)(2,1)}), bf16[16,24,832]{2,1,0:T(8,128)(2,1)S(1)}, u32[]{:S(2)}, u32[]{:S(2)}) async-start(bf16[16,24,832]{2,1,0:T(8,128)(2,1)} %bitcast.5), calls=%async_computation.1 | async-start | bytes 1376256 | tf_op jit(solution)/shard_map/all_to_all | solution.py:586
  136.7 1.1 collective-permute-done.34.refs_1_
  137.8 1.0 z_sum.1
  138.8 1.1 input_add.1
  139.9 1.3 collective-permute-start.35
  141.9 4.9 %collective-permute-done.41.refs_1_ = bf16[96,768]{1,0:T(8,128)(2,1)S(1)} collective-permute-done((bf16[96,768]{1,0:T(8,128)(2,1)S(1)}, bf16[96,768]{1,0:T(8,128)(2,1)S(1)}, u32[]{:S(2)}, u32[]{:S(2)}) %collective-permute-start.41) | collective-permute-done | bytes 147488 | tf_op jit(solution)/shard_map/ppermute | solution.py:993
  147.4 1.4 collective-permute-start.44
  148.7 1.3 collective-permute-done.35.refs_1_
  (107 shorter events, 22.9 us)
Async XLA Ops:
  3.2 21.3 %all-to-all-start = ((bf16[16,24,640]{2,1,0:T(8,128)(2,1)}), bf16[16,24,640]{2,1,0:T(8,128)(2,1)S(1)}, u32[]{:S(2)}, u32[]{:S(2)}) async-start(bf16[16,24,640]{2,1,0:T(8,128)(2,1)} %bitcast.16), calls=%async_computation | async-start | bytes 983040 | tf_op jit(solution)/shard_map/all_to_all | solution.py:586
  10.7 3.6 %collective-permute-start.3 = (bf16[24,1152]{1,0:T(8,128)(2,1)}, bf16[24,1152]{1,0:T(8,128)(2,1)S(1)}, u32[]{:S(2)}, u32[]{:S(2)}) collective-permute-start(bf16[24,1152]{1,0:T(8,128)(2,1)} %get-tuple-element.97), channel_id=1, source_target_pairs={{0,1},{1,0},{2,3},{3,2},{4,5},{5,4},{6,7},{7,6},{8,9},{9,8},{10,11... | collective-permute-start | bytes 165896 | tf_op jit(solution)/shard_map/ppermute | solution.py:683
  11.1 7.7 %collective-permute-start.4 = (bf16[24,1152]{1,0:T(8,128)(2,1)}, bf16[24,1152]{1,0:T(8,128)(2,1)S(1)}, u32[]{:S(2)}, u32[]{:S(2)}) collective-permute-start(bf16[24,1152]{1,0:T(8,128)(2,1)} %get-tuple-element.98), channel_id=1, source_target_pairs={{0,2},{1,3},{2,0},{3,1},{4,6},{5,7},{6,4},{7,5},{8,10},{9,11},{10,... | collective-permute-start | bytes 165896 | tf_op jit(solution)/shard_map/ppermute | solution.py:683
  12.8 6.2 %collective-permute-start.5 = (bf16[24,1152]{1,0:T(8,128)(2,1)}, bf16[24,1152]{1,0:T(8,128)(2,1)S(1)}, u32[]{:S(2)}, u32[]{:S(2)}) collective-permute-start(bf16[24,1152]{1,0:T(8,128)(2,1)} %get-tuple-element.99), channel_id=1, source_target_pairs={{0,3},{1,2},{2,1},{3,0},{4,7},{5,6},{6,5},{7,4},{8,11},{9,10},{10,... | collective-permute-start | bytes 165896 | tf_op jit(solution)/shard_map/ppermute | solution.py:683
  12.8 8.6 %collective-permute-start.12 = (bf16[96,768]{1,0:T(8,128)(2,1)}, bf16[96,768]{1,0:T(8,128)(2,1)S(1)}, u32[]{:S(2)}, u32[]{:S(2)}) collective-permute-start(bf16[96,768]{1,0:T(8,128)(2,1)} %bitcast.13), channel_id=1, source_target_pairs={{0,4},{4,0},{8,12},{12,8},{16,20},{20,16},{24,28},{28,24},{1,5},{5... | collective-permute-start | bytes 442376 | tf_op jit(solution)/shard_map/ppermute | solution.py:695
  19.9 8.1 %collective-permute-start.6 = (bf16[96,1152]{1,0:T(8,128)(2,1)S(1)}, bf16[96,1152]{1,0:T(8,128)(2,1)S(1)}, u32[]{:S(2)}, u32[]{:S(2)}) collective-permute-start(bf16[96,1152]{1,0:T(8,128)(2,1)S(1)} %bitcast.10), channel_id=1, source_target_pairs={{0,4},{4,0},{8,12},{12,8},{16,20},{20,16},{24,28},{28,24},{1,5},{5... | collective-permute-start | bytes 663560 | tf_op jit(solution)/shard_map/ppermute | solution.py:707
  21.5 11.8 %collective-permute-start.13 = (bf16[2,96,768]{2,1,0:T(8,128)(2,1)S(1)}, bf16[2,96,768]{2,1,0:T(8,128)(2,1)S(1)}, u32[]{:S(2)}, u32[]{:S(2)}) collective-permute-start(bf16[2,96,768]{2,1,0:T(8,128)(2,1)S(1)} %pair.1.refs_0_), channel_id=1, source_target_pairs={{0,8},{4,12},{8,16},{12,20},{16,24},{20,28},{24,0},{28,4},{1,9},{5... | collective-permute-start | bytes 884744 | tf_op jit(solution)/shard_map/ppermute | solution.py:706
  24.6 26.7 %copy-start.10 = (s32[512]{0:T(512)S(1)}, s32[512]{0:T(512)}, u32[]{:S(2)}) copy-start(s32[512]{0:T(512)} %param.19) | copy-start | bytes 6148
  28.0 22.0 %collective-permute-start.7 = (bf16[4,96,640]{2,1,0:T(8,128)(2,1)S(1)}, bf16[4,96,640]{2,1,0:T(8,128)(2,1)S(1)}, u32[]{:S(2)}, u32[]{:S(2)}) collective-permute-start(bf16[4,96,640]{2,1,0:T(8,128)(2,1)S(1)} %shard_map.306), channel_id=1, source_target_pairs={{0,4},{4,0},{8,12},{12,8},{16,20},{20,16},{24,28},{28,24},{1,5},{5... | collective-permute-start | bytes 1474568 | tf_op jit(solution)/shard_map/ppermute | solution.py:710
  29.5 9.1 %collective-permute-start.8 = (bf16[96,1152]{1,0:T(8,128)(2,1)S(1)}, bf16[96,1152]{1,0:T(8,128)(2,1)S(1)}, u32[]{:S(2)}, u32[]{:S(2)}) collective-permute-start(bf16[96,1152]{1,0:T(8,128)(2,1)S(1)} %bitcast.11), channel_id=1, source_target_pairs={{0,8},{4,12},{8,16},{12,20},{16,24},{20,28},{24,0},{28,4},{1,9},{5... | collective-permute-start | bytes 663560 | tf_op jit(solution)/shard_map/ppermute | solution.py:705
  30.7 7.8 %collective-permute-start = (bf16[128,768]{1,0:T(8,128)(2,1)S(1)}, bf16[128,768]{1,0:T(8,128)(2,1)S(1)}, u32[]{:S(2)}, u32[]{:S(2)}) collective-permute-start(bf16[128,768]{1,0:T(8,128)(2,1)S(1)} %copy-done.1), channel_id=1, source_target_pairs={{0,2},{1,3},{2,0},{3,1},{4,6},{5,7},{6,4},{7,5},{8,10},{9,11},{10,... | collective-permute-start | bytes 589832 | tf_op jit(solution)/shard_map/ppermute | solution.py:662
  33.2 16.8 %collective-permute-start.14 = (bf16[2,96,768]{2,1,0:T(8,128)(2,1)S(1)}, bf16[2,96,768]{2,1,0:T(8,128)(2,1)S(1)}, u32[]{:S(2)}, u32[]{:S(2)}) collective-permute-start(bf16[2,96,768]{2,1,0:T(8,128)(2,1)S(1)} %collective-permute-done.13.refs_1_), channel_id=1, source_target_pairs={{0,8},{4,12},{8,16},{12,20},{16,24},{20,28},{24,0},{28,4},{1,9},{5... | collective-permute-start | bytes 884744 | tf_op jit(solution)/shard_map/ppermute | solution.py:712
  38.5 10.9 %collective-permute-start.9 = (bf16[96,1152]{1,0:T(8,128)(2,1)S(1)}, bf16[96,1152]{1,0:T(8,128)(2,1)S(1)}, u32[]{:S(2)}, u32[]{:S(2)}) collective-permute-start(bf16[96,1152]{1,0:T(8,128)(2,1)S(1)} %collective-permute-done.8.refs_1_), channel_id=1, source_target_pairs={{0,8},{4,12},{8,16},{12,20},{16,24},{20,28},{24,0},{28,4},{1,9},{5... | collective-permute-start | bytes 663560 | tf_op jit(solution)/shard_map/ppermute | solution.py:711
  38.5 12.7 %collective-permute-start.1 = (bf16[128,768]{1,0:T(8,128)(2,1)S(1)}, bf16[128,768]{1,0:T(8,128)(2,1)S(1)}, u32[]{:S(2)}, u32[]{:S(2)}) collective-permute-start(bf16[128,768]{1,0:T(8,128)(2,1)S(1)} %copy-done.1), channel_id=1, source_target_pairs={{0,1},{1,0},{2,3},{3,2},{4,5},{5,4},{6,7},{7,6},{8,9},{9,8},{10,11... | collective-permute-start | bytes 589832 | tf_op jit(solution)/shard_map/ppermute | solution.py:663
  38.5 12.7 %collective-permute-start.2 = (bf16[128,768]{1,0:T(8,128)(2,1)S(1)}, bf16[128,768]{1,0:T(8,128)(2,1)S(1)}, u32[]{:S(2)}, u32[]{:S(2)}) collective-permute-start(bf16[128,768]{1,0:T(8,128)(2,1)S(1)} %collective-permute-done.refs_2_.refs_1_), channel_id=1, source_target_pairs={{0,1},{1,0},{2,3},{3,2},{4,5},{5,4},{6,7},{7,6},{8,9},{9,8},{10,11... | collective-permute-start | bytes 589832 | tf_op jit(solution)/shard_map/ppermute | solution.py:664
  49.4 10.8 %collective-permute-start.19 = (bf16[96,1152]{1,0:T(8,128)(2,1)S(1)}, bf16[96,1152]{1,0:T(8,128)(2,1)S(1)}, u32[]{:S(2)}, u32[]{:S(2)}) collective-permute-start(bf16[96,1152]{1,0:T(8,128)(2,1)S(1)} %collective-permute-done.9.refs_2_), channel_id=1, source_target_pairs={{0,4},{4,0},{8,12},{12,8},{16,20},{20,16},{24,28},{28,24},{1,5},{5... | collective-permute-start | bytes 663560 | tf_op jit(solution)/shard_map/ppermute | solution.py:742
  50.0 10.1 %collective-permute-start.17 = (bf16[96,1152]{1,0:T(8,128)(2,1)S(1)}, bf16[96,1152]{1,0:T(8,128)(2,1)S(1)}, u32[]{:S(2)}, u32[]{:S(2)}) collective-permute-start(bf16[96,1152]{1,0:T(8,128)(2,1)S(1)} %collective-permute-done.9.refs_2_), channel_id=1, source_target_pairs={{0,8},{4,12},{8,16},{12,20},{16,24},{20,28},{24,0},{28,4},{1,9},{5... | collective-permute-start | bytes 663560 | tf_op jit(solution)/shard_map/ppermute | solution.py:744
  50.0 15.4 %collective-permute-start.15 = (bf16[2,96,768]{2,1,0:T(8,128)(2,1)S(1)}, bf16[2,96,768]{2,1,0:T(8,128)(2,1)S(1)}, u32[]{:S(2)}, u32[]{:S(2)}) collective-permute-start(bf16[2,96,768]{2,1,0:T(8,128)(2,1)S(1)} %collective-permute-done.14.refs_2_), channel_id=1, source_target_pairs={{0,8},{4,12},{8,16},{12,20},{16,24},{20,28},{24,0},{28,4},{1,9},{5... | collective-permute-start | bytes 884744 | tf_op jit(solution)/shard_map/ppermute | solution.py:747
  56.3 9.0 %collective-permute-start.10 = (bf16[512,192]{1,0:T(8,128)(2,1)S(1)}, bf16[512,192]{1,0:T(8,128)(2,1)S(1)}, u32[]{:S(2)}, u32[]{:S(2)}) collective-permute-start(bf16[512,192]{1,0:T(8,128)(2,1)S(1)} %get-tuple-element.102.refs_2_.refs_0_), channel_id=1, source_target_pairs={{0,2},{1,3},{2,0},{3,1},{4,6},{5,7},{6,4},{7,5},{8,10},{9,11},{10,... | collective-permute-start | bytes 589832 | tf_op jit(solution)/shard_map/ppermute | solution.py:738
  57.3 10.5 %collective-permute-start.18 = (bf16[96,1152]{1,0:T(8,128)(2,1)S(1)}, bf16[96,1152]{1,0:T(8,128)(2,1)S(1)}, u32[]{:S(2)}, u32[]{:S(2)}) collective-permute-start(bf16[96,1152]{1,0:T(8,128)(2,1)S(1)} %collective-permute-done.8.refs_1_), channel_id=1, source_target_pairs={{0,4},{4,0},{8,12},{12,8},{16,20},{20,16},{24,28},{28,24},{1,5},{5... | collective-permute-start | bytes 663560 | tf_op jit(solution)/shard_map/ppermute | solution.py:741
  60.2 8.8 %collective-permute-start.20 = (bf16[96,1152]{1,0:T(8,128)(2,1)S(1)}, bf16[96,1152]{1,0:T(8,128)(2,1)S(1)}, u32[]{:S(2)}, u32[]{:S(2)}) collective-permute-start(bf16[96,1152]{1,0:T(8,128)(2,1)S(1)} %shard_map.308), channel_id=1, source_target_pairs={{0,4},{4,0},{8,12},{12,8},{16,20},{20,16},{24,28},{28,24},{1,5},{5... | collective-permute-start | bytes 663560 | tf_op jit(solution)/shard_map/ppermute | solution.py:746
  61.6 6.2 %collective-permute-start.21 = (bf16[128,768]{1,0:T(8,128)(2,1)S(1)}, bf16[128,768]{1,0:T(8,128)(2,1)S(1)}, u32[]{:S(2)}, u32[]{:S(2)}) collective-permute-start(bf16[128,768]{1,0:T(8,128)(2,1)S(1)} %copy-done.6), channel_id=1, source_target_pairs={{0,2},{1,3},{2,0},{3,1},{4,6},{5,7},{6,4},{7,5},{8,10},{9,11},{10,... | collective-permute-start | bytes 589832 | tf_op jit(solution)/shard_map/ppermute | solution.py:667
  65.4 3.5 %collective-permute-start.16 = (bf16[512,192]{1,0:T(8,128)(2,1)S(1)}, bf16[512,192]{1,0:T(8,128)(2,1)S(1)}, u32[]{:S(2)}, u32[]{:S(2)}) collective-permute-start(bf16[512,192]{1,0:T(8,128)(2,1)S(1)} %shard_map.307), channel_id=1, source_target_pairs={{0,1},{1,0},{2,3},{3,2},{4,5},{5,4},{6,7},{7,6},{8,9},{9,8},{10,11... | collective-permute-start | bytes 589832 | tf_op jit(solution)/shard_map/ppermute | solution.py:748
  69.1 2.4 %collective-permute-start.22 = (bf16[768,384]{1,0:T(8,128)(2,1)S(1)}, bf16[768,384]{1,0:T(8,128)(2,1)S(1)}, u32[]{:S(2)}, u32[]{:S(2)}) collective-permute-start(bf16[768,384]{1,0:T(8,128)(2,1)S(1)} %get-tuple-element.104.refs_6_.refs_2_), channel_id=1, source_target_pairs={{0,1},{1,0},{2,3},{3,2},{4,5},{5,4},{6,7},{7,6},{8,9},{9,8},{10,11... | collective-permute-start | bytes 1769480 | tf_op jit(solution)/shard_map/ppermute | solution.py:768
  69.2 2.4 %collective-permute-start.11 = (bf16[512,192]{1,0:T(8,128)(2,1)S(1)}, bf16[512,192]{1,0:T(8,128)(2,1)S(1)}, u32[]{:S(2)}, u32[]{:S(2)}) collective-permute-start(bf16[512,192]{1,0:T(8,128)(2,1)S(1)} %get-tuple-element.102.refs_2_.refs_0_), channel_id=1, source_target_pairs={{0,1},{1,0},{2,3},{3,2},{4,5},{5,4},{6,7},{7,6},{8,9},{9,8},{10,11... | collective-permute-start | bytes 589832 | tf_op jit(solution)/shard_map/ppermute | solution.py:739
  73.3 2.0 %collective-permute-start.23 = (bf16[256,768]{1,0:T(8,128)(2,1)S(1)}, bf16[256,768]{1,0:T(8,128)(2,1)S(1)}, u32[]{:S(2)}, u32[]{:S(2)}) collective-permute-start(bf16[256,768]{1,0:T(8,128)(2,1)S(1)} %get-tuple-element.108), channel_id=1, source_target_pairs={{0,1},{1,0},{2,3},{3,2},{4,5},{5,4},{6,7},{7,6},{8,9},{9,8},{10,11... | collective-permute-start | bytes 1179656 | tf_op jit(solution)/shard_map/ppermute | solution.py:793
  75.5 11.5 %collective-permute-start.24 = (bf16[256,768]{1,0:T(8,128)(2,1)S(1)}, bf16[256,768]{1,0:T(8,128)(2,1)S(1)}, u32[]{:S(2)}, u32[]{:S(2)}) collective-permute-start(bf16[256,768]{1,0:T(8,128)(2,1)S(1)} %get-tuple-element.110), channel_id=1, source_target_pairs={{0,2},{1,3},{2,0},{3,1},{4,6},{5,7},{6,4},{7,5},{8,10},{9,11},{10,... | collective-permute-start | bytes 1179656 | tf_op jit(solution)/shard_map/ppermute | solution.py:797
  88.1 1.7 %collective-permute-start.25 = (bf16[256,768]{1,0:T(8,128)(2,1)S(1)}, bf16[256,768]{1,0:T(8,128)(2,1)S(1)}, u32[]{:S(2)}, u32[]{:S(2)}) collective-permute-start(bf16[256,768]{1,0:T(8,128)(2,1)S(1)} %get-tuple-element.113.refs_0_.refs_2_), channel_id=1, source_target_pairs={{0,1},{1,0},{2,3},{3,2},{4,5},{5,4},{6,7},{7,6},{8,9},{9,8},{10,11... | collective-permute-start | bytes 1179656 | tf_op jit(solution)/shard_map/ppermute | solution.py:818
  90.8 1.8 %collective-permute-start.26 = (bf16[256,768]{1,0:T(8,128)(2,1)S(1)}, bf16[256,768]{1,0:T(8,128)(2,1)S(1)}, u32[]{:S(2)}, u32[]{:S(2)}) collective-permute-start(bf16[256,768]{1,0:T(8,128)(2,1)S(1)} %get-tuple-element.117), channel_id=1, source_target_pairs={{0,1},{1,0},{2,3},{3,2},{4,5},{5,4},{6,7},{7,6},{8,9},{9,8},{10,11... | collective-permute-start | bytes 1179656 | tf_op jit(solution)/shard_map/ppermute | solution.py:793
  92.7 12.5 %collective-permute-start.27 = (bf16[256,768]{1,0:T(8,128)(2,1)S(1)}, bf16[256,768]{1,0:T(8,128)(2,1)S(1)}, u32[]{:S(2)}, u32[]{:S(2)}) collective-permute-start(bf16[256,768]{1,0:T(8,128)(2,1)S(1)} %get-tuple-element.119), channel_id=1, source_target_pairs={{0,2},{1,3},{2,0},{3,1},{4,6},{5,7},{6,4},{7,5},{8,10},{9,11},{10,... | collective-permute-start | bytes 1179656 | tf_op jit(solution)/shard_map/ppermute | solution.py:797
  94.3 10.8 %collective-permute-start.28 = (bf16[2,96,768]{2,1,0:T(8,128)(2,1)S(1)}, bf16[2,96,768]{2,1,0:T(8,128)(2,1)S(1)}, u32[]{:S(2)}, u32[]{:S(2)}) collective-permute-start(bf16[2,96,768]{2,1,0:T(8,128)(2,1)S(1)} %get-tuple-element.129.refs_4_), channel_id=1, source_target_pairs={{0,8},{4,12},{8,16},{12,20},{16,24},{20,28},{24,0},{28,4},{1,9},{5... | collective-permute-start | bytes 884744 | tf_op jit(solution)/shard_map/ppermute | solution.py:858
  95.7 17.2 %collective-permute-start.31 = (bf16[4,96,768]{2,1,0:T(8,128)(2,1)S(1)}, bf16[4,96,768]{2,1,0:T(8,128)(2,1)S(1)}, u32[]{:S(2)}, u32[]{:S(2)}) collective-permute-start(bf16[4,96,768]{2,1,0:T(8,128)(2,1)S(1)} %get-tuple-element.130.refs_6_), channel_id=1, source_target_pairs={{0,4},{4,0},{8,12},{12,8},{16,20},{20,16},{24,28},{28,24},{1,5},{5... | collective-permute-start | bytes 1769480 | tf_op jit(solution)/shard_map/ppermute | solution.py:871
  105.6 1.8 %collective-permute-start.29 = (bf16[256,768]{1,0:T(8,128)(2,1)S(1)}, bf16[256,768]{1,0:T(8,128)(2,1)S(1)}, u32[]{:S(2)}, u32[]{:S(2)}) collective-permute-start(bf16[256,768]{1,0:T(8,128)(2,1)S(1)} %get-tuple-element.131.refs_2_.refs_4_.refs_0_), channel_id=1, source_target_pairs={{0,1},{1,0},{2,3},{3,2},{4,5},{5,4},{6,7},{7,6},{8,9},{9,8},{10,11... | collective-permute-start | bytes 1179656 | tf_op jit(solution)/shard_map/ppermute | solution.py:889
  106.4 11.7 %collective-permute-start.30 = (bf16[2,96,768]{2,1,0:T(8,128)(2,1)S(1)}, bf16[2,96,768]{2,1,0:T(8,128)(2,1)S(1)}, u32[]{:S(2)}, u32[]{:S(2)}) collective-permute-start(bf16[2,96,768]{2,1,0:T(8,128)(2,1)S(1)} %z_step.2.refs_6_), channel_id=1, source_target_pairs={{0,8},{4,12},{8,16},{12,20},{16,24},{20,28},{24,0},{28,4},{1,9},{5... | collective-permute-start | bytes 884744 | tf_op jit(solution)/shard_map/ppermute | solution.py:899
  108.3 12.6 %collective-permute-start.32 = (bf16[4,96,192]{2,1,0:T(8,128)(2,1)S(1)}, bf16[4,96,192]{2,1,0:T(8,128)(2,1)S(1)}, u32[]{:S(2)}, u32[]{:S(2)}) collective-permute-start(bf16[4,96,192]{2,1,0:T(8,128)(2,1)S(1)} %get-tuple-element.135.refs_6_), channel_id=1, source_target_pairs={{0,4},{4,0},{8,12},{12,8},{16,20},{20,16},{24,28},{28,24},{1,5},{5... | collective-permute-start | bytes 442376 | tf_op jit(solution)/shard_map/ppermute | solution.py:952
  113.9 15.4 %collective-permute-start.36 = (bf16[4,96,384]{2,1,0:T(8,128)(2,1)S(1)}, bf16[4,96,384]{2,1,0:T(8,128)(2,1)S(1)}, u32[]{:S(2)}, u32[]{:S(2)}) collective-permute-start(bf16[4,96,384]{2,1,0:T(8,128)(2,1)S(1)} %get-tuple-element.151), channel_id=1, source_target_pairs={{0,4},{4,0},{8,12},{12,8},{16,20},{20,16},{24,28},{28,24},{1,5},{5... | collective-permute-start | bytes 884744 | tf_op jit(solution)/shard_map/ppermute | solution.py:951
  114.5 14.8 %collective-permute-start.37 = (bf16[4,96,256]{2,1,0:T(8,128)(2,1)S(1)}, bf16[4,96,256]{2,1,0:T(8,128)(2,1)S(1)}, u32[]{:S(2)}, u32[]{:S(2)}) collective-permute-start(bf16[4,96,256]{2,1,0:T(8,128)(2,1)S(1)} %get-tuple-element.142.refs_2_), channel_id=1, source_target_pairs={{0,4},{4,0},{8,12},{12,8},{16,20},{20,16},{24,28},{28,24},{1,5},{5... | collective-permute-start | bytes 589832 | tf_op jit(solution)/shard_map/ppermute | solution.py:951
  115.9 12.5 %collective-permute-start.39 = (bf16[96,768]{1,0:T(8,128)(2,1)S(1)}, bf16[96,768]{1,0:T(8,128)(2,1)S(1)}, u32[]{:S(2)}, u32[]{:S(2)}) collective-permute-start(bf16[96,768]{1,0:T(8,128)(2,1)S(1)} %get-tuple-element.153), channel_id=1, source_target_pairs={{0,16},{4,20},{8,24},{12,28},{16,0},{20,4},{24,8},{28,12},{1,17},{... | collective-permute-start | bytes 442376 | tf_op jit(solution)/shard_map/ppermute | solution.py:955
  118.1 10.3 %collective-permute-start.40 = (bf16[96,768]{1,0:T(8,128)(2,1)S(1)}, bf16[96,768]{1,0:T(8,128)(2,1)S(1)}, u32[]{:S(2)}, u32[]{:S(2)}) collective-permute-start(bf16[96,768]{1,0:T(8,128)(2,1)S(1)} %get-tuple-element.154), channel_id=1, source_target_pairs={{0,24},{4,28},{8,0},{12,4},{16,8},{20,12},{24,16},{28,20},{1,25},{... | collective-permute-start | bytes 442376 | tf_op jit(solution)/shard_map/ppermute | solution.py:955
  120.9 7.5 %collective-permute-start.38 = (bf16[96,768]{1,0:T(8,128)(2,1)S(1)}, bf16[96,768]{1,0:T(8,128)(2,1)S(1)}, u32[]{:S(2)}, u32[]{:S(2)}) collective-permute-start(bf16[96,768]{1,0:T(8,128)(2,1)S(1)} %get-tuple-element.141.refs_9_), channel_id=1, source_target_pairs={{0,8},{4,12},{8,16},{12,20},{16,24},{20,28},{24,0},{28,4},{1,9},{5... | collective-permute-start | bytes 442376 | tf_op jit(solution)/shard_map/ppermute | solution.py:955
  128.4 9.4 %collective-permute-start.34 = (bf16[2,96,768]{2,1,0:T(8,128)(2,1)S(1)}, bf16[2,96,768]{2,1,0:T(8,128)(2,1)}, u32[]{:S(2)}, u32[]{:S(2)}) collective-permute-start(bf16[2,96,768]{2,1,0:T(8,128)(2,1)S(1)} %z_step.3.refs_2_), channel_id=1, source_target_pairs={{0,8},{4,12},{8,16},{12,20},{16,24},{20,28},{24,0},{28,4},{1,9},{5... | collective-permute-start | bytes 884744 | tf_op jit(solution)/shard_map/ppermute | solution.py:899
  128.4 10.4 %collective-permute-start.33 = (bf16[256,768]{1,0:T(8,128)(2,1)}, bf16[256,768]{1,0:T(8,128)(2,1)}, u32[]{:S(2)}, u32[]{:S(2)}) collective-permute-start(bf16[256,768]{1,0:T(8,128)(2,1)} %get-tuple-element.144), channel_id=1, source_target_pairs={{0,1},{1,0},{2,3},{3,2},{4,5},{5,4},{6,7},{7,6},{8,9},{9,8},{10,11... | collective-permute-start | bytes 1179656 | tf_op jit(solution)/shard_map/ppermute | solution.py:966
  130.2 23.6 %all-to-all-start.1 = ((bf16[16,24,832]{2,1,0:T(8,128)(2,1)}), bf16[16,24,832]{2,1,0:T(8,128)(2,1)S(1)}, u32[]{:S(2)}, u32[]{:S(2)}) async-start(bf16[16,24,832]{2,1,0:T(8,128)(2,1)} %bitcast.5), calls=%async_computation.1 | async-start | bytes 1376256 | tf_op jit(solution)/shard_map/all_to_all | solution.py:586
  139.9 10.1 %collective-permute-start.35 = (bf16[128,768]{1,0:T(8,128)(2,1)S(1)}, bf16[128,768]{1,0:T(8,128)(2,1)S(1)}, u32[]{:S(2)}, u32[]{:S(2)}) collective-permute-start(bf16[128,768]{1,0:T(8,128)(2,1)S(1)} %get-tuple-element.148), channel_id=1, source_target_pairs={{0,2},{1,3},{2,0},{3,1},{4,6},{5,7},{6,4},{7,5},{8,10},{9,11},{10,... | collective-permute-start | bytes 589832 | tf_op jit(solution)/shard_map/ppermute | solution.py:985
  141.2 5.5 %collective-permute-start.41 = (bf16[96,768]{1,0:T(8,128)(2,1)S(1)}, bf16[96,768]{1,0:T(8,128)(2,1)S(1)}, u32[]{:S(2)}, u32[]{:S(2)}) collective-permute-start(bf16[96,768]{1,0:T(8,128)(2,1)S(1)} %get-tuple-element.146.refs_3_), channel_id=1, source_target_pairs={{0,4},{4,0},{8,12},{12,8},{16,20},{20,16},{24,28},{28,24},{1,5},{5... | collective-permute-start | bytes 442376 | tf_op jit(solution)/shard_map/ppermute | solution.py:993
  146.8 4.0 %collective-permute-start.42 = (bf16[24,768]{1,0:T(8,128)(2,1)S(1)}, bf16[24,768]{1,0:T(8,128)(2,1)S(1)}, u32[]{:S(2)}, u32[]{:S(2)}) collective-permute-start(bf16[24,768]{1,0:T(8,128)(2,1)S(1)} %get-tuple-element.166), channel_id=1, source_target_pairs={{0,1},{1,0},{2,3},{3,2},{4,5},{5,4},{6,7},{7,6},{8,9},{9,8},{10,11... | collective-permute-start | bytes 110600 | tf_op jit(solution)/shard_map/ppermute | solution.py:999
  146.9 4.3 %collective-permute-start.43 = (bf16[24,768]{1,0:T(8,128)(2,1)S(1)}, bf16[24,768]{1,0:T(8,128)(2,1)S(1)}, u32[]{:S(2)}, u32[]{:S(2)}) collective-permute-start(bf16[24,768]{1,0:T(8,128)(2,1)S(1)} %get-tuple-element.167), channel_id=1, source_target_pairs={{0,2},{1,3},{2,0},{3,1},{4,6},{5,7},{6,4},{7,5},{8,10},{9,11},{10,... | collective-permute-start | bytes 110600 | tf_op jit(solution)/shard_map/ppermute | solution.py:999
  147.4 3.8 %collective-permute-start.44 = (bf16[24,768]{1,0:T(8,128)(2,1)S(1)}, bf16[24,768]{1,0:T(8,128)(2,1)S(1)}, u32[]{:S(2)}, u32[]{:S(2)}) collective-permute-start(bf16[24,768]{1,0:T(8,128)(2,1)S(1)} %get-tuple-element.168), channel_id=1, source_target_pairs={{0,3},{1,2},{2,1},{3,0},{4,7},{5,6},{6,5},{7,4},{8,11},{9,10},{10,... | collective-permute-start | bytes 110600 | tf_op jit(solution)/shard_map/ppermute | solution.py:999
  (10 other events, 46.6 us)
